TPU v7x, 32 devices: a whole 2x2x4 slice. The times are simulated.
32 devices in a mesh: crops: 2 (over x), row: 4 (over z), col: 4 (over y, core).
Axes of the slice: x: 2, y: 2, z: 4, core: 2. Of those that a mesh axis runs over, the one named last changes fastest.
Arguments:
- pair_state: bfloat16 [384, 192, 128], P(('crops', 'row'), 'col'), parts along dimension 0, may hold values from -6 to 6
- token_count: int32 [2], P('crops'), parts along dimension 0, may hold values from 96 to 192
- in_gain: float32 [128], replicated, may hold values from 0.1 to 1.9
- in_bias: float32 [128], replicated, may hold values from -3 to 3
- in_weights: bfloat16 [128, 512], replicated, may hold values from -0.5 to 0.5
- gate_weights: bfloat16 [128, 128], replicated, may hold values from -0.5 to 0.5
- out_gain: float32 [128], replicated, may hold values from 0.1 to 1.9
- out_bias: float32 [128], replicated, may hold values from -3 to 3
- out_weights: bfloat16 [128, 128], replicated, may hold values from -0.5 to 0.5
Outputs:
- update: bfloat16 [384, 192, 128], P(('crops', 'row'), 'col'), parts along dimension 0
There are 2 independent parts, one for each index of `crops`. A program takes and returns all parts, laid end to end along the dimension named above; an argument that names none is the same for every part. Nothing has to cross between parts.
Inputs may be any that keep to these rules, and one draw needn't show every extreme that they name: Tokens from index token_count on are padding.
All inputs are finite; a program needn't handle non-finite values.
Results may differ from a plain program's by a relative error of at most 0.0057.
Values may be sent and summed in bfloat16 or wider, within the bound.
No kernel may reach another device: no remote copies, remote signals or barrier semaphores. Data moves between devices by JAX's collectives and lax.ppermute only.
A program may use at most 128 MiB of HBM per device.

v0:
```python
import jax
import jax.numpy as jnp
from jax import lax
from jax.sharding import PartitionSpec as P


def shifted(array, axis, by):
    devices = lax.axis_size(axis)
    return lax.ppermute(array, axis, [(i, (i + by) % devices) for i in range(devices)])


def from_root(array, axis, root):
    mine = lax.axis_index(axis) == root
    return lax.psum(jnp.where(mine, array, jnp.zeros_like(array)), axis)


def layer_norm(values, gain, offset):
    average = jnp.mean(values, axis=-1, keepdims=True)
    centered = values - average
    variance = jnp.mean(centered * centered, axis=-1, keepdims=True)
    return centered * lax.rsqrt(variance + 1e-05) * gain + offset


def contract(summed, left_piece, right_piece):
    return summed + jnp.einsum(
        "ikh,jkh->ijh", left_piece, right_piece, preferred_element_type=jnp.float32
    )


def on_device(
    pair_state,
    token_count,
    in_gain,
    in_bias,
    in_weights,
    gate_weights,
    out_gain,
    out_bias,
    out_weights,
):
    rows_here, cols_here, channels = pair_state.shape
    hidden = out_weights.shape[0]
    col_count = lax.axis_size("col")
    row_count = lax.axis_size("row")
    blocks_per_row = col_count // row_count
    window = col_count // 2
    row_pos = lax.axis_index("row")
    col_pos = lax.axis_index("col")
    normed = layer_norm(pair_state.astype(jnp.float32), in_gain, in_bias).astype(jnp.bfloat16)
    flat_normed = normed.reshape(rows_here * cols_here, channels)
    projected = jnp.dot(flat_normed, in_weights, preferred_element_type=jnp.float32).reshape(
        rows_here, cols_here, 4, hidden
    )
    row_tokens = row_pos * rows_here + jnp.arange(rows_here, dtype=jnp.int32)
    col_tokens = col_pos * cols_here + jnp.arange(cols_here, dtype=jnp.int32)
    row_valid = (row_tokens < token_count[0]).astype(jnp.float32)
    col_valid = (col_tokens < token_count[0]).astype(jnp.float32)
    pair_mask = (row_valid[:, None] * col_valid[None, :])[:, :, None]
    left_factor = (pair_mask * jax.nn.sigmoid(projected[:, :, 0]) * projected[:, :, 1]).astype(
        jnp.bfloat16
    )
    right_factor = (pair_mask * jax.nn.sigmoid(projected[:, :, 2]) * projected[:, :, 3]).astype(
        jnp.bfloat16
    )
    out_gate = jax.nn.sigmoid(
        jnp.dot(flat_normed, gate_weights, preferred_element_type=jnp.float32)
    )
    summed = jnp.zeros((rows_here, cols_here, hidden), jnp.float32)
    carried = left_factor
    for offset in range(window):
        if offset > 0:
            carried = shifted(carried, "col", -1)
        root_row = (col_pos - offset) % col_count // blocks_per_row
        block_id = (col_pos - offset) % col_count
        start = block_id % blocks_per_row * cols_here
        received = from_root(
            lax.dynamic_slice_in_dim(right_factor, start, cols_here, 0), "row", root_row
        )
        right_piece = received if offset == 0 else shifted(received, "col", -offset)
        summed = contract(summed, carried, right_piece)
    mixed = layer_norm(summed, out_gain, out_bias).astype(jnp.bfloat16)
    projected_out = jnp.dot(
        mixed.reshape(rows_here * cols_here, hidden),
        out_weights,
        preferred_element_type=jnp.float32,
    )
    return (out_gate * projected_out).astype(jnp.bfloat16).reshape(rows_here, cols_here, channels)


def solution(mesh):
    placed = (P(("crops", "row"), "col", None), P("crops"), P(), P(), P(), P(), P(), P(), P())
    return jax.shard_map(
        on_device,
        mesh=mesh,
        in_specs=placed,
        out_specs=P(("crops", "row"), "col", None),
        check_vma=False,
    )
```

profile of v0, /device:TPU:1, one launch (start us, length us, event | category | flops | bytes accessed | tf_op | source)
XLA Modules:
  0.0 104.4 jit_solution(2022652236472056523)
XLA Ops:
  6.5 0.0 all-reduce.3.cloned.1.call-start
  7.3 1.4 %convert_reduce_fusion = f32[48,48]{1,0:T(8,128)S(1)} fusion(bf16[48,48,128]{2,1,0:T(8,128)(2,1)} %param.9), kind=kLoop, calls=%fused_computation.12 | loop fusion | flops 587520 | bytes 599040 | tf_op jit(solution)/shard_map/reduce_sum | solution.py:18
  8.8 1.8 %fusion.6 = f32[48,48]{1,0:T(8,128)S(1)} fusion(bf16[48,48,128]{2,1,0:T(8,128)(2,1)} %param.9, f32[48,48]{1,0:T(8,128)S(1)} %broadcast_multiply_fusion.2), kind=kLoop, calls=%fused_computation.15 | loop fusion | flops 1177344 | bytes 608256 | tf_op jit(solution)/shard_map/reduce_sum | solution.py:20
  10.6 0.1 copy.56
  10.7 0.1 broadcast_multiply_fusion
  10.8 0.8 fusion.9
  11.6 0.8 fusion.26
  12.4 2.1 %copy-done.1 = f32[48,48,4,128]{3,1,2,0:T(8,128)} copy-done((f32[48,48,4,128]{3,1,2,0:T(8,128)}, f32[48,48,4,128]{3,1,2,0:T(8,128)S(1)}, u32[]{:S(2)}) %copy-start.1) | copy-done | bytes 4718616
  14.5 1.3 %broadcast_select_fusion = (bf16[48,48,128]{2,1,0:T(8,128)(2,1)}, bf16[48,48,128]{2,1,0:T(8,128)(2,1)S(1)}) fusion(pred[]{:T(512)S(6)} %eq.14, f32[48,48,4,128]{3,1,2,0:T(8,128)S(1)} %fusion.26, f32[48,48]{1,0:T(8,128)S(1)} %broadcast_multiply_fusion), kind=kLoop, calls=%fused_computation.41 | loop fusion | flops 2064384 | bytes 3548161 | tf_op jit(solution)/shard_map/jit(_where)/select_n | solution.py:14
  15.8 0.9 broadcast_select_fusion.1
  16.7 0.0 all-reduce.3.cloned.1.call-update
  16.7 2.0 %fusion.11 = bf16[48,48,128]{2,1,0:T(8,128)(2,1)S(1)} fusion(f32[48,48,4,128]{3,1,2,0:T(8,128)} %copy-done.1, f32[48,48]{1,0:T(8,128)S(1)} %broadcast_multiply_fusion), kind=kLoop, calls=%fused_computation.21 | loop fusion | flops 1769472 | bytes 2958336 | tf_op jit(solution)/shard_map/convert_element_type | solution.py:59
  18.7 0.1 collective-permute-start.1
  18.8 1.0 copy.47
  19.8 55.6 %all-reduce.3.cloned.1.call-done = (bf16[48,48,128]{2,1,0:T(8,128)(2,1)}, bf16[48,48,128]{2,1,0:T(8,128)(2,1)}) async-done(((bf16[48,48,128]{2,1,0:T(8,128)(2,1)}, bf16[48,48,128]{2,1,0:T(8,128)(2,1)}), (bf16[48,48,128]{2,1,0:T(8,128)(2,1)}, bf16[48,48,128]{2,1,0:T(8,128)(2,1)})) %all-reduce.3.cloned.1.call-update) | async-done | bytes 1179664 | tf_op jit(solution)/shard_map/psum | solution.py:14
  75.4 0.5 collective-permute-start
  75.9 1.5 %fusion.2 = f32[2304,128]{1,0:T(8,128)} fusion(bf16[2304,128]{1,0:T(8,128)(2,1)S(1)} %bitcast.91, bf16[128,128]{1,0:T(8,128)(2,1)S(1)} %copy-done), kind=kOutput, calls=%fused_computation.4 | convolution fusion | flops 76382208 | bytes 1802240 | tf_op jit(solution)/shard_map/dot_general | solution.py:66
  77.4 1.7 %copy.49 = bf16[48,48,128]{1,0,2:T(8,128)(2,1)} copy(bf16[48,48,128]{2,1,0:T(8,128)(2,1)S(1)} %collective-permute-done.1) | data formatting | bytes 1179648 | tf_op jit(solution)/shard_map/ppermute | solution.py:9
  79.1 1.8 %copy.46 = bf16[48,48,128]{1,0,2:T(8,128)(2,1)S(1)} copy(bf16[48,48,128]{2,1,0:T(8,128)(2,1)} %get-tuple-element.5) | data formatting | bytes 1179648 | tf_op jit(solution)/shard_map/psum | solution.py:14
  80.9 2.6 %fusion.29 = f32[128,48,48]{2,1,0:T(8,128)} fusion(bf16[48,48,128]{1,0,2:T(8,128)(2,1)S(1)} %copy.46, bf16[48,48,128]{1,0,2:T(8,128)(2,1)S(1)} %copy.47), kind=kOutput, calls=%fused_computation.50 | convolution fusion | flops 28311552 | bytes 2359296 | tf_op jit(solution)/shard_map/ikh,jkh->ijh/dot_general | solution.py:25
  83.5 1.5 %collective-permute-done = bf16[48,48,128]{2,1,0:T(8,128)(2,1)} collective-permute-done((bf16[48,48,128]{2,1,0:T(8,128)(2,1)}, bf16[48,48,128]{2,1,0:T(8,128)(2,1)}, u32[]{:S(2)}, u32[]{:S(2)}) %collective-permute-start) | collective-permute-done | bytes 589856 | tf_op jit(solution)/shard_map/ppermute | solution.py:9
  85.0 2.7 %copy.48 = bf16[48,48,128]{1,0,2:T(8,128)(2,1)} copy(bf16[48,48,128]{2,1,0:T(8,128)(2,1)} %collective-permute-done) | data formatting | bytes 1179648 | tf_op jit(solution)/shard_map/ppermute | solution.py:9
  87.7 3.8 %bitcast_reduce_fusion = (f32[48,48]{0,1:T(8,128)S(1)}, f32[128,48,48]{2,1,0:T(8,128)S(1)}) fusion(f32[128,48,48]{2,1,0:T(8,128)} %fusion.29, bf16[48,48,128]{1,0,2:T(8,128)(2,1)} %copy.48, bf16[48,48,128]{1,0,2:T(8,128)(2,1)} %copy.49), kind=kOutput, calls=%fused_computation.7 | convolution fusion | flops 28899072 | bytes 3548160 | tf_op jit(solution)/shard_map/ikh,jkh->ijh/dot_general | solution.py:25
  91.5 0.1 copy.50
  91.6 0.1 copy.51
  91.7 0.5 multiply_reduce_fusion
  92.2 0.1 copy.52
  92.3 0.1 copy.53
  92.3 0.0 copy-done.8
  92.4 1.7 %add_convert_fusion = bf16[48,48,128]{0,1,2:T(8,128)(2,1)} fusion(f32[128,48,48]{2,1,0:T(8,128)S(1)} %get-tuple-element.10, f32[128]{0:T(128)S(1)} %copy-done.8, f32[128]{0:T(128)S(1)} %copy-done.9, f32[48,48]{0,1:T(8,128)S(1)} %copy.53, f32[48,48]{0,1:T(8,128)S(1)} %copy.51), kind=kLoop, calls=%fused_computation.8 | loop fusion | flops 1474560 | bytes 1788928 | tf_op jit(solution)/shard_map/convert_element_type | solution.py:81
  94.1 2.4 %copy.54 = bf16[48,48,128]{2,1,0:T(8,128)(2,1)S(1)} copy(bf16[48,48,128]{0,1,2:T(8,128)(2,1)} %add_convert_fusion) | data formatting | bytes 1179648 | tf_op jit(solution)/shard_map/convert_element_type | solution.py:81
  96.5 1.1 %fusion.3 = bf16[2304,128]{1,0:T(8,128)(2,1)} fusion(f32[2304,128]{1,0:T(8,128)S(1)} %copy-done.3, bf16[2304,128]{1,0:T(8,128)(2,1)S(1)} %bitcast.92, bf16[128,128]{1,0:T(8,128)(2,1)S(1)} %copy-done.5), kind=kOutput, calls=%fused_computation.5 | convolution fusion | flops 76087296 | bytes 2392064 | tf_op jit(solution)/shard_map/dot_general | solution.py:82
  (24 shorter events, 0.1 us)
Async XLA Ops:
  6.5 69.4 %copy-start = (bf16[128,128]{1,0:T(8,128)(2,1)S(1)}, bf16[128,128]{1,0:T(8,128)(2,1)}, u32[]{:S(2)}) copy-start(bf16[128,128]{1,0:T(8,128)(2,1)} %param.14) | copy-start | bytes 98308
  6.5 4.3 %copy-start.2 = (bf16[48,48,128]{2,1,0:T(8,128)(2,1)S(1)}, bf16[48,48,128]{2,1,0:T(8,128)(2,1)}, u32[]{:S(2)}) copy-start(bf16[48,48,128]{2,1,0:T(8,128)(2,1)} %param.9) | copy-start | bytes 1769476
  6.5 4.0 %copy-start.4 = (bf16[128,512]{1,0:T(8,128)(2,1)S(1)}, bf16[128,512]{1,0:T(8,128)(2,1)}, u32[]{:S(2)}) copy-start(bf16[128,512]{1,0:T(8,128)(2,1)} %param.13) | copy-start | bytes 393220
  6.5 4.3 %copy-start.7 = (f32[128]{0:T(128)S(1)}, f32[128]{0:T(128)}, u32[]{:S(2)}) copy-start(f32[128]{0:T(128)} %param.11) | copy-start | bytes 1540
  6.5 4.3 %copy-start.6 = (f32[128]{0:T(128)S(1)}, f32[128]{0:T(128)}, u32[]{:S(2)}) copy-start(f32[128]{0:T(128)} %param.12) | copy-start | bytes 1540
  6.5 68.9 %all-reduce.3.cloned.1.call-start = ((), (), s32[]{:S(2)}) async-start(), calls=%async_computation | async-start | bytes 2359296 | tf_op jit(solution)/shard_map/psum | solution.py:14
  12.4 2.1 %copy-start.1 = (f32[48,48,4,128]{3,1,2,0:T(8,128)}, f32[48,48,4,128]{3,1,2,0:T(8,128)S(1)}, u32[]{:S(2)}) copy-start(f32[48,48,4,128]{3,1,2,0:T(8,128)S(1)} %fusion.26) | copy-start | bytes 14155780
  18.7 58.7 %collective-permute-start.1 = (bf16[48,48,128]{2,1,0:T(8,128)(2,1)S(1)}, bf16[48,48,128]{2,1,0:T(8,128)(2,1)S(1)}, u32[]{:S(2)}, u32[]{:S(2)}) collective-permute-start(bf16[48,48,128]{2,1,0:T(8,128)(2,1)S(1)} %fusion.11), channel_id=1, source_target_pairs={{0,3},{1,0},{2,1},{3,2},{4,7},{5,4},{6,5},{7,6},{8,11},{9,8},{10,9... | collective-permute-start | bytes 1769480 | tf_op jit(solution)/shard_map/ppermute | solution.py:9
  75.4 9.6 %collective-permute-start = (bf16[48,48,128]{2,1,0:T(8,128)(2,1)}, bf16[48,48,128]{2,1,0:T(8,128)(2,1)}, u32[]{:S(2)}, u32[]{:S(2)}) collective-permute-start(bf16[48,48,128]{2,1,0:T(8,128)(2,1)} %get-tuple-element.6), channel_id=1, source_target_pairs={{0,3},{1,0},{2,1},{3,2},{4,7},{5,4},{6,5},{7,6},{8,11},{9,8},{10,9... | collective-permute-start | bytes 1769480 | tf_op jit(solution)/shard_map/ppermute | solution.py:9
  91.7 0.7 copy-start.8
  91.7 0.7 copy-start.9
  94.1 2.4 %copy-start.3 = (f32[2304,128]{1,0:T(8,128)S(1)}, f32[2304,128]{1,0:T(8,128)}, u32[]{:S(2)}) copy-start(f32[2304,128]{1,0:T(8,128)} %fusion.2) | copy-start | bytes 3538948
  94.1 2.4 %copy-start.5 = (bf16[128,128]{1,0:T(8,128)(2,1)S(1)}, bf16[128,128]{1,0:T(8,128)(2,1)}, u32[]{:S(2)}) copy-start(bf16[128,128]{1,0:T(8,128)(2,1)} %param.17) | copy-start | bytes 98308
Sparse Core Ops, SparseCore 0:
  16.9 58.5 all-reduce.2
where the time goes:
time: 105 us; the launch traced here: 104 us
  waiting for transfers between devices  57.1 us (54%)
  between operations  14.3 us (14%)
  local copies, waits for them, and re-layouts  12.1 us (12%)
  other arithmetic  10.5 us (10%)
  matrix products  9.77 us (9%)
    psum x1, waiting for transfers between devices, from_root(): return lax.psum(jnp.where(mine, array, jnp.zeros_like(array)), axis)  55.6 us
    dot_general x2, matrix products, contract(): jnp.einsum('ikh,jkh->ijh', left_piece, right_piece, preferred_element_typ...  6.37 us
    ppermute x2, local copies, waits for them, and re-layouts, shifted(): lax.ppermute(array, axis, [(i, (i + by) % devices) for i in range(devices)])  4.36 us
    convert_element_type x1, local copies, waits for them, and re-layouts, on_device(): mixed = layer_norm(summed, out_gain, out_bias).astype(jnp.bfloat16)  2.36 us
    reduce_sum x2, other arithmetic, layer_norm(): variance = jnp.mean(centered * centered, axis=-1, keepdims=True)  2.22 us
    unnamed x20, local copies, waits for them, and re-layouts  2.19 us
    select_n x2, other arithmetic, from_root(): return lax.psum(jnp.where(mine, array, jnp.zeros_like(array)), axis)  2.17 us
  transfers between devices with their start and end apart: 3, of which 2 were waited for; matrix products, arithmetic and copies ran while one was open for 10% of the time, Pallas kernels for 0%

commit v1 on v0

--- a/solution.py
+++ b/solution.py
@@ -27,6 +27,51 @@
     )
 
 
+def band_by_sums(right_factor, cols_here, window, row_count, col_count):
+    blocks_per_row = col_count // row_count
+    col_pos = lax.axis_index("col")
+    pieces = []
+    for offset in range(window):
+        block_id = (col_pos - offset) % col_count
+        start = block_id % blocks_per_row * cols_here
+        received = from_root(
+            lax.dynamic_slice_in_dim(right_factor, start, cols_here, 0),
+            "row",
+            block_id // blocks_per_row,
+        )
+        pieces.append(received if offset == 0 else shifted(received, "col", -offset))
+    return pieces
+
+
+def band_by_hops(right_factor):
+    row_pos = lax.axis_index("row")
+    col_pos = lax.axis_index("col")
+
+    def at(r, c):
+        return r % 4 * 4 + c % 4
+
+    def move(array, pairs):
+        return lax.ppermute(array, ("row", "col"), pairs)
+
+    everyone = [(r, c) for r in range(4) for c in range(4)]
+    roots = [(r, c) for r, c in everyone if (c - r) % 4 < 2]
+    far = move(right_factor, [(at(r, c), at(r ^ 2, c)) for r, c in roots])
+    is_root = (col_pos - row_pos) % 4 < 2
+    held = jnp.where(is_root, right_factor, far)
+    near = move(
+        held,
+        [
+            (at(r, c), at(r ^ 1, c) if (r + c) % 2 == 0 else at(r, c - 1))
+            for r, c in everyone
+        ],
+    )
+    cross = move(
+        held, [(at(r, c), at(r ^ 1, c - 1)) for r, c in everyone if (r + c) % 2 == 1]
+    )
+    even = (row_pos + col_pos) % 2 == 0
+    return [jnp.where(even, held, near), jnp.where(even, near, cross)]
+
+
 def on_device(
     pair_state,
     token_count,
@@ -42,7 +87,6 @@
     hidden = out_weights.shape[0]
     col_count = lax.axis_size("col")
     row_count = lax.axis_size("row")
-    blocks_per_row = col_count // row_count
     window = col_count // 2
     row_pos = lax.axis_index("row")
     col_pos = lax.axis_index("col")
@@ -65,19 +109,16 @@
     out_gate = jax.nn.sigmoid(
         jnp.dot(flat_normed, gate_weights, preferred_element_type=jnp.float32)
     )
+    if row_count == 4 and col_count == 4:
+        pieces = band_by_hops(right_factor)
+    else:
+        pieces = band_by_sums(right_factor, cols_here, window, row_count, col_count)
     summed = jnp.zeros((rows_here, cols_here, hidden), jnp.float32)
     carried = left_factor
     for offset in range(window):
         if offset > 0:
             carried = shifted(carried, "col", -1)
-        root_row = (col_pos - offset) % col_count // blocks_per_row
-        block_id = (col_pos - offset) % col_count
-        start = block_id % blocks_per_row * cols_here
-        received = from_root(
-            lax.dynamic_slice_in_dim(right_factor, start, cols_here, 0), "row", root_row
-        )
-        right_piece = received if offset == 0 else shifted(received, "col", -offset)
-        summed = contract(summed, carried, right_piece)
+        summed = contract(summed, carried, pieces[offset])
     mixed = layer_norm(summed, out_gain, out_bias).astype(jnp.bfloat16)
     projected_out = jnp.dot(
         mixed.reshape(rows_here * cols_here, hidden),

time: 105 us -> 63.1 us (0.60)
  waiting for transfers between devices: 57.1 us -> 25.6 us
  between operations: 14.3 us -> 0.96 us
  starting transfers between devices: 0.61 us -> 9.61 us
  matrix products: 9.77 us -> 5.22 us
    psum x1 -> x0, waiting for transfers between devices: 55.6 us -> none  [from_root(): return lax.psum(jnp.where(mine, array, jnp.zeros_like(array)), axis)]
    ppermute x0 -> x3, waiting for transfers between devices: none -> 25.6 us  [move(): return lax.ppermute(array, ('row', 'col'), pairs)]
    ppermute x0 -> x3, starting transfers between devices: none -> 8.6 us  [move(): return lax.ppermute(array, ('row', 'col'), pairs)]
    dot_general x2, matrix products: 6.37 us -> 1.86 us  [contract(): jnp.einsum('ikh,jkh->ijh', left_piece, right_piece, preferred_element_typ...]
    select_n x0 -> x2, local copies, waits for them, and re-layouts: none -> 4.47 us  [band_by_hops(): return [jnp.where(even, held, near), jnp.where(even, near, cross)]]
    ppermute x2 -> x1, local copies, waits for them, and re-layouts: 4.36 us -> 1.84 us  [shifted(): lax.ppermute(array, axis, [(i, (i + by) % devices) for i in range(devices)])]
    psum x1 -> x0, local copies, waits for them, and re-layouts: 1.84 us -> none  [from_root(): return lax.psum(jnp.where(mine, array, jnp.zeros_like(array)), axis)]
    ppermute x2 -> x1, waiting for transfers between devices: 1.52 us -> 0.01 us  [shifted(): lax.ppermute(array, axis, [(i, (i + by) % devices) for i in range(devices)])]
  transfers between devices with their start and end apart: 3 -> 4, of which waited for: 2 -> 3; matrix products, arithmetic and copies ran while one was open for 10% -> 8% of each run, Pallas kernels for 0% -> 0%
where the time goes in v1:
time: 63.1 us; the launch traced here: 62.7 us
  waiting for transfers between devices  25.6 us (41%)
  local copies, waits for them, and re-layouts  11.8 us (19%)
  starting transfers between devices  9.61 us (15%)
  other arithmetic  9.47 us (15%)
  matrix products  5.22 us (8%)
  between operations  0.96 us (2%)
    ppermute x3, waiting for transfers between devices, move(): return lax.ppermute(array, ('row', 'col'), pairs)  25.6 us
    ppermute x3, starting transfers between devices, move(): return lax.ppermute(array, ('row', 'col'), pairs)  8.6 us
    select_n x2, local copies, waits for them, and re-layouts, band_by_hops(): return [jnp.where(even, held, near), jnp.where(even, near, cross)]  4.47 us
    convert_element_type x1, local copies, waits for them, and re-layouts, on_device(): mixed = layer_norm(summed, out_gain, out_bias).astype(jnp.bfloat16)  2.36 us
    select_n x1, other arithmetic, band_by_hops(): return [jnp.where(even, held, near), jnp.where(even, near, cross)]  2.34 us
    reduce_sum x2, other arithmetic, layer_norm(): variance = jnp.mean(centered * centered, axis=-1, keepdims=True)  2.22 us
    dot_general x2, matrix products, contract(): jnp.einsum('ikh,jkh->ijh', left_piece, right_piece, preferred_element_typ...  1.86 us
    ppermute x1, local copies, waits for them, and re-layouts, shifted(): lax.ppermute(array, axis, [(i, (i + by) % devices) for i in range(devices)])  1.84 us
  transfers between devices with their start and end apart: 4, of which 3 were waited for; matrix products, arithmetic and copies ran while one was open for 8% of the time, Pallas kernels for 0%

profile of v1, /device:TPU:1, one launch (start us, length us, event | category | flops | bytes accessed | tf_op | source)
XLA Modules:
  0.0 62.7 jit_solution(8382116322541033647)
XLA Ops:
  0.8 1.4 %convert_reduce_fusion = f32[48,48]{1,0:T(8,128)S(1)} fusion(bf16[48,48,128]{2,1,0:T(8,128)(2,1)} %param.9), kind=kLoop, calls=%fused_computation.12 | loop fusion | flops 587520 | bytes 599040 | tf_op jit(solution)/shard_map/reduce_sum | solution.py:18
  2.2 1.8 %fusion.6 = f32[48,48]{1,0:T(8,128)S(1)} fusion(bf16[48,48,128]{2,1,0:T(8,128)(2,1)} %param.9, f32[48,48]{1,0:T(8,128)S(1)} %broadcast_multiply_fusion.2), kind=kLoop, calls=%fused_computation.15 | loop fusion | flops 1177344 | bytes 608256 | tf_op jit(solution)/shard_map/reduce_sum | solution.py:20
  4.0 0.1 copy.56
  4.2 0.1 broadcast_multiply_fusion
  4.3 0.8 %fusion.9 = bf16[48,48,128]{2,1,0:T(8,128)(2,1)S(1)} fusion(bf16[48,48,128]{2,1,0:T(8,128)(2,1)S(1)} %copy-done.3, f32[128]{0:T(128)S(1)} %copy-done.7, f32[128]{0:T(128)S(1)} %copy-done.8, f32[48,48]{1,0:T(8,128)S(1)} %add_rsqrt_fusion.1, f32[48,48]{1,0:T(8,128)S(1)} %broadcast_multiply_fusion.2), kind=kLoop, calls=%fused_computation.18 | loop fusion | flops 1769472 | bytes 1199104 | tf_op jit(solution)/shard_map/convert_element_type | solution.py:93
  5.1 0.8 %fusion.26 = f32[48,48,4,128]{3,1,2,0:T(8,128)S(1)} fusion(bf16[4,128,128,1]{2,1,0,3:T(8,128)(2,1)S(1)} %bitcast.90, bf16[48,48,128]{2,1,0:T(8,128)(2,1)S(1)} %fusion.9), kind=kOutput, calls=%fused_computation.39 | convolution fusion | flops 301989888 | bytes 5439488 | tf_op jit(solution)/shard_map/dot_general | solution.py:95
  5.8 0.8 %fusion.11 = (bf16[48,48,128]{2,1,0:T(8,128)(2,1)S(1)}, bf16[48,48,128]{2,1,0:T(8,128)(2,1)S(1)}) fusion(f32[48,48,4,128]{3,1,2,0:T(8,128)S(1)} %fusion.26, f32[48,48]{1,0:T(8,128)S(1)} %broadcast_multiply_fusion), kind=kLoop, calls=%fused_computation.21 | loop fusion | flops 3538944 | bytes 5907456 | tf_op jit(solution)/shard_map/convert_element_type | solution.py:103
  6.6 5.1 %collective-permute-start = (bf16[48,48,128]{2,1,0:T(8,128)(2,1)S(1)}, bf16[48,48,128]{2,1,0:T(8,128)(2,1)S(1)}, u32[]{:S(2)}, u32[]{:S(2)}) collective-permute-start(bf16[48,48,128]{2,1,0:T(8,128)(2,1)S(1)} %get-tuple-element.6), channel_id=1, source_target_pairs={{0,8},{1,9},{5,13},{6,14},{10,2},{11,3},{12,4},{15,7},{16,24},{17,... | collective-permute-start | bytes 1769480 | tf_op jit(solution)/shard_map/ppermute | solution.py:54
  11.7 1.0 %collective-permute-start.3 = (bf16[48,48,128]{2,1,0:T(8,128)(2,1)S(1)}, bf16[48,48,128]{2,1,0:T(8,128)(2,1)}, u32[]{:S(2)}, u32[]{:S(2)}) collective-permute-start(bf16[48,48,128]{2,1,0:T(8,128)(2,1)S(1)} %get-tuple-element.5), channel_id=1, source_target_pairs={{0,3},{1,0},{2,1},{3,2},{4,7},{5,4},{6,5},{7,6},{8,11},{9,8},{10,9... | collective-permute-start | bytes 1769480 | tf_op jit(solution)/shard_map/ppermute | solution.py:9
  12.7 11.0 %collective-permute-done = bf16[48,48,128]{2,1,0:T(8,128)(2,1)S(1)} collective-permute-done((bf16[48,48,128]{2,1,0:T(8,128)(2,1)S(1)}, bf16[48,48,128]{2,1,0:T(8,128)(2,1)S(1)}, u32[]{:S(2)}, u32[]{:S(2)}) %collective-permute-start) | collective-permute-done | bytes 589856 | tf_op jit(solution)/shard_map/ppermute | solution.py:54
  23.7 1.6 %collective-permute-start.1 = (bf16[48,48,128]{2,1,0:T(8,128)(2,1)S(1)}, bf16[48,48,128]{2,1,0:T(8,128)(2,1)}, u32[]{:S(2)}, u32[]{:S(2)}) collective-permute-start(bf16[48,48,128]{2,1,0:T(8,128)(2,1)S(1)} %broadcast_select_fusion), channel_id=1, source_target_pairs={{0,4},{1,0},{2,6},{3,2},{4,7},{5,1},{6,5},{7,3},{8,12},{9,8},{10,1... | collective-permute-start | bytes 1769480 | tf_op jit(solution)/shard_map/ppermute | solution.py:54
  25.4 1.9 %collective-permute-start.2 = (bf16[48,48,128]{2,1,0:T(8,128)(2,1)S(1)}, bf16[48,48,128]{2,1,0:T(8,128)(2,1)}, u32[]{:S(2)}, u32[]{:S(2)}) collective-permute-start(bf16[48,48,128]{2,1,0:T(8,128)(2,1)S(1)} %broadcast_select_fusion), channel_id=1, source_target_pairs={{1,4},{3,6},{4,3},{6,1},{9,12},{11,14},{12,11},{14,9},{17,20},{19,... | collective-permute-start | bytes 1769480 | tf_op jit(solution)/shard_map/ppermute | solution.py:54
  27.3 1.7 %copy.47 = bf16[48,48,128]{1,0,2:T(8,128)(2,1)} copy(bf16[48,48,128]{2,1,0:T(8,128)(2,1)S(1)} %get-tuple-element.5) | data formatting | bytes 1179648 | tf_op jit(solution)/shard_map/convert_element_type | solution.py:103
  29.0 1.5 %fusion.2 = f32[2304,128]{1,0:T(8,128)} fusion(bf16[2304,128]{1,0:T(8,128)(2,1)S(1)} %bitcast.88, bf16[128,128]{1,0:T(8,128)(2,1)S(1)} %copy-done), kind=kOutput, calls=%fused_computation.4 | convolution fusion | flops 76382208 | bytes 1802240 | tf_op jit(solution)/shard_map/dot_general | solution.py:110
  30.5 1.8 %copy.49 = bf16[48,48,128]{1,0,2:T(8,128)(2,1)S(1)} copy(bf16[48,48,128]{2,1,0:T(8,128)(2,1)} %collective-permute-done.3) | data formatting | bytes 1179648 | tf_op jit(solution)/shard_map/ppermute | solution.py:9
  32.4 8.9 %collective-permute-done.1 = bf16[48,48,128]{2,1,0:T(8,128)(2,1)} collective-permute-done((bf16[48,48,128]{2,1,0:T(8,128)(2,1)S(1)}, bf16[48,48,128]{2,1,0:T(8,128)(2,1)}, u32[]{:S(2)}, u32[]{:S(2)}) %collective-permute-start.1) | collective-permute-done | bytes 589856 | tf_op jit(solution)/shard_map/ppermute | solution.py:54
  41.3 5.8 %collective-permute-done.2 = bf16[48,48,128]{2,1,0:T(8,128)(2,1)} collective-permute-done((bf16[48,48,128]{2,1,0:T(8,128)(2,1)S(1)}, bf16[48,48,128]{2,1,0:T(8,128)(2,1)}, u32[]{:S(2)}, u32[]{:S(2)}) %collective-permute-start.2) | collective-permute-done | bytes 589856 | tf_op jit(solution)/shard_map/ppermute | solution.py:54
  47.0 2.3 %broadcast_select_fusion.2 = (bf16[48,48,128]{2,1,0:T(8,128)(2,1)}, bf16[48,48,128]{2,1,0:T(8,128)(2,1)}) fusion(bf16[48,48,128]{2,1,0:T(8,128)(2,1)S(1)} %broadcast_select_fusion, bf16[48,48,128]{2,1,0:T(8,128)(2,1)} %collective-permute-done.1, pred[]{:T(512)S(6)} %eq.6, bf16[48,48,128]{2,1,0:T(8,128)(2,1)} %collective-permute-done.2), kind=kLoop, calls=%fused_computation.43 | loop fusion | flops 589824 | bytes 2949121 | tf_op jit(solution)/shard_map/jit(_where)/select_n | solution.py:72
  49.4 1.8 %copy.48 = bf16[48,48,128]{1,0,2:T(8,128)(2,1)S(1)} copy(bf16[48,48,128]{2,1,0:T(8,128)(2,1)} %get-tuple-element.8) | data formatting | bytes 1179648 | tf_op jit(solution)/shard_map/jit(_where)/select_n | solution.py:72
  51.2 2.6 %copy.46 = bf16[48,48,128]{1,0,2:T(8,128)(2,1)} copy(bf16[48,48,128]{2,1,0:T(8,128)(2,1)} %get-tuple-element.7) | data formatting | bytes 1179648 | tf_op jit(solution)/shard_map/jit(_where)/select_n | solution.py:72
  53.8 0.9 %fusion.28 = f32[128,48,48]{2,1,0:T(8,128)S(1)} fusion(bf16[48,48,128]{1,0,2:T(8,128)(2,1)S(1)} %copy.48, bf16[48,48,128]{1,0,2:T(8,128)(2,1)S(1)} %copy.49), kind=kOutput, calls=%fused_computation.51 | convolution fusion | flops 28311552 | bytes 2359296 | tf_op jit(solution)/shard_map/ikh,jkh->ijh/dot_general | solution.py:25
  54.8 0.5 copy-done.1
  55.2 0.5 copy-done.2
  55.7 0.9 %bitcast_reduce_fusion = (f32[48,48]{0,1:T(8,128)S(1)}, f32[128,48,48]{2,1,0:T(8,128)S(1)}) fusion(f32[128,48,48]{2,1,0:T(8,128)S(1)} %fusion.28, bf16[48,48,128]{1,0,2:T(8,128)(2,1)S(1)} %copy-done.2, bf16[48,48,128]{1,0,2:T(8,128)(2,1)S(1)} %copy-done.1), kind=kOutput, calls=%fused_computation.7 | convolution fusion | flops 28899072 | bytes 3548160 | tf_op jit(solution)/shard_map/ikh,jkh->ijh/dot_general | solution.py:25
  56.7 0.1 copy.50
  56.7 0.1 copy.51
  56.8 0.5 multiply_reduce_fusion
  57.3 0.1 copy.52
  57.4 0.1 copy.53
  57.5 1.7 %add_convert_fusion = bf16[48,48,128]{0,1,2:T(8,128)(2,1)} fusion(f32[128,48,48]{2,1,0:T(8,128)S(1)} %get-tuple-element.10, f32[128]{0:T(128)S(1)} %copy-done.9, f32[128]{0:T(128)S(1)} %copy-done.10, f32[48,48]{0,1:T(8,128)S(1)} %copy.53, f32[48,48]{0,1:T(8,128)S(1)} %copy.51), kind=kLoop, calls=%fused_computation.8 | loop fusion | flops 1474560 | bytes 1788928 | tf_op jit(solution)/shard_map/convert_element_type | solution.py:122
  59.2 2.4 %copy.54 = bf16[48,48,128]{2,1,0:T(8,128)(2,1)S(1)} copy(bf16[48,48,128]{0,1,2:T(8,128)(2,1)} %add_convert_fusion) | data formatting | bytes 1179648 | tf_op jit(solution)/shard_map/convert_element_type | solution.py:122
  61.6 1.1 %fusion.3 = bf16[2304,128]{1,0:T(8,128)(2,1)} fusion(f32[2304,128]{1,0:T(8,128)S(1)} %copy-done.4, bf16[2304,128]{1,0:T(8,128)(2,1)S(1)} %bitcast.89, bf16[128,128]{1,0:T(8,128)(2,1)S(1)} %copy-done.6), kind=kOutput, calls=%fused_computation.5 | convolution fusion | flops 76087296 | bytes 2392064 | tf_op jit(solution)/shard_map/dot_general | solution.py:123
  (27 shorter events, 0.2 us)
Async XLA Ops:
  0.0 29.0 %copy-start = (bf16[128,128]{1,0:T(8,128)(2,1)S(1)}, bf16[128,128]{1,0:T(8,128)(2,1)}, u32[]{:S(2)}) copy-start(bf16[128,128]{1,0:T(8,128)(2,1)} %param.14) | copy-start | bytes 98308
  0.0 4.2 %copy-start.3 = (bf16[48,48,128]{2,1,0:T(8,128)(2,1)S(1)}, bf16[48,48,128]{2,1,0:T(8,128)(2,1)}, u32[]{:S(2)}) copy-start(bf16[48,48,128]{2,1,0:T(8,128)(2,1)} %param.9) | copy-start | bytes 1769476
  0.0 4.0 %copy-start.5 = (bf16[128,512]{1,0:T(8,128)(2,1)S(1)}, bf16[128,512]{1,0:T(8,128)(2,1)}, u32[]{:S(2)}) copy-start(bf16[128,512]{1,0:T(8,128)(2,1)} %param.13) | copy-start | bytes 393220
  0.0 4.2 %copy-start.8 = (f32[128]{0:T(128)S(1)}, f32[128]{0:T(128)}, u32[]{:S(2)}) copy-start(f32[128]{0:T(128)} %param.11) | copy-start | bytes 1540
  0.0 4.2 %copy-start.7 = (f32[128]{0:T(128)S(1)}, f32[128]{0:T(128)}, u32[]{:S(2)}) copy-start(f32[128]{0:T(128)} %param.12) | copy-start | bytes 1540
  6.6 17.1 %collective-permute-start = (bf16[48,48,128]{2,1,0:T(8,128)(2,1)S(1)}, bf16[48,48,128]{2,1,0:T(8,128)(2,1)S(1)}, u32[]{:S(2)}, u32[]{:S(2)}) collective-permute-start(bf16[48,48,128]{2,1,0:T(8,128)(2,1)S(1)} %get-tuple-element.6), channel_id=1, source_target_pairs={{0,8},{1,9},{5,13},{6,14},{10,2},{11,3},{12,4},{15,7},{16,24},{17,... | collective-permute-start | bytes 1769480 | tf_op jit(solution)/shard_map/ppermute | solution.py:54
  11.7 18.8 %collective-permute-start.3 = (bf16[48,48,128]{2,1,0:T(8,128)(2,1)S(1)}, bf16[48,48,128]{2,1,0:T(8,128)(2,1)}, u32[]{:S(2)}, u32[]{:S(2)}) collective-permute-start(bf16[48,48,128]{2,1,0:T(8,128)(2,1)S(1)} %get-tuple-element.5), channel_id=1, source_target_pairs={{0,3},{1,0},{2,1},{3,2},{4,7},{5,4},{6,5},{7,6},{8,11},{9,8},{10,9... | collective-permute-start | bytes 1769480 | tf_op jit(solution)/shard_map/ppermute | solution.py:9
  23.7 17.5 %collective-permute-start.1 = (bf16[48,48,128]{2,1,0:T(8,128)(2,1)S(1)}, bf16[48,48,128]{2,1,0:T(8,128)(2,1)}, u32[]{:S(2)}, u32[]{:S(2)}) collective-permute-start(bf16[48,48,128]{2,1,0:T(8,128)(2,1)S(1)} %broadcast_select_fusion), channel_id=1, source_target_pairs={{0,4},{1,0},{2,6},{3,2},{4,7},{5,1},{6,5},{7,3},{8,12},{9,8},{10,1... | collective-permute-start | bytes 1769480 | tf_op jit(solution)/shard_map/ppermute | solution.py:54
  25.4 21.7 %collective-permute-start.2 = (bf16[48,48,128]{2,1,0:T(8,128)(2,1)S(1)}, bf16[48,48,128]{2,1,0:T(8,128)(2,1)}, u32[]{:S(2)}, u32[]{:S(2)}) collective-permute-start(bf16[48,48,128]{2,1,0:T(8,128)(2,1)S(1)} %broadcast_select_fusion), channel_id=1, source_target_pairs={{1,4},{3,6},{4,3},{6,1},{9,12},{11,14},{12,11},{14,9},{17,20},{19,... | collective-permute-start | bytes 1769480 | tf_op jit(solution)/shard_map/ppermute | solution.py:54
  53.8 1.4 %copy-start.1 = (bf16[48,48,128]{1,0,2:T(8,128)(2,1)S(1)}, bf16[48,48,128]{1,0,2:T(8,128)(2,1)}, u32[]{:S(2)}) copy-start(bf16[48,48,128]{1,0,2:T(8,128)(2,1)} %copy.47) | copy-start | bytes 1769476
  53.8 1.9 %copy-start.2 = (bf16[48,48,128]{1,0,2:T(8,128)(2,1)S(1)}, bf16[48,48,128]{1,0,2:T(8,128)(2,1)}, u32[]{:S(2)}) copy-start(bf16[48,48,128]{1,0,2:T(8,128)(2,1)} %copy.46) | copy-start | bytes 1769476
  56.8 0.7 %copy-start.9 = (f32[128]{0:T(128)S(1)}, f32[128]{0:T(128)}, u32[]{:S(2)}) copy-start(f32[128]{0:T(128)} %param.16) | copy-start | bytes 1540
  56.8 0.7 %copy-start.10 = (f32[128]{0:T(128)S(1)}, f32[128]{0:T(128)}, u32[]{:S(2)}) copy-start(f32[128]{0:T(128)} %param.15) | copy-start | bytes 1540
  59.2 2.4 %copy-start.4 = (f32[2304,128]{1,0:T(8,128)S(1)}, f32[2304,128]{1,0:T(8,128)}, u32[]{:S(2)}) copy-start(f32[2304,128]{1,0:T(8,128)} %fusion.2) | copy-start | bytes 3538948
  59.2 2.4 %copy-start.6 = (bf16[128,128]{1,0:T(8,128)(2,1)S(1)}, bf16[128,128]{1,0:T(8,128)(2,1)}, u32[]{:S(2)}) copy-start(bf16[128,128]{1,0:T(8,128)(2,1)} %param.17) | copy-start | bytes 98308

commit v2 on v1

v2 whole, which is shorter than its diff:
```python
import functools

import jax
import jax.numpy as jnp
from jax import lax
from jax.experimental import pallas as pl
from jax.experimental.pallas import tpu as pltpu
from jax.sharding import PartitionSpec as P

CHUNK = 16
VMEM_LIMIT = 56 * 1024 * 1024


def whole(memory_space=pltpu.VMEM):
    return pl.BlockSpec(memory_space=memory_space)


def shifted(array, axis, by):
    devices = lax.axis_size(axis)
    return lax.ppermute(array, axis, [(i, (i + by) % devices) for i in range(devices)])


def from_root(array, axis, root):
    mine = lax.axis_index(axis) == root
    return lax.psum(jnp.where(mine, array, jnp.zeros_like(array)), axis)


def layer_norm(values, gain, offset):
    average = jnp.mean(values, axis=-1, keepdims=True)
    centered = values - average
    variance = jnp.mean(centered * centered, axis=-1, keepdims=True)
    return centered * lax.rsqrt(variance + 1e-05) * gain + offset


def normed_rows(pair_ref, gain_ref, bias_ref, first, count):
    _, columns, channels = pair_ref.shape
    values = pair_ref[pl.ds(first, count)].reshape(count * columns, channels)
    return layer_norm(values.astype(jnp.float32), gain_ref[...], bias_ref[...]).astype(jnp.bfloat16)


def gated(normed, weights_ref, start, hidden):
    both = jnp.dot(
        normed, weights_ref[:, start : start + 2 * hidden], preferred_element_type=jnp.float32
    )
    return jax.nn.sigmoid(both[:, :hidden]) * both[:, hidden:]


def masked(values, tokens_ref, first, count, rows, columns):
    tokens = tokens_ref[0]
    row_start = lax.axis_index("row") * rows + first
    col_start = lax.axis_index("col") * columns
    valid_columns = tokens - col_start
    position = lax.broadcasted_iota(jnp.int32, (columns, values.shape[-1]), 0)
    parts = []
    for row in range(count):
        limit = jnp.where(row_start + row < tokens, valid_columns, 0)
        part = values[row * columns : (row + 1) * columns]
        parts.append(jnp.where(position < limit, part, 0.0))
    return parts


def right_kernel(tokens_ref, pair_ref, gain_ref, bias_ref, weights_ref, *refs):
    outs, scratch = refs[:-1], refs[-1]
    rows, columns, _ = pair_ref.shape
    hidden = scratch.shape[1]
    step = 4
    for first in range(0, rows, step):
        normed = normed_rows(pair_ref, gain_ref, bias_ref, first, step)
        right = gated(normed, weights_ref, 2 * hidden, hidden)
        parts = masked(right, tokens_ref, first, step, rows, columns)
        for row, part in enumerate(parts):
            scratch[pl.ds((first + row) * columns, columns), :] = part
    for at, out in enumerate(outs):
        for third in range(columns):
            start = at * CHUNK * columns + third
            out[third] = scratch[pl.ds(start, CHUNK, stride=columns), :].astype(jnp.bfloat16)


def left_kernel(
    tokens_ref, pair_ref, gain_ref, bias_ref, weights_ref, gate_weights_ref, left_ref, gate_ref
):
    rows, columns, _ = pair_ref.shape
    hidden = left_ref.shape[2]
    channels = gate_ref.shape[2]
    step = 4
    for first in range(0, rows, step):
        normed = normed_rows(pair_ref, gain_ref, bias_ref, first, step)
        left = gated(normed, weights_ref, 0, hidden)
        for row, part in enumerate(masked(left, tokens_ref, first, step, rows, columns)):
            left_ref[first + row] = part.astype(jnp.bfloat16)
        gate = jax.nn.sigmoid(
            jnp.dot(normed, gate_weights_ref[...], preferred_element_type=jnp.float32)
        )
        gate_ref[pl.ds(first, step)] = gate.reshape(step, columns, channels)


def product_kernel(picks, lefts, rights, *refs):
    left_refs, refs = refs[:lefts], refs[lefts:]
    right_refs, refs = refs[:rights], refs[rights:]
    gate_ref, gain_ref, bias_ref, weights_ref, *_, out_ref, left_rows, right_rows, product = refs
    rows, columns, hidden = left_refs[0].shape
    depth = lefts * columns
    even = (lax.axis_index("row") + lax.axis_index("col")) % 2 == 0

    @pl.loop(0, rows)
    def _(row):
        for at, ref in enumerate(left_refs):
            left_rows[pl.ds(row * depth + at * columns, columns), :] = ref[row].astype(jnp.float32)

    for at, (at_even, at_odd) in enumerate(picks):
        for third in range(columns):
            piece = right_refs[at_even][third].astype(jnp.float32)
            if at_odd != at_even:
                piece = jnp.where(even, piece, right_refs[at_odd][third].astype(jnp.float32))
            right_rows[pl.ds((at * columns + third) * CHUNK, CHUNK), :] = piece

    group, unroll = 8, 8
    halves = CHUNK // 8

    @pl.loop(0, rows // group)
    def _(at):
        def add(step, sums):
            sums = list(sums)
            for inner in range(unroll):
                third = step * unroll + inner
                right = [
                    right_rows[pl.ds(third * CHUNK + 8 * half, 8), :] for half in range(halves)
                ]
                for row in range(group):
                    left = left_rows[pl.ds((at * group + row) * depth + third, 8, stride=0), :]
                    for half in range(halves):
                        sums[row * halves + half] += left * right[half]
            return tuple(sums)

        zeros = tuple(jnp.zeros((8, hidden), jnp.float32) for _ in range(group * halves))
        sums = lax.fori_loop(0, depth // unroll, add, zeros)
        for row in range(group):
            for half in range(halves):
                start = (at * group + row) * CHUNK + 8 * half
                product[pl.ds(start, 8), :] = sums[row * halves + half]

    for first in range(0, rows, group):
        values = product[pl.ds(first * CHUNK, group * CHUNK), :]
        mixed = layer_norm(values, gain_ref[...], bias_ref[...]).astype(jnp.bfloat16)
        update = jnp.dot(mixed, weights_ref[...], preferred_element_type=jnp.float32)
        gate = gate_ref[pl.ds(first, group)]
        out_ref[pl.ds(first, group)] = (gate * update.reshape(gate.shape)).astype(jnp.bfloat16)


def band_by_sums(chunks, window, row_count, col_count):
    blocks_per_row = col_count // row_count
    col_pos = lax.axis_index("col")
    per_block = len(chunks) // blocks_per_row
    stacked = jnp.stack(chunks)
    pieces = []
    for offset in range(window):
        block_id = (col_pos - offset) % col_count
        start = block_id % blocks_per_row * per_block
        received = from_root(
            lax.dynamic_slice_in_dim(stacked, start, per_block, 0), "row", block_id // blocks_per_row
        )
        pieces.append(received if offset == 0 else shifted(received, "col", -offset))
    bands = [[piece[at] for piece in pieces] for at in range(per_block)]
    return bands, [(offset, offset) for offset in range(window)]


def band_by_hops(chunks):
    row_pos = lax.axis_index("row")
    col_pos = lax.axis_index("col")

    def at(r, c):
        return r % 4 * 4 + c % 4

    def move(array, pairs):
        return lax.ppermute(array, ("row", "col"), pairs)

    everyone = [(r, c) for r in range(4) for c in range(4)]
    roots = [(r, c) for r, c in everyone if (c - r) % 4 < 2]
    is_root = (col_pos - row_pos) % 4 < 2
    bands = []
    for chunk in chunks:
        far = move(chunk, [(at(r, c), at(r ^ 2, c)) for r, c in roots])
        held = jnp.where(is_root, chunk, far)
        near = move(
            held,
            [
                (at(r, c), at(r ^ 1, c) if (r + c) % 2 == 0 else at(r, c - 1))
                for r, c in everyone
            ],
        )
        cross = move(
            held, [(at(r, c), at(r ^ 1, c - 1)) for r, c in everyone if (r + c) % 2 == 1]
        )
        bands.append([held, near, cross])
    return bands, [(0, 1), (1, 2)]


def on_device(
    pair_state,
    token_count,
    in_gain,
    in_bias,
    in_weights,
    gate_weights,
    out_gain,
    out_bias,
    out_weights,
):
    rows, columns, channels = pair_state.shape
    hidden = out_weights.shape[0]
    tokens = rows * columns
    col_count = lax.axis_size("col")
    row_count = lax.axis_size("row")
    window = col_count // 2
    in_gain, in_bias = in_gain.reshape(1, channels), in_bias.reshape(1, channels)
    out_gain, out_bias = out_gain.reshape(1, hidden), out_bias.reshape(1, hidden)
    params = pltpu.CompilerParams(vmem_limit_bytes=VMEM_LIMIT)
    smem, vmem = whole(pltpu.SMEM), whole()

    chunks = pl.pallas_call(
        right_kernel,
        out_shape=[jax.ShapeDtypeStruct((columns, CHUNK, hidden), jnp.bfloat16)] * (rows // CHUNK),
        in_specs=[smem] + [vmem] * 4,
        out_specs=[vmem] * (rows // CHUNK),
        scratch_shapes=[pltpu.VMEM((tokens, hidden), jnp.float32)],
        compiler_params=params,
        cost_estimate=pl.CostEstimate(
            flops=4 * tokens * channels * hidden, bytes_accessed=4 * tokens * channels, transcendentals=0
        ),
        name="right",
    )(token_count, pair_state, in_gain, in_bias, in_weights)

    left, gate = pl.pallas_call(
        left_kernel,
        out_shape=[
            jax.ShapeDtypeStruct((rows, columns, hidden), jnp.bfloat16),
            jax.ShapeDtypeStruct((rows, columns, channels), jnp.float32),
        ],
        in_specs=[smem] + [vmem] * 5,
        out_specs=[vmem] * 2,
        compiler_params=params,
        cost_estimate=pl.CostEstimate(
            flops=6 * tokens * channels * hidden, bytes_accessed=8 * tokens * channels, transcendentals=0
        ),
        name="left_and_gate",
    )(token_count, pair_state, in_gain, in_bias, in_weights, gate_weights)

    if row_count == 4 and col_count == 4:
        bands, picks = band_by_hops(chunks)
    else:
        bands, picks = band_by_sums(chunks, window, row_count, col_count)
    lefts = [left]
    for _ in range(window - 1):
        lefts.append(shifted(lefts[-1], "col", -1))

    update = []
    depth = window * columns
    for at, band in enumerate(bands):
        chunk_of = pl.BlockSpec((rows, CHUNK, channels), lambda step, at=at: (0, at, 0))
        filled = pl.pallas_call(
            functools.partial(product_kernel, picks, len(lefts), len(band)),
            grid=(1,),
            out_shape=jax.ShapeDtypeStruct((rows, columns, channels), jnp.bfloat16),
            in_specs=[vmem] * (len(lefts) + len(band))
            + [chunk_of]
            + [vmem] * 3
            + [whole(pl.ANY)] * len(update),
            out_specs=chunk_of,
            scratch_shapes=[
                pltpu.VMEM((rows * depth + 8, hidden), jnp.float32),
                pltpu.VMEM((depth * CHUNK, hidden), jnp.float32),
                pltpu.VMEM((rows * CHUNK, hidden), jnp.float32),
            ],
            input_output_aliases={len(lefts) + len(band) + 4: 0} if update else {},
            compiler_params=params,
            cost_estimate=pl.CostEstimate(
                flops=2 * rows * CHUNK * depth * hidden,
                bytes_accessed=2 * rows * depth * hidden,
                transcendentals=0,
            ),
            name="product",
        )(*lefts, *band, gate, out_gain, out_bias, out_weights, *update)
        update = [filled]
    return filled


def solution(mesh):
    placed = (P(("crops", "row"), "col", None), P("crops"), P(), P(), P(), P(), P(), P(), P())
    return jax.shard_map(
        on_device,
        mesh=mesh,
        in_specs=placed,
        out_specs=P(("crops", "row"), "col", None),
        check_vma=False,
    )
```

time: 63.1 us -> 56.8 us (0.900)
  Pallas kernels: 0 us -> 24.4 us
  waiting for transfers between devices: 25.6 us -> 5.22 us
  starting transfers between devices: 9.61 us -> 21.4 us
  other arithmetic: 9.47 us -> 1 us
  local copies, waits for them, and re-layouts: 11.8 us -> 3.5 us
  matrix products: 5.22 us -> 0 us
    pallas_call x0 -> x5, Pallas kernels: none -> 24.4 us  [the longest x3 17.7 us: on_device(): pl.pallas_call(functools.partial(product_kernel, picks, len(lefts), len(b...]
    ppermute x3 -> x9, waiting for transfers between devices: 25.6 us -> 5.22 us  [move(): return lax.ppermute(array, ('row', 'col'), pairs)]
    ppermute x3 -> x9, starting transfers between devices: 8.6 us -> 20.4 us  [move(): return lax.ppermute(array, ('row', 'col'), pairs)]
    dot_general x5 -> x0, matrix products: 5.22 us -> none  [the longest x2 1.86 us: contract(): jnp.einsum('ikh,jkh->ijh', left_piece, right_piece, preferred_element_typ...]
    select_n x2 -> x0, local copies, waits for them, and re-layouts: 4.47 us -> none  [band_by_hops(): return [jnp.where(even, held, near), jnp.where(even, near, cross)]]
    convert_element_type x2 -> x0, local copies, waits for them, and re-layouts: 4.09 us -> none  [the longest x1 2.36 us: on_device(): mixed = layer_norm(summed, out_gain, out_bias).astype(jnp.bfloat16)]
    reduce_sum x3 -> x0, other arithmetic: 3.67 us -> none  [the longest x2 2.22 us: layer_norm(): variance = jnp.mean(centered * centered, axis=-1, keepdims=True)]
    convert_element_type x4 -> x0, other arithmetic: 3.29 us -> none  [the longest x1 1.73 us: on_device(): mixed = layer_norm(summed, out_gain, out_bias).astype(jnp.bfloat16)]
  transfers between devices with their start and end apart: 4 -> 10, of which waited for: 3 -> 3; matrix products, arithmetic and copies ran while one was open for 8% -> 2% of each run, Pallas kernels for 0% -> 27%
where the time goes in v2:
time: 56.8 us; the launch traced here: 56.4 us
  Pallas kernels  24.4 us (43%)
  starting transfers between devices  21.4 us (38%)
  waiting for transfers between devices  5.22 us (9%)
  local copies, waits for them, and re-layouts  3.5 us (6%)
  other arithmetic  1 us (2%)
  between operations  0.89 us (2%)
    ppermute x9, starting transfers between devices, move(): return lax.ppermute(array, ('row', 'col'), pairs)  20.4 us
    pallas_call x3, Pallas kernels, on_device(): pl.pallas_call(functools.partial(product_kernel, picks, len(lefts), len(b...  17.7 us
    ppermute x9, waiting for transfers between devices, move(): return lax.ppermute(array, ('row', 'col'), pairs)  5.22 us
    pallas_call x1, Pallas kernels, on_device(): pl.pallas_call(left_kernel, out_shape=[jax.ShapeDtypeStruct((rows, column...  3.62 us
    unnamed x24, local copies, waits for them, and re-layouts  3.5 us
    pallas_call x1, Pallas kernels, on_device(): pl.pallas_call(right_kernel, out_shape=[jax.ShapeDtypeStruct((columns, CH...  3.11 us
  transfers between devices with their start and end apart: 10, of which 3 were waited for; matrix products, arithmetic and copies ran while one was open for 2% of the time, Pallas kernels for 27%

profile of v2, /device:TPU:1, one launch (start us, length us, event | category | flops | bytes accessed | tf_op | source)
XLA Modules:
  0.0 56.4 jit_solution(11769983203762573219)
XLA Ops:
  0.7 3.1 %right.1 = (bf16[48,16,128]{2,1,0:T(8,128)(2,1)}, bf16[48,16,128]{2,1,0:T(8,128)(2,1)}, bf16[48,16,128]{2,1,0:T(8,128)(2,1)}) custom-call(s32[1]{0:T(128)S(6)} %copy.14.tokens_ref, bf16[48,48,128]{2,1,0:T(8,128)(2,1)} %pair_ref.3, f32[1,128]{1,0:T(1,128)} %bitcast.10, f32[1,128]{1,0:T(1,128)} %bitcast.12, bf16[128,512]{1,0:T(8,128)(2,1)} %weights_ref.3), custom_call_target="tpu_custom_call" | custom-call | flops 150994944 | bytes 1179648 | tf_op jit(solution)/shard_map/right/pallas_call | solution.py:220
  3.8 5.2 %collective-permute-start.7 = (bf16[48,16,128]{2,1,0:T(8,128)(2,1)}, bf16[48,16,128]{2,1,0:T(8,128)(2,1)S(1)}, u32[]{:S(2)}, u32[]{:S(2)}) collective-permute-start(bf16[48,16,128]{2,1,0:T(8,128)(2,1)} %get-tuple-element.14), channel_id=1, source_target_pairs={{0,8},{1,9},{5,13},{6,14},{10,2},{11,3},{12,4},{15,7},{16,24},{17,... | collective-permute-start | bytes 589832 | tf_op jit(solution)/shard_map/ppermute | solution.py:175
  8.9 3.6 %left_and_gate.1 = (bf16[48,48,128]{2,1,0:T(8,128)(2,1)}, f32[48,48,128]{2,1,0:T(8,128)}) custom-call(s32[1]{0:T(128)S(6)} %copy.14.tokens_ref, bf16[48,48,128]{2,1,0:T(8,128)(2,1)} %pair_ref.3, f32[1,128]{1,0:T(1,128)} %bitcast.11, f32[1,128]{1,0:T(1,128)} %bitcast.13, bf16[128,512]{1,0:T(8,128)(2,1)} %weights_ref.3, bf16[128,128]{1,0:T(8,128)(2,1)} %gate_weights_ref.1), custom_call_target="tpu_custom_call" | custom-call | flops 226492416 | bytes 2359296 | tf_op jit(solution)/shard_map/left_and_gate/pallas_call | solution.py:233
  12.6 1.0 %collective-permute-start = (bf16[48,48,128]{2,1,0:T(8,128)(2,1)}, bf16[48,48,128]{2,1,0:T(8,128)(2,1)S(1)}, u32[]{:S(2)}, u32[]{:S(2)}) collective-permute-start(bf16[48,48,128]{2,1,0:T(8,128)(2,1)} %get-tuple-element.10.refs_0_), channel_id=1, source_target_pairs={{0,3},{1,0},{2,1},{3,2},{4,7},{5,4},{6,5},{7,6},{8,11},{9,8},{10,9... | collective-permute-start | bytes 1769480 | tf_op jit(solution)/shard_map/ppermute | solution.py:20
  13.5 1.3 %collective-permute-start.4 = (bf16[48,16,128]{2,1,0:T(8,128)(2,1)}, bf16[48,16,128]{2,1,0:T(8,128)(2,1)S(1)}, u32[]{:S(2)}, u32[]{:S(2)}) collective-permute-start(bf16[48,16,128]{2,1,0:T(8,128)(2,1)} %get-tuple-element.13), channel_id=1, source_target_pairs={{0,8},{1,9},{5,13},{6,14},{10,2},{11,3},{12,4},{15,7},{16,24},{17,... | collective-permute-start | bytes 589832 | tf_op jit(solution)/shard_map/ppermute | solution.py:175
  14.8 1.3 %collective-permute-start.1 = (bf16[48,16,128]{2,1,0:T(8,128)(2,1)}, bf16[48,16,128]{2,1,0:T(8,128)(2,1)S(1)}, u32[]{:S(2)}, u32[]{:S(2)}) collective-permute-start(bf16[48,16,128]{2,1,0:T(8,128)(2,1)} %get-tuple-element.11), channel_id=1, source_target_pairs={{0,8},{1,9},{5,13},{6,14},{10,2},{11,3},{12,4},{15,7},{16,24},{17,... | collective-permute-start | bytes 589832 | tf_op jit(solution)/shard_map/ppermute | solution.py:175
  16.1 0.0 collective-permute-done.7
  16.2 1.0 %broadcast_select_fusion.refs_2_ = bf16[48,16,128]{2,1,0:T(8,128)(2,1)S(1)} fusion(bf16[48,16,128]{2,1,0:T(8,128)(2,1)} %get-tuple-element.14, bf16[48,16,128]{2,1,0:T(8,128)(2,1)S(1)} %collective-permute-done.7, pred[]{:T(512)S(6)} %lt.10), kind=kLoop, calls=%fused_computation | loop fusion | flops 98304 | bytes 589825 | tf_op jit(solution)/shard_map/jit(_where)/select_n | solution.py:183
  17.1 1.7 %collective-permute-start.8 = (bf16[48,16,128]{2,1,0:T(8,128)(2,1)S(1)}, bf16[48,16,128]{2,1,0:T(8,128)(2,1)S(1)}, u32[]{:S(2)}, u32[]{:S(2)}) collective-permute-start(bf16[48,16,128]{2,1,0:T(8,128)(2,1)S(1)} %broadcast_select_fusion.refs_2_), channel_id=1, source_target_pairs={{0,4},{1,0},{2,6},{3,2},{4,7},{5,1},{6,5},{7,3},{8,12},{9,8},{10,1... | collective-permute-start | bytes 589832 | tf_op jit(solution)/shard_map/ppermute | solution.py:175
  18.8 2.1 %collective-permute-start.9 = (bf16[48,16,128]{2,1,0:T(8,128)(2,1)S(1)}, bf16[48,16,128]{2,1,0:T(8,128)(2,1)S(1)}, u32[]{:S(2)}, u32[]{:S(2)}) collective-permute-start(bf16[48,16,128]{2,1,0:T(8,128)(2,1)S(1)} %broadcast_select_fusion.refs_2_), channel_id=1, source_target_pairs={{1,4},{3,6},{4,3},{6,1},{9,12},{11,14},{12,11},{14,9},{17,20},{19,... | collective-permute-start | bytes 589832 | tf_op jit(solution)/shard_map/ppermute | solution.py:175
  21.0 0.0 collective-permute-done.4
  21.0 1.2 %collective-permute-start.5 = (bf16[48,16,128]{2,1,0:T(8,128)(2,1)S(1)}, bf16[48,16,128]{2,1,0:T(8,128)(2,1)S(1)}, u32[]{:S(2)}, u32[]{:S(2)}) collective-permute-start(bf16[48,16,128]{2,1,0:T(8,128)(2,1)S(1)} %broadcast_select_fusion.1.refs_2_), channel_id=1, source_target_pairs={{0,4},{1,0},{2,6},{3,2},{4,7},{5,1},{6,5},{7,3},{8,12},{9,8},{10,1... | collective-permute-start | bytes 589832 | tf_op jit(solution)/shard_map/ppermute | solution.py:175
  22.2 0.1 collective-permute-done.1
  22.2 3.7 %collective-permute-start.6 = (bf16[48,16,128]{2,1,0:T(8,128)(2,1)S(1)}, bf16[48,16,128]{2,1,0:T(8,128)(2,1)S(1)}, u32[]{:S(2)}, u32[]{:S(2)}) collective-permute-start(bf16[48,16,128]{2,1,0:T(8,128)(2,1)S(1)} %broadcast_select_fusion.1.refs_2_), channel_id=1, source_target_pairs={{1,4},{3,6},{4,3},{6,1},{9,12},{11,14},{12,11},{14,9},{17,20},{19,... | collective-permute-start | bytes 589832 | tf_op jit(solution)/shard_map/ppermute | solution.py:175
  26.0 2.2 %collective-permute-done.8.refs_3_ = bf16[48,16,128]{2,1,0:T(8,128)(2,1)S(1)} collective-permute-done((bf16[48,16,128]{2,1,0:T(8,128)(2,1)S(1)}, bf16[48,16,128]{2,1,0:T(8,128)(2,1)S(1)}, u32[]{:S(2)}, u32[]{:S(2)}) %collective-permute-start.8) | collective-permute-done | bytes 196640 | tf_op jit(solution)/shard_map/ppermute | solution.py:175
  28.2 2.1 %collective-permute-start.2 = (bf16[48,16,128]{2,1,0:T(8,128)(2,1)S(1)}, bf16[48,16,128]{2,1,0:T(8,128)(2,1)S(1)}, u32[]{:S(2)}, u32[]{:S(2)}) collective-permute-start(bf16[48,16,128]{2,1,0:T(8,128)(2,1)S(1)} %broadcast_select_fusion.2.refs_2_), channel_id=1, source_target_pairs={{0,4},{1,0},{2,6},{3,2},{4,7},{5,1},{6,5},{7,3},{8,12},{9,8},{10,1... | collective-permute-start | bytes 589832 | tf_op jit(solution)/shard_map/ppermute | solution.py:175
  30.3 3.0 %collective-permute-done.9.refs_4_ = bf16[48,16,128]{2,1,0:T(8,128)(2,1)S(1)} collective-permute-done((bf16[48,16,128]{2,1,0:T(8,128)(2,1)S(1)}, bf16[48,16,128]{2,1,0:T(8,128)(2,1)S(1)}, u32[]{:S(2)}, u32[]{:S(2)}) %collective-permute-start.9) | collective-permute-done | bytes 196640 | tf_op jit(solution)/shard_map/ppermute | solution.py:175
  33.2 1.9 %collective-permute-start.3 = (bf16[48,16,128]{2,1,0:T(8,128)(2,1)S(1)}, bf16[48,16,128]{2,1,0:T(8,128)(2,1)S(1)}, u32[]{:S(2)}, u32[]{:S(2)}) collective-permute-start(bf16[48,16,128]{2,1,0:T(8,128)(2,1)S(1)} %broadcast_select_fusion.2.refs_2_), channel_id=1, source_target_pairs={{1,4},{3,6},{4,3},{6,1},{9,12},{11,14},{12,11},{14,9},{17,20},{19,... | collective-permute-start | bytes 589832 | tf_op jit(solution)/shard_map/ppermute | solution.py:175
  35.2 0.0 collective-permute-done.refs_1_
  35.2 0.0 copy-start
  35.2 0.8 %copy-done = bf16[48,48,128]{2,1,0:T(8,128)(2,1)} copy-done((bf16[48,48,128]{2,1,0:T(8,128)(2,1)}, bf16[48,48,128]{2,1,0:T(8,128)(2,1)S(1)}, u32[]{:S(2)}) %copy-start) | copy-done | bytes 589848
  36.0 5.9 %product.3.refs_9_ = bf16[48,48,128]{2,1,0:T(8,128)(2,1)} custom-call(bf16[48,48,128]{2,1,0:T(8,128)(2,1)} %get-tuple-element.10.refs_0_, bf16[48,48,128]{2,1,0:T(8,128)(2,1)} %copy-done, bf16[48,16,128]{2,1,0:T(8,128)(2,1)} %copy-done.3, bf16[48,16,128]{2,1,0:T(8,128)(2,1)} %copy-done.10, bf16[48,16,128]{2,1,0:T(8,128)(2,1)} %copy-done.11, ...), custom_call_target="tpu_custom_call" | custom-call | flops 18874368 | bytes 1179648 | tf_op jit(solution)/shard_map/product/pallas_call | solution.py:260
  41.9 0.0 collective-permute-done.5.refs_3_
  41.9 0.0 collective-permute-done.6.refs_4_
  41.9 0.7 %copy-done.4 = bf16[48,16,128]{2,1,0:T(8,128)(2,1)} copy-done((bf16[48,16,128]{2,1,0:T(8,128)(2,1)}, bf16[48,16,128]{2,1,0:T(8,128)(2,1)S(1)}, u32[]{:S(2)}) %copy-start.4) | copy-done | bytes 196632
  42.6 0.7 %copy-done.6 = bf16[48,16,128]{2,1,0:T(8,128)(2,1)} copy-done((bf16[48,16,128]{2,1,0:T(8,128)(2,1)}, bf16[48,16,128]{2,1,0:T(8,128)(2,1)S(1)}, u32[]{:S(2)}) %copy-start.6) | copy-done | bytes 196632
  43.2 5.9 %product.4.refs_9_ = bf16[48,48,128]{2,1,0:T(8,128)(2,1)} custom-call(bf16[48,48,128]{2,1,0:T(8,128)(2,1)} %get-tuple-element.10.refs_0_, bf16[48,48,128]{2,1,0:T(8,128)(2,1)} %copy-done, bf16[48,16,128]{2,1,0:T(8,128)(2,1)} %copy-done.1, bf16[48,16,128]{2,1,0:T(8,128)(2,1)} %copy-done.4, ...), custom_call_target="tpu_custom_call", output_to_operand_aliasing={{}: (9, {})} | custom-call | flops 18874368 | bytes 1179648 | tf_op jit(solution)/shard_map/product/pallas_call | solution.py:260
  49.1 0.0 collective-permute-done.2.refs_3_
  49.1 0.0 collective-permute-done.3.refs_4_
  49.2 0.7 %copy-done.5 = bf16[48,16,128]{2,1,0:T(8,128)(2,1)} copy-done((bf16[48,16,128]{2,1,0:T(8,128)(2,1)}, bf16[48,16,128]{2,1,0:T(8,128)(2,1)S(1)}, u32[]{:S(2)}) %copy-start.5) | copy-done | bytes 196632
  49.8 0.7 %copy-done.7 = bf16[48,16,128]{2,1,0:T(8,128)(2,1)} copy-done((bf16[48,16,128]{2,1,0:T(8,128)(2,1)}, bf16[48,16,128]{2,1,0:T(8,128)(2,1)S(1)}, u32[]{:S(2)}) %copy-start.7) | copy-done | bytes 196632
  50.5 5.9 %product.5 = bf16[48,48,128]{2,1,0:T(8,128)(2,1)} custom-call(bf16[48,48,128]{2,1,0:T(8,128)(2,1)} %get-tuple-element.10.refs_0_, bf16[48,48,128]{2,1,0:T(8,128)(2,1)} %copy-done, bf16[48,16,128]{2,1,0:T(8,128)(2,1)} %copy-done.2, bf16[48,16,128]{2,1,0:T(8,128)(2,1)} %copy-done.5, bf16[48,16,128]{2,1,0:T(8,128)(2,1)} %copy-done.7, ...), custom_call_target="tpu_custom_call", output_to_operand_aliasing={{}: (9, {})} | custom-call | flops 18874368 | bytes 1179648 | tf_op jit(solution)/shard_map/product/pallas_call | solution.py:260
  (20 shorter events, 0.1 us)
Async XLA Ops:
  3.8 17.2 %copy-start.9 = (bf16[48,16,128]{2,1,0:T(8,128)(2,1)S(1)}, bf16[48,16,128]{2,1,0:T(8,128)(2,1)}, u32[]{:S(2)}) copy-start(bf16[48,16,128]{2,1,0:T(8,128)(2,1)} %get-tuple-element.13) | copy-start | bytes 589828
  3.8 22.2 %copy-start.8 = (bf16[48,16,128]{2,1,0:T(8,128)(2,1)S(1)}, bf16[48,16,128]{2,1,0:T(8,128)(2,1)}, u32[]{:S(2)}) copy-start(bf16[48,16,128]{2,1,0:T(8,128)(2,1)} %get-tuple-element.11) | copy-start | bytes 589828
  3.8 12.4 %collective-permute-start.7 = (bf16[48,16,128]{2,1,0:T(8,128)(2,1)}, bf16[48,16,128]{2,1,0:T(8,128)(2,1)S(1)}, u32[]{:S(2)}, u32[]{:S(2)}) collective-permute-start(bf16[48,16,128]{2,1,0:T(8,128)(2,1)} %get-tuple-element.14), channel_id=1, source_target_pairs={{0,8},{1,9},{5,13},{6,14},{10,2},{11,3},{12,4},{15,7},{16,24},{17,... | collective-permute-start | bytes 589832 | tf_op jit(solution)/shard_map/ppermute | solution.py:175
  12.6 22.6 %collective-permute-start = (bf16[48,48,128]{2,1,0:T(8,128)(2,1)}, bf16[48,48,128]{2,1,0:T(8,128)(2,1)S(1)}, u32[]{:S(2)}, u32[]{:S(2)}) collective-permute-start(bf16[48,48,128]{2,1,0:T(8,128)(2,1)} %get-tuple-element.10.refs_0_), channel_id=1, source_target_pairs={{0,3},{1,0},{2,1},{3,2},{4,7},{5,4},{6,5},{7,6},{8,11},{9,8},{10,9... | collective-permute-start | bytes 1769480 | tf_op jit(solution)/shard_map/ppermute | solution.py:20
  13.5 7.5 %collective-permute-start.4 = (bf16[48,16,128]{2,1,0:T(8,128)(2,1)}, bf16[48,16,128]{2,1,0:T(8,128)(2,1)S(1)}, u32[]{:S(2)}, u32[]{:S(2)}) collective-permute-start(bf16[48,16,128]{2,1,0:T(8,128)(2,1)} %get-tuple-element.13), channel_id=1, source_target_pairs={{0,8},{1,9},{5,13},{6,14},{10,2},{11,3},{12,4},{15,7},{16,24},{17,... | collective-permute-start | bytes 589832 | tf_op jit(solution)/shard_map/ppermute | solution.py:175
  14.8 7.4 %collective-permute-start.1 = (bf16[48,16,128]{2,1,0:T(8,128)(2,1)}, bf16[48,16,128]{2,1,0:T(8,128)(2,1)S(1)}, u32[]{:S(2)}, u32[]{:S(2)}) collective-permute-start(bf16[48,16,128]{2,1,0:T(8,128)(2,1)} %get-tuple-element.11), channel_id=1, source_target_pairs={{0,8},{1,9},{5,13},{6,14},{10,2},{11,3},{12,4},{15,7},{16,24},{17,... | collective-permute-start | bytes 589832 | tf_op jit(solution)/shard_map/ppermute | solution.py:175
  17.1 18.1 %copy-start.3 = (bf16[48,16,128]{2,1,0:T(8,128)(2,1)}, bf16[48,16,128]{2,1,0:T(8,128)(2,1)S(1)}, u32[]{:S(2)}) copy-start(bf16[48,16,128]{2,1,0:T(8,128)(2,1)S(1)} %broadcast_select_fusion.refs_2_) | copy-start | bytes 589828
  17.1 11.1 %collective-permute-start.8 = (bf16[48,16,128]{2,1,0:T(8,128)(2,1)S(1)}, bf16[48,16,128]{2,1,0:T(8,128)(2,1)S(1)}, u32[]{:S(2)}, u32[]{:S(2)}) collective-permute-start(bf16[48,16,128]{2,1,0:T(8,128)(2,1)S(1)} %broadcast_select_fusion.refs_2_), channel_id=1, source_target_pairs={{0,4},{1,0},{2,6},{3,2},{4,7},{5,1},{6,5},{7,3},{8,12},{9,8},{10,1... | collective-permute-start | bytes 589832 | tf_op jit(solution)/shard_map/ppermute | solution.py:175
  18.8 14.4 %collective-permute-start.9 = (bf16[48,16,128]{2,1,0:T(8,128)(2,1)S(1)}, bf16[48,16,128]{2,1,0:T(8,128)(2,1)S(1)}, u32[]{:S(2)}, u32[]{:S(2)}) collective-permute-start(bf16[48,16,128]{2,1,0:T(8,128)(2,1)S(1)} %broadcast_select_fusion.refs_2_), channel_id=1, source_target_pairs={{1,4},{3,6},{4,3},{6,1},{9,12},{11,14},{12,11},{14,9},{17,20},{19,... | collective-permute-start | bytes 589832 | tf_op jit(solution)/shard_map/ppermute | solution.py:175
  21.0 20.9 %copy-start.1 = (bf16[48,16,128]{2,1,0:T(8,128)(2,1)}, bf16[48,16,128]{2,1,0:T(8,128)(2,1)S(1)}, u32[]{:S(2)}) copy-start(bf16[48,16,128]{2,1,0:T(8,128)(2,1)S(1)} %broadcast_select_fusion.1.refs_2_) | copy-start | bytes 589828
  21.0 20.8 %collective-permute-start.5 = (bf16[48,16,128]{2,1,0:T(8,128)(2,1)S(1)}, bf16[48,16,128]{2,1,0:T(8,128)(2,1)S(1)}, u32[]{:S(2)}, u32[]{:S(2)}) collective-permute-start(bf16[48,16,128]{2,1,0:T(8,128)(2,1)S(1)} %broadcast_select_fusion.1.refs_2_), channel_id=1, source_target_pairs={{0,4},{1,0},{2,6},{3,2},{4,7},{5,1},{6,5},{7,3},{8,12},{9,8},{10,1... | collective-permute-start | bytes 589832 | tf_op jit(solution)/shard_map/ppermute | solution.py:175
  22.2 19.6 %collective-permute-start.6 = (bf16[48,16,128]{2,1,0:T(8,128)(2,1)S(1)}, bf16[48,16,128]{2,1,0:T(8,128)(2,1)S(1)}, u32[]{:S(2)}, u32[]{:S(2)}) collective-permute-start(bf16[48,16,128]{2,1,0:T(8,128)(2,1)S(1)} %broadcast_select_fusion.1.refs_2_), channel_id=1, source_target_pairs={{1,4},{3,6},{4,3},{6,1},{9,12},{11,14},{12,11},{14,9},{17,20},{19,... | collective-permute-start | bytes 589832 | tf_op jit(solution)/shard_map/ppermute | solution.py:175
  26.0 23.1 %copy-start.2 = (bf16[48,16,128]{2,1,0:T(8,128)(2,1)}, bf16[48,16,128]{2,1,0:T(8,128)(2,1)S(1)}, u32[]{:S(2)}) copy-start(bf16[48,16,128]{2,1,0:T(8,128)(2,1)S(1)} %broadcast_select_fusion.2.refs_2_) | copy-start | bytes 589828
  28.2 7.0 %copy-start.10 = (bf16[48,16,128]{2,1,0:T(8,128)(2,1)}, bf16[48,16,128]{2,1,0:T(8,128)(2,1)S(1)}, u32[]{:S(2)}) copy-start(bf16[48,16,128]{2,1,0:T(8,128)(2,1)S(1)} %collective-permute-done.8.refs_3_) | copy-start | bytes 589828
  28.2 20.9 %collective-permute-start.2 = (bf16[48,16,128]{2,1,0:T(8,128)(2,1)S(1)}, bf16[48,16,128]{2,1,0:T(8,128)(2,1)S(1)}, u32[]{:S(2)}, u32[]{:S(2)}) collective-permute-start(bf16[48,16,128]{2,1,0:T(8,128)(2,1)S(1)} %broadcast_select_fusion.2.refs_2_), channel_id=1, source_target_pairs={{0,4},{1,0},{2,6},{3,2},{4,7},{5,1},{6,5},{7,3},{8,12},{9,8},{10,1... | collective-permute-start | bytes 589832 | tf_op jit(solution)/shard_map/ppermute | solution.py:175
  33.2 2.0 %copy-start.11 = (bf16[48,16,128]{2,1,0:T(8,128)(2,1)}, bf16[48,16,128]{2,1,0:T(8,128)(2,1)S(1)}, u32[]{:S(2)}) copy-start(bf16[48,16,128]{2,1,0:T(8,128)(2,1)S(1)} %collective-permute-done.9.refs_4_) | copy-start | bytes 589828
  33.2 15.9 %collective-permute-start.3 = (bf16[48,16,128]{2,1,0:T(8,128)(2,1)S(1)}, bf16[48,16,128]{2,1,0:T(8,128)(2,1)S(1)}, u32[]{:S(2)}, u32[]{:S(2)}) collective-permute-start(bf16[48,16,128]{2,1,0:T(8,128)(2,1)S(1)} %broadcast_select_fusion.2.refs_2_), channel_id=1, source_target_pairs={{1,4},{3,6},{4,3},{6,1},{9,12},{11,14},{12,11},{14,9},{17,20},{19,... | collective-permute-start | bytes 589832 | tf_op jit(solution)/shard_map/ppermute | solution.py:175
  35.2 0.8 %copy-start = (bf16[48,48,128]{2,1,0:T(8,128)(2,1)}, bf16[48,48,128]{2,1,0:T(8,128)(2,1)S(1)}, u32[]{:S(2)}) copy-start(bf16[48,48,128]{2,1,0:T(8,128)(2,1)S(1)} %collective-permute-done.refs_1_) | copy-start | bytes 1769476
  41.9 0.7 %copy-start.4 = (bf16[48,16,128]{2,1,0:T(8,128)(2,1)}, bf16[48,16,128]{2,1,0:T(8,128)(2,1)S(1)}, u32[]{:S(2)}) copy-start(bf16[48,16,128]{2,1,0:T(8,128)(2,1)S(1)} %collective-permute-done.5.refs_3_) | copy-start | bytes 589828
  42.6 0.7 %copy-start.6 = (bf16[48,16,128]{2,1,0:T(8,128)(2,1)}, bf16[48,16,128]{2,1,0:T(8,128)(2,1)S(1)}, u32[]{:S(2)}) copy-start(bf16[48,16,128]{2,1,0:T(8,128)(2,1)S(1)} %collective-permute-done.6.refs_4_) | copy-start | bytes 589828
  49.1 0.7 %copy-start.5 = (bf16[48,16,128]{2,1,0:T(8,128)(2,1)}, bf16[48,16,128]{2,1,0:T(8,128)(2,1)S(1)}, u32[]{:S(2)}) copy-start(bf16[48,16,128]{2,1,0:T(8,128)(2,1)S(1)} %collective-permute-done.2.refs_3_) | copy-start | bytes 589828
  49.8 0.7 %copy-start.7 = (bf16[48,16,128]{2,1,0:T(8,128)(2,1)}, bf16[48,16,128]{2,1,0:T(8,128)(2,1)S(1)}, u32[]{:S(2)}) copy-start(bf16[48,16,128]{2,1,0:T(8,128)(2,1)S(1)} %collective-permute-done.3.refs_4_) | copy-start | bytes 589828

commit v3 on v2

--- a/solution.py
+++ b/solution.py
@@ -8,6 +8,7 @@
 from jax.sharding import PartitionSpec as P
 
 CHUNK = 16
+LANES = 128
 VMEM_LIMIT = 56 * 1024 * 1024
 
 
@@ -59,21 +60,15 @@
     return parts
 
 
-def right_kernel(tokens_ref, pair_ref, gain_ref, bias_ref, weights_ref, *refs):
-    outs, scratch = refs[:-1], refs[-1]
+def right_kernel(tokens_ref, pair_ref, gain_ref, bias_ref, weights_ref, *outs):
     rows, columns, _ = pair_ref.shape
-    hidden = scratch.shape[1]
+    hidden = outs[0].shape[2]
     step = 4
     for first in range(0, rows, step):
         normed = normed_rows(pair_ref, gain_ref, bias_ref, first, step)
         right = gated(normed, weights_ref, 2 * hidden, hidden)
-        parts = masked(right, tokens_ref, first, step, rows, columns)
-        for row, part in enumerate(parts):
-            scratch[pl.ds((first + row) * columns, columns), :] = part
-    for at, out in enumerate(outs):
-        for third in range(columns):
-            start = at * CHUNK * columns + third
-            out[third] = scratch[pl.ds(start, CHUNK, stride=columns), :].astype(jnp.bfloat16)
+        for row, part in enumerate(masked(right, tokens_ref, first, step, rows, columns)):
+            outs[(first + row) // CHUNK][(first + row) % CHUNK] = part.astype(jnp.bfloat16)
 
 
 def left_kernel(
@@ -94,57 +89,91 @@
         gate_ref[pl.ds(first, step)] = gate.reshape(step, columns, channels)
 
 
-def product_kernel(picks, lefts, rights, *refs):
-    left_refs, refs = refs[:lefts], refs[lefts:]
+def turned(pieces, width):
+    rows = sum(piece.shape[0] for piece in pieces)
+    hidden = pieces[0].shape[1]
+    if width > rows:
+        pieces = pieces + [jnp.zeros((width - rows, hidden), pieces[0].dtype)]
+    stacked = jnp.concatenate(pieces, axis=0)
+    row = lax.broadcasted_iota(jnp.int32, (hidden, hidden), 0)
+    column = lax.broadcasted_iota(jnp.int32, (hidden, hidden), 1)
+    identity = (row == column).astype(jnp.float32).astype(jnp.bfloat16)
+    return lax.dot_general(
+        identity, stacked, (((1,), (1,)), ((), ())), preferred_element_type=jnp.float32
+    )
+
+
+def turn_kernel(*refs):
+    pieces, (out_ref, scratch) = refs[:-2], refs[-2:]
+    rows, _, hidden = pieces[0].shape
+    width = out_ref.shape[2]
+    for row in range(rows):
+        one = turned([ref[row] for ref in pieces], width)
+        for at in range(0, width, LANES):
+            scratch[at // LANES, pl.ds(row, hidden, stride=rows), :] = one[:, at : at + LANES]
+    for channel in range(hidden):
+        for at in range(0, width, LANES):
+            one = scratch[at // LANES, pl.ds(channel * rows, rows), :]
+            out_ref[channel, :, at : at + LANES] = one.astype(jnp.bfloat16)
+
+
+def product_kernel(picks, rights, *refs):
     right_refs, refs = refs[:rights], refs[rights:]
-    gate_ref, gain_ref, bias_ref, weights_ref, *_, out_ref, left_rows, right_rows, product = refs
-    rows, columns, hidden = left_refs[0].shape
-    depth = lefts * columns
+    left_ref, gate_ref, gain_ref, bias_ref, weights_ref, *_, out_ref = refs[:-5]
+    held, arrived, right, product, updates = refs[-5:]
+    hidden, rows, width = left_ref.shape
     even = (lax.axis_index("row") + lax.axis_index("col")) % 2 == 0
 
-    @pl.loop(0, rows)
-    def _(row):
-        for at, ref in enumerate(left_refs):
-            left_rows[pl.ds(row * depth + at * columns, columns), :] = ref[row].astype(jnp.float32)
+    def fetch(source, at):
+        return pltpu.make_async_copy(right_refs[source], held.at[at], arrived.at[at])
 
     for at, (at_even, at_odd) in enumerate(picks):
-        for third in range(columns):
-            piece = right_refs[at_even][third].astype(jnp.float32)
-            if at_odd != at_even:
-                piece = jnp.where(even, piece, right_refs[at_odd][third].astype(jnp.float32))
-            right_rows[pl.ds((at * columns + third) * CHUNK, CHUNK), :] = piece
-
-    group, unroll = 8, 8
-    halves = CHUNK // 8
-
-    @pl.loop(0, rows // group)
-    def _(at):
-        def add(step, sums):
-            sums = list(sums)
-            for inner in range(unroll):
-                third = step * unroll + inner
-                right = [
-                    right_rows[pl.ds(third * CHUNK + 8 * half, 8), :] for half in range(halves)
-                ]
-                for row in range(group):
-                    left = left_rows[pl.ds((at * group + row) * depth + third, 8, stride=0), :]
-                    for half in range(halves):
-                        sums[row * halves + half] += left * right[half]
-            return tuple(sums)
-
-        zeros = tuple(jnp.zeros((8, hidden), jnp.float32) for _ in range(group * halves))
-        sums = lax.fori_loop(0, depth // unroll, add, zeros)
-        for row in range(group):
-            for half in range(halves):
-                start = (at * group + row) * CHUNK + 8 * half
-                product[pl.ds(start, 8), :] = sums[row * halves + half]
-
-    for first in range(0, rows, group):
-        values = product[pl.ds(first * CHUNK, group * CHUNK), :]
-        mixed = layer_norm(values, gain_ref[...], bias_ref[...]).astype(jnp.bfloat16)
-        update = jnp.dot(mixed, weights_ref[...], preferred_element_type=jnp.float32)
-        gate = gate_ref[pl.ds(first, group)]
-        out_ref[pl.ds(first, group)] = (gate * update.reshape(gate.shape)).astype(jnp.bfloat16)
+        if at_even == at_odd:
+            fetch(at_even, at).start()
+        else:
+            pl.when(even)(fetch(at_even, at).start)
+            pl.when(jnp.logical_not(even))(fetch(at_odd, at).start)
+    for at, (at_even, _) in enumerate(picks):
+        fetch(at_even, at).wait()
+
+    for token in range(CHUNK):
+        pieces = [held[at, token] for at in range(len(picks))]
+        one = turned(pieces, width)
+        for at in range(0, width, LANES):
+            right[at // LANES, pl.ds(token, hidden, stride=CHUNK), :] = one[:, at : at + LANES]
+
+    total = jnp.zeros((CHUNK, rows), jnp.float32)
+    for channel in range(hidden):
+        one = 0.0
+        for at in range(0, width, LANES):
+            one += lax.dot_general(
+                right[at // LANES, pl.ds(channel * CHUNK, CHUNK), :].astype(jnp.bfloat16),
+                left_ref[channel, :, at : at + LANES],
+                (((1,), (1,)), ((), ())),
+                preferred_element_type=jnp.float32,
+            )
+        product[pl.ds(channel * CHUNK, CHUNK), :rows] = one
+        total += one
+    average = total / hidden
+    total = jnp.zeros((CHUNK, rows), jnp.float32)
+    for channel in range(hidden):
+        centered = product[pl.ds(channel * CHUNK, CHUNK), :rows] - average
+        total += centered * centered
+    scale = lax.rsqrt(total / hidden + 1e-05)
+    for channel in range(hidden):
+        place = pl.ds(channel * CHUNK, CHUNK)
+        centered = product[place, :rows] - average
+        product[place, :rows] = centered * scale * gain_ref[channel] + bias_ref[channel]
+    for token in range(CHUNK):
+        mixed = product[pl.ds(token, hidden, stride=CHUNK), :][:, :rows].astype(jnp.bfloat16)
+        updates[pl.ds(token, rows, stride=CHUNK), :] = lax.dot_general(
+            mixed, weights_ref[...], (((0,), (0,)), ((), ())), preferred_element_type=jnp.float32
+        )
+    step = 8
+    for first in range(0, rows, step):
+        gate = gate_ref[pl.ds(first, step)]
+        update = updates[pl.ds(first * CHUNK, step * CHUNK), :].reshape(gate.shape)
+        out_ref[pl.ds(first, step)] = (gate * update).astype(jnp.bfloat16)
 
 
 def band_by_sums(chunks, window, row_count, col_count):
@@ -213,16 +242,14 @@
     row_count = lax.axis_size("row")
     window = col_count // 2
     in_gain, in_bias = in_gain.reshape(1, channels), in_bias.reshape(1, channels)
-    out_gain, out_bias = out_gain.reshape(1, hidden), out_bias.reshape(1, hidden)
     params = pltpu.CompilerParams(vmem_limit_bytes=VMEM_LIMIT)
     smem, vmem = whole(pltpu.SMEM), whole()
 
     chunks = pl.pallas_call(
         right_kernel,
-        out_shape=[jax.ShapeDtypeStruct((columns, CHUNK, hidden), jnp.bfloat16)] * (rows // CHUNK),
+        out_shape=[jax.ShapeDtypeStruct((CHUNK, columns, hidden), jnp.bfloat16)] * (rows // CHUNK),
         in_specs=[smem] + [vmem] * 4,
         out_specs=[vmem] * (rows // CHUNK),
-        scratch_shapes=[pltpu.VMEM((tokens, hidden), jnp.float32)],
         compiler_params=params,
         cost_estimate=pl.CostEstimate(
             flops=4 * tokens * channels * hidden, bytes_accessed=4 * tokens * channels, transcendentals=0
@@ -253,25 +280,42 @@
     for _ in range(window - 1):
         lefts.append(shifted(lefts[-1], "col", -1))
 
+    depth = window * columns
+    width = -(-depth // LANES) * LANES
+    turned_left = pl.pallas_call(
+        turn_kernel,
+        out_shape=jax.ShapeDtypeStruct((hidden, rows, width), jnp.bfloat16),
+        in_specs=[vmem] * window,
+        out_specs=vmem,
+        scratch_shapes=[pltpu.VMEM((width // LANES, hidden * rows, LANES), jnp.float32)],
+        compiler_params=params,
+        cost_estimate=pl.CostEstimate(
+            flops=2 * rows * width * hidden * hidden,
+            bytes_accessed=4 * rows * width * hidden,
+            transcendentals=0,
+        ),
+        name="turn_left",
+    )(*lefts)
+
     update = []
-    depth = window * columns
     for at, band in enumerate(bands):
         chunk_of = pl.BlockSpec((rows, CHUNK, channels), lambda step, at=at: (0, at, 0))
         filled = pl.pallas_call(
-            functools.partial(product_kernel, picks, len(lefts), len(band)),
+            functools.partial(product_kernel, picks, len(band)),
             grid=(1,),
             out_shape=jax.ShapeDtypeStruct((rows, columns, channels), jnp.bfloat16),
-            in_specs=[vmem] * (len(lefts) + len(band))
-            + [chunk_of]
-            + [vmem] * 3
+            in_specs=[whole(pl.ANY)] * len(band)
+            + [vmem, chunk_of, smem, smem, vmem]
             + [whole(pl.ANY)] * len(update),
             out_specs=chunk_of,
             scratch_shapes=[
-                pltpu.VMEM((rows * depth + 8, hidden), jnp.float32),
-                pltpu.VMEM((depth * CHUNK, hidden), jnp.float32),
-                pltpu.VMEM((rows * CHUNK, hidden), jnp.float32),
+                pltpu.VMEM((window, CHUNK, columns, hidden), jnp.bfloat16),
+                pltpu.SemaphoreType.DMA((window,)),
+                pltpu.VMEM((width // LANES, hidden * CHUNK, LANES), jnp.float32),
+                pltpu.VMEM((hidden * CHUNK, LANES), jnp.float32),
+                pltpu.VMEM((rows * CHUNK, channels), jnp.float32),
             ],
-            input_output_aliases={len(lefts) + len(band) + 4: 0} if update else {},
+            input_output_aliases={len(band) + 5: 0} if update else {},
             compiler_params=params,
             cost_estimate=pl.CostEstimate(
                 flops=2 * rows * CHUNK * depth * hidden,
@@ -279,7 +323,7 @@
                 transcendentals=0,
             ),
             name="product",
-        )(*lefts, *band, gate, out_gain, out_bias, out_weights, *update)
+        )(*band, turned_left, gate, out_gain, out_bias, out_weights, *update)
         update = [filled]
     return filled
 

time: 56.8 us -> 59.1 us (1.040)
  Pallas kernels: 24.4 us -> 27.4 us
  waiting for transfers between devices: 5.22 us -> 2.32 us
  starting transfers between devices: 21.4 us -> 23.7 us
    pallas_call x4 -> x5, Pallas kernels: 20.8 us -> 23.8 us  [the longest x3 16.9 us: on_device(): pl.pallas_call(functools.partial(product_kernel, picks, len(band)), grid=...]
    ppermute x9, waiting for transfers between devices: 5.22 us -> 2.31 us  [move(): return lax.ppermute(array, ('row', 'col'), pairs)]
    ppermute x9, starting transfers between devices: 20.4 us -> 22.7 us  [move(): return lax.ppermute(array, ('row', 'col'), pairs)]
  transfers between devices with their start and end apart: 10 -> 10, of which waited for: 3 -> 2; matrix products, arithmetic and copies ran while one was open for 2% -> 2% of each run, Pallas kernels for 27% -> 32%
where the time goes in v3:
time: 59.1 us; the launch traced here: 58.6 us
  Pallas kernels  27.4 us (46%)
  starting transfers between devices  23.7 us (40%)
  local copies, waits for them, and re-layouts  3.37 us (6%)
  waiting for transfers between devices  2.32 us (4%)
  other arithmetic  1 us (2%)
  between operations  0.91 us (2%)
    ppermute x9, starting transfers between devices, move(): return lax.ppermute(array, ('row', 'col'), pairs)  22.7 us
    pallas_call x3, Pallas kernels, on_device(): pl.pallas_call(functools.partial(product_kernel, picks, len(band)), grid=...  16.9 us
    pallas_call x1, Pallas kernels, on_device(): pl.pallas_call(turn_kernel, out_shape=jax.ShapeDtypeStruct((hidden, rows,...  3.98 us
    pallas_call x1, Pallas kernels, on_device(): pl.pallas_call(left_kernel, out_shape=[jax.ShapeDtypeStruct((rows, column...  3.58 us
    unnamed x24, local copies, waits for them, and re-layouts  3.37 us
    pallas_call x1, Pallas kernels, on_device(): pl.pallas_call(right_kernel, out_shape=[jax.ShapeDtypeStruct((CHUNK, colu...  2.88 us
    ppermute x9, waiting for transfers between devices, move(): return lax.ppermute(array, ('row', 'col'), pairs)  2.31 us
  transfers between devices with their start and end apart: 10, of which 2 were waited for; matrix products, arithmetic and copies ran while one was open for 2% of the time, Pallas kernels for 32%

profile of v3, /device:TPU:1, one launch (start us, length us, event | category | flops | bytes accessed | tf_op | source)
XLA Modules:
  0.0 58.6 jit_solution(8358478879213190526)
XLA Ops:
  0.7 2.9 %right.1 = (bf16[16,48,128]{2,1,0:T(8,128)(2,1)}, bf16[16,48,128]{2,1,0:T(8,128)(2,1)}, bf16[16,48,128]{2,1,0:T(8,128)(2,1)}) custom-call(s32[1]{0:T(128)S(6)} %copy.14.tokens_ref, bf16[48,48,128]{2,1,0:T(8,128)(2,1)} %pair_ref.3, f32[1,128]{1,0:T(1,128)} %bitcast.2, f32[1,128]{1,0:T(1,128)} %bitcast.4, bf16[128,512]{1,0:T(8,128)(2,1)} %weights_ref.3), custom_call_target="tpu_custom_call" | custom-call | flops 150994944 | bytes 1179648 | tf_op jit(solution)/shard_map/right/pallas_call | solution.py:248
  3.5 5.2 %collective-permute-start.7 = (bf16[16,48,128]{2,1,0:T(8,128)(2,1)}, bf16[16,48,128]{2,1,0:T(8,128)(2,1)S(1)}, u32[]{:S(2)}, u32[]{:S(2)}) collective-permute-start(bf16[16,48,128]{2,1,0:T(8,128)(2,1)} %get-tuple-element.14), channel_id=1, source_target_pairs={{0,8},{1,9},{5,13},{6,14},{10,2},{11,3},{12,4},{15,7},{16,24},{17,... | collective-permute-start | bytes 589832 | tf_op jit(solution)/shard_map/ppermute | solution.py:204
  8.7 3.6 %left_and_gate.1 = (bf16[48,48,128]{2,1,0:T(8,128)(2,1)}, f32[48,48,128]{2,1,0:T(8,128)}) custom-call(s32[1]{0:T(128)S(6)} %copy.14.tokens_ref, bf16[48,48,128]{2,1,0:T(8,128)(2,1)} %pair_ref.3, f32[1,128]{1,0:T(1,128)} %bitcast.3, f32[1,128]{1,0:T(1,128)} %bitcast.5, bf16[128,512]{1,0:T(8,128)(2,1)} %weights_ref.3, bf16[128,128]{1,0:T(8,128)(2,1)} %gate_weights_ref.1), custom_call_target="tpu_custom_call" | custom-call | flops 226492416 | bytes 2359296 | tf_op jit(solution)/shard_map/left_and_gate/pallas_call | solution.py:260
  12.3 1.0 %collective-permute-start.3 = (bf16[48,48,128]{2,1,0:T(8,128)(2,1)}, bf16[48,48,128]{2,1,0:T(8,128)(2,1)S(1)}, u32[]{:S(2)}, u32[]{:S(2)}) collective-permute-start(bf16[48,48,128]{2,1,0:T(8,128)(2,1)} %get-tuple-element.11.refs_0_), channel_id=1, source_target_pairs={{0,3},{1,0},{2,1},{3,2},{4,7},{5,4},{6,5},{7,6},{8,11},{9,8},{10,9... | collective-permute-start | bytes 1769480 | tf_op jit(solution)/shard_map/ppermute | solution.py:21
  13.3 1.3 %collective-permute-start.4 = (bf16[16,48,128]{2,1,0:T(8,128)(2,1)}, bf16[16,48,128]{2,1,0:T(8,128)(2,1)S(1)}, u32[]{:S(2)}, u32[]{:S(2)}) collective-permute-start(bf16[16,48,128]{2,1,0:T(8,128)(2,1)} %get-tuple-element.13), channel_id=1, source_target_pairs={{0,8},{1,9},{5,13},{6,14},{10,2},{11,3},{12,4},{15,7},{16,24},{17,... | collective-permute-start | bytes 589832 | tf_op jit(solution)/shard_map/ppermute | solution.py:204
  14.6 1.3 %collective-permute-start = (bf16[16,48,128]{2,1,0:T(8,128)(2,1)}, bf16[16,48,128]{2,1,0:T(8,128)(2,1)S(1)}, u32[]{:S(2)}, u32[]{:S(2)}) collective-permute-start(bf16[16,48,128]{2,1,0:T(8,128)(2,1)} %get-tuple-element.10), channel_id=1, source_target_pairs={{0,8},{1,9},{5,13},{6,14},{10,2},{11,3},{12,4},{15,7},{16,24},{17,... | collective-permute-start | bytes 589832 | tf_op jit(solution)/shard_map/ppermute | solution.py:204
  15.9 0.0 collective-permute-done.7
  15.9 1.0 %broadcast_select_fusion.refs_0_ = bf16[16,48,128]{2,1,0:T(8,128)(2,1)S(1)} fusion(bf16[16,48,128]{2,1,0:T(8,128)(2,1)} %get-tuple-element.14, bf16[16,48,128]{2,1,0:T(8,128)(2,1)S(1)} %collective-permute-done.7, pred[]{:T(512)S(6)} %lt.10), kind=kLoop, calls=%fused_computation | loop fusion | flops 98304 | bytes 589825 | tf_op jit(solution)/shard_map/jit(_where)/select_n | solution.py:212
  16.9 1.7 %collective-permute-start.8 = (bf16[16,48,128]{2,1,0:T(8,128)(2,1)S(1)}, bf16[16,48,128]{2,1,0:T(8,128)(2,1)S(1)}, u32[]{:S(2)}, u32[]{:S(2)}) collective-permute-start(bf16[16,48,128]{2,1,0:T(8,128)(2,1)S(1)} %broadcast_select_fusion.refs_0_), channel_id=1, source_target_pairs={{0,4},{1,0},{2,6},{3,2},{4,7},{5,1},{6,5},{7,3},{8,12},{9,8},{10,1... | collective-permute-start | bytes 589832 | tf_op jit(solution)/shard_map/ppermute | solution.py:204
  18.6 2.1 %collective-permute-start.9 = (bf16[16,48,128]{2,1,0:T(8,128)(2,1)S(1)}, bf16[16,48,128]{2,1,0:T(8,128)(2,1)S(1)}, u32[]{:S(2)}, u32[]{:S(2)}) collective-permute-start(bf16[16,48,128]{2,1,0:T(8,128)(2,1)S(1)} %broadcast_select_fusion.refs_0_), channel_id=1, source_target_pairs={{1,4},{3,6},{4,3},{6,1},{9,12},{11,14},{12,11},{14,9},{17,20},{19,... | collective-permute-start | bytes 589832 | tf_op jit(solution)/shard_map/ppermute | solution.py:204
  20.7 0.0 collective-permute-done.4
  20.8 1.2 %collective-permute-start.5 = (bf16[16,48,128]{2,1,0:T(8,128)(2,1)S(1)}, bf16[16,48,128]{2,1,0:T(8,128)(2,1)S(1)}, u32[]{:S(2)}, u32[]{:S(2)}) collective-permute-start(bf16[16,48,128]{2,1,0:T(8,128)(2,1)S(1)} %broadcast_select_fusion.1.refs_0_), channel_id=1, source_target_pairs={{0,4},{1,0},{2,6},{3,2},{4,7},{5,1},{6,5},{7,3},{8,12},{9,8},{10,1... | collective-permute-start | bytes 589832 | tf_op jit(solution)/shard_map/ppermute | solution.py:204
  21.9 0.1 collective-permute-done
  22.0 3.7 %collective-permute-start.6 = (bf16[16,48,128]{2,1,0:T(8,128)(2,1)S(1)}, bf16[16,48,128]{2,1,0:T(8,128)(2,1)S(1)}, u32[]{:S(2)}, u32[]{:S(2)}) collective-permute-start(bf16[16,48,128]{2,1,0:T(8,128)(2,1)S(1)} %broadcast_select_fusion.1.refs_0_), channel_id=1, source_target_pairs={{1,4},{3,6},{4,3},{6,1},{9,12},{11,14},{12,11},{14,9},{17,20},{19,... | collective-permute-start | bytes 589832 | tf_op jit(solution)/shard_map/ppermute | solution.py:204
  25.7 2.2 %collective-permute-done.8.refs_1_ = bf16[16,48,128]{2,1,0:T(8,128)(2,1)S(1)} collective-permute-done((bf16[16,48,128]{2,1,0:T(8,128)(2,1)S(1)}, bf16[16,48,128]{2,1,0:T(8,128)(2,1)S(1)}, u32[]{:S(2)}, u32[]{:S(2)}) %collective-permute-start.8) | collective-permute-done | bytes 196640 | tf_op jit(solution)/shard_map/ppermute | solution.py:204
  28.0 2.0 %collective-permute-start.1 = (bf16[16,48,128]{2,1,0:T(8,128)(2,1)S(1)}, bf16[16,48,128]{2,1,0:T(8,128)(2,1)S(1)}, u32[]{:S(2)}, u32[]{:S(2)}) collective-permute-start(bf16[16,48,128]{2,1,0:T(8,128)(2,1)S(1)} %broadcast_select_fusion.2.refs_0_), channel_id=1, source_target_pairs={{0,4},{1,0},{2,6},{3,2},{4,7},{5,1},{6,5},{7,3},{8,12},{9,8},{10,1... | collective-permute-start | bytes 589832 | tf_op jit(solution)/shard_map/ppermute | solution.py:204
  30.0 0.0 collective-permute-done.3.refs_1_
  30.0 4.2 %collective-permute-start.2 = (bf16[16,48,128]{2,1,0:T(8,128)(2,1)S(1)}, bf16[16,48,128]{2,1,0:T(8,128)(2,1)S(1)}, u32[]{:S(2)}, u32[]{:S(2)}) collective-permute-start(bf16[16,48,128]{2,1,0:T(8,128)(2,1)S(1)} %broadcast_select_fusion.2.refs_0_), channel_id=1, source_target_pairs={{1,4},{3,6},{4,3},{6,1},{9,12},{11,14},{12,11},{14,9},{17,20},{19,... | collective-permute-start | bytes 589832 | tf_op jit(solution)/shard_map/ppermute | solution.py:204
  34.2 4.0 %turn_left.1.refs_3_ = bf16[128,48,128]{2,1,0:T(8,128)(2,1)} custom-call(bf16[48,48,128]{2,1,0:T(8,128)(2,1)} %get-tuple-element.11.refs_0_, bf16[48,48,128]{2,1,0:T(8,128)(2,1)} %copy-done.3), custom_call_target="tpu_custom_call" | custom-call | flops 201326592 | bytes 3145728 | tf_op jit(solution)/shard_map/turn_left/pallas_call | solution.py:285
  38.2 0.0 collective-permute-done.9.refs_2_
  38.3 0.7 %copy-done.5 = bf16[16,48,128]{2,1,0:T(8,128)(2,1)} copy-done((bf16[16,48,128]{2,1,0:T(8,128)(2,1)}, bf16[16,48,128]{2,1,0:T(8,128)(2,1)S(1)}, u32[]{:S(2)}) %copy-start.5) | copy-done | bytes 196632
  38.9 5.6 %product.3.refs_8_ = bf16[48,48,128]{2,1,0:T(8,128)(2,1)} custom-call(bf16[16,48,128]{2,1,0:T(8,128)(2,1)} %copy-done, bf16[16,48,128]{2,1,0:T(8,128)(2,1)} %copy-done.4, bf16[16,48,128]{2,1,0:T(8,128)(2,1)} %copy-done.5, bf16[128,48,128]{2,1,0:T(8,128)(2,1)} %turn_left.1.refs_3_, f32[48,48,128]{2,1,0:T(8,128)} %get-tuple-element.12.refs_4_, f32[128]{0:T(128)} %refs_5_.5, ...), custom_call_target="tpu_custom_call" | custom-call | flops 18874368 | bytes 1179648 | tf_op jit(solution)/shard_map/product/pallas_call | solution.py:303
  44.6 0.0 collective-permute-done.5.refs_1_
  44.6 0.0 collective-permute-done.6.refs_2_
  44.6 0.7 %copy-done.6 = bf16[16,48,128]{2,1,0:T(8,128)(2,1)} copy-done((bf16[16,48,128]{2,1,0:T(8,128)(2,1)}, bf16[16,48,128]{2,1,0:T(8,128)(2,1)S(1)}, u32[]{:S(2)}) %copy-start.6) | copy-done | bytes 196632
  45.3 0.7 %copy-done.7 = bf16[16,48,128]{2,1,0:T(8,128)(2,1)} copy-done((bf16[16,48,128]{2,1,0:T(8,128)(2,1)}, bf16[16,48,128]{2,1,0:T(8,128)(2,1)S(1)}, u32[]{:S(2)}) %copy-start.7) | copy-done | bytes 196632
  45.9 5.6 %product.4.refs_8_ = bf16[48,48,128]{2,1,0:T(8,128)(2,1)} custom-call(bf16[16,48,128]{2,1,0:T(8,128)(2,1)} %copy-done.1, bf16[16,48,128]{2,1,0:T(8,128)(2,1)} %copy-done.6, bf16[16,48,128]{2,1,0:T(8,128)(2,1)} %copy-done.7, bf16[128,48,128]{2,1,0:T(8,128)(2,1)} %turn_left.1.refs_3_, ...), custom_call_target="tpu_custom_call", output_to_operand_aliasing={{}: (8, {})} | custom-call | flops 18874368 | bytes 1179648 | tf_op jit(solution)/shard_map/product/pallas_call | solution.py:303
  51.6 0.0 collective-permute-done.1.refs_1_
  51.6 0.0 collective-permute-done.2.refs_2_
  51.6 0.7 %copy-done.8 = bf16[16,48,128]{2,1,0:T(8,128)(2,1)} copy-done((bf16[16,48,128]{2,1,0:T(8,128)(2,1)}, bf16[16,48,128]{2,1,0:T(8,128)(2,1)S(1)}, u32[]{:S(2)}) %copy-start.8) | copy-done | bytes 196632
  52.3 0.7 %copy-done.9 = bf16[16,48,128]{2,1,0:T(8,128)(2,1)} copy-done((bf16[16,48,128]{2,1,0:T(8,128)(2,1)}, bf16[16,48,128]{2,1,0:T(8,128)(2,1)S(1)}, u32[]{:S(2)}) %copy-start.9) | copy-done | bytes 196632
  53.0 5.6 %product.5 = bf16[48,48,128]{2,1,0:T(8,128)(2,1)} custom-call(bf16[16,48,128]{2,1,0:T(8,128)(2,1)} %copy-done.2, bf16[16,48,128]{2,1,0:T(8,128)(2,1)} %copy-done.8, bf16[16,48,128]{2,1,0:T(8,128)(2,1)} %copy-done.9, bf16[128,48,128]{2,1,0:T(8,128)(2,1)} %turn_left.1.refs_3_, ...), custom_call_target="tpu_custom_call", output_to_operand_aliasing={{}: (8, {})} | custom-call | flops 18874368 | bytes 1179648 | tf_op jit(solution)/shard_map/product/pallas_call | solution.py:303
  (21 shorter events, 0.1 us)
Async XLA Ops:
  3.5 17.2 %copy-start.11 = (bf16[16,48,128]{2,1,0:T(8,128)(2,1)S(1)}, bf16[16,48,128]{2,1,0:T(8,128)(2,1)}, u32[]{:S(2)}) copy-start(bf16[16,48,128]{2,1,0:T(8,128)(2,1)} %get-tuple-element.13) | copy-start | bytes 589828
  3.5 22.2 %copy-start.10 = (bf16[16,48,128]{2,1,0:T(8,128)(2,1)S(1)}, bf16[16,48,128]{2,1,0:T(8,128)(2,1)}, u32[]{:S(2)}) copy-start(bf16[16,48,128]{2,1,0:T(8,128)(2,1)} %get-tuple-element.10) | copy-start | bytes 589828
  3.5 12.4 %collective-permute-start.7 = (bf16[16,48,128]{2,1,0:T(8,128)(2,1)}, bf16[16,48,128]{2,1,0:T(8,128)(2,1)S(1)}, u32[]{:S(2)}, u32[]{:S(2)}) collective-permute-start(bf16[16,48,128]{2,1,0:T(8,128)(2,1)} %get-tuple-element.14), channel_id=1, source_target_pairs={{0,8},{1,9},{5,13},{6,14},{10,2},{11,3},{12,4},{15,7},{16,24},{17,... | collective-permute-start | bytes 589832 | tf_op jit(solution)/shard_map/ppermute | solution.py:204
  12.3 17.7 %collective-permute-start.3 = (bf16[48,48,128]{2,1,0:T(8,128)(2,1)}, bf16[48,48,128]{2,1,0:T(8,128)(2,1)S(1)}, u32[]{:S(2)}, u32[]{:S(2)}) collective-permute-start(bf16[48,48,128]{2,1,0:T(8,128)(2,1)} %get-tuple-element.11.refs_0_), channel_id=1, source_target_pairs={{0,3},{1,0},{2,1},{3,2},{4,7},{5,4},{6,5},{7,6},{8,11},{9,8},{10,9... | collective-permute-start | bytes 1769480 | tf_op jit(solution)/shard_map/ppermute | solution.py:21
  13.3 7.5 %collective-permute-start.4 = (bf16[16,48,128]{2,1,0:T(8,128)(2,1)}, bf16[16,48,128]{2,1,0:T(8,128)(2,1)S(1)}, u32[]{:S(2)}, u32[]{:S(2)}) collective-permute-start(bf16[16,48,128]{2,1,0:T(8,128)(2,1)} %get-tuple-element.13), channel_id=1, source_target_pairs={{0,8},{1,9},{5,13},{6,14},{10,2},{11,3},{12,4},{15,7},{16,24},{17,... | collective-permute-start | bytes 589832 | tf_op jit(solution)/shard_map/ppermute | solution.py:204
  14.6 7.4 %collective-permute-start = (bf16[16,48,128]{2,1,0:T(8,128)(2,1)}, bf16[16,48,128]{2,1,0:T(8,128)(2,1)S(1)}, u32[]{:S(2)}, u32[]{:S(2)}) collective-permute-start(bf16[16,48,128]{2,1,0:T(8,128)(2,1)} %get-tuple-element.10), channel_id=1, source_target_pairs={{0,8},{1,9},{5,13},{6,14},{10,2},{11,3},{12,4},{15,7},{16,24},{17,... | collective-permute-start | bytes 589832 | tf_op jit(solution)/shard_map/ppermute | solution.py:204
  16.9 21.4 %copy-start = (bf16[16,48,128]{2,1,0:T(8,128)(2,1)}, bf16[16,48,128]{2,1,0:T(8,128)(2,1)S(1)}, u32[]{:S(2)}) copy-start(bf16[16,48,128]{2,1,0:T(8,128)(2,1)S(1)} %broadcast_select_fusion.refs_0_) | copy-start | bytes 589828
  16.9 11.1 %collective-permute-start.8 = (bf16[16,48,128]{2,1,0:T(8,128)(2,1)S(1)}, bf16[16,48,128]{2,1,0:T(8,128)(2,1)S(1)}, u32[]{:S(2)}, u32[]{:S(2)}) collective-permute-start(bf16[16,48,128]{2,1,0:T(8,128)(2,1)S(1)} %broadcast_select_fusion.refs_0_), channel_id=1, source_target_pairs={{0,4},{1,0},{2,6},{3,2},{4,7},{5,1},{6,5},{7,3},{8,12},{9,8},{10,1... | collective-permute-start | bytes 589832 | tf_op jit(solution)/shard_map/ppermute | solution.py:204
  18.6 19.7 %collective-permute-start.9 = (bf16[16,48,128]{2,1,0:T(8,128)(2,1)S(1)}, bf16[16,48,128]{2,1,0:T(8,128)(2,1)S(1)}, u32[]{:S(2)}, u32[]{:S(2)}) collective-permute-start(bf16[16,48,128]{2,1,0:T(8,128)(2,1)S(1)} %broadcast_select_fusion.refs_0_), channel_id=1, source_target_pairs={{1,4},{3,6},{4,3},{6,1},{9,12},{11,14},{12,11},{14,9},{17,20},{19,... | collective-permute-start | bytes 589832 | tf_op jit(solution)/shard_map/ppermute | solution.py:204
  20.8 17.5 %copy-start.1 = (bf16[16,48,128]{2,1,0:T(8,128)(2,1)}, bf16[16,48,128]{2,1,0:T(8,128)(2,1)S(1)}, u32[]{:S(2)}) copy-start(bf16[16,48,128]{2,1,0:T(8,128)(2,1)S(1)} %broadcast_select_fusion.1.refs_0_) | copy-start | bytes 589828
  20.8 23.8 %collective-permute-start.5 = (bf16[16,48,128]{2,1,0:T(8,128)(2,1)S(1)}, bf16[16,48,128]{2,1,0:T(8,128)(2,1)S(1)}, u32[]{:S(2)}, u32[]{:S(2)}) collective-permute-start(bf16[16,48,128]{2,1,0:T(8,128)(2,1)S(1)} %broadcast_select_fusion.1.refs_0_), channel_id=1, source_target_pairs={{0,4},{1,0},{2,6},{3,2},{4,7},{5,1},{6,5},{7,3},{8,12},{9,8},{10,1... | collective-permute-start | bytes 589832 | tf_op jit(solution)/shard_map/ppermute | solution.py:204
  22.0 22.6 %collective-permute-start.6 = (bf16[16,48,128]{2,1,0:T(8,128)(2,1)S(1)}, bf16[16,48,128]{2,1,0:T(8,128)(2,1)S(1)}, u32[]{:S(2)}, u32[]{:S(2)}) collective-permute-start(bf16[16,48,128]{2,1,0:T(8,128)(2,1)S(1)} %broadcast_select_fusion.1.refs_0_), channel_id=1, source_target_pairs={{1,4},{3,6},{4,3},{6,1},{9,12},{11,14},{12,11},{14,9},{17,20},{19,... | collective-permute-start | bytes 589832 | tf_op jit(solution)/shard_map/ppermute | solution.py:204
  25.7 18.8 %copy-start.2 = (bf16[16,48,128]{2,1,0:T(8,128)(2,1)}, bf16[16,48,128]{2,1,0:T(8,128)(2,1)S(1)}, u32[]{:S(2)}) copy-start(bf16[16,48,128]{2,1,0:T(8,128)(2,1)S(1)} %broadcast_select_fusion.2.refs_0_) | copy-start | bytes 589828
  28.0 10.3 %copy-start.4 = (bf16[16,48,128]{2,1,0:T(8,128)(2,1)}, bf16[16,48,128]{2,1,0:T(8,128)(2,1)S(1)}, u32[]{:S(2)}) copy-start(bf16[16,48,128]{2,1,0:T(8,128)(2,1)S(1)} %collective-permute-done.8.refs_1_) | copy-start | bytes 589828
  28.0 23.6 %collective-permute-start.1 = (bf16[16,48,128]{2,1,0:T(8,128)(2,1)S(1)}, bf16[16,48,128]{2,1,0:T(8,128)(2,1)S(1)}, u32[]{:S(2)}, u32[]{:S(2)}) collective-permute-start(bf16[16,48,128]{2,1,0:T(8,128)(2,1)S(1)} %broadcast_select_fusion.2.refs_0_), channel_id=1, source_target_pairs={{0,4},{1,0},{2,6},{3,2},{4,7},{5,1},{6,5},{7,3},{8,12},{9,8},{10,1... | collective-permute-start | bytes 589832 | tf_op jit(solution)/shard_map/ppermute | solution.py:204
  30.0 4.2 %copy-start.3 = (bf16[48,48,128]{2,1,0:T(8,128)(2,1)}, bf16[48,48,128]{2,1,0:T(8,128)(2,1)S(1)}, u32[]{:S(2)}) copy-start(bf16[48,48,128]{2,1,0:T(8,128)(2,1)S(1)} %collective-permute-done.3.refs_1_) | copy-start | bytes 1769476
  30.0 21.6 %collective-permute-start.2 = (bf16[16,48,128]{2,1,0:T(8,128)(2,1)S(1)}, bf16[16,48,128]{2,1,0:T(8,128)(2,1)S(1)}, u32[]{:S(2)}, u32[]{:S(2)}) collective-permute-start(bf16[16,48,128]{2,1,0:T(8,128)(2,1)S(1)} %broadcast_select_fusion.2.refs_0_), channel_id=1, source_target_pairs={{1,4},{3,6},{4,3},{6,1},{9,12},{11,14},{12,11},{14,9},{17,20},{19,... | collective-permute-start | bytes 589832 | tf_op jit(solution)/shard_map/ppermute | solution.py:204
  38.2 0.7 %copy-start.5 = (bf16[16,48,128]{2,1,0:T(8,128)(2,1)}, bf16[16,48,128]{2,1,0:T(8,128)(2,1)S(1)}, u32[]{:S(2)}) copy-start(bf16[16,48,128]{2,1,0:T(8,128)(2,1)S(1)} %collective-permute-done.9.refs_2_) | copy-start | bytes 589828
  44.6 0.7 %copy-start.6 = (bf16[16,48,128]{2,1,0:T(8,128)(2,1)}, bf16[16,48,128]{2,1,0:T(8,128)(2,1)S(1)}, u32[]{:S(2)}) copy-start(bf16[16,48,128]{2,1,0:T(8,128)(2,1)S(1)} %collective-permute-done.5.refs_1_) | copy-start | bytes 589828
  45.3 0.7 %copy-start.7 = (bf16[16,48,128]{2,1,0:T(8,128)(2,1)}, bf16[16,48,128]{2,1,0:T(8,128)(2,1)S(1)}, u32[]{:S(2)}) copy-start(bf16[16,48,128]{2,1,0:T(8,128)(2,1)S(1)} %collective-permute-done.6.refs_2_) | copy-start | bytes 589828
  51.6 0.7 %copy-start.8 = (bf16[16,48,128]{2,1,0:T(8,128)(2,1)}, bf16[16,48,128]{2,1,0:T(8,128)(2,1)S(1)}, u32[]{:S(2)}) copy-start(bf16[16,48,128]{2,1,0:T(8,128)(2,1)S(1)} %collective-permute-done.1.refs_1_) | copy-start | bytes 589828
  52.3 0.7 %copy-start.9 = (bf16[16,48,128]{2,1,0:T(8,128)(2,1)}, bf16[16,48,128]{2,1,0:T(8,128)(2,1)S(1)}, u32[]{:S(2)}) copy-start(bf16[16,48,128]{2,1,0:T(8,128)(2,1)S(1)} %collective-permute-done.2.refs_2_) | copy-start | bytes 589828

commit v4 on v3

--- a/solution.py
+++ b/solution.py
@@ -9,7 +9,11 @@
 
 CHUNK = 16
 LANES = 128
-VMEM_LIMIT = 56 * 1024 * 1024
+MIB = 1024 * 1024
+
+
+def params(*sizes):
+    return pltpu.CompilerParams(vmem_limit_bytes=min(6 * MIB + 2 * sum(sizes), 56 * MIB))
 
 
 def whole(memory_space=pltpu.VMEM):
@@ -242,7 +246,7 @@
     row_count = lax.axis_size("row")
     window = col_count // 2
     in_gain, in_bias = in_gain.reshape(1, channels), in_bias.reshape(1, channels)
-    params = pltpu.CompilerParams(vmem_limit_bytes=VMEM_LIMIT)
+    block = 2 * tokens * max(channels, hidden)
     smem, vmem = whole(pltpu.SMEM), whole()
 
     chunks = pl.pallas_call(
@@ -250,7 +254,7 @@
         out_shape=[jax.ShapeDtypeStruct((CHUNK, columns, hidden), jnp.bfloat16)] * (rows // CHUNK),
         in_specs=[smem] + [vmem] * 4,
         out_specs=[vmem] * (rows // CHUNK),
-        compiler_params=params,
+        compiler_params=params(2 * block),
         cost_estimate=pl.CostEstimate(
             flops=4 * tokens * channels * hidden, bytes_accessed=4 * tokens * channels, transcendentals=0
         ),
@@ -265,7 +269,7 @@
         ],
         in_specs=[smem] + [vmem] * 5,
         out_specs=[vmem] * 2,
-        compiler_params=params,
+        compiler_params=params(4 * block),
         cost_estimate=pl.CostEstimate(
             flops=6 * tokens * channels * hidden, bytes_accessed=8 * tokens * channels, transcendentals=0
         ),
@@ -288,7 +292,7 @@
         in_specs=[vmem] * window,
         out_specs=vmem,
         scratch_shapes=[pltpu.VMEM((width // LANES, hidden * rows, LANES), jnp.float32)],
-        compiler_params=params,
+        compiler_params=params(window * block, 6 * hidden * rows * width),
         cost_estimate=pl.CostEstimate(
             flops=2 * rows * width * hidden * hidden,
             bytes_accessed=4 * rows * width * hidden,
@@ -316,7 +320,7 @@
                 pltpu.VMEM((rows * CHUNK, channels), jnp.float32),
             ],
             input_output_aliases={len(band) + 5: 0} if update else {},
-            compiler_params=params,
+            compiler_params=params(2 * block, 2 * hidden * (rows + 2 * CHUNK) * width),
             cost_estimate=pl.CostEstimate(
                 flops=2 * rows * CHUNK * depth * hidden,
                 bytes_accessed=2 * rows * depth * hidden,

time: 59.1 us -> 51.4 us (0.87)
  Pallas kernels: 27.4 us -> 16.4 us
  local copies, waits for them, and re-layouts: 3.37 us -> 7.32 us
  starting transfers between devices: 23.7 us -> 26.2 us
  waiting for transfers between devices: 2.32 us -> 0.03 us
  other arithmetic: 1 us -> 0.07 us
    pallas_call x3, Pallas kernels: 16.9 us -> 12.6 us  [on_device(): pl.pallas_call(functools.partial(product_kernel, picks, len(band)), grid=...]
    unnamed x24, local copies, waits for them, and re-layouts: 3.37 us -> 7.32 us
    ppermute x9, starting transfers between devices: 22.7 us -> 25.2 us  [move(): return lax.ppermute(array, ('row', 'col'), pairs)]
    pallas_call x1, Pallas kernels: 3.98 us -> 1.56 us  [on_device(): pl.pallas_call(turn_kernel, out_shape=jax.ShapeDtypeStruct((hidden, rows,...]
    pallas_call x1, Pallas kernels: 3.58 us -> 1.21 us  [on_device(): pl.pallas_call(left_kernel, out_shape=[jax.ShapeDtypeStruct((rows, column...]
    ppermute x9, waiting for transfers between devices: 2.31 us -> 0.02 us  [move(): return lax.ppermute(array, ('row', 'col'), pairs)]
    pallas_call x1, Pallas kernels: 2.88 us -> 1.07 us  [on_device(): pl.pallas_call(right_kernel, out_shape=[jax.ShapeDtypeStruct((CHUNK, colu...]
    select_n x3, other arithmetic: 1 us -> 0.07 us  [band_by_hops(): held = jnp.where(is_root, chunk, far)]
  transfers between devices with their start and end apart: 10 -> 10, of which waited for: 2 -> 0; matrix products, arithmetic and copies ran while one was open for 2% -> 0% of each run, Pallas kernels for 32% -> 22%
where the time goes in v4:
time: 51.4 us; the launch traced here: 51 us
  starting transfers between devices  26.2 us (51%)
  Pallas kernels  16.4 us (32%)
  local copies, waits for them, and re-layouts  7.32 us (14%)
  between operations  0.92 us (2%)
    ppermute x9, starting transfers between devices, move(): return lax.ppermute(array, ('row', 'col'), pairs)  25.2 us
    pallas_call x3, Pallas kernels, on_device(): pl.pallas_call(functools.partial(product_kernel, picks, len(band)), grid=...  12.6 us
    unnamed x24, local copies, waits for them, and re-layouts  7.32 us
    pallas_call x1, Pallas kernels, on_device(): pl.pallas_call(turn_kernel, out_shape=jax.ShapeDtypeStruct((hidden, rows,...  1.56 us
    pallas_call x1, Pallas kernels, on_device(): pl.pallas_call(left_kernel, out_shape=[jax.ShapeDtypeStruct((rows, column...  1.21 us
    pallas_call x1, Pallas kernels, on_device(): pl.pallas_call(right_kernel, out_shape=[jax.ShapeDtypeStruct((CHUNK, colu...  1.07 us
  transfers between devices with their start and end apart: 10, of which 0 were waited for; matrix products, arithmetic and copies ran while one was open for 0% of the time, Pallas kernels for 22%

profile of v4, /device:TPU:1, one launch (start us, length us, event | category | flops | bytes accessed | tf_op | source)
XLA Modules:
  0.0 51.0 jit_solution(12090576193622115073)
XLA Ops:
  0.7 0.0 copy-start
  0.7 1.1 %copy-done = bf16[48,48,128]{2,1,0:T(8,128)(2,1)S(1)} copy-done((bf16[48,48,128]{2,1,0:T(8,128)(2,1)S(1)}, bf16[48,48,128]{2,1,0:T(8,128)(2,1)}, u32[]{:S(2)}) %copy-start) | copy-done | bytes 589848
  1.7 0.9 %copy-done.3 = bf16[128,512]{1,0:T(8,128)(2,1)S(1)} copy-done((bf16[128,512]{1,0:T(8,128)(2,1)S(1)}, bf16[128,512]{1,0:T(8,128)(2,1)}, u32[]{:S(2)}) %copy-start.3) | copy-done | bytes 131096
  2.6 0.7 %copy-done.7 = f32[128]{0:T(128)S(1)} copy-done((f32[128]{0:T(128)S(1)}, f32[128]{0:T(128)}, u32[]{:S(2)}) %copy-start.7) | copy-done | bytes 536
  3.3 0.7 %copy-done.9 = f32[128]{0:T(128)S(1)} copy-done((f32[128]{0:T(128)S(1)}, f32[128]{0:T(128)}, u32[]{:S(2)}) %copy-start.9) | copy-done | bytes 536
  3.9 1.1 %right.1 = (bf16[16,48,128]{2,1,0:T(8,128)(2,1)S(1)}, bf16[16,48,128]{2,1,0:T(8,128)(2,1)S(1)}, bf16[16,48,128]{2,1,0:T(8,128)(2,1)S(1)}) custom-call(s32[1]{0:T(128)S(6)} %copy.14.tokens_ref, bf16[48,48,128]{2,1,0:T(8,128)(2,1)S(1)} %copy-done, f32[1,128]{1,0:T(1,128)S(1)} %bitcast.2, f32[1,128]{1,0:T(1,128)S(1)} %bitcast.4, bf16[128,512]{1,0:T(8,128)(2,1)S(1)} %copy-done.3), custom_call_target="tpu_custom_call" | custom-call | flops 150994944 | bytes 1179648 | tf_op jit(solution)/shard_map/right/pallas_call | solution.py:252
  5.0 5.1 %collective-permute-start.7 = (bf16[16,48,128]{2,1,0:T(8,128)(2,1)S(1)}, bf16[16,48,128]{2,1,0:T(8,128)(2,1)S(1)}, u32[]{:S(2)}, u32[]{:S(2)}) collective-permute-start(bf16[16,48,128]{2,1,0:T(8,128)(2,1)S(1)} %get-tuple-element.14), channel_id=1, source_target_pairs={{0,8},{1,9},{5,13},{6,14},{10,2},{11,3},{12,4},{15,7},{16,24},{17,... | collective-permute-start | bytes 589832 | tf_op jit(solution)/shard_map/ppermute | solution.py:208
  10.1 0.0 copy-start.1
  10.1 1.1 %copy-done.1 = bf16[48,48,128]{2,1,0:T(8,128)(2,1)S(1)} copy-done((bf16[48,48,128]{2,1,0:T(8,128)(2,1)S(1)}, bf16[48,48,128]{2,1,0:T(8,128)(2,1)}, u32[]{:S(2)}) %copy-start.1) | copy-done | bytes 589848
  11.1 0.9 %copy-done.4 = bf16[128,512]{1,0:T(8,128)(2,1)S(1)} copy-done((bf16[128,512]{1,0:T(8,128)(2,1)S(1)}, bf16[128,512]{1,0:T(8,128)(2,1)}, u32[]{:S(2)}) %copy-start.4) | copy-done | bytes 131096
  12.0 0.7 %copy-done.8 = f32[128]{0:T(128)S(1)} copy-done((f32[128]{0:T(128)S(1)}, f32[128]{0:T(128)}, u32[]{:S(2)}) %copy-start.8) | copy-done | bytes 536
  12.7 0.7 %copy-done.10 = f32[128]{0:T(128)S(1)} copy-done((f32[128]{0:T(128)S(1)}, f32[128]{0:T(128)}, u32[]{:S(2)}) %copy-start.10) | copy-done | bytes 536
  13.4 0.8 %copy-done.11 = bf16[128,128]{1,0:T(8,128)(2,1)S(1)} copy-done((bf16[128,128]{1,0:T(8,128)(2,1)S(1)}, bf16[128,128]{1,0:T(8,128)(2,1)}, u32[]{:S(2)}) %copy-start.11) | copy-done | bytes 32792
  14.1 1.2 %left_and_gate.1 = (bf16[48,48,128]{2,1,0:T(8,128)(2,1)S(1)}, f32[48,48,128]{2,1,0:T(8,128)S(1)}) custom-call(s32[1]{0:T(128)S(6)} %copy.14.tokens_ref, bf16[48,48,128]{2,1,0:T(8,128)(2,1)S(1)} %copy-done.1, f32[1,128]{1,0:T(1,128)S(1)} %bitcast.3, f32[1,128]{1,0:T(1,128)S(1)} %bitcast.5, bf16[128,512]{1,0:T(8,128)(2,1)S(1)} %copy-done.4, ...), custom_call_target="tpu_custom_call" | custom-call | flops 226492416 | bytes 2359296 | tf_op jit(solution)/shard_map/left_and_gate/pallas_call | solution.py:264
  15.3 1.0 %collective-permute-start.3 = (bf16[48,48,128]{2,1,0:T(8,128)(2,1)S(1)}, bf16[48,48,128]{2,1,0:T(8,128)(2,1)S(1)}, u32[]{:S(2)}, u32[]{:S(2)}) collective-permute-start(bf16[48,48,128]{2,1,0:T(8,128)(2,1)S(1)} %get-tuple-element.11.refs_0_), channel_id=1, source_target_pairs={{0,3},{1,0},{2,1},{3,2},{4,7},{5,4},{6,5},{7,6},{8,11},{9,8},{10,9... | collective-permute-start | bytes 1769480 | tf_op jit(solution)/shard_map/ppermute | solution.py:25
  16.3 1.3 %collective-permute-start.4 = (bf16[16,48,128]{2,1,0:T(8,128)(2,1)S(1)}, bf16[16,48,128]{2,1,0:T(8,128)(2,1)S(1)}, u32[]{:S(2)}, u32[]{:S(2)}) collective-permute-start(bf16[16,48,128]{2,1,0:T(8,128)(2,1)S(1)} %get-tuple-element.13), channel_id=1, source_target_pairs={{0,8},{1,9},{5,13},{6,14},{10,2},{11,3},{12,4},{15,7},{16,24},{17,... | collective-permute-start | bytes 589832 | tf_op jit(solution)/shard_map/ppermute | solution.py:208
  17.6 1.3 %collective-permute-start = (bf16[16,48,128]{2,1,0:T(8,128)(2,1)S(1)}, bf16[16,48,128]{2,1,0:T(8,128)(2,1)S(1)}, u32[]{:S(2)}, u32[]{:S(2)}) collective-permute-start(bf16[16,48,128]{2,1,0:T(8,128)(2,1)S(1)} %get-tuple-element.10), channel_id=1, source_target_pairs={{0,8},{1,9},{5,13},{6,14},{10,2},{11,3},{12,4},{15,7},{16,24},{17,... | collective-permute-start | bytes 589832 | tf_op jit(solution)/shard_map/ppermute | solution.py:208
  19.0 0.0 collective-permute-done.7
  19.0 1.7 %collective-permute-start.8 = (bf16[16,48,128]{2,1,0:T(8,128)(2,1)S(1)}, bf16[16,48,128]{2,1,0:T(8,128)(2,1)S(1)}, u32[]{:S(2)}, u32[]{:S(2)}) collective-permute-start(bf16[16,48,128]{2,1,0:T(8,128)(2,1)S(1)} %broadcast_select_fusion.refs_0_), channel_id=1, source_target_pairs={{0,4},{1,0},{2,6},{3,2},{4,7},{5,1},{6,5},{7,3},{8,12},{9,8},{10,1... | collective-permute-start | bytes 589832 | tf_op jit(solution)/shard_map/ppermute | solution.py:208
  20.7 3.1 %collective-permute-start.9 = (bf16[16,48,128]{2,1,0:T(8,128)(2,1)S(1)}, bf16[16,48,128]{2,1,0:T(8,128)(2,1)S(1)}, u32[]{:S(2)}, u32[]{:S(2)}) collective-permute-start(bf16[16,48,128]{2,1,0:T(8,128)(2,1)S(1)} %broadcast_select_fusion.refs_0_), channel_id=1, source_target_pairs={{1,4},{3,6},{4,3},{6,1},{9,12},{11,14},{12,11},{14,9},{17,20},{19,... | collective-permute-start | bytes 589832 | tf_op jit(solution)/shard_map/ppermute | solution.py:208
  23.8 0.0 collective-permute-done.4
  23.8 0.0 copy-start.2
  23.8 0.0 copy-start.5
  23.8 0.0 copy-start.6
  23.9 0.9 %collective-permute-start.5 = (bf16[16,48,128]{2,1,0:T(8,128)(2,1)S(1)}, bf16[16,48,128]{2,1,0:T(8,128)(2,1)S(1)}, u32[]{:S(2)}, u32[]{:S(2)}) collective-permute-start(bf16[16,48,128]{2,1,0:T(8,128)(2,1)S(1)} %broadcast_select_fusion.1.refs_0_), channel_id=1, source_target_pairs={{0,4},{1,0},{2,6},{3,2},{4,7},{5,1},{6,5},{7,3},{8,12},{9,8},{10,1... | collective-permute-start | bytes 589832 | tf_op jit(solution)/shard_map/ppermute | solution.py:208
  24.8 5.1 %collective-permute-start.6 = (bf16[16,48,128]{2,1,0:T(8,128)(2,1)S(1)}, bf16[16,48,128]{2,1,0:T(8,128)(2,1)S(1)}, u32[]{:S(2)}, u32[]{:S(2)}) collective-permute-start(bf16[16,48,128]{2,1,0:T(8,128)(2,1)S(1)} %broadcast_select_fusion.1.refs_0_), channel_id=1, source_target_pairs={{1,4},{3,6},{4,3},{6,1},{9,12},{11,14},{12,11},{14,9},{17,20},{19,... | collective-permute-start | bytes 589832 | tf_op jit(solution)/shard_map/ppermute | solution.py:208
  29.9 1.7 %collective-permute-start.1 = (bf16[16,48,128]{2,1,0:T(8,128)(2,1)S(1)}, bf16[16,48,128]{2,1,0:T(8,128)(2,1)S(1)}, u32[]{:S(2)}, u32[]{:S(2)}) collective-permute-start(bf16[16,48,128]{2,1,0:T(8,128)(2,1)S(1)} %broadcast_select_fusion.2.refs_0_), channel_id=1, source_target_pairs={{0,4},{1,0},{2,6},{3,2},{4,7},{5,1},{6,5},{7,3},{8,12},{9,8},{10,1... | collective-permute-start | bytes 589832 | tf_op jit(solution)/shard_map/ppermute | solution.py:208
  31.6 5.1 %collective-permute-start.2 = (bf16[16,48,128]{2,1,0:T(8,128)(2,1)S(1)}, bf16[16,48,128]{2,1,0:T(8,128)(2,1)S(1)}, u32[]{:S(2)}, u32[]{:S(2)}) collective-permute-start(bf16[16,48,128]{2,1,0:T(8,128)(2,1)S(1)} %broadcast_select_fusion.2.refs_0_), channel_id=1, source_target_pairs={{1,4},{3,6},{4,3},{6,1},{9,12},{11,14},{12,11},{14,9},{17,20},{19,... | collective-permute-start | bytes 589832 | tf_op jit(solution)/shard_map/ppermute | solution.py:208
  36.7 1.6 %turn_left.1.refs_3_ = bf16[128,48,128]{2,1,0:T(8,128)(2,1)S(1)} custom-call(bf16[48,48,128]{2,1,0:T(8,128)(2,1)S(1)} %get-tuple-element.11.refs_0_, bf16[48,48,128]{2,1,0:T(8,128)(2,1)S(1)} %collective-permute-done.3.refs_1_), custom_call_target="tpu_custom_call" | custom-call | flops 201326592 | bytes 3145728 | tf_op jit(solution)/shard_map/turn_left/pallas_call | solution.py:289
  38.3 4.2 %product.3.refs_8_ = bf16[48,48,128]{2,1,0:T(8,128)(2,1)} custom-call(bf16[16,48,128]{2,1,0:T(8,128)(2,1)S(1)} %broadcast_select_fusion.refs_0_, bf16[16,48,128]{2,1,0:T(8,128)(2,1)S(1)} %collective-permute-done.8.refs_1_, bf16[16,48,128]{2,1,0:T(8,128)(2,1)S(1)} %collective-permute-done.9.refs_2_, bf16[128,48,128]{2,1,0:T(8,128)(2,1)S(1)} %turn_left.1.refs_3_, ...), custom_call_target="tpu_custom_call" | custom-call | flops 18874368 | bytes 1179648 | tf_op jit(solution)/shard_map/product/pallas_call | solution.py:307
  42.5 4.2 %product.4.refs_8_ = bf16[48,48,128]{2,1,0:T(8,128)(2,1)} custom-call(bf16[16,48,128]{2,1,0:T(8,128)(2,1)S(1)} %broadcast_select_fusion.1.refs_0_, bf16[16,48,128]{2,1,0:T(8,128)(2,1)S(1)} %collective-permute-done.5.refs_1_, bf16[16,48,128]{2,1,0:T(8,128)(2,1)S(1)} %collective-permute-done.6.refs_2_, ...), custom_call_target="tpu_custom_call", output_to_operand_aliasing={{}: (8, {})} | custom-call | flops 18874368 | bytes 1179648 | tf_op jit(solution)/shard_map/product/pallas_call | solution.py:307
  46.8 4.2 %product.5 = bf16[48,48,128]{2,1,0:T(8,128)(2,1)} custom-call(bf16[16,48,128]{2,1,0:T(8,128)(2,1)S(1)} %broadcast_select_fusion.2.refs_0_, bf16[16,48,128]{2,1,0:T(8,128)(2,1)S(1)} %collective-permute-done.1.refs_1_, bf16[16,48,128]{2,1,0:T(8,128)(2,1)S(1)} %collective-permute-done.2.refs_2_, ...), custom_call_target="tpu_custom_call", output_to_operand_aliasing={{}: (8, {})} | custom-call | flops 18874368 | bytes 1179648 | tf_op jit(solution)/shard_map/product/pallas_call | solution.py:307
  (21 shorter events, 0.1 us)
Async XLA Ops:
  0.7 1.1 %copy-start = (bf16[48,48,128]{2,1,0:T(8,128)(2,1)S(1)}, bf16[48,48,128]{2,1,0:T(8,128)(2,1)}, u32[]{:S(2)}) copy-start(bf16[48,48,128]{2,1,0:T(8,128)(2,1)} %pair_ref.3) | copy-start | bytes 1769476
  1.7 0.9 %copy-start.3 = (bf16[128,512]{1,0:T(8,128)(2,1)S(1)}, bf16[128,512]{1,0:T(8,128)(2,1)}, u32[]{:S(2)}) copy-start(bf16[128,512]{1,0:T(8,128)(2,1)} %weights_ref.3) | copy-start | bytes 393220
  2.6 0.7 %copy-start.7 = (f32[128]{0:T(128)S(1)}, f32[128]{0:T(128)}, u32[]{:S(2)}) copy-start(f32[128]{0:T(128)} %param.11) | copy-start | bytes 1540
  3.3 0.7 %copy-start.9 = (f32[128]{0:T(128)S(1)}, f32[128]{0:T(128)}, u32[]{:S(2)}) copy-start(f32[128]{0:T(128)} %param.12) | copy-start | bytes 1540
  5.0 14.0 %collective-permute-start.7 = (bf16[16,48,128]{2,1,0:T(8,128)(2,1)S(1)}, bf16[16,48,128]{2,1,0:T(8,128)(2,1)S(1)}, u32[]{:S(2)}, u32[]{:S(2)}) collective-permute-start(bf16[16,48,128]{2,1,0:T(8,128)(2,1)S(1)} %get-tuple-element.14), channel_id=1, source_target_pairs={{0,8},{1,9},{5,13},{6,14},{10,2},{11,3},{12,4},{15,7},{16,24},{17,... | collective-permute-start | bytes 589832 | tf_op jit(solution)/shard_map/ppermute | solution.py:208
  10.1 1.1 %copy-start.1 = (bf16[48,48,128]{2,1,0:T(8,128)(2,1)S(1)}, bf16[48,48,128]{2,1,0:T(8,128)(2,1)}, u32[]{:S(2)}) copy-start(bf16[48,48,128]{2,1,0:T(8,128)(2,1)} %pair_ref.3) | copy-start | bytes 1769476
  11.1 0.9 %copy-start.4 = (bf16[128,512]{1,0:T(8,128)(2,1)S(1)}, bf16[128,512]{1,0:T(8,128)(2,1)}, u32[]{:S(2)}) copy-start(bf16[128,512]{1,0:T(8,128)(2,1)} %weights_ref.3) | copy-start | bytes 393220
  12.0 0.7 %copy-start.8 = (f32[128]{0:T(128)S(1)}, f32[128]{0:T(128)}, u32[]{:S(2)}) copy-start(f32[128]{0:T(128)} %param.11) | copy-start | bytes 1540
  12.7 0.7 %copy-start.10 = (f32[128]{0:T(128)S(1)}, f32[128]{0:T(128)}, u32[]{:S(2)}) copy-start(f32[128]{0:T(128)} %param.12) | copy-start | bytes 1540
  13.4 0.8 %copy-start.11 = (bf16[128,128]{1,0:T(8,128)(2,1)S(1)}, bf16[128,128]{1,0:T(8,128)(2,1)}, u32[]{:S(2)}) copy-start(bf16[128,128]{1,0:T(8,128)(2,1)} %gate_weights_ref.1) | copy-start | bytes 98308
  15.3 16.3 %collective-permute-start.3 = (bf16[48,48,128]{2,1,0:T(8,128)(2,1)S(1)}, bf16[48,48,128]{2,1,0:T(8,128)(2,1)S(1)}, u32[]{:S(2)}, u32[]{:S(2)}) collective-permute-start(bf16[48,48,128]{2,1,0:T(8,128)(2,1)S(1)} %get-tuple-element.11.refs_0_), channel_id=1, source_target_pairs={{0,3},{1,0},{2,1},{3,2},{4,7},{5,4},{6,5},{7,6},{8,11},{9,8},{10,9... | collective-permute-start | bytes 1769480 | tf_op jit(solution)/shard_map/ppermute | solution.py:25
  16.3 7.4 %collective-permute-start.4 = (bf16[16,48,128]{2,1,0:T(8,128)(2,1)S(1)}, bf16[16,48,128]{2,1,0:T(8,128)(2,1)S(1)}, u32[]{:S(2)}, u32[]{:S(2)}) collective-permute-start(bf16[16,48,128]{2,1,0:T(8,128)(2,1)S(1)} %get-tuple-element.13), channel_id=1, source_target_pairs={{0,8},{1,9},{5,13},{6,14},{10,2},{11,3},{12,4},{15,7},{16,24},{17,... | collective-permute-start | bytes 589832 | tf_op jit(solution)/shard_map/ppermute | solution.py:208
  17.6 7.1 %collective-permute-start = (bf16[16,48,128]{2,1,0:T(8,128)(2,1)S(1)}, bf16[16,48,128]{2,1,0:T(8,128)(2,1)S(1)}, u32[]{:S(2)}, u32[]{:S(2)}) collective-permute-start(bf16[16,48,128]{2,1,0:T(8,128)(2,1)S(1)} %get-tuple-element.10), channel_id=1, source_target_pairs={{0,8},{1,9},{5,13},{6,14},{10,2},{11,3},{12,4},{15,7},{16,24},{17,... | collective-permute-start | bytes 589832 | tf_op jit(solution)/shard_map/ppermute | solution.py:208
  19.0 10.9 %collective-permute-start.8 = (bf16[16,48,128]{2,1,0:T(8,128)(2,1)S(1)}, bf16[16,48,128]{2,1,0:T(8,128)(2,1)S(1)}, u32[]{:S(2)}, u32[]{:S(2)}) collective-permute-start(bf16[16,48,128]{2,1,0:T(8,128)(2,1)S(1)} %broadcast_select_fusion.refs_0_), channel_id=1, source_target_pairs={{0,4},{1,0},{2,6},{3,2},{4,7},{5,1},{6,5},{7,3},{8,12},{9,8},{10,1... | collective-permute-start | bytes 589832 | tf_op jit(solution)/shard_map/ppermute | solution.py:208
  20.7 17.6 %collective-permute-start.9 = (bf16[16,48,128]{2,1,0:T(8,128)(2,1)S(1)}, bf16[16,48,128]{2,1,0:T(8,128)(2,1)S(1)}, u32[]{:S(2)}, u32[]{:S(2)}) collective-permute-start(bf16[16,48,128]{2,1,0:T(8,128)(2,1)S(1)} %broadcast_select_fusion.refs_0_), channel_id=1, source_target_pairs={{1,4},{3,6},{4,3},{6,1},{9,12},{11,14},{12,11},{14,9},{17,20},{19,... | collective-permute-start | bytes 589832 | tf_op jit(solution)/shard_map/ppermute | solution.py:208
  23.8 14.5 %copy-start.2 = (bf16[128,128]{1,0:T(8,128)(2,1)S(1)}, bf16[128,128]{1,0:T(8,128)(2,1)}, u32[]{:S(2)}) copy-start(bf16[128,128]{1,0:T(8,128)(2,1)} %refs_7_.5) | copy-start | bytes 98308
  23.8 14.5 %copy-start.5 = (f32[128]{0:T(128)S(1)}, f32[128]{0:T(128)}, u32[]{:S(2)}) copy-start(f32[128]{0:T(128)} %refs_5_.5) | copy-start | bytes 1540
  23.8 14.5 %copy-start.6 = (f32[128]{0:T(128)S(1)}, f32[128]{0:T(128)}, u32[]{:S(2)}) copy-start(f32[128]{0:T(128)} %refs_6_.5) | copy-start | bytes 1540
  23.9 18.7 %collective-permute-start.5 = (bf16[16,48,128]{2,1,0:T(8,128)(2,1)S(1)}, bf16[16,48,128]{2,1,0:T(8,128)(2,1)S(1)}, u32[]{:S(2)}, u32[]{:S(2)}) collective-permute-start(bf16[16,48,128]{2,1,0:T(8,128)(2,1)S(1)} %broadcast_select_fusion.1.refs_0_), channel_id=1, source_target_pairs={{0,4},{1,0},{2,6},{3,2},{4,7},{5,1},{6,5},{7,3},{8,12},{9,8},{10,1... | collective-permute-start | bytes 589832 | tf_op jit(solution)/shard_map/ppermute | solution.py:208
  24.8 17.8 %collective-permute-start.6 = (bf16[16,48,128]{2,1,0:T(8,128)(2,1)S(1)}, bf16[16,48,128]{2,1,0:T(8,128)(2,1)S(1)}, u32[]{:S(2)}, u32[]{:S(2)}) collective-permute-start(bf16[16,48,128]{2,1,0:T(8,128)(2,1)S(1)} %broadcast_select_fusion.1.refs_0_), channel_id=1, source_target_pairs={{1,4},{3,6},{4,3},{6,1},{9,12},{11,14},{12,11},{14,9},{17,20},{19,... | collective-permute-start | bytes 589832 | tf_op jit(solution)/shard_map/ppermute | solution.py:208
  29.9 16.9 %collective-permute-start.1 = (bf16[16,48,128]{2,1,0:T(8,128)(2,1)S(1)}, bf16[16,48,128]{2,1,0:T(8,128)(2,1)S(1)}, u32[]{:S(2)}, u32[]{:S(2)}) collective-permute-start(bf16[16,48,128]{2,1,0:T(8,128)(2,1)S(1)} %broadcast_select_fusion.2.refs_0_), channel_id=1, source_target_pairs={{0,4},{1,0},{2,6},{3,2},{4,7},{5,1},{6,5},{7,3},{8,12},{9,8},{10,1... | collective-permute-start | bytes 589832 | tf_op jit(solution)/shard_map/ppermute | solution.py:208
  31.6 15.1 %collective-permute-start.2 = (bf16[16,48,128]{2,1,0:T(8,128)(2,1)S(1)}, bf16[16,48,128]{2,1,0:T(8,128)(2,1)S(1)}, u32[]{:S(2)}, u32[]{:S(2)}) collective-permute-start(bf16[16,48,128]{2,1,0:T(8,128)(2,1)S(1)} %broadcast_select_fusion.2.refs_0_), channel_id=1, source_target_pairs={{1,4},{3,6},{4,3},{6,1},{9,12},{11,14},{12,11},{14,9},{17,20},{19,... | collective-permute-start | bytes 589832 | tf_op jit(solution)/shard_map/ppermute | solution.py:208

commit v5 on v0

v5 whole, which is shorter than its diff:
```python
import functools

import jax
import jax.numpy as jnp
from jax import lax
from jax.experimental import pallas as pl
from jax.experimental.pallas import tpu as pltpu
from jax.sharding import PartitionSpec as P

LANES = 128
MIB = 1024 * 1024


def params(*sizes):
    return pltpu.CompilerParams(vmem_limit_bytes=min(6 * MIB + 2 * sum(sizes), 56 * MIB))


def cost(flops, bytes_accessed):
    return pl.CostEstimate(flops=flops, bytes_accessed=bytes_accessed, transcendentals=0)


VMEM = pl.BlockSpec(memory_space=pltpu.VMEM)
SMEM = pl.BlockSpec(memory_space=pltpu.SMEM)
ANY = pl.BlockSpec(memory_space=pl.ANY)


def shifted(array, axis, by):
    devices = lax.axis_size(axis)
    return lax.ppermute(array, axis, [(i, (i + by) % devices) for i in range(devices)])


def from_root(array, axis, root):
    mine = lax.axis_index(axis) == root
    return lax.psum(jnp.where(mine, array, jnp.zeros_like(array)), axis)


def layer_norm(values, gain, offset):
    average = jnp.mean(values, axis=-1, keepdims=True)
    centered = values - average
    variance = jnp.mean(centered * centered, axis=-1, keepdims=True)
    return centered * lax.rsqrt(variance + 1e-05) * gain + offset


def normed_rows(block, gain_ref, bias_ref):
    rows, columns, channels = block.shape
    values = block.reshape(rows * columns, channels).astype(jnp.float32)
    return layer_norm(values, gain_ref[...], bias_ref[...]).astype(jnp.bfloat16)


def right_kernel(hops, first, tokens_ref, pair_ref, gain_ref, bias_ref, weights_ref, *refs):
    out_ref = refs[-1]
    count, columns, hidden = out_ref.shape
    row_pos, col_pos = lax.axis_index("row"), lax.axis_index("col")
    tokens = tokens_ref[0]
    block_row = row_pos
    if hops:
        is_root = (col_pos - row_pos + 4) % 4 < 2
        block_row = jnp.where((row_pos + col_pos) % 2 == 0, col_pos, (col_pos + 3) % 4)
    row_start = block_row * pair_ref.shape[0] + first
    valid_columns = tokens - col_pos * columns
    position = lax.broadcasted_iota(jnp.int32, (columns, hidden), 0)
    step = 4
    for at in range(0, count, step):
        block = pair_ref[pl.ds(first + at, step)]
        if hops:
            block = jnp.where(is_root, block, refs[0][pl.ds(at, step)])
        normed = normed_rows(block, gain_ref, bias_ref)
        both = jnp.dot(
            normed, weights_ref[...], preferred_element_type=jnp.float32
        )
        right = jax.nn.sigmoid(both[:, :hidden]) * both[:, hidden:]
        for row in range(step):
            limit = jnp.where(row_start + at + row < tokens, valid_columns, 0)
            part = right[row * columns : (row + 1) * columns]
            out_ref[at + row] = jnp.where(position < limit, part, 0.0).astype(jnp.bfloat16)


def left_kernel(blocks, tokens_ref, *refs):
    pair_refs, refs = refs[:blocks], refs[blocks:]
    gain_ref, bias_ref, weights_ref, gate_weights_ref, *passed, scratch = refs
    passed, (left_ref, gate_ref), handed = passed[:4], passed[4:6], passed[6:]
    for source, target in zip(passed, handed):
        target[...] = source[...]
    rows, columns, channels = pair_refs[0].shape
    hidden, _, width = left_ref.shape
    tokens = tokens_ref[0]
    row_start = lax.axis_index("row") * rows
    col_pos, col_count = lax.axis_index("col"), lax.axis_size("col")
    lane = lax.broadcasted_iota(jnp.int32, (1, width), 1)
    keep = jnp.zeros((1, width), jnp.float32)
    for at in range(blocks):
        end = at * columns + jnp.minimum(tokens - (col_pos + at) % col_count * columns, columns)
        keep += jnp.where((lane >= at * columns) & (lane < end), 1.0, 0.0)
    padding = [jnp.zeros((width - blocks * columns, channels), jnp.bfloat16)]
    if width == blocks * columns:
        padding = []
    step = 4
    for first in range(0, rows, step):
        normed = [normed_rows(ref[pl.ds(first, step)], gain_ref, bias_ref) for ref in pair_refs]
        gate = jnp.dot(normed[0], gate_weights_ref[...], preferred_element_type=jnp.float32)
        gate_ref[pl.ds(first, step)] = jax.nn.sigmoid(gate).reshape(step, columns, channels)
        for row in range(step):
            thirds = [piece[row * columns : (row + 1) * columns] for piece in normed]
            both = lax.dot_general(
                weights_ref[...],
                jnp.concatenate(thirds + padding, axis=0),
                (((1,), (1,)), ((), ())),
                preferred_element_type=jnp.float32,
            )
            left = jax.nn.sigmoid(both[:hidden]) * both[hidden:]
            valid = jnp.where(row_start + first + row < tokens, keep, 0.0)
            left = jnp.where(valid > 0.0, left, 0.0)
            for at in range(0, width, LANES):
                scratch[at // LANES, pl.ds(first + row, hidden, stride=rows), :] = left[
                    :, at : at + LANES
                ]
    for channel in range(hidden):
        for at in range(0, width, LANES):
            one = scratch[at // LANES, pl.ds(channel * rows, rows), :]
            left_ref[channel, :, at : at + LANES] = one.astype(jnp.bfloat16)


def turned(pieces, width):
    rows = sum(piece.shape[0] for piece in pieces)
    hidden = pieces[0].shape[1]
    if width > rows:
        pieces = pieces + [jnp.zeros((width - rows, hidden), pieces[0].dtype)]
    row = lax.broadcasted_iota(jnp.int32, (hidden, hidden), 0)
    column = lax.broadcasted_iota(jnp.int32, (hidden, hidden), 1)
    identity = (row == column).astype(jnp.float32).astype(jnp.bfloat16)
    return lax.dot_general(
        identity,
        jnp.concatenate(pieces, axis=0),
        (((1,), (1,)), ((), ())),
        preferred_element_type=jnp.float32,
    )


def product_kernel(picks, rights, first, *refs):
    right_refs, refs = refs[:rights], refs[rights:]
    left_ref, gate_ref, gain_ref, bias_ref, weights_ref, *_, out_ref = refs[:-5]
    right, product, updates, result, sent = refs[-5:]
    hidden, rows, width = left_ref.shape
    count = right_refs[0].shape[0]
    even = (lax.axis_index("row") + lax.axis_index("col")) % 2 == 0

    for token in range(count):
        pieces = []
        for at_even, at_odd in picks:
            piece = right_refs[at_even][token]
            if at_odd != at_even:
                piece = jnp.where(even, piece, right_refs[at_odd][token])
            pieces.append(piece)
        one = turned(pieces, width)
        for at in range(0, width, LANES):
            right[at // LANES, pl.ds(token, hidden, stride=count), :] = one[:, at : at + LANES]

    total = jnp.zeros((count, rows), jnp.float32)
    for channel in range(hidden):
        one = 0.0
        for at in range(0, width, LANES):
            one += lax.dot_general(
                right[at // LANES, pl.ds(channel * count, count), :].astype(jnp.bfloat16),
                left_ref[channel, :, at : at + LANES],
                (((1,), (1,)), ((), ())),
                preferred_element_type=jnp.float32,
            )
        product[pl.ds(channel * count, count), :rows] = one
        total += one
    average = total / hidden
    total = jnp.zeros((count, rows), jnp.float32)
    for channel in range(hidden):
        centered = product[pl.ds(channel * count, count), :rows] - average
        total += centered * centered
    scale = lax.rsqrt(total / hidden + 1e-05)
    for channel in range(hidden):
        place = pl.ds(channel * count, count)
        centered = product[place, :rows] - average
        product[place, :rows] = centered * scale * gain_ref[channel] + bias_ref[channel]
    for token in range(count):
        mixed = product[pl.ds(token, hidden, stride=count), :][:, :rows].astype(jnp.bfloat16)
        updates[pl.ds(token, rows, stride=count), :] = lax.dot_general(
            mixed, weights_ref[...], (((0,), (0,)), ((), ())), preferred_element_type=jnp.float32
        )
    step = 8
    for at in range(0, rows, step):
        gate = gate_ref[pl.ds(at, step), pl.ds(first, count)]
        update = updates[pl.ds(at * count, step * count), :].reshape(gate.shape)
        result[pl.ds(at, step)] = (gate * update).astype(jnp.bfloat16)
    copy = pltpu.make_async_copy(result, out_ref.at[:, pl.ds(first, count)], sent)
    copy.start()
    copy.wait()


def band_by_sums(right, spans, window, row_count, col_count, columns):
    blocks_per_row = col_count // row_count
    col_pos = lax.axis_index("col")
    pieces = []
    for offset in range(window):
        block_id = (col_pos - offset) % col_count
        start = block_id % blocks_per_row * columns
        received = from_root(
            lax.dynamic_slice_in_dim(right, start, columns, 0), "row", block_id // blocks_per_row
        )
        pieces.append(received if offset == 0 else shifted(received, "col", -offset))
    bands = [[piece[first : first + count] for piece in pieces] for first, count in spans]
    return bands, [(offset, offset) for offset in range(window)]


def band_by_hops(pair_state, right_of, spans):
    def at(r, c):
        return r % 4 * 4 + c % 4

    def move(array, pairs):
        return lax.ppermute(array, ("row", "col"), pairs)

    everyone = [(r, c) for r in range(4) for c in range(4)]
    roots = [(r, c) for r, c in everyone if (c - r) % 4 < 2]
    fars = [
        move(pair_state[first : first + count], [(at(r, c), at(r ^ 2, c)) for r, c in roots])
        for first, count in spans
    ]
    bands = []
    for (first, count), far in zip(spans, fars):
        held = right_of(first, count, far)
        near = move(
            held,
            [
                (at(r, c), at(r ^ 1, c) if (r + c) % 2 == 0 else at(r, c - 1))
                for r, c in everyone
            ],
        )
        cross = move(
            held, [(at(r, c), at(r ^ 1, c - 1)) for r, c in everyone if (r + c) % 2 == 1]
        )
        bands.append([held, near, cross])
    return bands, [(0, 1), (1, 2)]


def on_device(
    pair_state,
    token_count,
    in_gain,
    in_bias,
    in_weights,
    gate_weights,
    out_gain,
    out_bias,
    out_weights,
):
    rows, columns, channels = pair_state.shape
    hidden = out_weights.shape[0]
    tokens = rows * columns
    col_count = lax.axis_size("col")
    row_count = lax.axis_size("row")
    window = col_count // 2
    depth = window * columns
    width = -(-depth // LANES) * LANES
    in_gain, in_bias = in_gain.reshape(1, channels), in_bias.reshape(1, channels)
    block = 2 * tokens * max(channels, hidden)
    hops = row_count == 4 and col_count == 4
    last = 16
    spans = [(0, columns - last), (columns - last, last)]

    pairs = [pair_state]
    for _ in range(window - 1):
        pairs.append(shifted(pairs[-1], "col", -1))
    passed = [in_gain, in_bias, in_weights[:, 2 * hidden :], out_weights]
    left, gate, *handed = pl.pallas_call(
        functools.partial(left_kernel, window),
        out_shape=[
            jax.ShapeDtypeStruct((hidden, rows, width), jnp.bfloat16),
            jax.ShapeDtypeStruct((rows, columns, channels), jnp.float32),
        ]
        + [jax.ShapeDtypeStruct(array.shape, array.dtype) for array in passed],
        in_specs=[SMEM] + [VMEM] * (window + 8),
        out_specs=[VMEM] * 6,
        scratch_shapes=[pltpu.VMEM((width // LANES, hidden * rows, LANES), jnp.float32)],
        compiler_params=params((window + 2) * block, 6 * hidden * rows * width),
        cost_estimate=cost(
            4 * window * tokens * channels * hidden, 6 * rows * width * hidden
        ),
        name="left_and_gate",
    )(token_count, *pairs, in_gain, in_bias, in_weights[:, : 2 * hidden].T, gate_weights, *passed)
    in_gain, in_bias, right_weights, out_weights = handed

    def right_of(first, count, *far):
        return pl.pallas_call(
            functools.partial(right_kernel, hops, first),
            out_shape=jax.ShapeDtypeStruct((count, columns, hidden), jnp.bfloat16),
            in_specs=[SMEM] + [VMEM] * (4 + len(far)),
            out_specs=VMEM,
            compiler_params=params(2 * block),
            cost_estimate=cost(4 * count * columns * channels * hidden, 6 * count * columns * channels),
            name="right",
        )(token_count, pair_state, in_gain, in_bias, right_weights, *far)

    if hops:
        bands, picks = band_by_hops(pair_state, right_of, spans)
    else:
        bands, picks = band_by_sums(
            right_of(0, rows), spans, window, row_count, col_count, columns
        )

    update = []
    for (first, count), band in zip(spans, bands):
        filled = pl.pallas_call(
            functools.partial(product_kernel, picks, len(band), first),
            out_shape=jax.ShapeDtypeStruct((rows, columns, channels), jnp.bfloat16),
            in_specs=[VMEM] * (len(band) + 2) + [SMEM, SMEM, VMEM] + [ANY] * len(update),
            out_specs=ANY,
            scratch_shapes=[
                pltpu.VMEM((width // LANES, hidden * count, LANES), jnp.float32),
                pltpu.VMEM((hidden * count, LANES), jnp.float32),
                pltpu.VMEM((rows * count, channels), jnp.float32),
                pltpu.VMEM((rows, count, channels), jnp.bfloat16),
                pltpu.SemaphoreType.DMA,
            ],
            input_output_aliases={len(band) + 5: 0} if update else {},
            compiler_params=params(2 * block, 2 * hidden * (rows + 2 * count) * width),
            cost_estimate=cost(
                2 * rows * count * depth * hidden, 4 * rows * depth * hidden
            ),
            name="product",
        )(*band, left, gate, out_gain, out_bias, out_weights, *update)
        update = [filled]
    return filled


def solution(mesh):
    placed = (P(("crops", "row"), "col", None), P("crops"), P(), P(), P(), P(), P(), P(), P())
    return jax.shard_map(
        on_device,
        mesh=mesh,
        in_specs=placed,
        out_specs=P(("crops", "row"), "col", None),
        check_vma=False,
    )
```

time: 105 us -> 49 us (0.47)
  waiting for transfers between devices: 57.1 us -> 6.91 us
  starting transfers between devices: 0.61 us -> 23.1 us
  Pallas kernels: 0 us -> 14.8 us
  between operations: 14.3 us -> 0.84 us
  other arithmetic: 10.5 us -> 0 us
  matrix products: 9.77 us -> 0 us
  local copies, waits for them, and re-layouts: 12.1 us -> 3.09 us
    psum x1 -> x0, waiting for transfers between devices: 55.6 us -> none  [from_root(): return lax.psum(jnp.where(mine, array, jnp.zeros_like(array)), axis)]
    ppermute x0 -> x6, starting transfers between devices: none -> 23 us  [move(): return lax.ppermute(array, ('row', 'col'), pairs)]
    pallas_call x0 -> x5, Pallas kernels: none -> 14.8 us  [the longest x2 10.4 us: on_device(): pl.pallas_call(functools.partial(product_kernel, picks, len(band), first)...]
    dot_general x5 -> x0, matrix products: 9.77 us -> none  [the longest x2 6.37 us: contract(): jnp.einsum('ikh,jkh->ijh', left_piece, right_piece, preferred_element_typ...]
    ppermute x0 -> x6, waiting for transfers between devices: none -> 6.91 us  [move(): return lax.ppermute(array, ('row', 'col'), pairs)]
    convert_element_type x4 -> x0, other arithmetic: 4.54 us -> none  [the longest x1 2.01 us: on_device(): (pair_mask * jax.nn.sigmoid(projected[:, :, 0]) * projected[:, :, 1]).ast...]
    ppermute x2 -> x0, local copies, waits for them, and re-layouts: 4.36 us -> none  [shifted(): lax.ppermute(array, axis, [(i, (i + by) % devices) for i in range(devices)])]
    reduce_sum x3 -> x0, other arithmetic: 3.67 us -> none  [the longest x2 2.22 us: layer_norm(): variance = jnp.mean(centered * centered, axis=-1, keepdims=True)]
  transfers between devices with their start and end apart: 3 -> 7, of which waited for: 2 -> 3; matrix products, arithmetic and copies ran while one was open for 10% -> 6% of each run, Pallas kernels for 0% -> 23%
where the time goes in v5:
time: 49 us; the launch traced here: 48.7 us
  starting transfers between devices  23.1 us (47%)
  Pallas kernels  14.8 us (30%)
  waiting for transfers between devices  6.91 us (14%)
  local copies, waits for them, and re-layouts  3.09 us (6%)
  between operations  0.84 us (2%)
    ppermute x6, starting transfers between devices, move(): return lax.ppermute(array, ('row', 'col'), pairs)  23 us
    pallas_call x2, Pallas kernels, on_device(): pl.pallas_call(functools.partial(product_kernel, picks, len(band), first)...  10.4 us
    ppermute x6, waiting for transfers between devices, move(): return lax.ppermute(array, ('row', 'col'), pairs)  6.91 us
    pallas_call x1, Pallas kernels, on_device(): pl.pallas_call(functools.partial(left_kernel, window), out_shape=[jax.Sha...  3.2 us
    slice x2, local copies, waits for them, and re-layouts, band_by_hops(): pair_state[first:first + count]  2.06 us
    pallas_call x2, Pallas kernels, right_of(): pl.pallas_call(functools.partial(right_kernel, hops, first), out_shape=ja...  1.2 us
  transfers between devices with their start and end apart: 7, of which 3 were waited for; matrix products, arithmetic and copies ran while one was open for 6% of the time, Pallas kernels for 23%

profile of v5, /device:TPU:1, one launch (start us, length us, event | category | flops | bytes accessed | tf_op | source)
XLA Modules:
  0.0 48.7 jit_solution(15746298174511901016)
XLA Ops:
  0.0 0.0 copy-start.1
  0.0 0.0 copy-start.2
  0.0 0.1 collective-permute-start
  0.1 1.1 %slice.15 = bf16[32,48,128]{2,1,0:T(8,128)(2,1)S(1)} slice(bf16[48,48,128]{2,1,0:T(8,128)(2,1)} %pair_ref.3), slice={[0:32], [0:48], [0:128]} | slice | bytes 786432 | tf_op jit(solution)/shard_map/slice | solution.py:220
  1.2 5.6 %collective-permute-start.4 = (bf16[32,48,128]{2,1,0:T(8,128)(2,1)S(1)}, bf16[32,48,128]{2,1,0:T(8,128)(2,1)S(1)}, u32[]{:S(2)}, u32[]{:S(2)}) collective-permute-start(bf16[32,48,128]{2,1,0:T(8,128)(2,1)S(1)} %slice.15), channel_id=1, source_target_pairs={{0,8},{1,9},{5,13},{6,14},{10,2},{11,3},{12,4},{15,7},{16,24},{17,... | collective-permute-start | bytes 1179656 | tf_op jit(solution)/shard_map/ppermute | solution.py:215
  6.9 0.9 %slice.14 = bf16[16,48,128]{2,1,0:T(8,128)(2,1)S(1)} slice(bf16[48,48,128]{2,1,0:T(8,128)(2,1)} %pair_ref.3), slice={[32:48], [0:48], [0:128]} | slice | bytes 393216 | tf_op jit(solution)/shard_map/slice | solution.py:220
  7.8 1.3 %collective-permute-start.1 = (bf16[16,48,128]{2,1,0:T(8,128)(2,1)S(1)}, bf16[16,48,128]{2,1,0:T(8,128)(2,1)S(1)}, u32[]{:S(2)}, u32[]{:S(2)}) collective-permute-start(bf16[16,48,128]{2,1,0:T(8,128)(2,1)S(1)} %slice.14), channel_id=1, source_target_pairs={{0,8},{1,9},{5,13},{6,14},{10,2},{11,3},{12,4},{15,7},{16,24},{17,... | collective-permute-start | bytes 589832 | tf_op jit(solution)/shard_map/ppermute | solution.py:215
  9.8 0.9 %fusion = (bf16[128,256]{1,0:T(8,128)(2,1)S(1)}, bf16[128,256]{1,0:T(8,128)(2,1)S(1)}) fusion(bf16[128,512]{1,0:T(8,128)(2,1)} %param.13), kind=kLoop, calls=%fused_computation | loop fusion | bytes 262144 | tf_op jit(solution)/shard_map/slice | solution.py:268
  10.6 0.1 copy.12
  10.8 0.0 collective-permute-done.refs_1_
  10.8 0.0 copy-done
  10.8 0.0 copy-done.3
  10.8 0.0 copy-done.4
  10.8 0.0 copy-done.1
  10.8 3.2 %left_and_gate.1 = (bf16[128,48,128]{2,1,0:T(8,128)(2,1)S(1)}, f32[48,48,128]{2,1,0:T(8,128)S(1)}, f32[1,128]{1,0:T(1,128)S(1)}, f32[1,128]{1,0:T(1,128)S(1)}, b...) custom-call(s32[1]{0:T(128)S(6)} %copy.14.tokens_ref, bf16[48,48,128]{2,1,0:T(8,128)(2,1)S(1)} %copy-done, ...), custom_call_target="tpu_custom_call" | custom-call | flops 301989888 | bytes 4718592 | tf_op jit(solution)/shard_map/left_and_gate/pallas_call | solution.py:269
  14.0 0.0 copy-start.5
  14.0 0.0 copy-start.6
  14.1 0.2 collective-permute-done.4.refs_0_
  14.3 0.7 %right.3.refs_0_ = bf16[32,48,128]{2,1,0:T(8,128)(2,1)S(1)} custom-call(s32[1]{0:T(128)S(6)} %copy.14.tokens_ref, bf16[48,48,128]{2,1,0:T(8,128)(2,1)S(1)} %copy-done, f32[1,128]{1,0:T(1,128)S(1)} %get-tuple-element.11.gain_ref, f32[1,128]{1,0:T(1,128)S(1)} %get-tuple-element.12.bias_ref, bf16[128,256]{1,0:T(8,128)(2,1)S(1)} %get-tuple-element.13.weights_ref, ...), custom_call_target="tpu_custom_call" | custom-call | flops 100663296 | bytes 1179648 | tf_op jit(solution)/shard_map/right/pallas_call | solution.py:288
  15.0 3.5 %collective-permute-start.5 = (bf16[32,48,128]{2,1,0:T(8,128)(2,1)S(1)}, bf16[32,48,128]{2,1,0:T(8,128)(2,1)S(1)}, u32[]{:S(2)}, u32[]{:S(2)}) collective-permute-start(bf16[32,48,128]{2,1,0:T(8,128)(2,1)S(1)} %right.3.refs_0_), channel_id=1, source_target_pairs={{0,4},{1,0},{2,6},{3,2},{4,7},{5,1},{6,5},{7,3},{8,12},{9,8},{10,1... | collective-permute-start | bytes 1179656 | tf_op jit(solution)/shard_map/ppermute | solution.py:215
  18.5 1.9 %collective-permute-start.6 = (bf16[32,48,128]{2,1,0:T(8,128)(2,1)S(1)}, bf16[32,48,128]{2,1,0:T(8,128)(2,1)S(1)}, u32[]{:S(2)}, u32[]{:S(2)}) collective-permute-start(bf16[32,48,128]{2,1,0:T(8,128)(2,1)S(1)} %right.3.refs_0_), channel_id=1, source_target_pairs={{1,4},{3,6},{4,3},{6,1},{9,12},{11,14},{12,11},{14,9},{17,20},{19,... | collective-permute-start | bytes 1179656 | tf_op jit(solution)/shard_map/ppermute | solution.py:215
  20.4 0.0 collective-permute-done.1.refs_0_
  20.4 0.5 %right.2.refs_0_ = bf16[16,48,128]{2,1,0:T(8,128)(2,1)S(1)} custom-call(s32[1]{0:T(128)S(6)} %copy.14.tokens_ref, bf16[48,48,128]{2,1,0:T(8,128)(2,1)S(1)} %copy-done, f32[1,128]{1,0:T(1,128)S(1)} %get-tuple-element.11.gain_ref, f32[1,128]{1,0:T(1,128)S(1)} %get-tuple-element.12.bias_ref, bf16[128,256]{1,0:T(8,128)(2,1)S(1)} %get-tuple-element.13.weights_ref, ...), custom_call_target="tpu_custom_call" | custom-call | flops 50331648 | bytes 589824 | tf_op jit(solution)/shard_map/right/pallas_call | solution.py:288
  20.9 0.1 collective-permute-start.2
  21.0 10.6 %collective-permute-start.3 = (bf16[16,48,128]{2,1,0:T(8,128)(2,1)S(1)}, bf16[16,48,128]{2,1,0:T(8,128)(2,1)S(1)}, u32[]{:S(2)}, u32[]{:S(2)}) collective-permute-start(bf16[16,48,128]{2,1,0:T(8,128)(2,1)S(1)} %right.2.refs_0_), channel_id=1, source_target_pairs={{1,4},{3,6},{4,3},{6,1},{9,12},{11,14},{12,11},{14,9},{17,20},{19,... | collective-permute-start | bytes 589832 | tf_op jit(solution)/shard_map/ppermute | solution.py:215
  31.6 0.7 %collective-permute-done.5.refs_1_ = bf16[32,48,128]{2,1,0:T(8,128)(2,1)S(1)} collective-permute-done((bf16[32,48,128]{2,1,0:T(8,128)(2,1)S(1)}, bf16[32,48,128]{2,1,0:T(8,128)(2,1)S(1)}, u32[]{:S(2)}, u32[]{:S(2)}) %collective-permute-start.5) | collective-permute-done | bytes 393248 | tf_op jit(solution)/shard_map/ppermute | solution.py:215
  32.3 6.0 %collective-permute-done.6.refs_2_ = bf16[32,48,128]{2,1,0:T(8,128)(2,1)S(1)} collective-permute-done((bf16[32,48,128]{2,1,0:T(8,128)(2,1)S(1)}, bf16[32,48,128]{2,1,0:T(8,128)(2,1)S(1)}, u32[]{:S(2)}, u32[]{:S(2)}) %collective-permute-start.6) | collective-permute-done | bytes 393248 | tf_op jit(solution)/shard_map/ppermute | solution.py:215
  38.3 0.0 copy-done.5
  38.3 6.7 %product.2.refs_8_ = bf16[48,48,128]{2,1,0:T(8,128)(2,1)} custom-call(bf16[32,48,128]{2,1,0:T(8,128)(2,1)S(1)} %right.3.refs_0_, bf16[32,48,128]{2,1,0:T(8,128)(2,1)S(1)} %collective-permute-done.5.refs_1_, bf16[32,48,128]{2,1,0:T(8,128)(2,1)S(1)} %collective-permute-done.6.refs_2_, bf16[128,48,128]{2,1,0:T(8,128)(2,1)S(1)} %get-tuple-element.14.refs_3_, ...), custom_call_target="tpu_custom_call" | custom-call | flops 37748736 | bytes 2359296 | tf_op jit(solution)/shard_map/product/pallas_call | solution.py:307
  45.0 0.0 collective-permute-done.2.refs_1_
  45.0 0.0 collective-permute-done.3.refs_2_
  45.0 3.7 %product.3 = bf16[48,48,128]{2,1,0:T(8,128)(2,1)} custom-call(bf16[16,48,128]{2,1,0:T(8,128)(2,1)S(1)} %right.2.refs_0_, bf16[16,48,128]{2,1,0:T(8,128)(2,1)S(1)} %collective-permute-done.2.refs_1_, bf16[16,48,128]{2,1,0:T(8,128)(2,1)S(1)} %collective-permute-done.3.refs_2_, ...), custom_call_target="tpu_custom_call", output_to_operand_aliasing={{}: (8, {})} | custom-call | flops 18874368 | bytes 2359296 | tf_op jit(solution)/shard_map/product/pallas_call | solution.py:307
  (5 shorter events, 0.0 us)
Async XLA Ops:
  0.0 10.8 %copy-start = (bf16[48,48,128]{2,1,0:T(8,128)(2,1)S(1)}, bf16[48,48,128]{2,1,0:T(8,128)(2,1)}, u32[]{:S(2)}) copy-start(bf16[48,48,128]{2,1,0:T(8,128)(2,1)} %pair_ref.3) | copy-start | bytes 1769476
  0.0 10.8 %copy-start.3 = (f32[128]{0:T(128)S(1)}, f32[128]{0:T(128)}, u32[]{:S(2)}) copy-start(f32[128]{0:T(128)} %param.11) | copy-start | bytes 1540
  0.0 10.8 %copy-start.4 = (f32[128]{0:T(128)S(1)}, f32[128]{0:T(128)}, u32[]{:S(2)}) copy-start(f32[128]{0:T(128)} %param.12) | copy-start | bytes 1540
  0.0 10.8 %copy-start.1 = (bf16[128,128]{1,0:T(8,128)(2,1)S(1)}, bf16[128,128]{1,0:T(8,128)(2,1)}, u32[]{:S(2)}) copy-start(bf16[128,128]{1,0:T(8,128)(2,1)} %refs_5_.3) | copy-start | bytes 98308
  0.0 10.8 %copy-start.2 = (bf16[128,128]{1,0:T(8,128)(2,1)S(1)}, bf16[128,128]{1,0:T(8,128)(2,1)}, u32[]{:S(2)}) copy-start(bf16[128,128]{1,0:T(8,128)(2,1)} %refs_9_.1) | copy-start | bytes 98308
  0.0 10.7 %collective-permute-start = (bf16[48,48,128]{2,1,0:T(8,128)(2,1)}, bf16[48,48,128]{2,1,0:T(8,128)(2,1)S(1)}, u32[]{:S(2)}, u32[]{:S(2)}) collective-permute-start(bf16[48,48,128]{2,1,0:T(8,128)(2,1)} %pair_ref.3), channel_id=1, source_target_pairs={{0,3},{1,0},{2,1},{3,2},{4,7},{5,4},{6,5},{7,6},{8,11},{9,8},{10,9... | collective-permute-start | bytes 1769480 | tf_op jit(solution)/shard_map/ppermute | solution.py:29
  1.2 13.0 %collective-permute-start.4 = (bf16[32,48,128]{2,1,0:T(8,128)(2,1)S(1)}, bf16[32,48,128]{2,1,0:T(8,128)(2,1)S(1)}, u32[]{:S(2)}, u32[]{:S(2)}) collective-permute-start(bf16[32,48,128]{2,1,0:T(8,128)(2,1)S(1)} %slice.15), channel_id=1, source_target_pairs={{0,8},{1,9},{5,13},{6,14},{10,2},{11,3},{12,4},{15,7},{16,24},{17,... | collective-permute-start | bytes 1179656 | tf_op jit(solution)/shard_map/ppermute | solution.py:215
  7.8 12.6 %collective-permute-start.1 = (bf16[16,48,128]{2,1,0:T(8,128)(2,1)S(1)}, bf16[16,48,128]{2,1,0:T(8,128)(2,1)S(1)}, u32[]{:S(2)}, u32[]{:S(2)}) collective-permute-start(bf16[16,48,128]{2,1,0:T(8,128)(2,1)S(1)} %slice.14), channel_id=1, source_target_pairs={{0,8},{1,9},{5,13},{6,14},{10,2},{11,3},{12,4},{15,7},{16,24},{17,... | collective-permute-start | bytes 589832 | tf_op jit(solution)/shard_map/ppermute | solution.py:215
  14.0 24.3 %copy-start.5 = (f32[128]{0:T(128)S(1)}, f32[128]{0:T(128)}, u32[]{:S(2)}) copy-start(f32[128]{0:T(128)} %refs_5_.5) | copy-start | bytes 1540
  14.0 24.2 %copy-start.6 = (f32[128]{0:T(128)S(1)}, f32[128]{0:T(128)}, u32[]{:S(2)}) copy-start(f32[128]{0:T(128)} %refs_6_.3) | copy-start | bytes 1540
  15.0 17.3 %collective-permute-start.5 = (bf16[32,48,128]{2,1,0:T(8,128)(2,1)S(1)}, bf16[32,48,128]{2,1,0:T(8,128)(2,1)S(1)}, u32[]{:S(2)}, u32[]{:S(2)}) collective-permute-start(bf16[32,48,128]{2,1,0:T(8,128)(2,1)S(1)} %right.3.refs_0_), channel_id=1, source_target_pairs={{0,4},{1,0},{2,6},{3,2},{4,7},{5,1},{6,5},{7,3},{8,12},{9,8},{10,1... | collective-permute-start | bytes 1179656 | tf_op jit(solution)/shard_map/ppermute | solution.py:215
  18.5 19.8 %collective-permute-start.6 = (bf16[32,48,128]{2,1,0:T(8,128)(2,1)S(1)}, bf16[32,48,128]{2,1,0:T(8,128)(2,1)S(1)}, u32[]{:S(2)}, u32[]{:S(2)}) collective-permute-start(bf16[32,48,128]{2,1,0:T(8,128)(2,1)S(1)} %right.3.refs_0_), channel_id=1, source_target_pairs={{1,4},{3,6},{4,3},{6,1},{9,12},{11,14},{12,11},{14,9},{17,20},{19,... | collective-permute-start | bytes 1179656 | tf_op jit(solution)/shard_map/ppermute | solution.py:215
  20.9 24.1 %collective-permute-start.2 = (bf16[16,48,128]{2,1,0:T(8,128)(2,1)S(1)}, bf16[16,48,128]{2,1,0:T(8,128)(2,1)S(1)}, u32[]{:S(2)}, u32[]{:S(2)}) collective-permute-start(bf16[16,48,128]{2,1,0:T(8,128)(2,1)S(1)} %right.2.refs_0_), channel_id=1, source_target_pairs={{0,4},{1,0},{2,6},{3,2},{4,7},{5,1},{6,5},{7,3},{8,12},{9,8},{10,1... | collective-permute-start | bytes 589832 | tf_op jit(solution)/shard_map/ppermute | solution.py:215
  21.0 24.0 %collective-permute-start.3 = (bf16[16,48,128]{2,1,0:T(8,128)(2,1)S(1)}, bf16[16,48,128]{2,1,0:T(8,128)(2,1)S(1)}, u32[]{:S(2)}, u32[]{:S(2)}) collective-permute-start(bf16[16,48,128]{2,1,0:T(8,128)(2,1)S(1)} %right.2.refs_0_), channel_id=1, source_target_pairs={{1,4},{3,6},{4,3},{6,1},{9,12},{11,14},{12,11},{14,9},{17,20},{19,... | collective-permute-start | bytes 589832 | tf_op jit(solution)/shard_map/ppermute | solution.py:215

commit v6 on v5

--- a/solution.py
+++ b/solution.py
@@ -47,32 +47,25 @@
     return layer_norm(values, gain_ref[...], bias_ref[...]).astype(jnp.bfloat16)
 
 
-def right_kernel(hops, first, tokens_ref, pair_ref, gain_ref, bias_ref, weights_ref, *refs):
-    out_ref = refs[-1]
-    count, columns, hidden = out_ref.shape
-    row_pos, col_pos = lax.axis_index("row"), lax.axis_index("col")
+def right_kernel(origin, tokens_ref, pair_ref, gain_ref, bias_ref, weights_ref, *outs):
+    columns, hidden = outs[0].shape[1:]
+    row_block, third_block = origin()
     tokens = tokens_ref[0]
-    block_row = row_pos
-    if hops:
-        is_root = (col_pos - row_pos + 4) % 4 < 2
-        block_row = jnp.where((row_pos + col_pos) % 2 == 0, col_pos, (col_pos + 3) % 4)
-    row_start = block_row * pair_ref.shape[0] + first
-    valid_columns = tokens - col_pos * columns
+    row_start = row_block * pair_ref.shape[0]
+    valid_columns = tokens - third_block * columns
     position = lax.broadcasted_iota(jnp.int32, (columns, hidden), 0)
     step = 4
-    for at in range(0, count, step):
-        block = pair_ref[pl.ds(first + at, step)]
-        if hops:
-            block = jnp.where(is_root, block, refs[0][pl.ds(at, step)])
-        normed = normed_rows(block, gain_ref, bias_ref)
-        both = jnp.dot(
-            normed, weights_ref[...], preferred_element_type=jnp.float32
-        )
-        right = jax.nn.sigmoid(both[:, :hidden]) * both[:, hidden:]
-        for row in range(step):
-            limit = jnp.where(row_start + at + row < tokens, valid_columns, 0)
-            part = right[row * columns : (row + 1) * columns]
-            out_ref[at + row] = jnp.where(position < limit, part, 0.0).astype(jnp.bfloat16)
+    first = 0
+    for out_ref in outs:
+        for at in range(0, out_ref.shape[0], step):
+            normed = normed_rows(pair_ref[pl.ds(first + at, step)], gain_ref, bias_ref)
+            both = jnp.dot(normed, weights_ref[...], preferred_element_type=jnp.float32)
+            right = jax.nn.sigmoid(both[:, :hidden]) * both[:, hidden:]
+            for row in range(step):
+                limit = jnp.where(row_start + first + at + row < tokens, valid_columns, 0)
+                part = right[row * columns : (row + 1) * columns]
+                out_ref[at + row] = jnp.where(position < limit, part, 0.0).astype(jnp.bfloat16)
+        first += out_ref.shape[0]
 
 
 def left_kernel(blocks, tokens_ref, *refs):
@@ -136,20 +129,23 @@
     )
 
 
-def product_kernel(picks, rights, first, *refs):
+def product_kernel(picks, place, rights, first, count, *refs):
     right_refs, refs = refs[:rights], refs[rights:]
     left_ref, gate_ref, gain_ref, bias_ref, weights_ref, *_, out_ref = refs[:-5]
     right, product, updates, result, sent = refs[-5:]
     hidden, rows, width = left_ref.shape
-    count = right_refs[0].shape[0]
-    even = (lax.axis_index("row") + lax.axis_index("col")) % 2 == 0
+    mine = place()
+
+    def row_of(source, token):
+        ref = right_refs[source]
+        return ref[token if ref.shape[0] == count else first + token]
 
     for token in range(count):
         pieces = []
-        for at_even, at_odd in picks:
-            piece = right_refs[at_even][token]
-            if at_odd != at_even:
-                piece = jnp.where(even, piece, right_refs[at_odd][token])
+        for sources in picks:
+            piece = row_of(sources[0], token)
+            for at, source in enumerate(sources[1:], 1):
+                piece = jnp.where(mine == at, row_of(source, token), piece)
             pieces.append(piece)
         one = turned(pieces, width)
         for at in range(0, width, LANES):
@@ -192,7 +188,7 @@
     copy.wait()
 
 
-def band_by_sums(right, spans, window, row_count, col_count, columns):
+def band_by_sums(right, window, row_count, col_count, columns):
     blocks_per_row = col_count // row_count
     col_pos = lax.axis_index("col")
     pieces = []
@@ -203,38 +199,37 @@
             lax.dynamic_slice_in_dim(right, start, columns, 0), "row", block_id // blocks_per_row
         )
         pieces.append(received if offset == 0 else shifted(received, "col", -offset))
-    bands = [[piece[first : first + count] for piece in pieces] for first, count in spans]
-    return bands, [(offset, offset) for offset in range(window)]
-
-
-def band_by_hops(pair_state, right_of, spans):
-    def at(r, c):
-        return r % 4 * 4 + c % 4
-
-    def move(array, pairs):
-        return lax.ppermute(array, ("row", "col"), pairs)
-
-    everyone = [(r, c) for r in range(4) for c in range(4)]
-    roots = [(r, c) for r, c in everyone if (c - r) % 4 < 2]
-    fars = [
-        move(pair_state[first : first + count], [(at(r, c), at(r ^ 2, c)) for r, c in roots])
-        for first, count in spans
-    ]
-    bands = []
-    for (first, count), far in zip(spans, fars):
-        held = right_of(first, count, far)
-        near = move(
-            held,
-            [
-                (at(r, c), at(r ^ 1, c) if (r + c) % 2 == 0 else at(r, c - 1))
-                for r, c in everyone
-            ],
-        )
-        cross = move(
-            held, [(at(r, c), at(r ^ 1, c - 1)) for r, c in everyone if (r + c) % 2 == 1]
-        )
-        bands.append([held, near, cross])
-    return bands, [(0, 1), (1, 2)]
+    return pieces
+
+
+def hop_place():
+    return lax.axis_index("row") ^ lax.axis_index("col")
+
+
+def far_origin():
+    row_pos, col_pos = lax.axis_index("row"), lax.axis_index("col")
+    diagonal = hop_place() == 2
+    row_block = jnp.where(diagonal, col_pos, jnp.where(col_pos == 2, row_pos - 2, 3 - row_pos))
+    return row_block, jnp.where(diagonal, col_pos, (row_block + 1) % 4)
+
+
+def hops():
+    relay = {0: (2, 2), 1: (3, 2), 2: (1, 0), 3: (0, 0)}
+    column = range(4)
+    out, near, near_more, far, far_more = [], [], [], [], []
+    for c in column:
+        out += [((c, c), (c ^ 2, c)), ((c, (c + 1) % 4), relay[c])]
+        near += [((c, c), (c ^ 1, c)), ((c, (c + 1) % 4), (c, c))]
+        near_more += [((c, (c + 1) % 4), (c ^ 1, c))]
+        far += [((c ^ 2, c), (c ^ 3, c)), (relay[c], (c ^ 2, c))]
+        far_more += [(relay[c], (c ^ 3, c))]
+    return out, near, near_more, far, far_more
+
+
+def move(array, pairs):
+    return lax.ppermute(
+        array, ("row", "col"), [(r * 4 + c, to_r * 4 + to_c) for (r, c), (to_r, to_c) in pairs]
+    )
 
 
 def on_device(
@@ -258,14 +253,35 @@
     width = -(-depth // LANES) * LANES
     in_gain, in_bias = in_gain.reshape(1, channels), in_bias.reshape(1, channels)
     block = 2 * tokens * max(channels, hidden)
-    hops = row_count == 4 and col_count == 4
+    by_hops = row_count == 4 and col_count == 4
     last = 16
     spans = [(0, columns - last), (columns - last, last)]
 
+    def right_of(origin, pair, parts):
+        return pl.pallas_call(
+            functools.partial(right_kernel, origin),
+            out_shape=[
+                jax.ShapeDtypeStruct((count, columns, hidden), jnp.bfloat16) for count in parts
+            ],
+            in_specs=[SMEM] + [VMEM] * 4,
+            out_specs=[VMEM] * len(parts),
+            compiler_params=params(2 * block),
+            cost_estimate=cost(4 * tokens * channels * hidden, 6 * tokens * channels),
+            name="right",
+        )(token_count, pair, in_gain, in_bias, right_weights)
+
+    def here():
+        return lax.axis_index("row"), lax.axis_index("col")
+
+    right_weights = in_weights[:, 2 * hidden :]
+    if by_hops:
+        out, near, near_more, far, far_more = hops()
+        arrived = move(pair_state, out)
     pairs = [pair_state]
     for _ in range(window - 1):
         pairs.append(shifted(pairs[-1], "col", -1))
-    passed = [in_gain, in_bias, in_weights[:, 2 * hidden :], out_weights]
+    (right,) = right_of(here, pair_state, [rows])
+    passed = [in_gain, in_bias, right_weights, out_weights]
     left, gate, *handed = pl.pallas_call(
         functools.partial(left_kernel, window),
         out_shape=[
@@ -284,28 +300,20 @@
     )(token_count, *pairs, in_gain, in_bias, in_weights[:, : 2 * hidden].T, gate_weights, *passed)
     in_gain, in_bias, right_weights, out_weights = handed
 
-    def right_of(first, count, *far):
-        return pl.pallas_call(
-            functools.partial(right_kernel, hops, first),
-            out_shape=jax.ShapeDtypeStruct((count, columns, hidden), jnp.bfloat16),
-            in_specs=[SMEM] + [VMEM] * (4 + len(far)),
-            out_specs=VMEM,
-            compiler_params=params(2 * block),
-            cost_estimate=cost(4 * count * columns * channels * hidden, 6 * count * columns * channels),
-            name="right",
-        )(token_count, pair_state, in_gain, in_bias, right_weights, *far)
-
-    if hops:
-        bands, picks = band_by_hops(pair_state, right_of, spans)
+    if by_hops:
+        near, near_more = move(right, near), move(right, near_more)
+        bands = []
+        for mine in right_of(far_origin, arrived, [count for _, count in spans]):
+            bands.append([right, near, near_more, mine, move(mine, far), move(mine, far_more)])
+        picks, place = [(0, 1, 3, 4), (1, 2, 4, 5)], hop_place
     else:
-        bands, picks = band_by_sums(
-            right_of(0, rows), spans, window, row_count, col_count, columns
-        )
+        bands = [band_by_sums(right, window, row_count, col_count, columns)] * len(spans)
+        picks, place = [(at,) for at in range(window)], lambda: 0
 
     update = []
     for (first, count), band in zip(spans, bands):
         filled = pl.pallas_call(
-            functools.partial(product_kernel, picks, len(band), first),
+            functools.partial(product_kernel, picks, place, len(band), first, count),
             out_shape=jax.ShapeDtypeStruct((rows, columns, channels), jnp.bfloat16),
             in_specs=[VMEM] * (len(band) + 2) + [SMEM, SMEM, VMEM] + [ANY] * len(update),
             out_specs=ANY,

time: 49 us -> 54.6 us (1.11)
  the two profiles are of different devices: /device:TPU:1 before, /device:TPU:12 now
where the time goes in v6:
time: 54.6 us; the launch traced here: 54 us
  Pallas kernels  16.1 us (29%)
  starting transfers between devices  15.1 us (28%)
  waiting for transfers between devices  12.5 us (23%)
  local copies, waits for them, and re-layouts  9.26 us (17%)
  between operations  0.97 us (2%)
    ppermute x7, starting transfers between devices, move(): lax.ppermute(array, ('row', 'col'), [(r * 4 + c, to_r * 4 + to_c) for (r,...  15.1 us
    ppermute x7, waiting for transfers between devices, move(): lax.ppermute(array, ('row', 'col'), [(r * 4 + c, to_r * 4 + to_c) for (r,...  12.5 us
    pallas_call x2, Pallas kernels, on_device(): pl.pallas_call(functools.partial(product_kernel, picks, place, len(band),...  10.8 us
    unnamed x27, local copies, waits for them, and re-layouts  7.75 us
    pallas_call x1, Pallas kernels, on_device(): pl.pallas_call(functools.partial(left_kernel, window), out_shape=[jax.Sha...  3.19 us
    pallas_call x2, Pallas kernels, right_of(): pl.pallas_call(functools.partial(right_kernel, origin), out_shape=[jax.Sh...  2.15 us
    slice x1, local copies, waits for them, and re-layouts, on_device(): in_weights[:, :2 * hidden]  1.51 us
  transfers between devices with their start and end apart: 8, of which 3 were waited for; matrix products, arithmetic and copies ran while one was open for 6% of the time, Pallas kernels for 23%

profile of v6, /device:TPU:12, one launch (start us, length us, event | category | flops | bytes accessed | tf_op | source)
XLA Modules:
  0.0 54.0 jit_solution(5469342408973249065)
XLA Ops:
  0.0 0.0 collective-permute-start.3
  0.0 4.7 %collective-permute-start.2 = (bf16[48,48,128]{2,1,0:T(8,128)(2,1)}, bf16[48,48,128]{2,1,0:T(8,128)(2,1)S(1)}, u32[]{:S(2)}, u32[]{:S(2)}) collective-permute-start(bf16[48,48,128]{2,1,0:T(8,128)(2,1)} %refs_0_.1), channel_id=1, source_target_pairs={{0,8},{1,10},{5,13},{6,14},{10,2},{11,4},{15,7},{12,0},{16,24},{17... | collective-permute-start | bytes 1769480 | tf_op jit(solution)/shard_map/ppermute | solution.py:230
  5.3 1.5 %fusion = (bf16[128,256]{1,0:T(8,128)(2,1)}, bf16[128,256]{1,0:T(8,128)(2,1)S(1)}) fusion(bf16[128,512]{1,0:T(8,128)(2,1)} %param.13), kind=kLoop, calls=%fused_computation | loop fusion | bytes 262144 | tf_op jit(solution)/shard_map/slice | solution.py:300
  6.8 1.1 %copy-done = bf16[48,48,128]{2,1,0:T(8,128)(2,1)S(1)} copy-done((bf16[48,48,128]{2,1,0:T(8,128)(2,1)S(1)}, bf16[48,48,128]{2,1,0:T(8,128)(2,1)}, u32[]{:S(2)}) %copy-start) | copy-done | bytes 589848
  7.9 0.7 %copy-done.7 = f32[128]{0:T(128)S(1)} copy-done((f32[128]{0:T(128)S(1)}, f32[128]{0:T(128)}, u32[]{:S(2)}) %copy-start.7) | copy-done | bytes 536
  8.6 0.7 %copy-done.9 = f32[128]{0:T(128)S(1)} copy-done((f32[128]{0:T(128)S(1)}, f32[128]{0:T(128)}, u32[]{:S(2)}) %copy-start.9) | copy-done | bytes 536
  9.2 1.1 %right.2.refs_0_ = bf16[48,48,128]{2,1,0:T(8,128)(2,1)S(1)} custom-call(s32[1]{0:T(128)S(6)} %copy.14.tokens_ref, bf16[48,48,128]{2,1,0:T(8,128)(2,1)S(1)} %copy-done, f32[1,128]{1,0:T(1,128)S(1)} %bitcast.4, f32[1,128]{1,0:T(1,128)S(1)} %bitcast.7, bf16[128,256]{1,0:T(8,128)(2,1)S(1)} %get-tuple-element.22.weights_ref.refs_8_), custom_call_target="tpu_custom_call" | custom-call | flops 150994944 | bytes 1769472 | tf_op jit(solution)/shard_map/right/pallas_call | solution.py:261
  10.3 0.0 copy-start.2
  10.3 0.6 %copy-done.2 = bf16[128,256]{1,0:T(8,128)(2,1)} copy-done((bf16[128,256]{1,0:T(8,128)(2,1)}, bf16[128,256]{1,0:T(8,128)(2,1)S(1)}, u32[]{:S(2)}) %copy-start.2) | copy-done | bytes 65560
  10.9 2.1 %collective-permute-start = (bf16[48,48,128]{2,1,0:T(8,128)(2,1)S(1)}, bf16[48,48,128]{2,1,0:T(8,128)(2,1)S(1)}, u32[]{:S(2)}, u32[]{:S(2)}) collective-permute-start(bf16[48,48,128]{2,1,0:T(8,128)(2,1)S(1)} %right.2.refs_0_), channel_id=1, source_target_pairs={{0,4},{1,0},{5,1},{6,5},{10,14},{11,10},{15,11},{12,15},{16,20},{1... | collective-permute-start | bytes 1769480 | tf_op jit(solution)/shard_map/ppermute | solution.py:230
  13.0 3.0 %collective-permute-start.1 = (bf16[48,48,128]{2,1,0:T(8,128)(2,1)S(1)}, bf16[48,48,128]{2,1,0:T(8,128)(2,1)S(1)}, u32[]{:S(2)}, u32[]{:S(2)}) collective-permute-start(bf16[48,48,128]{2,1,0:T(8,128)(2,1)S(1)} %right.2.refs_0_), channel_id=1, source_target_pairs={{1,4},{6,1},{11,14},{12,11},{17,20},{22,17},{27,30},{28,27}} | collective-permute-start | bytes 1769480 | tf_op jit(solution)/shard_map/ppermute | solution.py:230
  16.1 1.6 %copy.12 = bf16[128,256]{0,1:T(8,128)(2,1)} copy(bf16[128,256]{1,0:T(8,128)(2,1)} %get-tuple-element.21) | data formatting | bytes 131072
  17.6 0.0 collective-permute-done.3.refs_1_
  17.6 0.8 %copy-done.3 = bf16[128,256]{1,0:T(8,128)(2,1)S(1)} copy-done((bf16[128,256]{1,0:T(8,128)(2,1)S(1)}, bf16[128,256]{1,0:T(8,128)(2,1)}, u32[]{:S(2)}) %copy-start.3) | copy-done | bytes 65560
  18.5 0.8 %copy-done.4 = bf16[128,256]{0,1:T(8,128)(2,1)S(1)} copy-done((bf16[128,256]{0,1:T(8,128)(2,1)S(1)}, bf16[128,256]{0,1:T(8,128)(2,1)}, u32[]{:S(2)}) %copy-start.4) | copy-done | bytes 65560
  19.3 0.8 %copy-done.5 = bf16[128,128]{1,0:T(8,128)(2,1)S(1)} copy-done((bf16[128,128]{1,0:T(8,128)(2,1)S(1)}, bf16[128,128]{1,0:T(8,128)(2,1)}, u32[]{:S(2)}) %copy-start.5) | copy-done | bytes 32792
  20.1 0.8 %copy-done.6 = bf16[128,128]{1,0:T(8,128)(2,1)S(1)} copy-done((bf16[128,128]{1,0:T(8,128)(2,1)S(1)}, bf16[128,128]{1,0:T(8,128)(2,1)}, u32[]{:S(2)}) %copy-start.6) | copy-done | bytes 32792
  20.8 3.2 %left_and_gate.1 = (bf16[128,48,128]{2,1,0:T(8,128)(2,1)S(1)}, f32[48,48,128]{2,1,0:T(8,128)S(1)}, f32[1,128]{1,0:T(1,128)S(1)}, f32[1,128]{1,0:T(1,128)S(1)}, b...) custom-call(s32[1]{0:T(128)S(6)} %copy.14.tokens_ref, bf16[48,48,128]{2,1,0:T(8,128)(2,1)S(1)} %copy-done.1, ...), custom_call_target="tpu_custom_call" | custom-call | flops 301989888 | bytes 4718592 | tf_op jit(solution)/shard_map/left_and_gate/pallas_call | solution.py:285
  24.0 0.0 collective-permute-done.2.pair_ref
  24.0 1.1 %right.3 = (bf16[32,48,128]{2,1,0:T(8,128)(2,1)S(1)}, bf16[16,48,128]{2,1,0:T(8,128)(2,1)S(1)}) custom-call(s32[1]{0:T(128)S(6)} %copy.14.tokens_ref, bf16[48,48,128]{2,1,0:T(8,128)(2,1)S(1)} %collective-permute-done.2.pair_ref, f32[1,128]{1,0:T(1,128)S(1)} %get-tuple-element.13.gain_ref, f32[1,128]{1,0:T(1,128)S(1)} %get-tuple-element.14.bias_ref, ...), custom_call_target="tpu_custom_call" | custom-call | flops 150994944 | bytes 1769472 | tf_op jit(solution)/shard_map/right/pallas_call | solution.py:261
  25.1 1.3 %collective-permute-start.6 = (bf16[32,48,128]{2,1,0:T(8,128)(2,1)S(1)}, bf16[32,48,128]{2,1,0:T(8,128)(2,1)S(1)}, u32[]{:S(2)}, u32[]{:S(2)}) collective-permute-start(bf16[32,48,128]{2,1,0:T(8,128)(2,1)S(1)} %get-tuple-element.20.refs_3_), channel_id=1, source_target_pairs={{8,12},{10,8},{13,9},{14,13},{2,6},{4,2},{7,3},{0,7},{24,28},{26,2... | collective-permute-start | bytes 1179656 | tf_op jit(solution)/shard_map/ppermute | solution.py:230
  26.4 1.3 %collective-permute-start.7 = (bf16[32,48,128]{2,1,0:T(8,128)(2,1)S(1)}, bf16[32,48,128]{2,1,0:T(8,128)(2,1)S(1)}, u32[]{:S(2)}, u32[]{:S(2)}) collective-permute-start(bf16[32,48,128]{2,1,0:T(8,128)(2,1)S(1)} %get-tuple-element.20.refs_3_), channel_id=1, source_target_pairs={{10,12},{14,9},{4,6},{0,3},{26,28},{30,25},{20,22},{16,19}} | collective-permute-start | bytes 1179656 | tf_op jit(solution)/shard_map/ppermute | solution.py:230
  27.7 1.3 %collective-permute-start.4 = (bf16[16,48,128]{2,1,0:T(8,128)(2,1)S(1)}, bf16[16,48,128]{2,1,0:T(8,128)(2,1)S(1)}, u32[]{:S(2)}, u32[]{:S(2)}) collective-permute-start(bf16[16,48,128]{2,1,0:T(8,128)(2,1)S(1)} %get-tuple-element.16.refs_3_), channel_id=1, source_target_pairs={{8,12},{10,8},{13,9},{14,13},{2,6},{4,2},{7,3},{0,7},{24,28},{26,2... | collective-permute-start | bytes 589832 | tf_op jit(solution)/shard_map/ppermute | solution.py:230
  29.0 0.0 collective-permute-done.refs_1_
  29.0 1.5 %collective-permute-start.5 = (bf16[16,48,128]{2,1,0:T(8,128)(2,1)S(1)}, bf16[16,48,128]{2,1,0:T(8,128)(2,1)S(1)}, u32[]{:S(2)}, u32[]{:S(2)}) collective-permute-start(bf16[16,48,128]{2,1,0:T(8,128)(2,1)S(1)} %get-tuple-element.16.refs_3_), channel_id=1, source_target_pairs={{10,12},{14,9},{4,6},{0,3},{26,28},{30,25},{20,22},{16,19}} | collective-permute-start | bytes 589832 | tf_op jit(solution)/shard_map/ppermute | solution.py:230
  30.5 0.4 collective-permute-done.1.refs_2_
  30.9 3.9 %collective-permute-done.6.refs_4_ = bf16[32,48,128]{2,1,0:T(8,128)(2,1)S(1)} collective-permute-done((bf16[32,48,128]{2,1,0:T(8,128)(2,1)S(1)}, bf16[32,48,128]{2,1,0:T(8,128)(2,1)S(1)}, u32[]{:S(2)}, u32[]{:S(2)}) %collective-permute-start.6) | collective-permute-done | bytes 393248 | tf_op jit(solution)/shard_map/ppermute | solution.py:230
  34.8 8.2 %collective-permute-done.7.refs_5_ = bf16[32,48,128]{2,1,0:T(8,128)(2,1)S(1)} collective-permute-done((bf16[32,48,128]{2,1,0:T(8,128)(2,1)S(1)}, bf16[32,48,128]{2,1,0:T(8,128)(2,1)S(1)}, u32[]{:S(2)}, u32[]{:S(2)}) %collective-permute-start.7) | collective-permute-done | bytes 393248 | tf_op jit(solution)/shard_map/ppermute | solution.py:230
  43.0 7.0 %product.2.refs_11_ = bf16[48,48,128]{2,1,0:T(8,128)(2,1)} custom-call(bf16[48,48,128]{2,1,0:T(8,128)(2,1)S(1)} %right.2.refs_0_, bf16[48,48,128]{2,1,0:T(8,128)(2,1)S(1)} %collective-permute-done.refs_1_, bf16[48,48,128]{2,1,0:T(8,128)(2,1)S(1)} %collective-permute-done.1.refs_2_, bf16[32,48,128]{2,1,0:T(8,128)(2,1)S(1)} %get-tuple-element.20.refs_3_, ...), custom_call_target="tpu_custom_call" | custom-call | flops 37748736 | bytes 2359296 | tf_op jit(solution)/shard_map/product/pallas_call | solution.py:315
  50.1 0.0 collective-permute-done.4.refs_4_
  50.1 0.0 collective-permute-done.5.refs_5_
  50.1 3.8 %product.3 = bf16[48,48,128]{2,1,0:T(8,128)(2,1)} custom-call(bf16[48,48,128]{2,1,0:T(8,128)(2,1)S(1)} %right.2.refs_0_, bf16[48,48,128]{2,1,0:T(8,128)(2,1)S(1)} %collective-permute-done.refs_1_, bf16[48,48,128]{2,1,0:T(8,128)(2,1)S(1)} %collective-permute-done.1.refs_2_, ...), custom_call_target="tpu_custom_call", output_to_operand_aliasing={{}: (11, {})} | custom-call | flops 18874368 | bytes 2359296 | tf_op jit(solution)/shard_map/product/pallas_call | solution.py:315
  (17 shorter events, 0.0 us)
Async XLA Ops:
  0.0 17.6 %copy-start.8 = (f32[128]{0:T(128)S(1)}, f32[128]{0:T(128)}, u32[]{:S(2)}) copy-start(f32[128]{0:T(128)} %param.11) | copy-start | bytes 1540
  0.0 17.6 %copy-start.10 = (f32[128]{0:T(128)S(1)}, f32[128]{0:T(128)}, u32[]{:S(2)}) copy-start(f32[128]{0:T(128)} %param.12) | copy-start | bytes 1540
  0.0 17.6 %collective-permute-start.3 = (bf16[48,48,128]{2,1,0:T(8,128)(2,1)}, bf16[48,48,128]{2,1,0:T(8,128)(2,1)S(1)}, u32[]{:S(2)}, u32[]{:S(2)}) collective-permute-start(bf16[48,48,128]{2,1,0:T(8,128)(2,1)} %refs_0_.1), channel_id=1, source_target_pairs={{0,3},{1,0},{2,1},{3,2},{4,7},{5,4},{6,5},{7,6},{8,11},{9,8},{10,9... | collective-permute-start | bytes 1769480 | tf_op jit(solution)/shard_map/ppermute | solution.py:29
  0.0 24.0 %collective-permute-start.2 = (bf16[48,48,128]{2,1,0:T(8,128)(2,1)}, bf16[48,48,128]{2,1,0:T(8,128)(2,1)S(1)}, u32[]{:S(2)}, u32[]{:S(2)}) collective-permute-start(bf16[48,48,128]{2,1,0:T(8,128)(2,1)} %refs_0_.1), channel_id=1, source_target_pairs={{0,8},{1,10},{5,13},{6,14},{10,2},{11,4},{15,7},{12,0},{16,24},{17... | collective-permute-start | bytes 1769480 | tf_op jit(solution)/shard_map/ppermute | solution.py:230
  6.8 1.1 %copy-start = (bf16[48,48,128]{2,1,0:T(8,128)(2,1)S(1)}, bf16[48,48,128]{2,1,0:T(8,128)(2,1)}, u32[]{:S(2)}) copy-start(bf16[48,48,128]{2,1,0:T(8,128)(2,1)} %refs_0_.1) | copy-start | bytes 1769476
  7.9 0.7 %copy-start.7 = (f32[128]{0:T(128)S(1)}, f32[128]{0:T(128)}, u32[]{:S(2)}) copy-start(f32[128]{0:T(128)} %param.11) | copy-start | bytes 1540
  8.6 0.7 %copy-start.9 = (f32[128]{0:T(128)S(1)}, f32[128]{0:T(128)}, u32[]{:S(2)}) copy-start(f32[128]{0:T(128)} %param.12) | copy-start | bytes 1540
  9.2 8.4 %copy-start.1 = (bf16[48,48,128]{2,1,0:T(8,128)(2,1)S(1)}, bf16[48,48,128]{2,1,0:T(8,128)(2,1)}, u32[]{:S(2)}) copy-start(bf16[48,48,128]{2,1,0:T(8,128)(2,1)} %refs_0_.1) | copy-start | bytes 1769476
  9.2 33.8 %copy-start.11 = (f32[128]{0:T(128)S(1)}, f32[128]{0:T(128)}, u32[]{:S(2)}) copy-start(f32[128]{0:T(128)} %refs_8_.3) | copy-start | bytes 1540
  9.2 33.8 %copy-start.12 = (f32[128]{0:T(128)S(1)}, f32[128]{0:T(128)}, u32[]{:S(2)}) copy-start(f32[128]{0:T(128)} %refs_9_.5) | copy-start | bytes 1540
  10.3 0.6 %copy-start.2 = (bf16[128,256]{1,0:T(8,128)(2,1)}, bf16[128,256]{1,0:T(8,128)(2,1)S(1)}, u32[]{:S(2)}) copy-start(bf16[128,256]{1,0:T(8,128)(2,1)S(1)} %get-tuple-element.22.weights_ref.refs_8_) | copy-start | bytes 196612
  10.9 18.1 %collective-permute-start = (bf16[48,48,128]{2,1,0:T(8,128)(2,1)S(1)}, bf16[48,48,128]{2,1,0:T(8,128)(2,1)S(1)}, u32[]{:S(2)}, u32[]{:S(2)}) collective-permute-start(bf16[48,48,128]{2,1,0:T(8,128)(2,1)S(1)} %right.2.refs_0_), channel_id=1, source_target_pairs={{0,4},{1,0},{5,1},{6,5},{10,14},{11,10},{15,11},{12,15},{16,20},{1... | collective-permute-start | bytes 1769480 | tf_op jit(solution)/shard_map/ppermute | solution.py:230
  13.0 17.9 %collective-permute-start.1 = (bf16[48,48,128]{2,1,0:T(8,128)(2,1)S(1)}, bf16[48,48,128]{2,1,0:T(8,128)(2,1)S(1)}, u32[]{:S(2)}, u32[]{:S(2)}) collective-permute-start(bf16[48,48,128]{2,1,0:T(8,128)(2,1)S(1)} %right.2.refs_0_), channel_id=1, source_target_pairs={{1,4},{6,1},{11,14},{12,11},{17,20},{22,17},{27,30},{28,27}} | collective-permute-start | bytes 1769480 | tf_op jit(solution)/shard_map/ppermute | solution.py:230
  17.6 0.8 %copy-start.3 = (bf16[128,256]{1,0:T(8,128)(2,1)S(1)}, bf16[128,256]{1,0:T(8,128)(2,1)}, u32[]{:S(2)}) copy-start(bf16[128,256]{1,0:T(8,128)(2,1)} %copy-done.2) | copy-start | bytes 196612
  18.5 0.8 %copy-start.4 = (bf16[128,256]{0,1:T(8,128)(2,1)S(1)}, bf16[128,256]{0,1:T(8,128)(2,1)}, u32[]{:S(2)}) copy-start(bf16[128,256]{0,1:T(8,128)(2,1)} %copy.12) | copy-start | bytes 196612
  19.3 0.8 %copy-start.5 = (bf16[128,128]{1,0:T(8,128)(2,1)S(1)}, bf16[128,128]{1,0:T(8,128)(2,1)}, u32[]{:S(2)}) copy-start(bf16[128,128]{1,0:T(8,128)(2,1)} %refs_5_.1) | copy-start | bytes 98308
  20.1 0.8 %copy-start.6 = (bf16[128,128]{1,0:T(8,128)(2,1)S(1)}, bf16[128,128]{1,0:T(8,128)(2,1)}, u32[]{:S(2)}) copy-start(bf16[128,128]{1,0:T(8,128)(2,1)} %refs_9_.3) | copy-start | bytes 98308
  25.1 9.7 %collective-permute-start.6 = (bf16[32,48,128]{2,1,0:T(8,128)(2,1)S(1)}, bf16[32,48,128]{2,1,0:T(8,128)(2,1)S(1)}, u32[]{:S(2)}, u32[]{:S(2)}) collective-permute-start(bf16[32,48,128]{2,1,0:T(8,128)(2,1)S(1)} %get-tuple-element.20.refs_3_), channel_id=1, source_target_pairs={{8,12},{10,8},{13,9},{14,13},{2,6},{4,2},{7,3},{0,7},{24,28},{26,2... | collective-permute-start | bytes 1179656 | tf_op jit(solution)/shard_map/ppermute | solution.py:230
  26.4 16.6 %collective-permute-start.7 = (bf16[32,48,128]{2,1,0:T(8,128)(2,1)S(1)}, bf16[32,48,128]{2,1,0:T(8,128)(2,1)S(1)}, u32[]{:S(2)}, u32[]{:S(2)}) collective-permute-start(bf16[32,48,128]{2,1,0:T(8,128)(2,1)S(1)} %get-tuple-element.20.refs_3_), channel_id=1, source_target_pairs={{10,12},{14,9},{4,6},{0,3},{26,28},{30,25},{20,22},{16,19}} | collective-permute-start | bytes 1179656 | tf_op jit(solution)/shard_map/ppermute | solution.py:230
  27.7 22.3 %collective-permute-start.4 = (bf16[16,48,128]{2,1,0:T(8,128)(2,1)S(1)}, bf16[16,48,128]{2,1,0:T(8,128)(2,1)S(1)}, u32[]{:S(2)}, u32[]{:S(2)}) collective-permute-start(bf16[16,48,128]{2,1,0:T(8,128)(2,1)S(1)} %get-tuple-element.16.refs_3_), channel_id=1, source_target_pairs={{8,12},{10,8},{13,9},{14,13},{2,6},{4,2},{7,3},{0,7},{24,28},{26,2... | collective-permute-start | bytes 589832 | tf_op jit(solution)/shard_map/ppermute | solution.py:230
  29.0 21.0 %collective-permute-start.5 = (bf16[16,48,128]{2,1,0:T(8,128)(2,1)S(1)}, bf16[16,48,128]{2,1,0:T(8,128)(2,1)S(1)}, u32[]{:S(2)}, u32[]{:S(2)}) collective-permute-start(bf16[16,48,128]{2,1,0:T(8,128)(2,1)S(1)} %get-tuple-element.16.refs_3_), channel_id=1, source_target_pairs={{10,12},{14,9},{4,6},{0,3},{26,28},{30,25},{20,22},{16,19}} | collective-permute-start | bytes 589832 | tf_op jit(solution)/shard_map/ppermute | solution.py:230

commit v7 on v6

--- a/solution.py
+++ b/solution.py
@@ -47,35 +47,41 @@
     return layer_norm(values, gain_ref[...], bias_ref[...]).astype(jnp.bfloat16)
 
 
-def right_kernel(origin, tokens_ref, pair_ref, gain_ref, bias_ref, weights_ref, *outs):
-    columns, hidden = outs[0].shape[1:]
-    row_block, third_block = origin()
-    tokens = tokens_ref[0]
-    row_start = row_block * pair_ref.shape[0]
-    valid_columns = tokens - third_block * columns
+def masked_right(both, tokens, row_token, third_block, columns):
+    hidden = both.shape[1] // 2
+    right = jax.nn.sigmoid(both[:, :hidden]) * both[:, hidden:]
     position = lax.broadcasted_iota(jnp.int32, (columns, hidden), 0)
+    parts = []
+    for row in range(both.shape[0] // columns):
+        limit = jnp.where(row_token + row < tokens, tokens - third_block * columns, 0)
+        part = right[row * columns : (row + 1) * columns]
+        parts.append(jnp.where(position < limit, part, 0.0).astype(jnp.bfloat16))
+    return parts
+
+
+def right_kernel(origin, first, tokens_ref, pair_ref, gain_ref, bias_ref, weights_ref, out_ref):
+    count, columns, _ = out_ref.shape
+    row_token, third_block = origin()
     step = 4
-    first = 0
-    for out_ref in outs:
-        for at in range(0, out_ref.shape[0], step):
-            normed = normed_rows(pair_ref[pl.ds(first + at, step)], gain_ref, bias_ref)
-            both = jnp.dot(normed, weights_ref[...], preferred_element_type=jnp.float32)
-            right = jax.nn.sigmoid(both[:, :hidden]) * both[:, hidden:]
-            for row in range(step):
-                limit = jnp.where(row_start + first + at + row < tokens, valid_columns, 0)
-                part = right[row * columns : (row + 1) * columns]
-                out_ref[at + row] = jnp.where(position < limit, part, 0.0).astype(jnp.bfloat16)
-        first += out_ref.shape[0]
-
-
-def left_kernel(blocks, tokens_ref, *refs):
+    for at in range(0, count, step):
+        normed = normed_rows(pair_ref[pl.ds(at, step)], gain_ref, bias_ref)
+        both = jnp.dot(normed, weights_ref[...], preferred_element_type=jnp.float32)
+        parts = masked_right(both, tokens_ref[0], row_token + first + at, third_block, columns)
+        for row, part in enumerate(parts):
+            out_ref[at + row] = part
+
+
+def near_kernel(blocks, later, passes, tokens_ref, *refs):
     pair_refs, refs = refs[:blocks], refs[blocks:]
-    gain_ref, bias_ref, weights_ref, gate_weights_ref, *passed, scratch = refs
-    passed, (left_ref, gate_ref), handed = passed[:4], passed[4:6], passed[6:]
+    left_weights_ref, gate_weights_ref, *refs = refs
+    passed, refs = refs[:passes], refs[passes:]
+    (left_ref, gate_ref, right_ref, later_ref), handed, scratch = refs[:4], refs[4:-1], refs[-1]
+    gain_ref, bias_ref, right_weights_ref = passed[:3]
+    rows, columns, channels = pair_refs[0].shape
+    hidden, _, width = left_ref.shape
     for source, target in zip(passed, handed):
         target[...] = source[...]
-    rows, columns, channels = pair_refs[0].shape
-    hidden, _, width = left_ref.shape
+    later_ref[...] = pair_refs[0][pl.ds(later, rows - later)]
     tokens = tokens_ref[0]
     row_start = lax.axis_index("row") * rows
     col_pos, col_count = lax.axis_index("col"), lax.axis_size("col")
@@ -92,10 +98,14 @@
         normed = [normed_rows(ref[pl.ds(first, step)], gain_ref, bias_ref) for ref in pair_refs]
         gate = jnp.dot(normed[0], gate_weights_ref[...], preferred_element_type=jnp.float32)
         gate_ref[pl.ds(first, step)] = jax.nn.sigmoid(gate).reshape(step, columns, channels)
+        both = jnp.dot(normed[0], right_weights_ref[...], preferred_element_type=jnp.float32)
+        parts = masked_right(both, tokens, row_start + first, col_pos, columns)
+        for row, part in enumerate(parts):
+            right_ref[first + row] = part
         for row in range(step):
             thirds = [piece[row * columns : (row + 1) * columns] for piece in normed]
             both = lax.dot_general(
-                weights_ref[...],
+                left_weights_ref[...],
                 jnp.concatenate(thirds + padding, axis=0),
                 (((1,), (1,)), ((), ())),
                 preferred_element_type=jnp.float32,
@@ -206,23 +216,15 @@
     return lax.axis_index("row") ^ lax.axis_index("col")
 
 
-def far_origin():
-    row_pos, col_pos = lax.axis_index("row"), lax.axis_index("col")
-    diagonal = hop_place() == 2
-    row_block = jnp.where(diagonal, col_pos, jnp.where(col_pos == 2, row_pos - 2, 3 - row_pos))
-    return row_block, jnp.where(diagonal, col_pos, (row_block + 1) % 4)
-
-
 def hops():
-    relay = {0: (2, 2), 1: (3, 2), 2: (1, 0), 3: (0, 0)}
-    column = range(4)
     out, near, near_more, far, far_more = [], [], [], [], []
-    for c in column:
-        out += [((c, c), (c ^ 2, c)), ((c, (c + 1) % 4), relay[c])]
-        near += [((c, c), (c ^ 1, c)), ((c, (c + 1) % 4), (c, c))]
-        near_more += [((c, (c + 1) % 4), (c ^ 1, c))]
-        far += [((c ^ 2, c), (c ^ 3, c)), (relay[c], (c ^ 2, c))]
-        far_more += [(relay[c], (c ^ 3, c))]
+    for c in range(4):
+        after = (c + 1) % 4
+        out += [((c, c), (c ^ 2, c)), ((c, after), (c ^ 2, after))]
+        near += [((c, c), (c ^ 1, c)), ((c, after), (c, c))]
+        near_more += [((c, after), (c ^ 1, c))]
+        far += [((c ^ 2, c), (c ^ 3, c)), ((c ^ 2, after), (c ^ 2, c))]
+        far_more += [((c ^ 2, after), (c ^ 3, c))]
     return out, near, near_more, far, far_more
 
 
@@ -257,53 +259,60 @@
     last = 16
     spans = [(0, columns - last), (columns - last, last)]
 
-    def right_of(origin, pair, parts):
+    def right_of(origin, first, pair):
+        count = pair.shape[0]
         return pl.pallas_call(
-            functools.partial(right_kernel, origin),
-            out_shape=[
-                jax.ShapeDtypeStruct((count, columns, hidden), jnp.bfloat16) for count in parts
-            ],
+            functools.partial(right_kernel, origin, first),
+            out_shape=jax.ShapeDtypeStruct((count, columns, hidden), jnp.bfloat16),
             in_specs=[SMEM] + [VMEM] * 4,
-            out_specs=[VMEM] * len(parts),
+            out_specs=VMEM,
             compiler_params=params(2 * block),
-            cost_estimate=cost(4 * tokens * channels * hidden, 6 * tokens * channels),
+            cost_estimate=cost(
+                4 * count * columns * channels * hidden, 4 * count * columns * channels
+            ),
             name="right",
         )(token_count, pair, in_gain, in_bias, right_weights)
 
-    def here():
-        return lax.axis_index("row"), lax.axis_index("col")
-
-    right_weights = in_weights[:, 2 * hidden :]
+    def far_origin():
+        col_pos = lax.axis_index("col")
+        row_block = jnp.where(hop_place() == 2, col_pos, (col_pos + 3) % 4)
+        return row_block * rows, col_pos
+
+    arrived = []
     if by_hops:
         out, near, near_more, far, far_more = hops()
-        arrived = move(pair_state, out)
+        arrived.append(move(pair_state[: spans[0][1]], out))
     pairs = [pair_state]
     for _ in range(window - 1):
         pairs.append(shifted(pairs[-1], "col", -1))
-    (right,) = right_of(here, pair_state, [rows])
-    passed = [in_gain, in_bias, right_weights, out_weights]
-    left, gate, *handed = pl.pallas_call(
-        functools.partial(left_kernel, window),
+    later = spans[1][0]
+    passed = [in_gain, in_bias, in_weights[:, 2 * hidden :], out_weights]
+    left, gate, right, later_pair, *handed = pl.pallas_call(
+        functools.partial(near_kernel, window, later, len(passed)),
         out_shape=[
             jax.ShapeDtypeStruct((hidden, rows, width), jnp.bfloat16),
             jax.ShapeDtypeStruct((rows, columns, channels), jnp.float32),
+            jax.ShapeDtypeStruct((rows, columns, hidden), jnp.bfloat16),
+            jax.ShapeDtypeStruct((rows - later, columns, channels), jnp.bfloat16),
         ]
         + [jax.ShapeDtypeStruct(array.shape, array.dtype) for array in passed],
-        in_specs=[SMEM] + [VMEM] * (window + 8),
-        out_specs=[VMEM] * 6,
+        in_specs=[SMEM] + [VMEM] * (window + 2 + len(passed)),
+        out_specs=[VMEM] * (4 + len(passed)),
         scratch_shapes=[pltpu.VMEM((width // LANES, hidden * rows, LANES), jnp.float32)],
-        compiler_params=params((window + 2) * block, 6 * hidden * rows * width),
+        compiler_params=params((window + 4) * block, 6 * hidden * rows * width),
         cost_estimate=cost(
-            4 * window * tokens * channels * hidden, 6 * rows * width * hidden
+            4 * (window + 1) * tokens * channels * hidden, 6 * rows * width * hidden
         ),
-        name="left_and_gate",
-    )(token_count, *pairs, in_gain, in_bias, in_weights[:, : 2 * hidden].T, gate_weights, *passed)
+        name="near",
+    )(token_count, *pairs, in_weights[:, : 2 * hidden].T, gate_weights, *passed)
     in_gain, in_bias, right_weights, out_weights = handed
 
     if by_hops:
+        arrived.append(move(later_pair, out))
         near, near_more = move(right, near), move(right, near_more)
         bands = []
-        for mine in right_of(far_origin, arrived, [count for _, count in spans]):
+        for (first, _), pair in zip(spans, arrived):
+            mine = right_of(far_origin, first, pair)
             bands.append([right, near, near_more, mine, move(mine, far), move(mine, far_more)])
         picks, place = [(0, 1, 3, 4), (1, 2, 4, 5)], hop_place
     else:

time: 54.6 us -> 54.2 us (level)
  the two profiles are of different devices: /device:TPU:12 before, /device:TPU:17 now
where the time goes in v7:
time: 54.2 us; the launch traced here: 53.7 us
  starting transfers between devices  16.5 us (30%)
  Pallas kernels  15.6 us (29%)
  waiting for transfers between devices  14.7 us (27%)
  local copies, waits for them, and re-layouts  5.92 us (11%)
  between operations  0.85 us (2%)
    ppermute x8, starting transfers between devices, move(): lax.ppermute(array, ('row', 'col'), [(r * 4 + c, to_r * 4 + to_c) for (r,...  15.9 us
    pallas_call x2, Pallas kernels, on_device(): pl.pallas_call(functools.partial(product_kernel, picks, place, len(band),...  10.8 us
    ppermute x8, waiting for transfers between devices, move(): lax.ppermute(array, ('row', 'col'), [(r * 4 + c, to_r * 4 + to_c) for (r,...  9.53 us
    ppermute x1, waiting for transfers between devices, shifted(): lax.ppermute(array, axis, [(i, (i + by) % devices) for i in range(devices)])  5.19 us
    unnamed x15, local copies, waits for them, and re-layouts  4.01 us
    pallas_call x1, Pallas kernels, on_device(): pl.pallas_call(functools.partial(near_kernel, window, later, len(passed))...  3.66 us
    pallas_call x2, Pallas kernels, right_of(): pl.pallas_call(functools.partial(right_kernel, origin, first), out_shape=...  1.19 us
  transfers between devices with their start and end apart: 9, of which 2 were waited for; matrix products, arithmetic and copies ran while one was open for 4% of the time, Pallas kernels for 22%

profile of v7, /device:TPU:17, one launch (start us, length us, event | category | flops | bytes accessed | tf_op | source)
XLA Modules:
  0.0 53.7 jit_solution(104119902003231588)
XLA Ops:
  0.0 0.7 %collective-permute-start = (bf16[48,48,128]{2,1,0:T(8,128)(2,1)}, bf16[48,48,128]{2,1,0:T(8,128)(2,1)S(1)}, u32[]{:S(2)}, u32[]{:S(2)}) collective-permute-start(bf16[48,48,128]{2,1,0:T(8,128)(2,1)} %refs_0_.1), channel_id=1, source_target_pairs={{0,3},{1,0},{2,1},{3,2},{4,7},{5,4},{6,5},{7,6},{8,11},{9,8},{10,9... | collective-permute-start | bytes 1769480 | tf_op jit(solution)/shard_map/ppermute | solution.py:29
  0.7 1.0 %slice.11 = bf16[32,48,128]{2,1,0:T(8,128)(2,1)S(1)} slice(bf16[48,48,128]{2,1,0:T(8,128)(2,1)} %refs_0_.1), slice={[0:32], [0:48], [0:128]} | slice | bytes 786432 | tf_op jit(solution)/shard_map/slice | solution.py:284
  1.7 1.3 %collective-permute-start.6 = (bf16[32,48,128]{2,1,0:T(8,128)(2,1)S(1)}, bf16[32,48,128]{2,1,0:T(8,128)(2,1)S(1)}, u32[]{:S(2)}, u32[]{:S(2)}) collective-permute-start(bf16[32,48,128]{2,1,0:T(8,128)(2,1)S(1)} %slice.11), channel_id=1, source_target_pairs={{0,8},{1,9},{5,13},{6,14},{10,2},{11,3},{15,7},{12,4},{16,24},{17,... | collective-permute-start | bytes 1179656 | tf_op jit(solution)/shard_map/ppermute | solution.py:232
  3.6 0.9 %fusion = (bf16[128,256]{1,0:T(8,128)(2,1)S(1)}, bf16[128,256]{1,0:T(8,128)(2,1)S(1)}) fusion(bf16[128,512]{1,0:T(8,128)(2,1)} %param.13), kind=kLoop, calls=%fused_computation | loop fusion | bytes 262144 | tf_op jit(solution)/shard_map/slice | solution.py:289
  4.5 0.0 copy-start.1
  4.5 0.0 copy-start.2
  4.6 0.1 copy.12
  4.7 5.2 %collective-permute-done.refs_1_ = bf16[48,48,128]{2,1,0:T(8,128)(2,1)S(1)} collective-permute-done((bf16[48,48,128]{2,1,0:T(8,128)(2,1)}, bf16[48,48,128]{2,1,0:T(8,128)(2,1)S(1)}, u32[]{:S(2)}, u32[]{:S(2)}) %collective-permute-start) | collective-permute-done | bytes 589856 | tf_op jit(solution)/shard_map/ppermute | solution.py:29
  9.9 1.1 %copy-done = bf16[48,48,128]{2,1,0:T(8,128)(2,1)S(1)} copy-done((bf16[48,48,128]{2,1,0:T(8,128)(2,1)S(1)}, bf16[48,48,128]{2,1,0:T(8,128)(2,1)}, u32[]{:S(2)}) %copy-start) | copy-done | bytes 589848
  10.9 0.8 %copy-done.3 = bf16[128,128]{1,0:T(8,128)(2,1)S(1)} copy-done((bf16[128,128]{1,0:T(8,128)(2,1)S(1)}, bf16[128,128]{1,0:T(8,128)(2,1)}, u32[]{:S(2)}) %copy-start.3) | copy-done | bytes 32792
  11.7 0.8 %copy-done.4 = bf16[128,128]{1,0:T(8,128)(2,1)S(1)} copy-done((bf16[128,128]{1,0:T(8,128)(2,1)S(1)}, bf16[128,128]{1,0:T(8,128)(2,1)}, u32[]{:S(2)}) %copy-start.4) | copy-done | bytes 32792
  12.5 0.7 %copy-done.5 = f32[128]{0:T(128)S(1)} copy-done((f32[128]{0:T(128)S(1)}, f32[128]{0:T(128)}, u32[]{:S(2)}) %copy-start.5) | copy-done | bytes 536
  13.1 0.7 %copy-done.6 = f32[128]{0:T(128)S(1)} copy-done((f32[128]{0:T(128)S(1)}, f32[128]{0:T(128)}, u32[]{:S(2)}) %copy-start.6) | copy-done | bytes 536
  13.8 3.7 %near.1 = (bf16[128,48,128]{2,1,0:T(8,128)(2,1)S(1)}, f32[48,48,128]{2,1,0:T(8,128)S(1)}, bf16[48,48,128]{2,1,0:T(8,128)(2,1)S(1)}, bf16[16,48,128]{2,1,0:T(8,12...) custom-call(s32[1]{0:T(128)S(6)} %copy.14.tokens_ref, ...), custom_call_target="tpu_custom_call" | custom-call | flops 452984832 | bytes 4718592 | tf_op jit(solution)/shard_map/near/pallas_call | solution.py:290
  17.4 0.7 %collective-permute-start.1 = (bf16[48,48,128]{2,1,0:T(8,128)(2,1)S(1)}, bf16[48,48,128]{2,1,0:T(8,128)(2,1)S(1)}, u32[]{:S(2)}, u32[]{:S(2)}) collective-permute-start(bf16[48,48,128]{2,1,0:T(8,128)(2,1)S(1)} %get-tuple-element.13.refs_0_), channel_id=1, source_target_pairs={{0,4},{1,0},{5,1},{6,5},{10,14},{11,10},{15,11},{12,15},{16,20},{1... | collective-permute-start | bytes 1769480 | tf_op jit(solution)/shard_map/ppermute | solution.py:232
  18.1 0.7 %collective-permute-start.2 = (bf16[48,48,128]{2,1,0:T(8,128)(2,1)S(1)}, bf16[48,48,128]{2,1,0:T(8,128)(2,1)S(1)}, u32[]{:S(2)}, u32[]{:S(2)}) collective-permute-start(bf16[48,48,128]{2,1,0:T(8,128)(2,1)S(1)} %get-tuple-element.13.refs_0_), channel_id=1, source_target_pairs={{1,4},{6,1},{11,14},{12,11},{17,20},{22,17},{27,30},{28,27}} | collective-permute-start | bytes 1769480 | tf_op jit(solution)/shard_map/ppermute | solution.py:232
  18.8 0.0 collective-permute-done.6.pair_ref
  18.9 0.7 %right.3.refs_3_ = bf16[32,48,128]{2,1,0:T(8,128)(2,1)S(1)} custom-call(s32[1]{0:T(128)S(6)} %copy.14.tokens_ref, bf16[32,48,128]{2,1,0:T(8,128)(2,1)S(1)} %collective-permute-done.6.pair_ref, f32[1,128]{1,0:T(1,128)S(1)} %get-tuple-element.15.gain_ref, f32[1,128]{1,0:T(1,128)S(1)} %get-tuple-element.16.bias_ref, ...), custom_call_target="tpu_custom_call" | custom-call | flops 100663296 | bytes 786432 | tf_op jit(solution)/shard_map/right/pallas_call | solution.py:264
  19.6 1.9 %collective-permute-start.7 = (bf16[32,48,128]{2,1,0:T(8,128)(2,1)S(1)}, bf16[32,48,128]{2,1,0:T(8,128)(2,1)S(1)}, u32[]{:S(2)}, u32[]{:S(2)}) collective-permute-start(bf16[32,48,128]{2,1,0:T(8,128)(2,1)S(1)} %right.3.refs_3_), channel_id=1, source_target_pairs={{8,12},{9,8},{13,9},{14,13},{2,6},{3,2},{7,3},{4,7},{24,28},{25,24... | collective-permute-start | bytes 1179656 | tf_op jit(solution)/shard_map/ppermute | solution.py:232
  21.5 1.3 %collective-permute-start.3 = (bf16[16,48,128]{2,1,0:T(8,128)(2,1)S(1)}, bf16[16,48,128]{2,1,0:T(8,128)(2,1)S(1)}, u32[]{:S(2)}, u32[]{:S(2)}) collective-permute-start(bf16[16,48,128]{2,1,0:T(8,128)(2,1)S(1)} %get-tuple-element.14), channel_id=1, source_target_pairs={{0,8},{1,9},{5,13},{6,14},{10,2},{11,3},{15,7},{12,4},{16,24},{17,... | collective-permute-start | bytes 589832 | tf_op jit(solution)/shard_map/ppermute | solution.py:232
  22.8 6.1 %collective-permute-start.8 = (bf16[32,48,128]{2,1,0:T(8,128)(2,1)S(1)}, bf16[32,48,128]{2,1,0:T(8,128)(2,1)S(1)}, u32[]{:S(2)}, u32[]{:S(2)}) collective-permute-start(bf16[32,48,128]{2,1,0:T(8,128)(2,1)S(1)} %right.3.refs_3_), channel_id=1, source_target_pairs={{9,12},{14,9},{3,6},{4,3},{25,28},{30,25},{19,22},{20,19}} | collective-permute-start | bytes 1179656 | tf_op jit(solution)/shard_map/ppermute | solution.py:232
  28.9 9.5 %collective-permute-done.3.pair_ref = bf16[16,48,128]{2,1,0:T(8,128)(2,1)S(1)} collective-permute-done((bf16[16,48,128]{2,1,0:T(8,128)(2,1)S(1)}, bf16[16,48,128]{2,1,0:T(8,128)(2,1)S(1)}, u32[]{:S(2)}, u32[]{:S(2)}) %collective-permute-start.3) | collective-permute-done | bytes 196640 | tf_op jit(solution)/shard_map/ppermute | solution.py:232
  38.4 0.5 right.2.refs_3_
  38.9 1.9 %collective-permute-start.4 = (bf16[16,48,128]{2,1,0:T(8,128)(2,1)S(1)}, bf16[16,48,128]{2,1,0:T(8,128)(2,1)S(1)}, u32[]{:S(2)}, u32[]{:S(2)}) collective-permute-start(bf16[16,48,128]{2,1,0:T(8,128)(2,1)S(1)} %right.2.refs_3_), channel_id=1, source_target_pairs={{8,12},{9,8},{13,9},{14,13},{2,6},{3,2},{7,3},{4,7},{24,28},{25,24... | collective-permute-start | bytes 589832 | tf_op jit(solution)/shard_map/ppermute | solution.py:232
  40.8 0.0 collective-permute-done.7.refs_4_
  40.9 1.9 %collective-permute-start.5 = (bf16[16,48,128]{2,1,0:T(8,128)(2,1)S(1)}, bf16[16,48,128]{2,1,0:T(8,128)(2,1)S(1)}, u32[]{:S(2)}, u32[]{:S(2)}) collective-permute-start(bf16[16,48,128]{2,1,0:T(8,128)(2,1)S(1)} %right.2.refs_3_), channel_id=1, source_target_pairs={{9,12},{14,9},{3,6},{4,3},{25,28},{30,25},{19,22},{20,19}} | collective-permute-start | bytes 589832 | tf_op jit(solution)/shard_map/ppermute | solution.py:232
  42.8 0.0 collective-permute-done.8.refs_5_
  42.8 0.0 collective-permute-done.1.refs_1_
  42.8 0.0 collective-permute-done.2.refs_2_
  42.8 7.0 %product.2.refs_11_ = bf16[48,48,128]{2,1,0:T(8,128)(2,1)} custom-call(bf16[48,48,128]{2,1,0:T(8,128)(2,1)S(1)} %get-tuple-element.13.refs_0_, bf16[48,48,128]{2,1,0:T(8,128)(2,1)S(1)} %collective-permute-done.1.refs_1_, bf16[48,48,128]{2,1,0:T(8,128)(2,1)S(1)} %collective-permute-done.2.refs_2_, bf16[32,48,128]{2,1,0:T(8,128)(2,1)S(1)} %right.3.refs_3_, ...), custom_call_target="tpu_custom_call" | custom-call | flops 37748736 | bytes 2359296 | tf_op jit(solution)/shard_map/product/pallas_call | solution.py:324
  49.9 0.0 collective-permute-done.5.refs_5_
  49.9 3.8 %product.3 = bf16[48,48,128]{2,1,0:T(8,128)(2,1)} custom-call(bf16[48,48,128]{2,1,0:T(8,128)(2,1)S(1)} %get-tuple-element.13.refs_0_, bf16[48,48,128]{2,1,0:T(8,128)(2,1)S(1)} %collective-permute-done.1.refs_1_, bf16[48,48,128]{2,1,0:T(8,128)(2,1)S(1)} %collective-permute-done.2.refs_2_, ...), custom_call_target="tpu_custom_call", output_to_operand_aliasing={{}: (11, {})} | custom-call | flops 18874368 | bytes 2359296 | tf_op jit(solution)/shard_map/product/pallas_call | solution.py:324
  (8 shorter events, 0.0 us)
Async XLA Ops:
  0.0 9.9 %collective-permute-start = (bf16[48,48,128]{2,1,0:T(8,128)(2,1)}, bf16[48,48,128]{2,1,0:T(8,128)(2,1)S(1)}, u32[]{:S(2)}, u32[]{:S(2)}) collective-permute-start(bf16[48,48,128]{2,1,0:T(8,128)(2,1)} %refs_0_.1), channel_id=1, source_target_pairs={{0,3},{1,0},{2,1},{3,2},{4,7},{5,4},{6,5},{7,6},{8,11},{9,8},{10,9... | collective-permute-start | bytes 1769480 | tf_op jit(solution)/shard_map/ppermute | solution.py:29
  1.7 17.1 %collective-permute-start.6 = (bf16[32,48,128]{2,1,0:T(8,128)(2,1)S(1)}, bf16[32,48,128]{2,1,0:T(8,128)(2,1)S(1)}, u32[]{:S(2)}, u32[]{:S(2)}) collective-permute-start(bf16[32,48,128]{2,1,0:T(8,128)(2,1)S(1)} %slice.11), channel_id=1, source_target_pairs={{0,8},{1,9},{5,13},{6,14},{10,2},{11,3},{15,7},{12,4},{16,24},{17,... | collective-permute-start | bytes 1179656 | tf_op jit(solution)/shard_map/ppermute | solution.py:232
  4.5 38.3 %copy-start.1 = (f32[128]{0:T(128)S(1)}, f32[128]{0:T(128)}, u32[]{:S(2)}) copy-start(f32[128]{0:T(128)} %refs_8_.3) | copy-start | bytes 1540
  4.5 38.3 %copy-start.2 = (f32[128]{0:T(128)S(1)}, f32[128]{0:T(128)}, u32[]{:S(2)}) copy-start(f32[128]{0:T(128)} %refs_9_.3) | copy-start | bytes 1540
  9.9 1.1 %copy-start = (bf16[48,48,128]{2,1,0:T(8,128)(2,1)S(1)}, bf16[48,48,128]{2,1,0:T(8,128)(2,1)}, u32[]{:S(2)}) copy-start(bf16[48,48,128]{2,1,0:T(8,128)(2,1)} %refs_0_.1) | copy-start | bytes 1769476
  10.9 0.8 %copy-start.3 = (bf16[128,128]{1,0:T(8,128)(2,1)S(1)}, bf16[128,128]{1,0:T(8,128)(2,1)}, u32[]{:S(2)}) copy-start(bf16[128,128]{1,0:T(8,128)(2,1)} %refs_3_.1) | copy-start | bytes 98308
  11.7 0.8 %copy-start.4 = (bf16[128,128]{1,0:T(8,128)(2,1)S(1)}, bf16[128,128]{1,0:T(8,128)(2,1)}, u32[]{:S(2)}) copy-start(bf16[128,128]{1,0:T(8,128)(2,1)} %refs_7_.1) | copy-start | bytes 98308
  12.5 0.7 %copy-start.5 = (f32[128]{0:T(128)S(1)}, f32[128]{0:T(128)}, u32[]{:S(2)}) copy-start(f32[128]{0:T(128)} %param.11) | copy-start | bytes 1540
  13.1 0.7 %copy-start.6 = (f32[128]{0:T(128)S(1)}, f32[128]{0:T(128)}, u32[]{:S(2)}) copy-start(f32[128]{0:T(128)} %param.12) | copy-start | bytes 1540
  17.4 25.4 %collective-permute-start.1 = (bf16[48,48,128]{2,1,0:T(8,128)(2,1)S(1)}, bf16[48,48,128]{2,1,0:T(8,128)(2,1)S(1)}, u32[]{:S(2)}, u32[]{:S(2)}) collective-permute-start(bf16[48,48,128]{2,1,0:T(8,128)(2,1)S(1)} %get-tuple-element.13.refs_0_), channel_id=1, source_target_pairs={{0,4},{1,0},{5,1},{6,5},{10,14},{11,10},{15,11},{12,15},{16,20},{1... | collective-permute-start | bytes 1769480 | tf_op jit(solution)/shard_map/ppermute | solution.py:232
  18.1 24.7 %collective-permute-start.2 = (bf16[48,48,128]{2,1,0:T(8,128)(2,1)S(1)}, bf16[48,48,128]{2,1,0:T(8,128)(2,1)S(1)}, u32[]{:S(2)}, u32[]{:S(2)}) collective-permute-start(bf16[48,48,128]{2,1,0:T(8,128)(2,1)S(1)} %get-tuple-element.13.refs_0_), channel_id=1, source_target_pairs={{1,4},{6,1},{11,14},{12,11},{17,20},{22,17},{27,30},{28,27}} | collective-permute-start | bytes 1769480 | tf_op jit(solution)/shard_map/ppermute | solution.py:232
  19.6 21.3 %collective-permute-start.7 = (bf16[32,48,128]{2,1,0:T(8,128)(2,1)S(1)}, bf16[32,48,128]{2,1,0:T(8,128)(2,1)S(1)}, u32[]{:S(2)}, u32[]{:S(2)}) collective-permute-start(bf16[32,48,128]{2,1,0:T(8,128)(2,1)S(1)} %right.3.refs_3_), channel_id=1, source_target_pairs={{8,12},{9,8},{13,9},{14,13},{2,6},{3,2},{7,3},{4,7},{24,28},{25,24... | collective-permute-start | bytes 1179656 | tf_op jit(solution)/shard_map/ppermute | solution.py:232
  21.5 16.9 %collective-permute-start.3 = (bf16[16,48,128]{2,1,0:T(8,128)(2,1)S(1)}, bf16[16,48,128]{2,1,0:T(8,128)(2,1)S(1)}, u32[]{:S(2)}, u32[]{:S(2)}) collective-permute-start(bf16[16,48,128]{2,1,0:T(8,128)(2,1)S(1)} %get-tuple-element.14), channel_id=1, source_target_pairs={{0,8},{1,9},{5,13},{6,14},{10,2},{11,3},{15,7},{12,4},{16,24},{17,... | collective-permute-start | bytes 589832 | tf_op jit(solution)/shard_map/ppermute | solution.py:232
  22.8 20.0 %collective-permute-start.8 = (bf16[32,48,128]{2,1,0:T(8,128)(2,1)S(1)}, bf16[32,48,128]{2,1,0:T(8,128)(2,1)S(1)}, u32[]{:S(2)}, u32[]{:S(2)}) collective-permute-start(bf16[32,48,128]{2,1,0:T(8,128)(2,1)S(1)} %right.3.refs_3_), channel_id=1, source_target_pairs={{9,12},{14,9},{3,6},{4,3},{25,28},{30,25},{19,22},{20,19}} | collective-permute-start | bytes 1179656 | tf_op jit(solution)/shard_map/ppermute | solution.py:232
  38.9 10.9 %collective-permute-start.4 = (bf16[16,48,128]{2,1,0:T(8,128)(2,1)S(1)}, bf16[16,48,128]{2,1,0:T(8,128)(2,1)S(1)}, u32[]{:S(2)}, u32[]{:S(2)}) collective-permute-start(bf16[16,48,128]{2,1,0:T(8,128)(2,1)S(1)} %right.2.refs_3_), channel_id=1, source_target_pairs={{8,12},{9,8},{13,9},{14,13},{2,6},{3,2},{7,3},{4,7},{24,28},{25,24... | collective-permute-start | bytes 589832 | tf_op jit(solution)/shard_map/ppermute | solution.py:232
  40.9 9.0 %collective-permute-start.5 = (bf16[16,48,128]{2,1,0:T(8,128)(2,1)S(1)}, bf16[16,48,128]{2,1,0:T(8,128)(2,1)S(1)}, u32[]{:S(2)}, u32[]{:S(2)}) collective-permute-start(bf16[16,48,128]{2,1,0:T(8,128)(2,1)S(1)} %right.2.refs_3_), channel_id=1, source_target_pairs={{9,12},{14,9},{3,6},{4,3},{25,28},{30,25},{19,22},{20,19}} | collective-permute-start | bytes 589832 | tf_op jit(solution)/shard_map/ppermute | solution.py:232

commit v8 on v6

--- a/solution.py
+++ b/solution.py
@@ -47,33 +47,55 @@
     return layer_norm(values, gain_ref[...], bias_ref[...]).astype(jnp.bfloat16)
 
 
+def masked_right(both, tokens, row_token, third_block, columns):
+    hidden = both.shape[1] // 2
+    right = jax.nn.sigmoid(both[:, :hidden]) * both[:, hidden:]
+    position = lax.broadcasted_iota(jnp.int32, (columns, hidden), 0)
+    parts = []
+    for row in range(both.shape[0] // columns):
+        limit = jnp.where(row_token + row < tokens, tokens - third_block * columns, 0)
+        part = right[row * columns : (row + 1) * columns]
+        parts.append(jnp.where(position < limit, part, 0.0).astype(jnp.bfloat16))
+    return parts
+
+
 def right_kernel(origin, tokens_ref, pair_ref, gain_ref, bias_ref, weights_ref, *outs):
-    columns, hidden = outs[0].shape[1:]
-    row_block, third_block = origin()
-    tokens = tokens_ref[0]
-    row_start = row_block * pair_ref.shape[0]
-    valid_columns = tokens - third_block * columns
-    position = lax.broadcasted_iota(jnp.int32, (columns, hidden), 0)
+    columns = pair_ref.shape[1]
+    row_token, third_block = origin()
     step = 4
     first = 0
     for out_ref in outs:
         for at in range(0, out_ref.shape[0], step):
             normed = normed_rows(pair_ref[pl.ds(first + at, step)], gain_ref, bias_ref)
             both = jnp.dot(normed, weights_ref[...], preferred_element_type=jnp.float32)
-            right = jax.nn.sigmoid(both[:, :hidden]) * both[:, hidden:]
-            for row in range(step):
-                limit = jnp.where(row_start + first + at + row < tokens, valid_columns, 0)
-                part = right[row * columns : (row + 1) * columns]
-                out_ref[at + row] = jnp.where(position < limit, part, 0.0).astype(jnp.bfloat16)
+            parts = masked_right(both, tokens_ref[0], row_token + first + at, third_block, columns)
+            for row, part in enumerate(parts):
+                out_ref[at + row] = part
         first += out_ref.shape[0]
 
 
-def left_kernel(blocks, tokens_ref, *refs):
-    pair_refs, refs = refs[:blocks], refs[blocks:]
-    gain_ref, bias_ref, weights_ref, gate_weights_ref, *passed, scratch = refs
-    passed, (left_ref, gate_ref), handed = passed[:4], passed[4:6], passed[6:]
+def own_kernel(passes, tokens_ref, pair_ref, gate_weights_ref, *refs):
+    passed, (right_ref, gate_ref), handed = refs[:passes], refs[passes : passes + 2], refs[passes + 2 :]
+    gain_ref, bias_ref, right_weights_ref = passed[:3]
+    rows, columns, channels = pair_ref.shape
     for source, target in zip(passed, handed):
         target[...] = source[...]
+    row_start = lax.axis_index("row") * rows
+    step = 4
+    for first in range(0, rows, step):
+        normed = normed_rows(pair_ref[pl.ds(first, step)], gain_ref, bias_ref)
+        gate = jnp.dot(normed, gate_weights_ref[...], preferred_element_type=jnp.float32)
+        gate_ref[pl.ds(first, step)] = jax.nn.sigmoid(gate).reshape(step, columns, channels)
+        both = jnp.dot(normed, right_weights_ref[...], preferred_element_type=jnp.float32)
+        parts = masked_right(
+            both, tokens_ref[0], row_start + first, lax.axis_index("col"), columns
+        )
+        for row, part in enumerate(parts):
+            right_ref[first + row] = part
+
+
+def left_kernel(blocks, tokens_ref, *refs):
+    pair_refs, (gain_ref, bias_ref, weights_ref, left_ref, scratch) = refs[:blocks], refs[blocks:]
     rows, columns, channels = pair_refs[0].shape
     hidden, _, width = left_ref.shape
     tokens = tokens_ref[0]
@@ -90,8 +112,6 @@
     step = 4
     for first in range(0, rows, step):
         normed = [normed_rows(ref[pl.ds(first, step)], gain_ref, bias_ref) for ref in pair_refs]
-        gate = jnp.dot(normed[0], gate_weights_ref[...], preferred_element_type=jnp.float32)
-        gate_ref[pl.ds(first, step)] = jax.nn.sigmoid(gate).reshape(step, columns, channels)
         for row in range(step):
             thirds = [piece[row * columns : (row + 1) * columns] for piece in normed]
             both = lax.dot_general(
@@ -151,32 +171,66 @@
         for at in range(0, width, LANES):
             right[at // LANES, pl.ds(token, hidden, stride=count), :] = one[:, at : at + LANES]
 
-    total = jnp.zeros((count, rows), jnp.float32)
-    for channel in range(hidden):
+    group = max(1, LANES // rows)
+    share, lanes = hidden // group, group * rows
+    low = [lax.broadcasted_iota(jnp.int32, (count, lanes), 1) < rows * at for at in range(group)]
+
+    def per_lane(values_ref, channel):
+        values = jnp.full((count, lanes), values_ref[channel + (group - 1) * share], jnp.float32)
+        for at in range(group - 1, 0, -1):
+            values = jnp.where(low[at], values_ref[channel + (at - 1) * share], values)
+        return values
+
+    def folded(total):
+        mean = sum(total[:, at * rows : (at + 1) * rows] for at in range(group)) / hidden
+        return jnp.concatenate([mean] * group, axis=1)
+
+    total = jnp.zeros((count, lanes), jnp.float32)
+    nothing = jnp.zeros((rows, LANES), jnp.bfloat16)
+    for channel in range(share):
         one = 0.0
         for at in range(0, width, LANES):
+            rights = [
+                right[at // LANES, pl.ds((channel + member * share) * count, count), :].astype(jnp.bfloat16)
+                for member in range(group)
+            ]
+            lefts = [
+                jnp.concatenate(
+                    [
+                        left_ref[channel + member * share, :, at : at + LANES] if here == member else nothing
+                        for here in range(group)
+                    ],
+                    axis=1,
+                )
+                for member in range(group)
+            ]
             one += lax.dot_general(
-                right[at // LANES, pl.ds(channel * count, count), :].astype(jnp.bfloat16),
-                left_ref[channel, :, at : at + LANES],
+                jnp.concatenate(rights, axis=1),
+                jnp.concatenate(lefts, axis=0),
                 (((1,), (1,)), ((), ())),
                 preferred_element_type=jnp.float32,
             )
-        product[pl.ds(channel * count, count), :rows] = one
+        product[pl.ds(channel * count, count), :lanes] = one
         total += one
-    average = total / hidden
-    total = jnp.zeros((count, rows), jnp.float32)
-    for channel in range(hidden):
-        centered = product[pl.ds(channel * count, count), :rows] - average
+    average = folded(total)
+    total = jnp.zeros((count, lanes), jnp.float32)
+    for channel in range(share):
+        centered = product[pl.ds(channel * count, count), :lanes] - average
         total += centered * centered
-    scale = lax.rsqrt(total / hidden + 1e-05)
-    for channel in range(hidden):
+    scale = lax.rsqrt(folded(total) + 1e-05)
+    for channel in range(share):
         place = pl.ds(channel * count, count)
-        centered = product[place, :rows] - average
-        product[place, :rows] = centered * scale * gain_ref[channel] + bias_ref[channel]
+        centered = product[place, :lanes] - average
+        product[place, :lanes] = centered * scale * per_lane(gain_ref, channel) + per_lane(bias_ref, channel)
     for token in range(count):
-        mixed = product[pl.ds(token, hidden, stride=count), :][:, :rows].astype(jnp.bfloat16)
-        updates[pl.ds(token, rows, stride=count), :] = lax.dot_general(
-            mixed, weights_ref[...], (((0,), (0,)), ((), ())), preferred_element_type=jnp.float32
+        mixed = product[pl.ds(token, share, stride=count), :].T.astype(jnp.bfloat16)
+        updates[pl.ds(token, rows, stride=count), :] = sum(
+            jnp.dot(
+                mixed[member * rows : (member + 1) * rows],
+                weights_ref[pl.ds(member * share, share)],
+                preferred_element_type=jnp.float32,
+            )
+            for member in range(group)
         )
     step = 8
     for at in range(0, rows, step):
@@ -203,27 +257,24 @@
 
 
 def hop_place():
-    return lax.axis_index("row") ^ lax.axis_index("col")
-
-
-def far_origin():
-    row_pos, col_pos = lax.axis_index("row"), lax.axis_index("col")
-    diagonal = hop_place() == 2
-    row_block = jnp.where(diagonal, col_pos, jnp.where(col_pos == 2, row_pos - 2, 3 - row_pos))
-    return row_block, jnp.where(diagonal, col_pos, (row_block + 1) % 4)
+    col_pos = lax.axis_index("col")
+    place = lax.axis_index("row") ^ col_pos
+    return jnp.where((place > 1) & (col_pos % 2 == 1), place + 2, place)
 
 
 def hops():
-    relay = {0: (2, 2), 1: (3, 2), 2: (1, 0), 3: (0, 0)}
-    column = range(4)
-    out, near, near_more, far, far_more = [], [], [], [], []
-    for c in column:
-        out += [((c, c), (c ^ 2, c)), ((c, (c + 1) % 4), relay[c])]
-        near += [((c, c), (c ^ 1, c)), ((c, (c + 1) % 4), (c, c))]
-        near_more += [((c, (c + 1) % 4), (c ^ 1, c))]
-        far += [((c ^ 2, c), (c ^ 3, c)), (relay[c], (c ^ 2, c))]
-        far_more += [(relay[c], (c ^ 3, c))]
-    return out, near, near_more, far, far_more
+    out, near, near_more, direct, swap = [], [], [], [], []
+    for c in range(4):
+        first, second = (c, c), (c, (c + 1) % 4)
+        out += [(first, (c ^ 2, c)), (second, (c ^ 3, c))]
+        near += [(first, (c ^ 1, c)), (second, (c, c))]
+        near_more += [(second, (c ^ 1, c))]
+        swap += [((c ^ 2, c), (c ^ 3, c))]
+        if c % 2:
+            direct += [(second, (c ^ 2, c))]
+        else:
+            swap += [((c ^ 3, c), (c ^ 2, c))]
+    return out, near, near_more, direct, swap
 
 
 def move(array, pairs):
@@ -257,55 +308,65 @@
     last = 16
     spans = [(0, columns - last), (columns - last, last)]
 
-    def right_of(origin, pair, parts):
+    def right_of(origin, pair, counts):
         return pl.pallas_call(
             functools.partial(right_kernel, origin),
             out_shape=[
-                jax.ShapeDtypeStruct((count, columns, hidden), jnp.bfloat16) for count in parts
+                jax.ShapeDtypeStruct((count, columns, hidden), jnp.bfloat16) for count in counts
             ],
             in_specs=[SMEM] + [VMEM] * 4,
-            out_specs=[VMEM] * len(parts),
+            out_specs=[VMEM] * len(counts),
             compiler_params=params(2 * block),
-            cost_estimate=cost(4 * tokens * channels * hidden, 6 * tokens * channels),
+            cost_estimate=cost(4 * tokens * channels * hidden, 4 * tokens * channels),
             name="right",
         )(token_count, pair, in_gain, in_bias, right_weights)
 
-    def here():
-        return lax.axis_index("row"), lax.axis_index("col")
-
-    right_weights = in_weights[:, 2 * hidden :]
+    def far_origin():
+        col_pos = lax.axis_index("col")
+        return col_pos * rows, jnp.where(hop_place() % 2 == 0, col_pos, (col_pos + 1) % 4)
+
     if by_hops:
-        out, near, near_more, far, far_more = hops()
+        out, near, near_more, direct, swap = hops()
         arrived = move(pair_state, out)
     pairs = [pair_state]
     for _ in range(window - 1):
         pairs.append(shifted(pairs[-1], "col", -1))
-    (right,) = right_of(here, pair_state, [rows])
-    passed = [in_gain, in_bias, right_weights, out_weights]
-    left, gate, *handed = pl.pallas_call(
-        functools.partial(left_kernel, window),
+    passed = [in_gain, in_bias, in_weights[:, 2 * hidden :], out_weights]
+    right, gate, *handed = pl.pallas_call(
+        functools.partial(own_kernel, len(passed)),
         out_shape=[
-            jax.ShapeDtypeStruct((hidden, rows, width), jnp.bfloat16),
+            jax.ShapeDtypeStruct((rows, columns, hidden), jnp.bfloat16),
             jax.ShapeDtypeStruct((rows, columns, channels), jnp.float32),
         ]
         + [jax.ShapeDtypeStruct(array.shape, array.dtype) for array in passed],
-        in_specs=[SMEM] + [VMEM] * (window + 8),
-        out_specs=[VMEM] * 6,
+        in_specs=[SMEM] + [VMEM] * (2 + len(passed)),
+        out_specs=[VMEM] * (2 + len(passed)),
+        compiler_params=params(4 * block),
+        cost_estimate=cost(6 * tokens * channels * hidden, 8 * tokens * channels),
+        name="own",
+    )(token_count, pair_state, gate_weights, *passed)
+    in_gain, in_bias, right_weights, out_weights = handed
+    if by_hops:
+        near, direct = move(right, near), move(right, direct)
+    left = pl.pallas_call(
+        functools.partial(left_kernel, window),
+        out_shape=jax.ShapeDtypeStruct((hidden, rows, width), jnp.bfloat16),
+        in_specs=[SMEM] + [VMEM] * (window + 3),
+        out_specs=VMEM,
         scratch_shapes=[pltpu.VMEM((width // LANES, hidden * rows, LANES), jnp.float32)],
         compiler_params=params((window + 2) * block, 6 * hidden * rows * width),
-        cost_estimate=cost(
-            4 * window * tokens * channels * hidden, 6 * rows * width * hidden
-        ),
-        name="left_and_gate",
-    )(token_count, *pairs, in_gain, in_bias, in_weights[:, : 2 * hidden].T, gate_weights, *passed)
-    in_gain, in_bias, right_weights, out_weights = handed
+        cost_estimate=cost(4 * window * tokens * channels * hidden, 6 * rows * width * hidden),
+        name="left",
+    )(token_count, *pairs, in_gain, in_bias, in_weights[:, : 2 * hidden].T)
 
     if by_hops:
-        near, near_more = move(right, near), move(right, near_more)
+        mine = right_of(far_origin, arrived, [count for _, count in spans])
+        later, *mine = lax.optimization_barrier((right, *mine))
+        near_more = move(later, near_more)
         bands = []
-        for mine in right_of(far_origin, arrived, [count for _, count in spans]):
-            bands.append([right, near, near_more, mine, move(mine, far), move(mine, far_more)])
-        picks, place = [(0, 1, 3, 4), (1, 2, 4, 5)], hop_place
+        for piece in mine:
+            bands.append([right, near, near_more, piece, move(piece, swap), direct])
+        picks, place = [(0, 1, 3, 4, 3, 4), (1, 2, 4, 3, 5, 3)], hop_place
     else:
         bands = [band_by_sums(right, window, row_count, col_count, columns)] * len(spans)
         picks, place = [(at,) for at in range(window)], lambda: 0
@@ -319,7 +380,7 @@
             out_specs=ANY,
             scratch_shapes=[
                 pltpu.VMEM((width // LANES, hidden * count, LANES), jnp.float32),
-                pltpu.VMEM((hidden * count, LANES), jnp.float32),
+                pltpu.VMEM((hidden // max(1, LANES // rows) * count, LANES), jnp.float32),
                 pltpu.VMEM((rows * count, channels), jnp.float32),
                 pltpu.VMEM((rows, count, channels), jnp.bfloat16),
                 pltpu.SemaphoreType.DMA,

time: 54.6 us -> 58.9 us (1.079)
  the two profiles are of different devices: /device:TPU:12 before, /device:TPU:18 now
where the time goes in v8:
time: 58.9 us; the launch traced here: 58.2 us
  Pallas kernels  17.8 us (30%)
  starting transfers between devices  16.5 us (28%)
  waiting for transfers between devices  12.4 us (21%)
  local copies, waits for them, and re-layouts  10.7 us (18%)
  between operations  0.8 us (1%)
    ppermute x6, starting transfers between devices, move(): lax.ppermute(array, ('row', 'col'), [(r * 4 + c, to_r * 4 + to_c) for (r,...  14.1 us
    ppermute x6, waiting for transfers between devices, move(): lax.ppermute(array, ('row', 'col'), [(r * 4 + c, to_r * 4 + to_c) for (r,...  12.4 us
    pallas_call x2, Pallas kernels, on_device(): pl.pallas_call(functools.partial(product_kernel, picks, place, len(band),...  11.4 us
    unnamed x27, local copies, waits for them, and re-layouts  9.25 us
    pallas_call x1, Pallas kernels, on_device(): pl.pallas_call(functools.partial(left_kernel, window), out_shape=jax.Shap...  3.44 us
    ppermute x1, starting transfers between devices, shifted(): lax.ppermute(array, axis, [(i, (i + by) % devices) for i in range(devices)])  2.39 us
    pallas_call x1, Pallas kernels, right_of(): pl.pallas_call(functools.partial(right_kernel, origin), out_shape=[jax.Sh...  1.79 us
    slice x1, local copies, waits for them, and re-layouts, on_device(): in_weights[:, :2 * hidden]  1.5 us
  transfers between devices with their start and end apart: 7, of which 2 were waited for; matrix products, arithmetic and copies ran while one was open for 5% of the time, Pallas kernels for 23%

profile of v8, /device:TPU:18, one launch (start us, length us, event | category | flops | bytes accessed | tf_op | source)
XLA Modules:
  0.0 58.2 jit_solution(558188119566666551)
XLA Ops:
  0.0 1.3 %collective-permute-start.1 = (bf16[48,48,128]{2,1,0:T(8,128)(2,1)}, bf16[48,48,128]{2,1,0:T(8,128)(2,1)S(1)}, u32[]{:S(2)}, u32[]{:S(2)}) collective-permute-start(bf16[48,48,128]{2,1,0:T(8,128)(2,1)} %refs_0_.1), channel_id=1, source_target_pairs={{0,8},{1,12},{5,13},{6,9},{10,2},{11,6},{15,7},{12,3},{16,24},{17,... | collective-permute-start | bytes 1769480 | tf_op jit(solution)/shard_map/ppermute | solution.py:281
  1.3 2.4 %collective-permute-start.5 = (bf16[48,48,128]{2,1,0:T(8,128)(2,1)}, bf16[48,48,128]{2,1,0:T(8,128)(2,1)S(1)}, u32[]{:S(2)}, u32[]{:S(2)}) collective-permute-start(bf16[48,48,128]{2,1,0:T(8,128)(2,1)} %refs_0_.1), channel_id=1, source_target_pairs={{0,3},{1,0},{2,1},{3,2},{4,7},{5,4},{6,5},{7,6},{8,11},{9,8},{10,9... | collective-permute-start | bytes 1769480 | tf_op jit(solution)/shard_map/ppermute | solution.py:29
  4.3 1.5 %fusion = (bf16[128,256]{1,0:T(8,128)(2,1)}, bf16[128,256]{1,0:T(8,128)(2,1)S(1)}) fusion(bf16[128,512]{1,0:T(8,128)(2,1)} %param.13), kind=kLoop, calls=%fused_computation | loop fusion | bytes 262144 | tf_op jit(solution)/shard_map/slice | solution.py:360
  5.8 1.1 %copy-done = bf16[48,48,128]{2,1,0:T(8,128)(2,1)S(1)} copy-done((bf16[48,48,128]{2,1,0:T(8,128)(2,1)S(1)}, bf16[48,48,128]{2,1,0:T(8,128)(2,1)}, u32[]{:S(2)}) %copy-start) | copy-done | bytes 589848
  6.9 0.8 %copy-done.9 = bf16[128,128]{1,0:T(8,128)(2,1)S(1)} copy-done((bf16[128,128]{1,0:T(8,128)(2,1)S(1)}, bf16[128,128]{1,0:T(8,128)(2,1)}, u32[]{:S(2)}) %copy-start.9) | copy-done | bytes 32792
  7.7 0.8 %copy-done.10 = bf16[128,128]{1,0:T(8,128)(2,1)S(1)} copy-done((bf16[128,128]{1,0:T(8,128)(2,1)S(1)}, bf16[128,128]{1,0:T(8,128)(2,1)}, u32[]{:S(2)}) %copy-start.10) | copy-done | bytes 32792
  8.4 0.7 %copy-done.11 = f32[128]{0:T(128)S(1)} copy-done((f32[128]{0:T(128)S(1)}, f32[128]{0:T(128)}, u32[]{:S(2)}) %copy-start.11) | copy-done | bytes 536
  9.1 0.7 %copy-done.12 = f32[128]{0:T(128)S(1)} copy-done((f32[128]{0:T(128)S(1)}, f32[128]{0:T(128)}, u32[]{:S(2)}) %copy-start.12) | copy-done | bytes 536
  9.7 1.2 %own.1 = (bf16[48,48,128]{2,1,0:T(8,128)(2,1)S(1)}, f32[48,48,128]{2,1,0:T(8,128)S(1)}, f32[1,128]{1,0:T(1,128)S(1)}, f32[1,128]{1,0:T(1,128)S(1)}, bf16[128,256...) custom-call(s32[1]{0:T(128)S(6)} %copy.14.tokens_ref, bf16[48,48,128]{2,1,0:T(8,128)(2,1)S(1)} %copy-done, ...), custom_call_target="tpu_custom_call" | custom-call | flops 226492416 | bytes 2359296 | tf_op jit(solution)/shard_map/own/pallas_call | solution.py:335
  10.9 0.7 %collective-permute-start = (bf16[48,48,128]{2,1,0:T(8,128)(2,1)S(1)}, bf16[48,48,128]{2,1,0:T(8,128)(2,1)S(1)}, u32[]{:S(2)}, u32[]{:S(2)}) collective-permute-start(bf16[48,48,128]{2,1,0:T(8,128)(2,1)S(1)} %get-tuple-element.22.refs_0_), channel_id=1, source_target_pairs={{0,4},{1,0},{5,1},{6,5},{10,14},{11,10},{15,11},{12,15},{16,20},{1... | collective-permute-start | bytes 1769480 | tf_op jit(solution)/shard_map/ppermute | solution.py:281
  11.6 0.7 %collective-permute-start.4 = (bf16[48,48,128]{2,1,0:T(8,128)(2,1)S(1)}, bf16[48,48,128]{2,1,0:T(8,128)(2,1)S(1)}, u32[]{:S(2)}, u32[]{:S(2)}) collective-permute-start(bf16[48,48,128]{2,1,0:T(8,128)(2,1)S(1)} %get-tuple-element.22.refs_0_), channel_id=1, source_target_pairs={{6,13},{12,7},{22,29},{28,23}} | collective-permute-start | bytes 1769480 | tf_op jit(solution)/shard_map/ppermute | solution.py:281
  12.3 6.6 %collective-permute-done.1.pair_ref = bf16[48,48,128]{2,1,0:T(8,128)(2,1)S(1)} collective-permute-done((bf16[48,48,128]{2,1,0:T(8,128)(2,1)}, bf16[48,48,128]{2,1,0:T(8,128)(2,1)S(1)}, u32[]{:S(2)}, u32[]{:S(2)}) %collective-permute-start.1) | collective-permute-done | bytes 589856 | tf_op jit(solution)/shard_map/ppermute | solution.py:281
  18.9 1.8 %right.1 = (bf16[32,48,128]{2,1,0:T(8,128)(2,1)}, bf16[16,48,128]{2,1,0:T(8,128)(2,1)}) custom-call(s32[1]{0:T(128)S(6)} %copy.14.tokens_ref, bf16[48,48,128]{2,1,0:T(8,128)(2,1)S(1)} %collective-permute-done.1.pair_ref, f32[1,128]{1,0:T(1,128)S(1)} %get-tuple-element.17.gain_ref.refs_2_, f32[1,128]{1,0:T(1,128)S(1)} %get-tuple-element.18.bias_ref.refs_3_, ...), custom_call_target="tpu_custom_call" | custom-call | flops 150994944 | bytes 1179648 | tf_op jit(solution)/shard_map/right/pallas_call | solution.py:312
  20.7 0.8 %collective-permute-start.2 = (bf16[48,48,128]{2,1,0:T(8,128)(2,1)S(1)}, bf16[48,48,128]{2,1,0:T(8,128)(2,1)S(1)}, u32[]{:S(2)}, u32[]{:S(2)}) collective-permute-start(bf16[48,48,128]{2,1,0:T(8,128)(2,1)S(1)} %get-tuple-element.22.refs_0_), channel_id=1, source_target_pairs={{1,4},{6,1},{11,14},{12,11},{17,20},{22,17},{27,30},{28,27}} | collective-permute-start | bytes 1769480 | tf_op jit(solution)/shard_map/ppermute | solution.py:281
  21.6 8.7 %collective-permute-start.6 = (bf16[32,48,128]{2,1,0:T(8,128)(2,1)}, bf16[32,48,128]{2,1,0:T(8,128)(2,1)}, u32[]{:S(2)}, u32[]{:S(2)}) collective-permute-start(bf16[32,48,128]{2,1,0:T(8,128)(2,1)} %get-tuple-element.26.refs_3_), channel_id=1, source_target_pairs={{8,12},{12,8},{13,9},{2,6},{6,2},{7,3},{24,28},{28,24},{29,25},{18... | collective-permute-start | bytes 1179656 | tf_op jit(solution)/shard_map/ppermute | solution.py:281
  30.2 0.0 collective-permute-done.5.refs_1_
  30.3 0.0 copy-start.2
  30.3 0.8 %copy-done.2 = bf16[48,48,128]{2,1,0:T(8,128)(2,1)} copy-done((bf16[48,48,128]{2,1,0:T(8,128)(2,1)}, bf16[48,48,128]{2,1,0:T(8,128)(2,1)S(1)}, u32[]{:S(2)}) %copy-start.2) | copy-done | bytes 589848
  31.1 1.9 %collective-permute-start.3 = (bf16[16,48,128]{2,1,0:T(8,128)(2,1)}, bf16[16,48,128]{2,1,0:T(8,128)(2,1)}, u32[]{:S(2)}, u32[]{:S(2)}) collective-permute-start(bf16[16,48,128]{2,1,0:T(8,128)(2,1)} %get-tuple-element.23.refs_3_), channel_id=1, source_target_pairs={{8,12},{12,8},{13,9},{2,6},{6,2},{7,3},{24,28},{28,24},{29,25},{18... | collective-permute-start | bytes 589832 | tf_op jit(solution)/shard_map/ppermute | solution.py:281
  33.0 1.6 %copy.12 = bf16[128,256]{0,1:T(8,128)(2,1)} copy(bf16[128,256]{1,0:T(8,128)(2,1)} %get-tuple-element.27) | data formatting | bytes 131072
  34.6 1.1 %copy-done.1 = bf16[48,48,128]{2,1,0:T(8,128)(2,1)S(1)} copy-done((bf16[48,48,128]{2,1,0:T(8,128)(2,1)S(1)}, bf16[48,48,128]{2,1,0:T(8,128)(2,1)}, u32[]{:S(2)}) %copy-start.1) | copy-done | bytes 589848
  35.6 1.1 %copy-done.3 = bf16[48,48,128]{2,1,0:T(8,128)(2,1)S(1)} copy-done((bf16[48,48,128]{2,1,0:T(8,128)(2,1)S(1)}, bf16[48,48,128]{2,1,0:T(8,128)(2,1)}, u32[]{:S(2)}) %copy-start.3) | copy-done | bytes 589848
  36.7 0.8 %copy-done.4 = bf16[128,256]{0,1:T(8,128)(2,1)S(1)} copy-done((bf16[128,256]{0,1:T(8,128)(2,1)S(1)}, bf16[128,256]{0,1:T(8,128)(2,1)}, u32[]{:S(2)}) %copy-start.4) | copy-done | bytes 65560
  37.5 3.4 %left.1.refs_6_ = bf16[128,48,128]{2,1,0:T(8,128)(2,1)S(1)} custom-call(s32[1]{0:T(128)S(6)} %copy.14.tokens_ref, bf16[48,48,128]{2,1,0:T(8,128)(2,1)S(1)} %copy-done.1, bf16[48,48,128]{2,1,0:T(8,128)(2,1)S(1)} %copy-done.3, f32[1,128]{1,0:T(1,128)S(1)} %get-tuple-element.17.gain_ref.refs_2_, f32[1,128]{1,0:T(1,128)S(1)} %get-tuple-element.18.bias_ref.refs_3_, ...), custom_call_target="tpu_custom_call" | custom-call | flops 301989888 | bytes 4718592 | tf_op jit(solution)/shard_map/left/pallas_call | solution.py:351
  41.0 0.0 collective-permute-done.refs_1_
  41.0 0.0 collective-permute-done.4.refs_5_
  41.0 5.8 %collective-permute-done.6.refs_4_ = bf16[32,48,128]{2,1,0:T(8,128)(2,1)} collective-permute-done((bf16[32,48,128]{2,1,0:T(8,128)(2,1)}, bf16[32,48,128]{2,1,0:T(8,128)(2,1)}, u32[]{:S(2)}, u32[]{:S(2)}) %collective-permute-start.6) | collective-permute-done | bytes 393248 | tf_op jit(solution)/shard_map/ppermute | solution.py:281
  46.8 0.0 collective-permute-done.2.refs_2_
  46.8 0.0 copy-done.7
  46.8 7.1 %product.2.refs_11_ = bf16[48,48,128]{2,1,0:T(8,128)(2,1)} custom-call(bf16[48,48,128]{2,1,0:T(8,128)(2,1)S(1)} %get-tuple-element.22.refs_0_, bf16[48,48,128]{2,1,0:T(8,128)(2,1)S(1)} %collective-permute-done.refs_1_, bf16[48,48,128]{2,1,0:T(8,128)(2,1)S(1)} %collective-permute-done.2.refs_2_, bf16[32,48,128]{2,1,0:T(8,128)(2,1)} %get-tuple-element.26.refs_3_, ...), custom_call_target="tpu_custom_call" | custom-call | flops 37748736 | bytes 2359296 | tf_op jit(solution)/shard_map/product/pallas_call | solution.py:376
  53.8 0.0 collective-permute-done.3.refs_4_
  53.9 4.4 %product.3 = bf16[48,48,128]{2,1,0:T(8,128)(2,1)} custom-call(bf16[48,48,128]{2,1,0:T(8,128)(2,1)S(1)} %get-tuple-element.22.refs_0_, bf16[48,48,128]{2,1,0:T(8,128)(2,1)S(1)} %collective-permute-done.refs_1_, bf16[48,48,128]{2,1,0:T(8,128)(2,1)S(1)} %collective-permute-done.2.refs_2_, ...), custom_call_target="tpu_custom_call", output_to_operand_aliasing={{}: (11, {})} | custom-call | flops 18874368 | bytes 2359296 | tf_op jit(solution)/shard_map/product/pallas_call | solution.py:376
  (15 shorter events, 0.0 us)
Async XLA Ops:
  0.0 18.9 %collective-permute-start.1 = (bf16[48,48,128]{2,1,0:T(8,128)(2,1)}, bf16[48,48,128]{2,1,0:T(8,128)(2,1)S(1)}, u32[]{:S(2)}, u32[]{:S(2)}) collective-permute-start(bf16[48,48,128]{2,1,0:T(8,128)(2,1)} %refs_0_.1), channel_id=1, source_target_pairs={{0,8},{1,12},{5,13},{6,9},{10,2},{11,6},{15,7},{12,3},{16,24},{17,... | collective-permute-start | bytes 1769480 | tf_op jit(solution)/shard_map/ppermute | solution.py:281
  1.3 28.9 %collective-permute-start.5 = (bf16[48,48,128]{2,1,0:T(8,128)(2,1)}, bf16[48,48,128]{2,1,0:T(8,128)(2,1)S(1)}, u32[]{:S(2)}, u32[]{:S(2)}) collective-permute-start(bf16[48,48,128]{2,1,0:T(8,128)(2,1)} %refs_0_.1), channel_id=1, source_target_pairs={{0,3},{1,0},{2,1},{3,2},{4,7},{5,4},{6,5},{7,6},{8,11},{9,8},{10,9... | collective-permute-start | bytes 1769480 | tf_op jit(solution)/shard_map/ppermute | solution.py:29
  5.8 1.1 %copy-start = (bf16[48,48,128]{2,1,0:T(8,128)(2,1)S(1)}, bf16[48,48,128]{2,1,0:T(8,128)(2,1)}, u32[]{:S(2)}) copy-start(bf16[48,48,128]{2,1,0:T(8,128)(2,1)} %refs_0_.1) | copy-start | bytes 1769476
  6.9 0.8 %copy-start.9 = (bf16[128,128]{1,0:T(8,128)(2,1)S(1)}, bf16[128,128]{1,0:T(8,128)(2,1)}, u32[]{:S(2)}) copy-start(bf16[128,128]{1,0:T(8,128)(2,1)} %gate_weights_ref.1) | copy-start | bytes 98308
  7.7 0.8 %copy-start.10 = (bf16[128,128]{1,0:T(8,128)(2,1)S(1)}, bf16[128,128]{1,0:T(8,128)(2,1)}, u32[]{:S(2)}) copy-start(bf16[128,128]{1,0:T(8,128)(2,1)} %refs_3_.1) | copy-start | bytes 98308
  8.4 0.7 %copy-start.11 = (f32[128]{0:T(128)S(1)}, f32[128]{0:T(128)}, u32[]{:S(2)}) copy-start(f32[128]{0:T(128)} %param.11) | copy-start | bytes 1540
  9.1 0.7 %copy-start.12 = (f32[128]{0:T(128)S(1)}, f32[128]{0:T(128)}, u32[]{:S(2)}) copy-start(f32[128]{0:T(128)} %param.12) | copy-start | bytes 1540
  10.9 19.3 %copy-start.5 = (bf16[128,128]{1,0:T(8,128)(2,1)}, bf16[128,128]{1,0:T(8,128)(2,1)S(1)}, u32[]{:S(2)}) copy-start(bf16[128,128]{1,0:T(8,128)(2,1)S(1)} %get-tuple-element.25.refs_10_) | copy-start | bytes 98308
  10.9 30.1 %collective-permute-start = (bf16[48,48,128]{2,1,0:T(8,128)(2,1)S(1)}, bf16[48,48,128]{2,1,0:T(8,128)(2,1)S(1)}, u32[]{:S(2)}, u32[]{:S(2)}) collective-permute-start(bf16[48,48,128]{2,1,0:T(8,128)(2,1)S(1)} %get-tuple-element.22.refs_0_), channel_id=1, source_target_pairs={{0,4},{1,0},{5,1},{6,5},{10,14},{11,10},{15,11},{12,15},{16,20},{1... | collective-permute-start | bytes 1769480 | tf_op jit(solution)/shard_map/ppermute | solution.py:281
  11.6 29.4 %collective-permute-start.4 = (bf16[48,48,128]{2,1,0:T(8,128)(2,1)S(1)}, bf16[48,48,128]{2,1,0:T(8,128)(2,1)S(1)}, u32[]{:S(2)}, u32[]{:S(2)}) collective-permute-start(bf16[48,48,128]{2,1,0:T(8,128)(2,1)S(1)} %get-tuple-element.22.refs_0_), channel_id=1, source_target_pairs={{6,13},{12,7},{22,29},{28,23}} | collective-permute-start | bytes 1769480 | tf_op jit(solution)/shard_map/ppermute | solution.py:281
  20.7 26.0 %copy-start.7 = (f32[128]{0:T(128)S(1)}, f32[128]{0:T(128)}, u32[]{:S(2)}) copy-start(f32[128]{0:T(128)} %refs_8_.3) | copy-start | bytes 1540
  20.7 26.0 %copy-start.8 = (f32[128]{0:T(128)S(1)}, f32[128]{0:T(128)}, u32[]{:S(2)}) copy-start(f32[128]{0:T(128)} %refs_9_.3) | copy-start | bytes 1540
  20.7 26.0 %collective-permute-start.2 = (bf16[48,48,128]{2,1,0:T(8,128)(2,1)S(1)}, bf16[48,48,128]{2,1,0:T(8,128)(2,1)S(1)}, u32[]{:S(2)}, u32[]{:S(2)}) collective-permute-start(bf16[48,48,128]{2,1,0:T(8,128)(2,1)S(1)} %get-tuple-element.22.refs_0_), channel_id=1, source_target_pairs={{1,4},{6,1},{11,14},{12,11},{17,20},{22,17},{27,30},{28,27}} | collective-permute-start | bytes 1769480 | tf_op jit(solution)/shard_map/ppermute | solution.py:281
  21.6 25.2 %collective-permute-start.6 = (bf16[32,48,128]{2,1,0:T(8,128)(2,1)}, bf16[32,48,128]{2,1,0:T(8,128)(2,1)}, u32[]{:S(2)}, u32[]{:S(2)}) collective-permute-start(bf16[32,48,128]{2,1,0:T(8,128)(2,1)} %get-tuple-element.26.refs_3_), channel_id=1, source_target_pairs={{8,12},{12,8},{13,9},{2,6},{6,2},{7,3},{24,28},{28,24},{29,25},{18... | collective-permute-start | bytes 1179656 | tf_op jit(solution)/shard_map/ppermute | solution.py:281
  30.3 0.8 %copy-start.2 = (bf16[48,48,128]{2,1,0:T(8,128)(2,1)}, bf16[48,48,128]{2,1,0:T(8,128)(2,1)S(1)}, u32[]{:S(2)}) copy-start(bf16[48,48,128]{2,1,0:T(8,128)(2,1)S(1)} %collective-permute-done.5.refs_1_) | copy-start | bytes 1769476
  31.1 22.8 %collective-permute-start.3 = (bf16[16,48,128]{2,1,0:T(8,128)(2,1)}, bf16[16,48,128]{2,1,0:T(8,128)(2,1)}, u32[]{:S(2)}, u32[]{:S(2)}) collective-permute-start(bf16[16,48,128]{2,1,0:T(8,128)(2,1)} %get-tuple-element.23.refs_3_), channel_id=1, source_target_pairs={{8,12},{12,8},{13,9},{2,6},{6,2},{7,3},{24,28},{28,24},{29,25},{18... | collective-permute-start | bytes 589832 | tf_op jit(solution)/shard_map/ppermute | solution.py:281
  34.6 1.1 %copy-start.1 = (bf16[48,48,128]{2,1,0:T(8,128)(2,1)S(1)}, bf16[48,48,128]{2,1,0:T(8,128)(2,1)}, u32[]{:S(2)}) copy-start(bf16[48,48,128]{2,1,0:T(8,128)(2,1)} %refs_0_.1) | copy-start | bytes 1769476
  35.6 1.1 %copy-start.3 = (bf16[48,48,128]{2,1,0:T(8,128)(2,1)S(1)}, bf16[48,48,128]{2,1,0:T(8,128)(2,1)}, u32[]{:S(2)}) copy-start(bf16[48,48,128]{2,1,0:T(8,128)(2,1)} %copy-done.2) | copy-start | bytes 1769476
  36.7 0.8 %copy-start.4 = (bf16[128,256]{0,1:T(8,128)(2,1)S(1)}, bf16[128,256]{0,1:T(8,128)(2,1)}, u32[]{:S(2)}) copy-start(bf16[128,256]{0,1:T(8,128)(2,1)} %copy.12) | copy-start | bytes 196612
  37.5 9.2 %copy-start.6 = (bf16[128,128]{1,0:T(8,128)(2,1)S(1)}, bf16[128,128]{1,0:T(8,128)(2,1)}, u32[]{:S(2)}) copy-start(bf16[128,128]{1,0:T(8,128)(2,1)} %copy-done.5) | copy-start | bytes 98308

commit v9 on v5

--- a/solution.py
+++ b/solution.py
@@ -22,6 +22,10 @@
 VMEM = pl.BlockSpec(memory_space=pltpu.VMEM)
 SMEM = pl.BlockSpec(memory_space=pltpu.SMEM)
 ANY = pl.BlockSpec(memory_space=pl.ANY)
+
+
+def pitch(rows):
+    return (rows // 8 | 1) * 8
 
 
 def shifted(array, axis, by):
@@ -75,10 +79,11 @@
             out_ref[at + row] = jnp.where(position < limit, part, 0.0).astype(jnp.bfloat16)
 
 
-def left_kernel(blocks, tokens_ref, *refs):
+def left_kernel(blocks, later, tokens_ref, *refs):
     pair_refs, refs = refs[:blocks], refs[blocks:]
     gain_ref, bias_ref, weights_ref, gate_weights_ref, *passed, scratch = refs
-    passed, (left_ref, gate_ref), handed = passed[:4], passed[4:6], passed[6:]
+    passed, (left_ref, gate_ref, later_ref), handed = passed[:4], passed[4:7], passed[7:]
+    later_ref[...] = pair_refs[0][pl.ds(later, later_ref.shape[0])]
     for source, target in zip(passed, handed):
         target[...] = source[...]
     rows, columns, channels = pair_refs[0].shape
@@ -111,12 +116,12 @@
             valid = jnp.where(row_start + first + row < tokens, keep, 0.0)
             left = jnp.where(valid > 0.0, left, 0.0)
             for at in range(0, width, LANES):
-                scratch[at // LANES, pl.ds(first + row, hidden, stride=rows), :] = left[
+                scratch[at // LANES, pl.ds(first + row, hidden, stride=pitch(rows)), :] = left[
                     :, at : at + LANES
                 ]
     for channel in range(hidden):
         for at in range(0, width, LANES):
-            one = scratch[at // LANES, pl.ds(channel * rows, rows), :]
+            one = scratch[at // LANES, pl.ds(channel * pitch(rows), rows), :]
             left_ref[channel, :, at : at + LANES] = one.astype(jnp.bfloat16)
 
 
@@ -142,6 +147,7 @@
     right, product, updates, result, sent = refs[-5:]
     hidden, rows, width = left_ref.shape
     count = right_refs[0].shape[0]
+    apart = pitch(count)
     even = (lax.axis_index("row") + lax.axis_index("col")) % 2 == 0
 
     for token in range(count):
@@ -153,40 +159,41 @@
             pieces.append(piece)
         one = turned(pieces, width)
         for at in range(0, width, LANES):
-            right[at // LANES, pl.ds(token, hidden, stride=count), :] = one[:, at : at + LANES]
+            right[at // LANES, pl.ds(token, hidden, stride=apart), :] = one[:, at : at + LANES]
 
     total = jnp.zeros((count, rows), jnp.float32)
     for channel in range(hidden):
         one = 0.0
         for at in range(0, width, LANES):
             one += lax.dot_general(
-                right[at // LANES, pl.ds(channel * count, count), :].astype(jnp.bfloat16),
+                right[at // LANES, pl.ds(channel * apart, count), :].astype(jnp.bfloat16),
                 left_ref[channel, :, at : at + LANES],
                 (((1,), (1,)), ((), ())),
                 preferred_element_type=jnp.float32,
             )
-        product[pl.ds(channel * count, count), :rows] = one
+        product[pl.ds(channel * apart, count), :rows] = one
         total += one
     average = total / hidden
     total = jnp.zeros((count, rows), jnp.float32)
     for channel in range(hidden):
-        centered = product[pl.ds(channel * count, count), :rows] - average
+        centered = product[pl.ds(channel * apart, count), :rows] - average
         total += centered * centered
     scale = lax.rsqrt(total / hidden + 1e-05)
     for channel in range(hidden):
-        place = pl.ds(channel * count, count)
+        place = pl.ds(channel * apart, count)
         centered = product[place, :rows] - average
         product[place, :rows] = centered * scale * gain_ref[channel] + bias_ref[channel]
     for token in range(count):
-        mixed = product[pl.ds(token, hidden, stride=count), :][:, :rows].astype(jnp.bfloat16)
-        updates[pl.ds(token, rows, stride=count), :] = lax.dot_general(
+        mixed = product[pl.ds(token, hidden, stride=apart), :][:, :rows].astype(jnp.bfloat16)
+        updates[pl.ds(token, rows, stride=apart), :] = lax.dot_general(
             mixed, weights_ref[...], (((0,), (0,)), ((), ())), preferred_element_type=jnp.float32
         )
     step = 8
     for at in range(0, rows, step):
         gate = gate_ref[pl.ds(at, step), pl.ds(first, count)]
-        update = updates[pl.ds(at * count, step * count), :].reshape(gate.shape)
-        result[pl.ds(at, step)] = (gate * update).astype(jnp.bfloat16)
+        for row in range(step):
+            update = updates[pl.ds((at + row) * apart, count), :]
+            result[at + row] = (gate[row] * update).astype(jnp.bfloat16)
     copy = pltpu.make_async_copy(result, out_ref.at[:, pl.ds(first, count)], sent)
     copy.start()
     copy.wait()
@@ -207,34 +214,25 @@
     return bands, [(offset, offset) for offset in range(window)]
 
 
-def band_by_hops(pair_state, right_of, spans):
-    def at(r, c):
-        return r % 4 * 4 + c % 4
-
-    def move(array, pairs):
-        return lax.ppermute(array, ("row", "col"), pairs)
-
-    everyone = [(r, c) for r in range(4) for c in range(4)]
-    roots = [(r, c) for r, c in everyone if (c - r) % 4 < 2]
-    fars = [
-        move(pair_state[first : first + count], [(at(r, c), at(r ^ 2, c)) for r, c in roots])
-        for first, count in spans
-    ]
-    bands = []
-    for (first, count), far in zip(spans, fars):
-        held = right_of(first, count, far)
-        near = move(
-            held,
-            [
-                (at(r, c), at(r ^ 1, c) if (r + c) % 2 == 0 else at(r, c - 1))
-                for r, c in everyone
-            ],
-        )
-        cross = move(
-            held, [(at(r, c), at(r ^ 1, c - 1)) for r, c in everyone if (r + c) % 2 == 1]
-        )
-        bands.append([held, near, cross])
-    return bands, [(0, 1), (1, 2)]
+def hops():
+    out, near, cross = [], [], []
+    for r in range(4):
+        for c in range(4):
+            before = (c - 1) % 4
+            if (c - r) % 4 < 2:
+                out.append(((r, c), (r ^ 2, c)))
+            if (r + c) % 2 == 0:
+                near.append(((r, c), (r ^ 1, c)))
+            else:
+                near.append(((r, c), (r, before)))
+                cross.append(((r, c), (r ^ 1, before)))
+    return out, near, cross
+
+
+def move(array, pairs):
+    return lax.ppermute(
+        array, ("row", "col"), [(r * 4 + c, to_r * 4 + to_c) for (r, c), (to_r, to_c) in pairs]
+    )
 
 
 def on_device(
@@ -258,24 +256,30 @@
     width = -(-depth // LANES) * LANES
     in_gain, in_bias = in_gain.reshape(1, channels), in_bias.reshape(1, channels)
     block = 2 * tokens * max(channels, hidden)
-    hops = row_count == 4 and col_count == 4
+    by_hops = row_count == 4 and col_count == 4
     last = 16
     spans = [(0, columns - last), (columns - last, last)]
 
+    arrived = []
+    if by_hops:
+        out, near, cross = hops()
+        arrived.append(move(pair_state[: spans[0][1]], out))
     pairs = [pair_state]
     for _ in range(window - 1):
         pairs.append(shifted(pairs[-1], "col", -1))
     passed = [in_gain, in_bias, in_weights[:, 2 * hidden :], out_weights]
-    left, gate, *handed = pl.pallas_call(
-        functools.partial(left_kernel, window),
+    later = spans[1][0]
+    left, gate, later_pair, *handed = pl.pallas_call(
+        functools.partial(left_kernel, window, later),
         out_shape=[
             jax.ShapeDtypeStruct((hidden, rows, width), jnp.bfloat16),
             jax.ShapeDtypeStruct((rows, columns, channels), jnp.float32),
+            jax.ShapeDtypeStruct((rows - later, columns, channels), jnp.bfloat16),
         ]
         + [jax.ShapeDtypeStruct(array.shape, array.dtype) for array in passed],
         in_specs=[SMEM] + [VMEM] * (window + 8),
-        out_specs=[VMEM] * 6,
-        scratch_shapes=[pltpu.VMEM((width // LANES, hidden * rows, LANES), jnp.float32)],
+        out_specs=[VMEM] * 7,
+        scratch_shapes=[pltpu.VMEM((width // LANES, hidden * pitch(rows), LANES), jnp.float32)],
         compiler_params=params((window + 2) * block, 6 * hidden * rows * width),
         cost_estimate=cost(
             4 * window * tokens * channels * hidden, 6 * rows * width * hidden
@@ -286,7 +290,7 @@
 
     def right_of(first, count, *far):
         return pl.pallas_call(
-            functools.partial(right_kernel, hops, first),
+            functools.partial(right_kernel, by_hops, first),
             out_shape=jax.ShapeDtypeStruct((count, columns, hidden), jnp.bfloat16),
             in_specs=[SMEM] + [VMEM] * (4 + len(far)),
             out_specs=VMEM,
@@ -295,8 +299,13 @@
             name="right",
         )(token_count, pair_state, in_gain, in_bias, right_weights, *far)
 
-    if hops:
-        bands, picks = band_by_hops(pair_state, right_of, spans)
+    if by_hops:
+        arrived.append(move(later_pair, out))
+        bands = []
+        for (first, count), far in zip(spans, arrived):
+            held = right_of(first, count, far)
+            bands.append([held, move(held, near), move(held, cross)])
+        picks = [(0, 1), (1, 2)]
     else:
         bands, picks = band_by_sums(
             right_of(0, rows), spans, window, row_count, col_count, columns
@@ -310,9 +319,9 @@
             in_specs=[VMEM] * (len(band) + 2) + [SMEM, SMEM, VMEM] + [ANY] * len(update),
             out_specs=ANY,
             scratch_shapes=[
-                pltpu.VMEM((width // LANES, hidden * count, LANES), jnp.float32),
-                pltpu.VMEM((hidden * count, LANES), jnp.float32),
-                pltpu.VMEM((rows * count, channels), jnp.float32),
+                pltpu.VMEM((width // LANES, hidden * pitch(count), LANES), jnp.float32),
+                pltpu.VMEM((hidden * pitch(count), LANES), jnp.float32),
+                pltpu.VMEM((rows * pitch(count), channels), jnp.float32),
                 pltpu.VMEM((rows, count, channels), jnp.bfloat16),
                 pltpu.SemaphoreType.DMA,
             ],

time: 49 us -> 45.4 us (0.927)
  starting transfers between devices: 23.1 us -> 15.1 us
  waiting for transfers between devices: 6.91 us -> 11.7 us
  Pallas kernels: 14.8 us -> 11.4 us
  local copies, waits for them, and re-layouts: 3.09 us -> 5.92 us
    ppermute x6, starting transfers between devices: 23 us -> 15.1 us  [move(): lax.ppermute(array, ('row', 'col'), [(r * 4 + c, to_r * 4 + to_c) for (r,...]
    unnamed x15, local copies, waits for them, and re-layouts: 0.14 us -> 4.01 us
    ppermute x6, waiting for transfers between devices: 6.91 us -> 9.73 us  [move(): lax.ppermute(array, ('row', 'col'), [(r * 4 + c, to_r * 4 + to_c) for (r,...]
    pallas_call x2, Pallas kernels: 10.4 us -> 7.72 us  [on_device(): pl.pallas_call(functools.partial(product_kernel, picks, len(band), first)...]
    ppermute x1, waiting for transfers between devices: 0.01 us -> 1.98 us  [shifted(): lax.ppermute(array, axis, [(i, (i + by) % devices) for i in range(devices)])]
    slice x2 -> x1, local copies, waits for them, and re-layouts: 2.06 us -> 1.02 us  [on_device(): arrived.append(move(pair_state[:spans[0][1]], out))]
    pallas_call x3, Pallas kernels: 4.4 us -> 3.73 us  [the longest x1 2.53 us: on_device(): pl.pallas_call(functools.partial(left_kernel, window, later), out_shape=[...]
  transfers between devices with their start and end apart: 7 -> 7, of which waited for: 3 -> 4; matrix products, arithmetic and copies ran while one was open for 6% -> 4% of each run, Pallas kernels for 23% -> 18%
where the time goes in v9:
time: 45.4 us; the launch traced here: 45 us
  starting transfers between devices  15.1 us (33%)
  waiting for transfers between devices  11.7 us (26%)
  Pallas kernels  11.4 us (25%)
  local copies, waits for them, and re-layouts  5.92 us (13%)
  between operations  0.78 us (2%)
    ppermute x6, starting transfers between devices, move(): lax.ppermute(array, ('row', 'col'), [(r * 4 + c, to_r * 4 + to_c) for (r,...  15.1 us
    ppermute x6, waiting for transfers between devices, move(): lax.ppermute(array, ('row', 'col'), [(r * 4 + c, to_r * 4 + to_c) for (r,...  9.73 us
    pallas_call x2, Pallas kernels, on_device(): pl.pallas_call(functools.partial(product_kernel, picks, len(band), first)...  7.72 us
    unnamed x15, local copies, waits for them, and re-layouts  4.01 us
    pallas_call x1, Pallas kernels, on_device(): pl.pallas_call(functools.partial(left_kernel, window, later), out_shape=[...  2.53 us
    ppermute x1, waiting for transfers between devices, shifted(): lax.ppermute(array, axis, [(i, (i + by) % devices) for i in range(devices)])  1.98 us
    pallas_call x2, Pallas kernels, right_of(): pl.pallas_call(functools.partial(right_kernel, by_hops, first), out_shape...  1.2 us
    slice x1, local copies, waits for them, and re-layouts, on_device(): arrived.append(move(pair_state[:spans[0][1]], out))  1.02 us
  transfers between devices with their start and end apart: 7, of which 4 were waited for; matrix products, arithmetic and copies ran while one was open for 4% of the time, Pallas kernels for 18%

profile of v9, /device:TPU:1, one launch (start us, length us, event | category | flops | bytes accessed | tf_op | source)
XLA Modules:
  0.0 45.0 jit_solution(17619097241123732511)
XLA Ops:
  0.0 0.1 collective-permute-start
  0.1 1.0 %slice.11 = bf16[32,48,128]{2,1,0:T(8,128)(2,1)S(1)} slice(bf16[48,48,128]{2,1,0:T(8,128)(2,1)} %pair_ref.3), slice={[0:32], [0:48], [0:128]} | slice | bytes 786432 | tf_op jit(solution)/shard_map/slice | solution.py:266
  1.1 5.7 %collective-permute-start.4 = (bf16[32,48,128]{2,1,0:T(8,128)(2,1)S(1)}, bf16[32,48,128]{2,1,0:T(8,128)(2,1)S(1)}, u32[]{:S(2)}, u32[]{:S(2)}) collective-permute-start(bf16[32,48,128]{2,1,0:T(8,128)(2,1)S(1)} %slice.11), channel_id=1, source_target_pairs={{0,8},{1,9},{5,13},{6,14},{10,2},{11,3},{12,4},{15,7},{16,24},{17,... | collective-permute-start | bytes 1179656 | tf_op jit(solution)/shard_map/ppermute | solution.py:233
  7.4 0.9 %fusion = (bf16[128,256]{1,0:T(8,128)(2,1)S(1)}, bf16[128,256]{1,0:T(8,128)(2,1)S(1)}) fusion(bf16[128,512]{1,0:T(8,128)(2,1)} %param.13), kind=kLoop, calls=%fused_computation | loop fusion | bytes 262144 | tf_op jit(solution)/shard_map/slice | solution.py:270
  8.3 0.1 copy.12
  8.4 2.0 %collective-permute-done.refs_1_ = bf16[48,48,128]{2,1,0:T(8,128)(2,1)S(1)} collective-permute-done((bf16[48,48,128]{2,1,0:T(8,128)(2,1)}, bf16[48,48,128]{2,1,0:T(8,128)(2,1)S(1)}, u32[]{:S(2)}, u32[]{:S(2)}) %collective-permute-start) | collective-permute-done | bytes 589856 | tf_op jit(solution)/shard_map/ppermute | solution.py:33
  10.4 1.1 %copy-done = bf16[48,48,128]{2,1,0:T(8,128)(2,1)S(1)} copy-done((bf16[48,48,128]{2,1,0:T(8,128)(2,1)S(1)}, bf16[48,48,128]{2,1,0:T(8,128)(2,1)}, u32[]{:S(2)}) %copy-start) | copy-done | bytes 589848
  11.5 0.0 copy-start.1
  11.5 0.8 %copy-done.1 = bf16[128,128]{1,0:T(8,128)(2,1)S(1)} copy-done((bf16[128,128]{1,0:T(8,128)(2,1)S(1)}, bf16[128,128]{1,0:T(8,128)(2,1)}, u32[]{:S(2)}) %copy-start.1) | copy-done | bytes 32792
  12.2 0.8 %copy-done.2 = bf16[128,128]{1,0:T(8,128)(2,1)S(1)} copy-done((bf16[128,128]{1,0:T(8,128)(2,1)S(1)}, bf16[128,128]{1,0:T(8,128)(2,1)}, u32[]{:S(2)}) %copy-start.2) | copy-done | bytes 32792
  13.0 0.7 %copy-done.3 = f32[128]{0:T(128)S(1)} copy-done((f32[128]{0:T(128)S(1)}, f32[128]{0:T(128)}, u32[]{:S(2)}) %copy-start.3) | copy-done | bytes 536
  13.6 0.7 %copy-done.4 = f32[128]{0:T(128)S(1)} copy-done((f32[128]{0:T(128)S(1)}, f32[128]{0:T(128)}, u32[]{:S(2)}) %copy-start.4) | copy-done | bytes 536
  14.3 2.5 %left_and_gate.1 = (bf16[128,48,128]{2,1,0:T(8,128)(2,1)S(1)}, f32[48,48,128]{2,1,0:T(8,128)S(1)}, bf16[16,48,128]{2,1,0:T(8,128)(2,1)S(1)}, f32[1,128]{1,0:T(1,...) custom-call(s32[1]{0:T(128)S(6)} %copy.14.tokens_ref, ...), custom_call_target="tpu_custom_call" | custom-call | flops 301989888 | bytes 4718592 | tf_op jit(solution)/shard_map/left_and_gate/pallas_call | solution.py:272
  16.8 0.0 copy-start.5
  16.9 0.0 copy-start.6
  16.9 4.5 %collective-permute-start.1 = (bf16[16,48,128]{2,1,0:T(8,128)(2,1)S(1)}, bf16[16,48,128]{2,1,0:T(8,128)(2,1)S(1)}, u32[]{:S(2)}, u32[]{:S(2)}) collective-permute-start(bf16[16,48,128]{2,1,0:T(8,128)(2,1)S(1)} %get-tuple-element.15), channel_id=1, source_target_pairs={{0,8},{1,9},{5,13},{6,14},{10,2},{11,3},{12,4},{15,7},{16,24},{17,... | collective-permute-start | bytes 589832 | tf_op jit(solution)/shard_map/ppermute | solution.py:233
  21.4 0.0 collective-permute-done.4.refs_0_
  21.4 0.7 %right.3.refs_0_ = bf16[32,48,128]{2,1,0:T(8,128)(2,1)S(1)} custom-call(s32[1]{0:T(128)S(6)} %copy.14.tokens_ref, bf16[48,48,128]{2,1,0:T(8,128)(2,1)S(1)} %copy-done, f32[1,128]{1,0:T(1,128)S(1)} %get-tuple-element.12.gain_ref, f32[1,128]{1,0:T(1,128)S(1)} %get-tuple-element.13.bias_ref, bf16[128,256]{1,0:T(8,128)(2,1)S(1)} %get-tuple-element.14.weights_ref, ...), custom_call_target="tpu_custom_call" | custom-call | flops 100663296 | bytes 1179648 | tf_op jit(solution)/shard_map/right/pallas_call | solution.py:292
  22.1 0.1 collective-permute-start.5
  22.2 1.9 %collective-permute-start.6 = (bf16[32,48,128]{2,1,0:T(8,128)(2,1)S(1)}, bf16[32,48,128]{2,1,0:T(8,128)(2,1)S(1)}, u32[]{:S(2)}, u32[]{:S(2)}) collective-permute-start(bf16[32,48,128]{2,1,0:T(8,128)(2,1)S(1)} %right.3.refs_0_), channel_id=1, source_target_pairs={{1,4},{3,6},{4,3},{6,1},{9,12},{11,14},{12,11},{14,9},{17,20},{19,... | collective-permute-start | bytes 1179656 | tf_op jit(solution)/shard_map/ppermute | solution.py:233
  24.1 2.0 %collective-permute-done.1.refs_0_ = bf16[16,48,128]{2,1,0:T(8,128)(2,1)S(1)} collective-permute-done((bf16[16,48,128]{2,1,0:T(8,128)(2,1)S(1)}, bf16[16,48,128]{2,1,0:T(8,128)(2,1)S(1)}, u32[]{:S(2)}, u32[]{:S(2)}) %collective-permute-start.1) | collective-permute-done | bytes 196640 | tf_op jit(solution)/shard_map/ppermute | solution.py:233
  26.1 0.5 %right.2.refs_0_ = bf16[16,48,128]{2,1,0:T(8,128)(2,1)S(1)} custom-call(s32[1]{0:T(128)S(6)} %copy.14.tokens_ref, bf16[48,48,128]{2,1,0:T(8,128)(2,1)S(1)} %copy-done, f32[1,128]{1,0:T(1,128)S(1)} %get-tuple-element.12.gain_ref, f32[1,128]{1,0:T(1,128)S(1)} %get-tuple-element.13.bias_ref, bf16[128,256]{1,0:T(8,128)(2,1)S(1)} %get-tuple-element.14.weights_ref, ...), custom_call_target="tpu_custom_call" | custom-call | flops 50331648 | bytes 589824 | tf_op jit(solution)/shard_map/right/pallas_call | solution.py:292
  26.6 0.3 collective-permute-start.2
  26.9 2.5 %collective-permute-start.3 = (bf16[16,48,128]{2,1,0:T(8,128)(2,1)S(1)}, bf16[16,48,128]{2,1,0:T(8,128)(2,1)S(1)}, u32[]{:S(2)}, u32[]{:S(2)}) collective-permute-start(bf16[16,48,128]{2,1,0:T(8,128)(2,1)S(1)} %right.2.refs_0_), channel_id=1, source_target_pairs={{1,4},{3,6},{4,3},{6,1},{9,12},{11,14},{12,11},{14,9},{17,20},{19,... | collective-permute-start | bytes 589832 | tf_op jit(solution)/shard_map/ppermute | solution.py:233
  29.5 0.4 collective-permute-done.5.refs_1_
  29.9 7.3 %collective-permute-done.6.refs_2_ = bf16[32,48,128]{2,1,0:T(8,128)(2,1)S(1)} collective-permute-done((bf16[32,48,128]{2,1,0:T(8,128)(2,1)S(1)}, bf16[32,48,128]{2,1,0:T(8,128)(2,1)S(1)}, u32[]{:S(2)}, u32[]{:S(2)}) %collective-permute-start.6) | collective-permute-done | bytes 393248 | tf_op jit(solution)/shard_map/ppermute | solution.py:233
  37.2 0.0 copy-done.5
  37.2 0.0 copy-done.6
  37.2 4.4 %product.2.refs_8_ = bf16[48,48,128]{2,1,0:T(8,128)(2,1)} custom-call(bf16[32,48,128]{2,1,0:T(8,128)(2,1)S(1)} %right.3.refs_0_, bf16[32,48,128]{2,1,0:T(8,128)(2,1)S(1)} %collective-permute-done.5.refs_1_, bf16[32,48,128]{2,1,0:T(8,128)(2,1)S(1)} %collective-permute-done.6.refs_2_, bf16[128,48,128]{2,1,0:T(8,128)(2,1)S(1)} %get-tuple-element.16.refs_3_, ...), custom_call_target="tpu_custom_call" | custom-call | flops 37748736 | bytes 2359296 | tf_op jit(solution)/shard_map/product/pallas_call | solution.py:316
  41.6 0.0 collective-permute-done.2.refs_1_
  41.6 0.0 collective-permute-done.3.refs_2_
  41.6 3.3 %product.3 = bf16[48,48,128]{2,1,0:T(8,128)(2,1)} custom-call(bf16[16,48,128]{2,1,0:T(8,128)(2,1)S(1)} %right.2.refs_0_, bf16[16,48,128]{2,1,0:T(8,128)(2,1)S(1)} %collective-permute-done.2.refs_1_, bf16[16,48,128]{2,1,0:T(8,128)(2,1)S(1)} %collective-permute-done.3.refs_2_, ...), custom_call_target="tpu_custom_call", output_to_operand_aliasing={{}: (8, {})} | custom-call | flops 18874368 | bytes 2359296 | tf_op jit(solution)/shard_map/product/pallas_call | solution.py:316
  (4 shorter events, 0.0 us)
Async XLA Ops:
  0.0 10.4 %collective-permute-start = (bf16[48,48,128]{2,1,0:T(8,128)(2,1)}, bf16[48,48,128]{2,1,0:T(8,128)(2,1)S(1)}, u32[]{:S(2)}, u32[]{:S(2)}) collective-permute-start(bf16[48,48,128]{2,1,0:T(8,128)(2,1)} %pair_ref.3), channel_id=1, source_target_pairs={{0,3},{1,0},{2,1},{3,2},{4,7},{5,4},{6,5},{7,6},{8,11},{9,8},{10,9... | collective-permute-start | bytes 1769480 | tf_op jit(solution)/shard_map/ppermute | solution.py:33
  1.1 20.3 %collective-permute-start.4 = (bf16[32,48,128]{2,1,0:T(8,128)(2,1)S(1)}, bf16[32,48,128]{2,1,0:T(8,128)(2,1)S(1)}, u32[]{:S(2)}, u32[]{:S(2)}) collective-permute-start(bf16[32,48,128]{2,1,0:T(8,128)(2,1)S(1)} %slice.11), channel_id=1, source_target_pairs={{0,8},{1,9},{5,13},{6,14},{10,2},{11,3},{12,4},{15,7},{16,24},{17,... | collective-permute-start | bytes 1179656 | tf_op jit(solution)/shard_map/ppermute | solution.py:233
  10.4 1.1 %copy-start = (bf16[48,48,128]{2,1,0:T(8,128)(2,1)S(1)}, bf16[48,48,128]{2,1,0:T(8,128)(2,1)}, u32[]{:S(2)}) copy-start(bf16[48,48,128]{2,1,0:T(8,128)(2,1)} %pair_ref.3) | copy-start | bytes 1769476
  11.5 0.8 %copy-start.1 = (bf16[128,128]{1,0:T(8,128)(2,1)S(1)}, bf16[128,128]{1,0:T(8,128)(2,1)}, u32[]{:S(2)}) copy-start(bf16[128,128]{1,0:T(8,128)(2,1)} %refs_5_.3) | copy-start | bytes 98308
  12.2 0.8 %copy-start.2 = (bf16[128,128]{1,0:T(8,128)(2,1)S(1)}, bf16[128,128]{1,0:T(8,128)(2,1)}, u32[]{:S(2)}) copy-start(bf16[128,128]{1,0:T(8,128)(2,1)} %refs_9_.1) | copy-start | bytes 98308
  13.0 0.7 %copy-start.3 = (f32[128]{0:T(128)S(1)}, f32[128]{0:T(128)}, u32[]{:S(2)}) copy-start(f32[128]{0:T(128)} %param.11) | copy-start | bytes 1540
  13.6 0.7 %copy-start.4 = (f32[128]{0:T(128)S(1)}, f32[128]{0:T(128)}, u32[]{:S(2)}) copy-start(f32[128]{0:T(128)} %param.12) | copy-start | bytes 1540
  16.8 20.4 %copy-start.5 = (f32[128]{0:T(128)S(1)}, f32[128]{0:T(128)}, u32[]{:S(2)}) copy-start(f32[128]{0:T(128)} %refs_5_.5) | copy-start | bytes 1540
  16.9 20.4 %copy-start.6 = (f32[128]{0:T(128)S(1)}, f32[128]{0:T(128)}, u32[]{:S(2)}) copy-start(f32[128]{0:T(128)} %refs_6_.3) | copy-start | bytes 1540
  16.9 9.3 %collective-permute-start.1 = (bf16[16,48,128]{2,1,0:T(8,128)(2,1)S(1)}, bf16[16,48,128]{2,1,0:T(8,128)(2,1)S(1)}, u32[]{:S(2)}, u32[]{:S(2)}) collective-permute-start(bf16[16,48,128]{2,1,0:T(8,128)(2,1)S(1)} %get-tuple-element.15), channel_id=1, source_target_pairs={{0,8},{1,9},{5,13},{6,14},{10,2},{11,3},{12,4},{15,7},{16,24},{17,... | collective-permute-start | bytes 589832 | tf_op jit(solution)/shard_map/ppermute | solution.py:233
  22.1 7.8 %collective-permute-start.5 = (bf16[32,48,128]{2,1,0:T(8,128)(2,1)S(1)}, bf16[32,48,128]{2,1,0:T(8,128)(2,1)S(1)}, u32[]{:S(2)}, u32[]{:S(2)}) collective-permute-start(bf16[32,48,128]{2,1,0:T(8,128)(2,1)S(1)} %right.3.refs_0_), channel_id=1, source_target_pairs={{0,4},{1,0},{2,6},{3,2},{4,7},{5,1},{6,5},{7,3},{8,12},{9,8},{10,1... | collective-permute-start | bytes 1179656 | tf_op jit(solution)/shard_map/ppermute | solution.py:233
  22.2 15.0 %collective-permute-start.6 = (bf16[32,48,128]{2,1,0:T(8,128)(2,1)S(1)}, bf16[32,48,128]{2,1,0:T(8,128)(2,1)S(1)}, u32[]{:S(2)}, u32[]{:S(2)}) collective-permute-start(bf16[32,48,128]{2,1,0:T(8,128)(2,1)S(1)} %right.3.refs_0_), channel_id=1, source_target_pairs={{1,4},{3,6},{4,3},{6,1},{9,12},{11,14},{12,11},{14,9},{17,20},{19,... | collective-permute-start | bytes 1179656 | tf_op jit(solution)/shard_map/ppermute | solution.py:233
  26.6 15.0 %collective-permute-start.2 = (bf16[16,48,128]{2,1,0:T(8,128)(2,1)S(1)}, bf16[16,48,128]{2,1,0:T(8,128)(2,1)S(1)}, u32[]{:S(2)}, u32[]{:S(2)}) collective-permute-start(bf16[16,48,128]{2,1,0:T(8,128)(2,1)S(1)} %right.2.refs_0_), channel_id=1, source_target_pairs={{0,4},{1,0},{2,6},{3,2},{4,7},{5,1},{6,5},{7,3},{8,12},{9,8},{10,1... | collective-permute-start | bytes 589832 | tf_op jit(solution)/shard_map/ppermute | solution.py:233
  26.9 14.7 %collective-permute-start.3 = (bf16[16,48,128]{2,1,0:T(8,128)(2,1)S(1)}, bf16[16,48,128]{2,1,0:T(8,128)(2,1)S(1)}, u32[]{:S(2)}, u32[]{:S(2)}) collective-permute-start(bf16[16,48,128]{2,1,0:T(8,128)(2,1)S(1)} %right.2.refs_0_), channel_id=1, source_target_pairs={{1,4},{3,6},{4,3},{6,1},{9,12},{11,14},{12,11},{14,9},{17,20},{19,... | collective-permute-start | bytes 589832 | tf_op jit(solution)/shard_map/ppermute | solution.py:233

commit v10 on v9

--- a/solution.py
+++ b/solution.py
@@ -67,7 +67,7 @@
     for at in range(0, count, step):
         block = pair_ref[pl.ds(first + at, step)]
         if hops:
-            block = jnp.where(is_root, block, refs[0][pl.ds(at, step)])
+            block = jnp.where(is_root, block, refs[0][pl.ds(first + at, step)])
         normed = normed_rows(block, gain_ref, bias_ref)
         both = jnp.dot(
             normed, weights_ref[...], preferred_element_type=jnp.float32
@@ -79,13 +79,20 @@
             out_ref[at + row] = jnp.where(position < limit, part, 0.0).astype(jnp.bfloat16)
 
 
-def left_kernel(blocks, later, tokens_ref, *refs):
-    pair_refs, refs = refs[:blocks], refs[blocks:]
-    gain_ref, bias_ref, weights_ref, gate_weights_ref, *passed, scratch = refs
-    passed, (left_ref, gate_ref, later_ref), handed = passed[:4], passed[4:7], passed[7:]
-    later_ref[...] = pair_refs[0][pl.ds(later, later_ref.shape[0])]
+def gate_kernel(passes, pair_ref, weights_ref, *refs):
+    passed, gate_ref, handed = refs[:passes], refs[passes], refs[passes + 1 :]
     for source, target in zip(passed, handed):
         target[...] = source[...]
+    rows, columns, channels = pair_ref.shape
+    step = 4
+    for first in range(0, rows, step):
+        normed = normed_rows(pair_ref[pl.ds(first, step)], passed[0], passed[1])
+        gate = jnp.dot(normed, weights_ref[...], preferred_element_type=jnp.float32)
+        gate_ref[pl.ds(first, step)] = jax.nn.sigmoid(gate).reshape(step, columns, channels)
+
+
+def left_kernel(blocks, tokens_ref, *refs):
+    pair_refs, (gain_ref, bias_ref, weights_ref, left_ref, scratch) = refs[:blocks], refs[blocks:]
     rows, columns, channels = pair_refs[0].shape
     hidden, _, width = left_ref.shape
     tokens = tokens_ref[0]
@@ -102,8 +109,6 @@
     step = 4
     for first in range(0, rows, step):
         normed = [normed_rows(ref[pl.ds(first, step)], gain_ref, bias_ref) for ref in pair_refs]
-        gate = jnp.dot(normed[0], gate_weights_ref[...], preferred_element_type=jnp.float32)
-        gate_ref[pl.ds(first, step)] = jax.nn.sigmoid(gate).reshape(step, columns, channels)
         for row in range(step):
             thirds = [piece[row * columns : (row + 1) * columns] for piece in normed]
             both = lax.dot_general(
@@ -141,14 +146,22 @@
     )
 
 
-def product_kernel(picks, rights, first, *refs):
+def product_kernel(picks, rights, first, last, *refs):
     right_refs, refs = refs[:rights], refs[rights:]
-    left_ref, gate_ref, gain_ref, bias_ref, weights_ref, *_, out_ref = refs[:-5]
-    right, product, updates, result, sent = refs[-5:]
+    left_ref, gate_ref, gain_ref, bias_ref, weights_ref, *done, out_ref = refs[: -5 if last else -3]
+    right, product, updates = refs[-5:-2] if last else refs[-3:]
+    result, sent = refs[-2:] if last else (out_ref, None)
     hidden, rows, width = left_ref.shape
     count = right_refs[0].shape[0]
     apart = pitch(count)
     even = (lax.axis_index("row") + lax.axis_index("col")) % 2 == 0
+
+    copies, start = [], 0
+    for at, ref in enumerate(done):
+        columns = pl.ds(start, ref.shape[1])
+        copies.append(pltpu.make_async_copy(ref, out_ref.at[:, columns], sent.at[at]))
+        copies[-1].start()
+        start += ref.shape[1]
 
     for token in range(count):
         pieces = []
@@ -161,7 +174,8 @@
         for at in range(0, width, LANES):
             right[at // LANES, pl.ds(token, hidden, stride=apart), :] = one[:, at : at + LANES]
 
-    total = jnp.zeros((count, rows), jnp.float32)
+    ways = 4
+    totals = [jnp.zeros((count, rows), jnp.float32)] * ways
     for channel in range(hidden):
         one = 0.0
         for at in range(0, width, LANES):
@@ -172,13 +186,13 @@
                 preferred_element_type=jnp.float32,
             )
         product[pl.ds(channel * apart, count), :rows] = one
-        total += one
-    average = total / hidden
-    total = jnp.zeros((count, rows), jnp.float32)
+        totals[channel % ways] += one
+    average = sum(totals) / hidden
+    totals = [jnp.zeros((count, rows), jnp.float32)] * ways
     for channel in range(hidden):
         centered = product[pl.ds(channel * apart, count), :rows] - average
-        total += centered * centered
-    scale = lax.rsqrt(total / hidden + 1e-05)
+        totals[channel % ways] += centered * centered
+    scale = lax.rsqrt(sum(totals) / hidden + 1e-05)
     for channel in range(hidden):
         place = pl.ds(channel * apart, count)
         centered = product[place, :rows] - average
@@ -188,15 +202,19 @@
         updates[pl.ds(token, rows, stride=apart), :] = lax.dot_general(
             mixed, weights_ref[...], (((0,), (0,)), ((), ())), preferred_element_type=jnp.float32
         )
-    step = 8
+    step = 16
     for at in range(0, rows, step):
         gate = gate_ref[pl.ds(at, step), pl.ds(first, count)]
         for row in range(step):
             update = updates[pl.ds((at + row) * apart, count), :]
             result[at + row] = (gate[row] * update).astype(jnp.bfloat16)
-    copy = pltpu.make_async_copy(result, out_ref.at[:, pl.ds(first, count)], sent)
-    copy.start()
-    copy.wait()
+        if last:
+            target = out_ref.at[pl.ds(at, step), pl.ds(first, count)]
+            place = sent.at[len(done) + at // step]
+            copies.append(pltpu.make_async_copy(result.at[pl.ds(at, step)], target, place))
+            copies[-1].start()
+    for copy in copies:
+        copy.wait()
 
 
 def band_by_sums(right, spans, window, row_count, col_count, columns):
@@ -257,36 +275,25 @@
     in_gain, in_bias = in_gain.reshape(1, channels), in_bias.reshape(1, channels)
     block = 2 * tokens * max(channels, hidden)
     by_hops = row_count == 4 and col_count == 4
-    last = 16
-    spans = [(0, columns - last), (columns - last, last)]
-
-    arrived = []
+    few = 16
+    spans = [(0, few), (few, columns - few)]
+
     if by_hops:
         out, near, cross = hops()
-        arrived.append(move(pair_state[: spans[0][1]], out))
-    pairs = [pair_state]
-    for _ in range(window - 1):
-        pairs.append(shifted(pairs[-1], "col", -1))
-    passed = [in_gain, in_bias, in_weights[:, 2 * hidden :], out_weights]
-    later = spans[1][0]
-    left, gate, later_pair, *handed = pl.pallas_call(
-        functools.partial(left_kernel, window, later),
-        out_shape=[
-            jax.ShapeDtypeStruct((hidden, rows, width), jnp.bfloat16),
-            jax.ShapeDtypeStruct((rows, columns, channels), jnp.float32),
-            jax.ShapeDtypeStruct((rows - later, columns, channels), jnp.bfloat16),
-        ]
+        arrived = move(pair_state, out)
+    left_weights, right_weights = in_weights[:, : 2 * hidden].T, in_weights[:, 2 * hidden :]
+    passed = [in_gain, in_bias, left_weights, right_weights, out_weights, pair_state]
+    gate, *handed = pl.pallas_call(
+        functools.partial(gate_kernel, len(passed)),
+        out_shape=[jax.ShapeDtypeStruct((rows, columns, channels), jnp.float32)]
         + [jax.ShapeDtypeStruct(array.shape, array.dtype) for array in passed],
-        in_specs=[SMEM] + [VMEM] * (window + 8),
-        out_specs=[VMEM] * 7,
-        scratch_shapes=[pltpu.VMEM((width // LANES, hidden * pitch(rows), LANES), jnp.float32)],
-        compiler_params=params((window + 2) * block, 6 * hidden * rows * width),
-        cost_estimate=cost(
-            4 * window * tokens * channels * hidden, 6 * rows * width * hidden
-        ),
-        name="left_and_gate",
-    )(token_count, *pairs, in_gain, in_bias, in_weights[:, : 2 * hidden].T, gate_weights, *passed)
-    in_gain, in_bias, right_weights, out_weights = handed
+        in_specs=[VMEM] * (2 + len(passed)),
+        out_specs=[VMEM] * (1 + len(passed)),
+        compiler_params=params(5 * block),
+        cost_estimate=cost(2 * tokens * channels * channels, 6 * tokens * channels),
+        name="gate",
+    )(pair_state, gate_weights, *passed)
+    in_gain, in_bias, left_weights, right_weights, out_weights, own = handed
 
     def right_of(first, count, *far):
         return pl.pallas_call(
@@ -297,42 +304,60 @@
             compiler_params=params(2 * block),
             cost_estimate=cost(4 * count * columns * channels * hidden, 6 * count * columns * channels),
             name="right",
-        )(token_count, pair_state, in_gain, in_bias, right_weights, *far)
-
+        )(token_count, own, in_gain, in_bias, right_weights, *far)
+
+    pairs = [pair_state]
+    for _ in range(window - 1):
+        pairs.append(shifted(pairs[-1], "col", -1))
+    pairs[0] = own
     if by_hops:
-        arrived.append(move(later_pair, out))
-        bands = []
-        for (first, count), far in zip(spans, arrived):
-            held = right_of(first, count, far)
-            bands.append([held, move(held, near), move(held, cross)])
+        out, near, cross = hops()
+        arrived = move(pair_state, out)
+        held = [right_of(first, count, arrived) for first, count in spans]
+        *held, pairs[-1] = lax.optimization_barrier((*held, pairs[-1]))
+        bands = [[piece, move(piece, near), move(piece, cross)] for piece in held]
         picks = [(0, 1), (1, 2)]
     else:
         bands, picks = band_by_sums(
             right_of(0, rows), spans, window, row_count, col_count, columns
         )
-
-    update = []
+    left = pl.pallas_call(
+        functools.partial(left_kernel, window),
+        out_shape=jax.ShapeDtypeStruct((hidden, rows, width), jnp.bfloat16),
+        in_specs=[SMEM] + [VMEM] * (window + 3),
+        out_specs=VMEM,
+        scratch_shapes=[pltpu.VMEM((width // LANES, hidden * pitch(rows), LANES), jnp.float32)],
+        compiler_params=params((window + 2) * block, 6 * hidden * rows * width),
+        cost_estimate=cost(4 * window * tokens * channels * hidden, 6 * rows * width * hidden),
+        name="left",
+    )(token_count, *pairs, in_gain, in_bias, left_weights)
+
+    done = []
     for (first, count), band in zip(spans, bands):
+        last = first + count == columns
+        scratch = [
+            pltpu.VMEM((width // LANES, hidden * pitch(count), LANES), jnp.float32),
+            pltpu.VMEM((hidden * pitch(count), LANES), jnp.float32),
+            pltpu.VMEM((rows * pitch(count), channels), jnp.float32),
+        ]
+        if last:
+            scratch += [
+                pltpu.VMEM((rows, count, channels), jnp.bfloat16),
+                pltpu.SemaphoreType.DMA((len(done) + rows // 16,)),
+            ]
         filled = pl.pallas_call(
-            functools.partial(product_kernel, picks, len(band), first),
-            out_shape=jax.ShapeDtypeStruct((rows, columns, channels), jnp.bfloat16),
-            in_specs=[VMEM] * (len(band) + 2) + [SMEM, SMEM, VMEM] + [ANY] * len(update),
-            out_specs=ANY,
-            scratch_shapes=[
-                pltpu.VMEM((width // LANES, hidden * pitch(count), LANES), jnp.float32),
-                pltpu.VMEM((hidden * pitch(count), LANES), jnp.float32),
-                pltpu.VMEM((rows * pitch(count), channels), jnp.float32),
-                pltpu.VMEM((rows, count, channels), jnp.bfloat16),
-                pltpu.SemaphoreType.DMA,
-            ],
-            input_output_aliases={len(band) + 5: 0} if update else {},
+            functools.partial(product_kernel, picks, len(band), first, last),
+            out_shape=jax.ShapeDtypeStruct(
+                (rows, columns if last else count, channels), jnp.bfloat16
+            ),
+            in_specs=[VMEM] * (len(band) + 2) + [SMEM, SMEM, VMEM] + [VMEM] * len(done) * last,
+            out_specs=ANY if last else VMEM,
+            scratch_shapes=scratch,
             compiler_params=params(2 * block, 2 * hidden * (rows + 2 * count) * width),
-            cost_estimate=cost(
-                2 * rows * count * depth * hidden, 4 * rows * depth * hidden
-            ),
+            cost_estimate=cost(2 * rows * count * depth * hidden, 4 * rows * depth * hidden),
             name="product",
-        )(*band, left, gate, out_gain, out_bias, out_weights, *update)
-        update = [filled]
+        )(*band, left, gate, out_gain, out_bias, out_weights, *(done if last else []))
+        done.append(filled)
     return filled
 
 

time: 45.4 us -> 49.2 us (1.084)
  starting transfers between devices: 15.1 us -> 21.2 us
  waiting for transfers between devices: 11.7 us -> 9.49 us
  local copies, waits for them, and re-layouts: 5.92 us -> 4.89 us
  Pallas kernels: 11.4 us -> 12.4 us
    ppermute x6 -> x5, starting transfers between devices: 15.1 us -> 20.2 us  [move(): lax.ppermute(array, ('row', 'col'), [(r * 4 + c, to_r * 4 + to_c) for (r,...]
    ppermute x1, waiting for transfers between devices: 1.98 us -> 0.01 us  [shifted(): lax.ppermute(array, axis, [(i, (i + by) % devices) for i in range(devices)])]
    slice x2 -> x1, local copies, waits for them, and re-layouts: 1.91 us -> 0.88 us  [on_device(): in_weights[:, 2 * hidden:]]
    pallas_call x3 -> x4, Pallas kernels: 10.2 us -> 11.2 us  [the longest x2 7.09 us: on_device(): pl.pallas_call(functools.partial(product_kernel, picks, len(band), first,...]
    ppermute x1, starting transfers between devices: 0.06 us -> 1.01 us  [shifted(): lax.ppermute(array, axis, [(i, (i + by) % devices) for i in range(devices)])]
    ppermute x6 -> x5, waiting for transfers between devices: 9.73 us -> 9.49 us  [move(): lax.ppermute(array, ('row', 'col'), [(r * 4 + c, to_r * 4 + to_c) for (r,...]
  transfers between devices with their start and end apart: 7 -> 6, of which waited for: 4 -> 2; matrix products, arithmetic and copies ran while one was open for 4% -> 2% of each run, Pallas kernels for 18% -> 16%
where the time goes in v10:
time: 49.2 us; the launch traced here: 48.8 us
  starting transfers between devices  21.2 us (43%)
  Pallas kernels  12.4 us (25%)
  waiting for transfers between devices  9.49 us (19%)
  local copies, waits for them, and re-layouts  4.89 us (10%)
  between operations  0.8 us (2%)
    ppermute x5, starting transfers between devices, move(): lax.ppermute(array, ('row', 'col'), [(r * 4 + c, to_r * 4 + to_c) for (r,...  20.2 us
    ppermute x5, waiting for transfers between devices, move(): lax.ppermute(array, ('row', 'col'), [(r * 4 + c, to_r * 4 + to_c) for (r,...  9.49 us
    pallas_call x2, Pallas kernels, on_device(): pl.pallas_call(functools.partial(product_kernel, picks, len(band), first,...  7.09 us
    unnamed x15, local copies, waits for them, and re-layouts  4.01 us
    pallas_call x1, Pallas kernels, on_device(): pl.pallas_call(functools.partial(left_kernel, window), out_shape=jax.Shap...  3.02 us
    pallas_call x2, Pallas kernels, right_of(): pl.pallas_call(functools.partial(right_kernel, by_hops, first), out_shape...  1.2 us
    pallas_call x1, Pallas kernels, on_device(): pl.pallas_call(functools.partial(gate_kernel, len(passed)), out_shape=[ja...  1.09 us
    ppermute x1, starting transfers between devices, shifted(): lax.ppermute(array, axis, [(i, (i + by) % devices) for i in range(devices)])  1.01 us
  transfers between devices with their start and end apart: 6, of which 2 were waited for; matrix products, arithmetic and copies ran while one was open for 2% of the time, Pallas kernels for 16%

profile of v10, /device:TPU:1, one launch (start us, length us, event | category | flops | bytes accessed | tf_op | source)
XLA Modules:
  0.0 48.8 jit_solution(11844188544823635563)
XLA Ops:
  0.0 5.1 %collective-permute-start = (bf16[48,48,128]{2,1,0:T(8,128)(2,1)}, bf16[48,48,128]{2,1,0:T(8,128)(2,1)S(1)}, u32[]{:S(2)}, u32[]{:S(2)}) collective-permute-start(bf16[48,48,128]{2,1,0:T(8,128)(2,1)} %refs_5_.3), channel_id=1, source_target_pairs={{0,8},{1,9},{5,13},{6,14},{10,2},{11,3},{12,4},{15,7},{16,24},{17,... | collective-permute-start | bytes 1769480 | tf_op jit(solution)/shard_map/ppermute | solution.py:251
  5.1 1.0 %collective-permute-start.1 = (bf16[48,48,128]{2,1,0:T(8,128)(2,1)}, bf16[48,48,128]{2,1,0:T(8,128)(2,1)S(1)}, u32[]{:S(2)}, u32[]{:S(2)}) collective-permute-start(bf16[48,48,128]{2,1,0:T(8,128)(2,1)} %refs_5_.3), channel_id=1, source_target_pairs={{0,3},{1,0},{2,1},{3,2},{4,7},{5,4},{6,5},{7,6},{8,11},{9,8},{10,9... | collective-permute-start | bytes 1769480 | tf_op jit(solution)/shard_map/ppermute | solution.py:33
  6.1 0.9 %fusion = (bf16[128,256]{1,0:T(8,128)(2,1)S(1)}, bf16[128,256]{1,0:T(8,128)(2,1)S(1)}) fusion(bf16[128,512]{1,0:T(8,128)(2,1)} %param.13), kind=kLoop, calls=%fused_computation | loop fusion | bytes 262144 | tf_op jit(solution)/shard_map/slice | solution.py:284
  7.0 0.1 copy.11
  7.7 0.0 copy-start
  7.8 1.1 %copy-done = bf16[48,48,128]{2,1,0:T(8,128)(2,1)S(1)} copy-done((bf16[48,48,128]{2,1,0:T(8,128)(2,1)S(1)}, bf16[48,48,128]{2,1,0:T(8,128)(2,1)}, u32[]{:S(2)}) %copy-start) | copy-done | bytes 589848
  8.8 0.0 copy-start.1
  8.8 0.8 %copy-done.1 = bf16[128,128]{1,0:T(8,128)(2,1)S(1)} copy-done((bf16[128,128]{1,0:T(8,128)(2,1)S(1)}, bf16[128,128]{1,0:T(8,128)(2,1)}, u32[]{:S(2)}) %copy-start.1) | copy-done | bytes 32792
  9.6 0.0 copy-start.2
  9.6 0.8 %copy-done.2 = bf16[128,128]{1,0:T(8,128)(2,1)S(1)} copy-done((bf16[128,128]{1,0:T(8,128)(2,1)S(1)}, bf16[128,128]{1,0:T(8,128)(2,1)}, u32[]{:S(2)}) %copy-start.2) | copy-done | bytes 32792
  10.3 0.7 %copy-done.5 = f32[128]{0:T(128)S(1)} copy-done((f32[128]{0:T(128)S(1)}, f32[128]{0:T(128)}, u32[]{:S(2)}) %copy-start.5) | copy-done | bytes 536
  11.0 0.7 %copy-done.6 = f32[128]{0:T(128)S(1)} copy-done((f32[128]{0:T(128)S(1)}, f32[128]{0:T(128)}, u32[]{:S(2)}) %copy-start.6) | copy-done | bytes 536
  11.6 1.1 %gate.1 = (f32[48,48,128]{2,1,0:T(8,128)S(1)}, f32[1,128]{1,0:T(1,128)S(1)}, f32[1,128]{1,0:T(1,128)S(1)}, bf16[256,128]{1,0:T(8,128)(2,1)S(1)}, bf16[128,256]{1...) custom-call(bf16[48,48,128]{2,1,0:T(8,128)(2,1)S(1)} %copy-done, ...), custom_call_target="tpu_custom_call" | custom-call | flops 75497472 | bytes 1769472 | tf_op jit(solution)/shard_map/gate/pallas_call | solution.py:286
  12.7 4.6 %collective-permute-done.refs_0_ = bf16[48,48,128]{2,1,0:T(8,128)(2,1)S(1)} collective-permute-done((bf16[48,48,128]{2,1,0:T(8,128)(2,1)}, bf16[48,48,128]{2,1,0:T(8,128)(2,1)S(1)}, u32[]{:S(2)}, u32[]{:S(2)}) %collective-permute-start) | collective-permute-done | bytes 589856 | tf_op jit(solution)/shard_map/ppermute | solution.py:251
  17.4 0.5 right.2.refs_0_
  17.9 0.7 %right.3.refs_0_ = bf16[32,48,128]{2,1,0:T(8,128)(2,1)S(1)} custom-call(s32[1]{0:T(128)S(6)} %copy.12.tokens_ref, bf16[48,48,128]{2,1,0:T(8,128)(2,1)S(1)} %get-tuple-element.15.pair_ref.refs_0_, f32[1,128]{1,0:T(1,128)S(1)} %get-tuple-element.16.gain_ref.refs_2_, f32[1,128]{1,0:T(1,128)S(1)} %get-tuple-element.17.bias_ref.refs_3_, ...), custom_call_target="tpu_custom_call" | custom-call | flops 100663296 | bytes 1179648 | tf_op jit(solution)/shard_map/right/pallas_call | solution.py:299
  18.6 0.0 copy-start.3
  18.6 0.0 copy-start.4
  18.6 0.0 collective-permute-done.1.refs_1_
  18.6 1.6 %collective-permute-start.2 = (bf16[32,48,128]{2,1,0:T(8,128)(2,1)S(1)}, bf16[32,48,128]{2,1,0:T(8,128)(2,1)S(1)}, u32[]{:S(2)}, u32[]{:S(2)}) collective-permute-start(bf16[32,48,128]{2,1,0:T(8,128)(2,1)S(1)} %right.3.refs_0_), channel_id=1, source_target_pairs={{0,4},{1,0},{2,6},{3,2},{4,7},{5,1},{6,5},{7,3},{8,12},{9,8},{10,1... | collective-permute-start | bytes 1179656 | tf_op jit(solution)/shard_map/ppermute | solution.py:251
  20.2 1.9 %collective-permute-start.3 = (bf16[32,48,128]{2,1,0:T(8,128)(2,1)S(1)}, bf16[32,48,128]{2,1,0:T(8,128)(2,1)S(1)}, u32[]{:S(2)}, u32[]{:S(2)}) collective-permute-start(bf16[32,48,128]{2,1,0:T(8,128)(2,1)S(1)} %right.3.refs_0_), channel_id=1, source_target_pairs={{1,4},{3,6},{4,3},{6,1},{9,12},{11,14},{12,11},{14,9},{17,20},{19,... | collective-permute-start | bytes 1179656 | tf_op jit(solution)/shard_map/ppermute | solution.py:251
  22.2 0.1 collective-permute-start.4
  22.2 11.6 %collective-permute-start.5 = (bf16[16,48,128]{2,1,0:T(8,128)(2,1)S(1)}, bf16[16,48,128]{2,1,0:T(8,128)(2,1)S(1)}, u32[]{:S(2)}, u32[]{:S(2)}) collective-permute-start(bf16[16,48,128]{2,1,0:T(8,128)(2,1)S(1)} %right.2.refs_0_), channel_id=1, source_target_pairs={{1,4},{3,6},{4,3},{6,1},{9,12},{11,14},{12,11},{14,9},{17,20},{19,... | collective-permute-start | bytes 589832 | tf_op jit(solution)/shard_map/ppermute | solution.py:251
  33.8 3.0 %left.1.refs_3_ = bf16[128,48,128]{2,1,0:T(8,128)(2,1)S(1)} custom-call(s32[1]{0:T(128)S(6)} %copy.12.tokens_ref, bf16[48,48,128]{2,1,0:T(8,128)(2,1)S(1)} %get-tuple-element.15.pair_ref.refs_0_, bf16[48,48,128]{2,1,0:T(8,128)(2,1)S(1)} %collective-permute-done.1.refs_1_, f32[1,128]{1,0:T(1,128)S(1)} %get-tuple-element.16.gain_ref.refs_2_, ...), custom_call_target="tpu_custom_call" | custom-call | flops 301989888 | bytes 4718592 | tf_op jit(solution)/shard_map/left/pallas_call | solution.py:324
  36.8 0.0 collective-permute-done.4.refs_1_
  36.8 4.8 %collective-permute-done.5.refs_2_ = bf16[16,48,128]{2,1,0:T(8,128)(2,1)S(1)} collective-permute-done((bf16[16,48,128]{2,1,0:T(8,128)(2,1)S(1)}, bf16[16,48,128]{2,1,0:T(8,128)(2,1)S(1)}, u32[]{:S(2)}, u32[]{:S(2)}) %collective-permute-start.5) | collective-permute-done | bytes 196640 | tf_op jit(solution)/shard_map/ppermute | solution.py:251
  41.7 0.0 copy-done.3
  41.7 0.0 copy-done.4
  41.7 2.6 %product.2.refs_8_ = bf16[48,16,128]{2,1,0:T(8,128)(2,1)S(1)} custom-call(bf16[16,48,128]{2,1,0:T(8,128)(2,1)S(1)} %right.2.refs_0_, bf16[16,48,128]{2,1,0:T(8,128)(2,1)S(1)} %collective-permute-done.4.refs_1_, bf16[16,48,128]{2,1,0:T(8,128)(2,1)S(1)} %collective-permute-done.5.refs_2_, bf16[128,48,128]{2,1,0:T(8,128)(2,1)S(1)} %left.1.refs_3_, ...), custom_call_target="tpu_custom_call" | custom-call | flops 18874368 | bytes 2359296 | tf_op jit(solution)/shard_map/product/pallas_call | solution.py:348
  44.3 0.0 collective-permute-done.2.refs_1_
  44.3 0.0 collective-permute-done.3.refs_2_
  44.3 4.5 %product.3 = bf16[48,48,128]{2,1,0:T(8,128)(2,1)} custom-call(bf16[32,48,128]{2,1,0:T(8,128)(2,1)S(1)} %right.3.refs_0_, bf16[32,48,128]{2,1,0:T(8,128)(2,1)S(1)} %collective-permute-done.2.refs_1_, bf16[32,48,128]{2,1,0:T(8,128)(2,1)S(1)} %collective-permute-done.3.refs_2_, bf16[128,48,128]{2,1,0:T(8,128)(2,1)S(1)} %left.1.refs_3_, ...), custom_call_target="tpu_custom_call" | custom-call | flops 37748736 | bytes 2359296 | tf_op jit(solution)/shard_map/product/pallas_call | solution.py:348
  (2 shorter events, 0.0 us)
Async XLA Ops:
  0.0 17.4 %collective-permute-start = (bf16[48,48,128]{2,1,0:T(8,128)(2,1)}, bf16[48,48,128]{2,1,0:T(8,128)(2,1)S(1)}, u32[]{:S(2)}, u32[]{:S(2)}) collective-permute-start(bf16[48,48,128]{2,1,0:T(8,128)(2,1)} %refs_5_.3), channel_id=1, source_target_pairs={{0,8},{1,9},{5,13},{6,14},{10,2},{11,3},{12,4},{15,7},{16,24},{17,... | collective-permute-start | bytes 1769480 | tf_op jit(solution)/shard_map/ppermute | solution.py:251
  5.1 13.5 %collective-permute-start.1 = (bf16[48,48,128]{2,1,0:T(8,128)(2,1)}, bf16[48,48,128]{2,1,0:T(8,128)(2,1)S(1)}, u32[]{:S(2)}, u32[]{:S(2)}) collective-permute-start(bf16[48,48,128]{2,1,0:T(8,128)(2,1)} %refs_5_.3), channel_id=1, source_target_pairs={{0,3},{1,0},{2,1},{3,2},{4,7},{5,4},{6,5},{7,6},{8,11},{9,8},{10,9... | collective-permute-start | bytes 1769480 | tf_op jit(solution)/shard_map/ppermute | solution.py:33
  7.7 1.1 %copy-start = (bf16[48,48,128]{2,1,0:T(8,128)(2,1)S(1)}, bf16[48,48,128]{2,1,0:T(8,128)(2,1)}, u32[]{:S(2)}) copy-start(bf16[48,48,128]{2,1,0:T(8,128)(2,1)} %refs_5_.3) | copy-start | bytes 1769476
  8.8 0.8 %copy-start.1 = (bf16[128,128]{1,0:T(8,128)(2,1)S(1)}, bf16[128,128]{1,0:T(8,128)(2,1)}, u32[]{:S(2)}) copy-start(bf16[128,128]{1,0:T(8,128)(2,1)} %weights_ref.1) | copy-start | bytes 98308
  9.6 0.8 %copy-start.2 = (bf16[128,128]{1,0:T(8,128)(2,1)S(1)}, bf16[128,128]{1,0:T(8,128)(2,1)}, u32[]{:S(2)}) copy-start(bf16[128,128]{1,0:T(8,128)(2,1)} %refs_4_.1) | copy-start | bytes 98308
  10.3 0.7 %copy-start.5 = (f32[128]{0:T(128)S(1)}, f32[128]{0:T(128)}, u32[]{:S(2)}) copy-start(f32[128]{0:T(128)} %param.11) | copy-start | bytes 1540
  11.0 0.7 %copy-start.6 = (f32[128]{0:T(128)S(1)}, f32[128]{0:T(128)}, u32[]{:S(2)}) copy-start(f32[128]{0:T(128)} %param.12) | copy-start | bytes 1540
  18.6 23.1 %copy-start.3 = (f32[128]{0:T(128)S(1)}, f32[128]{0:T(128)}, u32[]{:S(2)}) copy-start(f32[128]{0:T(128)} %refs_5_.5) | copy-start | bytes 1540
  18.6 23.1 %copy-start.4 = (f32[128]{0:T(128)S(1)}, f32[128]{0:T(128)}, u32[]{:S(2)}) copy-start(f32[128]{0:T(128)} %refs_6_.3) | copy-start | bytes 1540
  18.6 25.7 %collective-permute-start.2 = (bf16[32,48,128]{2,1,0:T(8,128)(2,1)S(1)}, bf16[32,48,128]{2,1,0:T(8,128)(2,1)S(1)}, u32[]{:S(2)}, u32[]{:S(2)}) collective-permute-start(bf16[32,48,128]{2,1,0:T(8,128)(2,1)S(1)} %right.3.refs_0_), channel_id=1, source_target_pairs={{0,4},{1,0},{2,6},{3,2},{4,7},{5,1},{6,5},{7,3},{8,12},{9,8},{10,1... | collective-permute-start | bytes 1179656 | tf_op jit(solution)/shard_map/ppermute | solution.py:251
  20.2 24.1 %collective-permute-start.3 = (bf16[32,48,128]{2,1,0:T(8,128)(2,1)S(1)}, bf16[32,48,128]{2,1,0:T(8,128)(2,1)S(1)}, u32[]{:S(2)}, u32[]{:S(2)}) collective-permute-start(bf16[32,48,128]{2,1,0:T(8,128)(2,1)S(1)} %right.3.refs_0_), channel_id=1, source_target_pairs={{1,4},{3,6},{4,3},{6,1},{9,12},{11,14},{12,11},{14,9},{17,20},{19,... | collective-permute-start | bytes 1179656 | tf_op jit(solution)/shard_map/ppermute | solution.py:251
  22.2 14.7 %collective-permute-start.4 = (bf16[16,48,128]{2,1,0:T(8,128)(2,1)S(1)}, bf16[16,48,128]{2,1,0:T(8,128)(2,1)S(1)}, u32[]{:S(2)}, u32[]{:S(2)}) collective-permute-start(bf16[16,48,128]{2,1,0:T(8,128)(2,1)S(1)} %right.2.refs_0_), channel_id=1, source_target_pairs={{0,4},{1,0},{2,6},{3,2},{4,7},{5,1},{6,5},{7,3},{8,12},{9,8},{10,1... | collective-permute-start | bytes 589832 | tf_op jit(solution)/shard_map/ppermute | solution.py:251
  22.2 19.5 %collective-permute-start.5 = (bf16[16,48,128]{2,1,0:T(8,128)(2,1)S(1)}, bf16[16,48,128]{2,1,0:T(8,128)(2,1)S(1)}, u32[]{:S(2)}, u32[]{:S(2)}) collective-permute-start(bf16[16,48,128]{2,1,0:T(8,128)(2,1)S(1)} %right.2.refs_0_), channel_id=1, source_target_pairs={{1,4},{3,6},{4,3},{6,1},{9,12},{11,14},{12,11},{14,9},{17,20},{19,... | collective-permute-start | bytes 589832 | tf_op jit(solution)/shard_map/ppermute | solution.py:251

commit v11 on v9

--- a/solution.py
+++ b/solution.py
@@ -141,14 +141,22 @@
     )
 
 
-def product_kernel(picks, rights, first, *refs):
+def product_kernel(picks, rights, first, last, *refs):
     right_refs, refs = refs[:rights], refs[rights:]
-    left_ref, gate_ref, gain_ref, bias_ref, weights_ref, *_, out_ref = refs[:-5]
-    right, product, updates, result, sent = refs[-5:]
+    left_ref, gate_ref, gain_ref, bias_ref, weights_ref, *done, out_ref = refs[: -5 if last else -3]
+    right, product, updates = refs[-5:-2] if last else refs[-3:]
+    result, sent = refs[-2:] if last else (out_ref, None)
     hidden, rows, width = left_ref.shape
     count = right_refs[0].shape[0]
     apart = pitch(count)
     even = (lax.axis_index("row") + lax.axis_index("col")) % 2 == 0
+
+    copies, start = [], 0
+    for at, ref in enumerate(done):
+        columns = pl.ds(start, ref.shape[1])
+        copies.append(pltpu.make_async_copy(ref, out_ref.at[:, columns], sent.at[at]))
+        copies[-1].start()
+        start += ref.shape[1]
 
     for token in range(count):
         pieces = []
@@ -161,7 +169,8 @@
         for at in range(0, width, LANES):
             right[at // LANES, pl.ds(token, hidden, stride=apart), :] = one[:, at : at + LANES]
 
-    total = jnp.zeros((count, rows), jnp.float32)
+    ways = 4
+    totals = [jnp.zeros((count, rows), jnp.float32)] * ways
     for channel in range(hidden):
         one = 0.0
         for at in range(0, width, LANES):
@@ -172,13 +181,13 @@
                 preferred_element_type=jnp.float32,
             )
         product[pl.ds(channel * apart, count), :rows] = one
-        total += one
-    average = total / hidden
-    total = jnp.zeros((count, rows), jnp.float32)
+        totals[channel % ways] += one
+    average = sum(totals) / hidden
+    totals = [jnp.zeros((count, rows), jnp.float32)] * ways
     for channel in range(hidden):
         centered = product[pl.ds(channel * apart, count), :rows] - average
-        total += centered * centered
-    scale = lax.rsqrt(total / hidden + 1e-05)
+        totals[channel % ways] += centered * centered
+    scale = lax.rsqrt(sum(totals) / hidden + 1e-05)
     for channel in range(hidden):
         place = pl.ds(channel * apart, count)
         centered = product[place, :rows] - average
@@ -188,15 +197,19 @@
         updates[pl.ds(token, rows, stride=apart), :] = lax.dot_general(
             mixed, weights_ref[...], (((0,), (0,)), ((), ())), preferred_element_type=jnp.float32
         )
-    step = 8
+    step = 16
     for at in range(0, rows, step):
         gate = gate_ref[pl.ds(at, step), pl.ds(first, count)]
         for row in range(step):
             update = updates[pl.ds((at + row) * apart, count), :]
             result[at + row] = (gate[row] * update).astype(jnp.bfloat16)
-    copy = pltpu.make_async_copy(result, out_ref.at[:, pl.ds(first, count)], sent)
-    copy.start()
-    copy.wait()
+        if last:
+            target = out_ref.at[pl.ds(at, step), pl.ds(first, count)]
+            place = sent.at[len(done) + at // step]
+            copies.append(pltpu.make_async_copy(result.at[pl.ds(at, step)], target, place))
+            copies[-1].start()
+    for copy in copies:
+        copy.wait()
 
 
 def band_by_sums(right, spans, window, row_count, col_count, columns):
@@ -311,28 +324,32 @@
             right_of(0, rows), spans, window, row_count, col_count, columns
         )
 
-    update = []
+    done = []
     for (first, count), band in zip(spans, bands):
+        last = first + count == columns
+        scratch = [
+            pltpu.VMEM((width // LANES, hidden * pitch(count), LANES), jnp.float32),
+            pltpu.VMEM((hidden * pitch(count), LANES), jnp.float32),
+            pltpu.VMEM((rows * pitch(count), channels), jnp.float32),
+        ]
+        if last:
+            scratch += [
+                pltpu.VMEM((rows, count, channels), jnp.bfloat16),
+                pltpu.SemaphoreType.DMA((len(done) + rows // 16,)),
+            ]
         filled = pl.pallas_call(
-            functools.partial(product_kernel, picks, len(band), first),
-            out_shape=jax.ShapeDtypeStruct((rows, columns, channels), jnp.bfloat16),
-            in_specs=[VMEM] * (len(band) + 2) + [SMEM, SMEM, VMEM] + [ANY] * len(update),
-            out_specs=ANY,
-            scratch_shapes=[
-                pltpu.VMEM((width // LANES, hidden * pitch(count), LANES), jnp.float32),
-                pltpu.VMEM((hidden * pitch(count), LANES), jnp.float32),
-                pltpu.VMEM((rows * pitch(count), channels), jnp.float32),
-                pltpu.VMEM((rows, count, channels), jnp.bfloat16),
-                pltpu.SemaphoreType.DMA,
-            ],
-            input_output_aliases={len(band) + 5: 0} if update else {},
+            functools.partial(product_kernel, picks, len(band), first, last),
+            out_shape=jax.ShapeDtypeStruct(
+                (rows, columns if last else count, channels), jnp.bfloat16
+            ),
+            in_specs=[VMEM] * (len(band) + 2) + [SMEM, SMEM, VMEM] + [VMEM] * len(done) * last,
+            out_specs=ANY if last else VMEM,
+            scratch_shapes=scratch,
             compiler_params=params(2 * block, 2 * hidden * (rows + 2 * count) * width),
-            cost_estimate=cost(
-                2 * rows * count * depth * hidden, 4 * rows * depth * hidden
-            ),
+            cost_estimate=cost(2 * rows * count * depth * hidden, 4 * rows * depth * hidden),
             name="product",
-        )(*band, left, gate, out_gain, out_bias, out_weights, *update)
-        update = [filled]
+        )(*band, left, gate, out_gain, out_bias, out_weights, *(done if last else []))
+        done.append(filled)
     return filled
 
 

time: 45.4 us -> 44.7 us (0.985)
  Pallas kernels: 11.4 us -> 10.8 us
    pallas_call x2, Pallas kernels: 7.72 us -> 7.02 us  [on_device(): pl.pallas_call(functools.partial(product_kernel, picks, len(band), first,...]
  transfers between devices with their start and end apart: 7 -> 7, of which waited for: 4 -> 4; matrix products, arithmetic and copies ran while one was open for 4% -> 5% of each run, Pallas kernels for 18% -> 17%
where the time goes in v11:
time: 44.7 us; the launch traced here: 44.3 us
  starting transfers between devices  15.1 us (34%)
  waiting for transfers between devices  11.7 us (26%)
  Pallas kernels  10.8 us (24%)
  local copies, waits for them, and re-layouts  5.92 us (13%)
  between operations  0.78 us (2%)
    ppermute x6, starting transfers between devices, move(): lax.ppermute(array, ('row', 'col'), [(r * 4 + c, to_r * 4 + to_c) for (r,...  15.1 us
    ppermute x6, waiting for transfers between devices, move(): lax.ppermute(array, ('row', 'col'), [(r * 4 + c, to_r * 4 + to_c) for (r,...  9.73 us
    pallas_call x2, Pallas kernels, on_device(): pl.pallas_call(functools.partial(product_kernel, picks, len(band), first,...  7.02 us
    unnamed x15, local copies, waits for them, and re-layouts  4.01 us
    pallas_call x1, Pallas kernels, on_device(): pl.pallas_call(functools.partial(left_kernel, window, later), out_shape=[...  2.53 us
    ppermute x1, waiting for transfers between devices, shifted(): lax.ppermute(array, axis, [(i, (i + by) % devices) for i in range(devices)])  1.98 us
    pallas_call x2, Pallas kernels, right_of(): pl.pallas_call(functools.partial(right_kernel, by_hops, first), out_shape...  1.2 us
    slice x1, local copies, waits for them, and re-layouts, on_device(): arrived.append(move(pair_state[:spans[0][1]], out))  1.02 us
  transfers between devices with their start and end apart: 7, of which 4 were waited for; matrix products, arithmetic and copies ran while one was open for 5% of the time, Pallas kernels for 17%

profile of v11, /device:TPU:1, one launch (start us, length us, event | category | flops | bytes accessed | tf_op | source)
XLA Modules:
  0.0 44.3 jit_solution(13404872263195637985)
XLA Ops:
  0.0 0.1 collective-permute-start
  0.1 1.0 %slice.11 = bf16[32,48,128]{2,1,0:T(8,128)(2,1)S(1)} slice(bf16[48,48,128]{2,1,0:T(8,128)(2,1)} %pair_ref.3), slice={[0:32], [0:48], [0:128]} | slice | bytes 786432 | tf_op jit(solution)/shard_map/slice | solution.py:279
  1.1 5.7 %collective-permute-start.4 = (bf16[32,48,128]{2,1,0:T(8,128)(2,1)S(1)}, bf16[32,48,128]{2,1,0:T(8,128)(2,1)S(1)}, u32[]{:S(2)}, u32[]{:S(2)}) collective-permute-start(bf16[32,48,128]{2,1,0:T(8,128)(2,1)S(1)} %slice.11), channel_id=1, source_target_pairs={{0,8},{1,9},{5,13},{6,14},{10,2},{11,3},{12,4},{15,7},{16,24},{17,... | collective-permute-start | bytes 1179656 | tf_op jit(solution)/shard_map/ppermute | solution.py:246
  7.4 0.9 %fusion = (bf16[128,256]{1,0:T(8,128)(2,1)S(1)}, bf16[128,256]{1,0:T(8,128)(2,1)S(1)}) fusion(bf16[128,512]{1,0:T(8,128)(2,1)} %param.13), kind=kLoop, calls=%fused_computation | loop fusion | bytes 262144 | tf_op jit(solution)/shard_map/slice | solution.py:283
  8.3 0.1 copy.11
  8.4 2.0 %collective-permute-done.refs_1_ = bf16[48,48,128]{2,1,0:T(8,128)(2,1)S(1)} collective-permute-done((bf16[48,48,128]{2,1,0:T(8,128)(2,1)}, bf16[48,48,128]{2,1,0:T(8,128)(2,1)S(1)}, u32[]{:S(2)}, u32[]{:S(2)}) %collective-permute-start) | collective-permute-done | bytes 589856 | tf_op jit(solution)/shard_map/ppermute | solution.py:33
  10.4 1.1 %copy-done = bf16[48,48,128]{2,1,0:T(8,128)(2,1)S(1)} copy-done((bf16[48,48,128]{2,1,0:T(8,128)(2,1)S(1)}, bf16[48,48,128]{2,1,0:T(8,128)(2,1)}, u32[]{:S(2)}) %copy-start) | copy-done | bytes 589848
  11.5 0.0 copy-start.1
  11.5 0.8 %copy-done.1 = bf16[128,128]{1,0:T(8,128)(2,1)S(1)} copy-done((bf16[128,128]{1,0:T(8,128)(2,1)S(1)}, bf16[128,128]{1,0:T(8,128)(2,1)}, u32[]{:S(2)}) %copy-start.1) | copy-done | bytes 32792
  12.2 0.8 %copy-done.2 = bf16[128,128]{1,0:T(8,128)(2,1)S(1)} copy-done((bf16[128,128]{1,0:T(8,128)(2,1)S(1)}, bf16[128,128]{1,0:T(8,128)(2,1)}, u32[]{:S(2)}) %copy-start.2) | copy-done | bytes 32792
  13.0 0.7 %copy-done.3 = f32[128]{0:T(128)S(1)} copy-done((f32[128]{0:T(128)S(1)}, f32[128]{0:T(128)}, u32[]{:S(2)}) %copy-start.3) | copy-done | bytes 536
  13.6 0.7 %copy-done.4 = f32[128]{0:T(128)S(1)} copy-done((f32[128]{0:T(128)S(1)}, f32[128]{0:T(128)}, u32[]{:S(2)}) %copy-start.4) | copy-done | bytes 536
  14.3 2.5 %left_and_gate.1 = (bf16[128,48,128]{2,1,0:T(8,128)(2,1)S(1)}, f32[48,48,128]{2,1,0:T(8,128)S(1)}, bf16[16,48,128]{2,1,0:T(8,128)(2,1)S(1)}, f32[1,128]{1,0:T(1,...) custom-call(s32[1]{0:T(128)S(6)} %copy.12.tokens_ref, ...), custom_call_target="tpu_custom_call" | custom-call | flops 301989888 | bytes 4718592 | tf_op jit(solution)/shard_map/left_and_gate/pallas_call | solution.py:285
  16.8 0.0 copy-start.5
  16.9 0.0 copy-start.6
  16.9 4.5 %collective-permute-start.1 = (bf16[16,48,128]{2,1,0:T(8,128)(2,1)S(1)}, bf16[16,48,128]{2,1,0:T(8,128)(2,1)S(1)}, u32[]{:S(2)}, u32[]{:S(2)}) collective-permute-start(bf16[16,48,128]{2,1,0:T(8,128)(2,1)S(1)} %get-tuple-element.15), channel_id=1, source_target_pairs={{0,8},{1,9},{5,13},{6,14},{10,2},{11,3},{12,4},{15,7},{16,24},{17,... | collective-permute-start | bytes 589832 | tf_op jit(solution)/shard_map/ppermute | solution.py:246
  21.4 0.0 collective-permute-done.4.refs_0_
  21.4 0.7 %right.3.refs_0_ = bf16[32,48,128]{2,1,0:T(8,128)(2,1)S(1)} custom-call(s32[1]{0:T(128)S(6)} %copy.12.tokens_ref, bf16[48,48,128]{2,1,0:T(8,128)(2,1)S(1)} %copy-done, f32[1,128]{1,0:T(1,128)S(1)} %get-tuple-element.12.gain_ref, f32[1,128]{1,0:T(1,128)S(1)} %get-tuple-element.13.bias_ref, bf16[128,256]{1,0:T(8,128)(2,1)S(1)} %get-tuple-element.14.weights_ref, ...), custom_call_target="tpu_custom_call" | custom-call | flops 100663296 | bytes 1179648 | tf_op jit(solution)/shard_map/right/pallas_call | solution.py:305
  22.1 0.1 collective-permute-start.5
  22.2 1.9 %collective-permute-start.6 = (bf16[32,48,128]{2,1,0:T(8,128)(2,1)S(1)}, bf16[32,48,128]{2,1,0:T(8,128)(2,1)S(1)}, u32[]{:S(2)}, u32[]{:S(2)}) collective-permute-start(bf16[32,48,128]{2,1,0:T(8,128)(2,1)S(1)} %right.3.refs_0_), channel_id=1, source_target_pairs={{1,4},{3,6},{4,3},{6,1},{9,12},{11,14},{12,11},{14,9},{17,20},{19,... | collective-permute-start | bytes 1179656 | tf_op jit(solution)/shard_map/ppermute | solution.py:246
  24.1 2.0 %collective-permute-done.1.refs_0_ = bf16[16,48,128]{2,1,0:T(8,128)(2,1)S(1)} collective-permute-done((bf16[16,48,128]{2,1,0:T(8,128)(2,1)S(1)}, bf16[16,48,128]{2,1,0:T(8,128)(2,1)S(1)}, u32[]{:S(2)}, u32[]{:S(2)}) %collective-permute-start.1) | collective-permute-done | bytes 196640 | tf_op jit(solution)/shard_map/ppermute | solution.py:246
  26.1 0.5 %right.2.refs_0_ = bf16[16,48,128]{2,1,0:T(8,128)(2,1)S(1)} custom-call(s32[1]{0:T(128)S(6)} %copy.12.tokens_ref, bf16[48,48,128]{2,1,0:T(8,128)(2,1)S(1)} %copy-done, f32[1,128]{1,0:T(1,128)S(1)} %get-tuple-element.12.gain_ref, f32[1,128]{1,0:T(1,128)S(1)} %get-tuple-element.13.bias_ref, bf16[128,256]{1,0:T(8,128)(2,1)S(1)} %get-tuple-element.14.weights_ref, ...), custom_call_target="tpu_custom_call" | custom-call | flops 50331648 | bytes 589824 | tf_op jit(solution)/shard_map/right/pallas_call | solution.py:305
  26.6 0.3 collective-permute-start.2
  26.9 2.5 %collective-permute-start.3 = (bf16[16,48,128]{2,1,0:T(8,128)(2,1)S(1)}, bf16[16,48,128]{2,1,0:T(8,128)(2,1)S(1)}, u32[]{:S(2)}, u32[]{:S(2)}) collective-permute-start(bf16[16,48,128]{2,1,0:T(8,128)(2,1)S(1)} %right.2.refs_0_), channel_id=1, source_target_pairs={{1,4},{3,6},{4,3},{6,1},{9,12},{11,14},{12,11},{14,9},{17,20},{19,... | collective-permute-start | bytes 589832 | tf_op jit(solution)/shard_map/ppermute | solution.py:246
  29.5 0.4 collective-permute-done.5.refs_1_
  29.9 7.3 %collective-permute-done.6.refs_2_ = bf16[32,48,128]{2,1,0:T(8,128)(2,1)S(1)} collective-permute-done((bf16[32,48,128]{2,1,0:T(8,128)(2,1)S(1)}, bf16[32,48,128]{2,1,0:T(8,128)(2,1)S(1)}, u32[]{:S(2)}, u32[]{:S(2)}) %collective-permute-start.6) | collective-permute-done | bytes 393248 | tf_op jit(solution)/shard_map/ppermute | solution.py:246
  37.2 0.0 copy-done.5
  37.2 0.0 copy-done.6
  37.2 3.7 %product.2.refs_8_ = bf16[48,32,128]{2,1,0:T(8,128)(2,1)S(1)} custom-call(bf16[32,48,128]{2,1,0:T(8,128)(2,1)S(1)} %right.3.refs_0_, bf16[32,48,128]{2,1,0:T(8,128)(2,1)S(1)} %collective-permute-done.5.refs_1_, bf16[32,48,128]{2,1,0:T(8,128)(2,1)S(1)} %collective-permute-done.6.refs_2_, bf16[128,48,128]{2,1,0:T(8,128)(2,1)S(1)} %get-tuple-element.16.refs_3_, ...), custom_call_target="tpu_custom_call" | custom-call | flops 37748736 | bytes 2359296 | tf_op jit(solution)/shard_map/product/pallas_call | solution.py:340
  41.0 0.0 collective-permute-done.2.refs_1_
  41.0 0.0 collective-permute-done.3.refs_2_
  41.0 3.3 %product.3 = bf16[48,48,128]{2,1,0:T(8,128)(2,1)} custom-call(bf16[16,48,128]{2,1,0:T(8,128)(2,1)S(1)} %right.2.refs_0_, bf16[16,48,128]{2,1,0:T(8,128)(2,1)S(1)} %collective-permute-done.2.refs_1_, bf16[16,48,128]{2,1,0:T(8,128)(2,1)S(1)} %collective-permute-done.3.refs_2_, bf16[128,48,128]{2,1,0:T(8,128)(2,1)S(1)} %get-tuple-element.16.refs_3_, ...), custom_call_target="tpu_custom_call" | custom-call | flops 18874368 | bytes 2359296 | tf_op jit(solution)/shard_map/product/pallas_call | solution.py:340
  (4 shorter events, 0.0 us)
Async XLA Ops:
  0.0 10.4 %collective-permute-start = (bf16[48,48,128]{2,1,0:T(8,128)(2,1)}, bf16[48,48,128]{2,1,0:T(8,128)(2,1)S(1)}, u32[]{:S(2)}, u32[]{:S(2)}) collective-permute-start(bf16[48,48,128]{2,1,0:T(8,128)(2,1)} %pair_ref.3), channel_id=1, source_target_pairs={{0,3},{1,0},{2,1},{3,2},{4,7},{5,4},{6,5},{7,6},{8,11},{9,8},{10,9... | collective-permute-start | bytes 1769480 | tf_op jit(solution)/shard_map/ppermute | solution.py:33
  1.1 20.3 %collective-permute-start.4 = (bf16[32,48,128]{2,1,0:T(8,128)(2,1)S(1)}, bf16[32,48,128]{2,1,0:T(8,128)(2,1)S(1)}, u32[]{:S(2)}, u32[]{:S(2)}) collective-permute-start(bf16[32,48,128]{2,1,0:T(8,128)(2,1)S(1)} %slice.11), channel_id=1, source_target_pairs={{0,8},{1,9},{5,13},{6,14},{10,2},{11,3},{12,4},{15,7},{16,24},{17,... | collective-permute-start | bytes 1179656 | tf_op jit(solution)/shard_map/ppermute | solution.py:246
  10.4 1.1 %copy-start = (bf16[48,48,128]{2,1,0:T(8,128)(2,1)S(1)}, bf16[48,48,128]{2,1,0:T(8,128)(2,1)}, u32[]{:S(2)}) copy-start(bf16[48,48,128]{2,1,0:T(8,128)(2,1)} %pair_ref.3) | copy-start | bytes 1769476
  11.5 0.8 %copy-start.1 = (bf16[128,128]{1,0:T(8,128)(2,1)S(1)}, bf16[128,128]{1,0:T(8,128)(2,1)}, u32[]{:S(2)}) copy-start(bf16[128,128]{1,0:T(8,128)(2,1)} %refs_5_.3) | copy-start | bytes 98308
  12.2 0.8 %copy-start.2 = (bf16[128,128]{1,0:T(8,128)(2,1)S(1)}, bf16[128,128]{1,0:T(8,128)(2,1)}, u32[]{:S(2)}) copy-start(bf16[128,128]{1,0:T(8,128)(2,1)} %refs_9_.1) | copy-start | bytes 98308
  13.0 0.7 %copy-start.3 = (f32[128]{0:T(128)S(1)}, f32[128]{0:T(128)}, u32[]{:S(2)}) copy-start(f32[128]{0:T(128)} %param.11) | copy-start | bytes 1540
  13.6 0.7 %copy-start.4 = (f32[128]{0:T(128)S(1)}, f32[128]{0:T(128)}, u32[]{:S(2)}) copy-start(f32[128]{0:T(128)} %param.12) | copy-start | bytes 1540
  16.8 20.4 %copy-start.5 = (f32[128]{0:T(128)S(1)}, f32[128]{0:T(128)}, u32[]{:S(2)}) copy-start(f32[128]{0:T(128)} %refs_5_.5) | copy-start | bytes 1540
  16.9 20.4 %copy-start.6 = (f32[128]{0:T(128)S(1)}, f32[128]{0:T(128)}, u32[]{:S(2)}) copy-start(f32[128]{0:T(128)} %refs_6_.3) | copy-start | bytes 1540
  16.9 9.3 %collective-permute-start.1 = (bf16[16,48,128]{2,1,0:T(8,128)(2,1)S(1)}, bf16[16,48,128]{2,1,0:T(8,128)(2,1)S(1)}, u32[]{:S(2)}, u32[]{:S(2)}) collective-permute-start(bf16[16,48,128]{2,1,0:T(8,128)(2,1)S(1)} %get-tuple-element.15), channel_id=1, source_target_pairs={{0,8},{1,9},{5,13},{6,14},{10,2},{11,3},{12,4},{15,7},{16,24},{17,... | collective-permute-start | bytes 589832 | tf_op jit(solution)/shard_map/ppermute | solution.py:246
  22.1 7.8 %collective-permute-start.5 = (bf16[32,48,128]{2,1,0:T(8,128)(2,1)S(1)}, bf16[32,48,128]{2,1,0:T(8,128)(2,1)S(1)}, u32[]{:S(2)}, u32[]{:S(2)}) collective-permute-start(bf16[32,48,128]{2,1,0:T(8,128)(2,1)S(1)} %right.3.refs_0_), channel_id=1, source_target_pairs={{0,4},{1,0},{2,6},{3,2},{4,7},{5,1},{6,5},{7,3},{8,12},{9,8},{10,1... | collective-permute-start | bytes 1179656 | tf_op jit(solution)/shard_map/ppermute | solution.py:246
  22.2 15.0 %collective-permute-start.6 = (bf16[32,48,128]{2,1,0:T(8,128)(2,1)S(1)}, bf16[32,48,128]{2,1,0:T(8,128)(2,1)S(1)}, u32[]{:S(2)}, u32[]{:S(2)}) collective-permute-start(bf16[32,48,128]{2,1,0:T(8,128)(2,1)S(1)} %right.3.refs_0_), channel_id=1, source_target_pairs={{1,4},{3,6},{4,3},{6,1},{9,12},{11,14},{12,11},{14,9},{17,20},{19,... | collective-permute-start | bytes 1179656 | tf_op jit(solution)/shard_map/ppermute | solution.py:246
  26.6 14.3 %collective-permute-start.2 = (bf16[16,48,128]{2,1,0:T(8,128)(2,1)S(1)}, bf16[16,48,128]{2,1,0:T(8,128)(2,1)S(1)}, u32[]{:S(2)}, u32[]{:S(2)}) collective-permute-start(bf16[16,48,128]{2,1,0:T(8,128)(2,1)S(1)} %right.2.refs_0_), channel_id=1, source_target_pairs={{0,4},{1,0},{2,6},{3,2},{4,7},{5,1},{6,5},{7,3},{8,12},{9,8},{10,1... | collective-permute-start | bytes 589832 | tf_op jit(solution)/shard_map/ppermute | solution.py:246
  26.9 14.0 %collective-permute-start.3 = (bf16[16,48,128]{2,1,0:T(8,128)(2,1)S(1)}, bf16[16,48,128]{2,1,0:T(8,128)(2,1)S(1)}, u32[]{:S(2)}, u32[]{:S(2)}) collective-permute-start(bf16[16,48,128]{2,1,0:T(8,128)(2,1)S(1)} %right.2.refs_0_), channel_id=1, source_target_pairs={{1,4},{3,6},{4,3},{6,1},{9,12},{11,14},{12,11},{14,9},{17,20},{19,... | collective-permute-start | bytes 589832 | tf_op jit(solution)/shard_map/ppermute | solution.py:246

commit v12 on v11

--- a/solution.py
+++ b/solution.py
@@ -61,8 +61,6 @@
         is_root = (col_pos - row_pos + 4) % 4 < 2
         block_row = jnp.where((row_pos + col_pos) % 2 == 0, col_pos, (col_pos + 3) % 4)
     row_start = block_row * pair_ref.shape[0] + first
-    valid_columns = tokens - col_pos * columns
-    position = lax.broadcasted_iota(jnp.int32, (columns, hidden), 0)
     step = 4
     for at in range(0, count, step):
         block = pair_ref[pl.ds(first + at, step)]
@@ -72,17 +70,26 @@
         both = jnp.dot(
             normed, weights_ref[...], preferred_element_type=jnp.float32
         )
-        right = jax.nn.sigmoid(both[:, :hidden]) * both[:, hidden:]
-        for row in range(step):
-            limit = jnp.where(row_start + at + row < tokens, valid_columns, 0)
-            part = right[row * columns : (row + 1) * columns]
-            out_ref[at + row] = jnp.where(position < limit, part, 0.0).astype(jnp.bfloat16)
+        for row, part in enumerate(masked_right(both, tokens, row_start + at, col_pos, columns)):
+            out_ref[at + row] = part
+
+
+def masked_right(both, tokens, row_token, third_block, columns):
+    hidden = both.shape[1] // 2
+    right = jax.nn.sigmoid(both[:, :hidden]) * both[:, hidden:]
+    position = lax.broadcasted_iota(jnp.int32, (columns, hidden), 0)
+    parts = []
+    for row in range(both.shape[0] // columns):
+        limit = jnp.where(row_token + row < tokens, tokens - third_block * columns, 0)
+        part = right[row * columns : (row + 1) * columns]
+        parts.append(jnp.where(position < limit, part, 0.0).astype(jnp.bfloat16))
+    return parts
 
 
 def left_kernel(blocks, later, tokens_ref, *refs):
     pair_refs, refs = refs[:blocks], refs[blocks:]
     gain_ref, bias_ref, weights_ref, gate_weights_ref, *passed, scratch = refs
-    passed, (left_ref, gate_ref, later_ref), handed = passed[:4], passed[4:7], passed[7:]
+    passed, (left_ref, gate_ref, right_ref, later_ref), handed = passed[:4], passed[4:8], passed[8:]
     later_ref[...] = pair_refs[0][pl.ds(later, later_ref.shape[0])]
     for source, target in zip(passed, handed):
         target[...] = source[...]
@@ -104,6 +111,9 @@
         normed = [normed_rows(ref[pl.ds(first, step)], gain_ref, bias_ref) for ref in pair_refs]
         gate = jnp.dot(normed[0], gate_weights_ref[...], preferred_element_type=jnp.float32)
         gate_ref[pl.ds(first, step)] = jax.nn.sigmoid(gate).reshape(step, columns, channels)
+        both = jnp.dot(normed[0], passed[2][...], preferred_element_type=jnp.float32)
+        for row, part in enumerate(masked_right(both, tokens, row_start + first, col_pos, columns)):
+            right_ref[first + row] = part
         for row in range(step):
             thirds = [piece[row * columns : (row + 1) * columns] for piece in normed]
             both = lax.dot_general(
@@ -141,7 +151,7 @@
     )
 
 
-def product_kernel(picks, rights, first, last, *refs):
+def product_kernel(picks, place, rights, first, last, *refs):
     right_refs, refs = refs[:rights], refs[rights:]
     left_ref, gate_ref, gain_ref, bias_ref, weights_ref, *done, out_ref = refs[: -5 if last else -3]
     right, product, updates = refs[-5:-2] if last else refs[-3:]
@@ -149,7 +159,11 @@
     hidden, rows, width = left_ref.shape
     count = right_refs[0].shape[0]
     apart = pitch(count)
-    even = (lax.axis_index("row") + lax.axis_index("col")) % 2 == 0
+    mine = place()
+
+    def row_of(source, token):
+        ref = right_refs[source]
+        return ref[token if ref.shape[0] == count else first + token]
 
     copies, start = [], 0
     for at, ref in enumerate(done):
@@ -160,10 +174,11 @@
 
     for token in range(count):
         pieces = []
-        for at_even, at_odd in picks:
-            piece = right_refs[at_even][token]
-            if at_odd != at_even:
-                piece = jnp.where(even, piece, right_refs[at_odd][token])
+        for sources in picks:
+            piece = row_of(sources[0], token)
+            for at, source in enumerate(sources[1:], 1):
+                if source != sources[at - 1]:
+                    piece = jnp.where(mine >= at, row_of(source, token), piece)
             pieces.append(piece)
         one = turned(pieces, width)
         for at in range(0, width, LANES):
@@ -228,7 +243,7 @@
 
 
 def hops():
-    out, near, cross = [], [], []
+    out, near, cross, early = [], [], [], []
     for r in range(4):
         for c in range(4):
             before = (c - 1) % 4
@@ -238,8 +253,14 @@
                 near.append(((r, c), (r ^ 1, c)))
             else:
                 near.append(((r, c), (r, before)))
-                cross.append(((r, c), (r ^ 1, before)))
-    return out, near, cross
+                (early if (r, c) in ((0, 1), (1, 2)) else cross).append(((r, c), (r ^ 1, before)))
+    return out, near, cross, early
+
+
+def hop_place():
+    row_pos, col_pos = lax.axis_index("row"), lax.axis_index("col")
+    odd = (row_pos + col_pos) % 2
+    return jnp.where((row_pos < 2) & (col_pos < 2), 2 * odd, odd)
 
 
 def move(array, pairs):
@@ -275,25 +296,26 @@
 
     arrived = []
     if by_hops:
-        out, near, cross = hops()
+        out, near, cross, early = hops()
         arrived.append(move(pair_state[: spans[0][1]], out))
     pairs = [pair_state]
     for _ in range(window - 1):
         pairs.append(shifted(pairs[-1], "col", -1))
     passed = [in_gain, in_bias, in_weights[:, 2 * hidden :], out_weights]
     later = spans[1][0]
-    left, gate, later_pair, *handed = pl.pallas_call(
+    left, gate, right, later_pair, *handed = pl.pallas_call(
         functools.partial(left_kernel, window, later),
         out_shape=[
             jax.ShapeDtypeStruct((hidden, rows, width), jnp.bfloat16),
             jax.ShapeDtypeStruct((rows, columns, channels), jnp.float32),
+            jax.ShapeDtypeStruct((rows, columns, hidden), jnp.bfloat16),
             jax.ShapeDtypeStruct((rows - later, columns, channels), jnp.bfloat16),
         ]
         + [jax.ShapeDtypeStruct(array.shape, array.dtype) for array in passed],
         in_specs=[SMEM] + [VMEM] * (window + 8),
-        out_specs=[VMEM] * 7,
+        out_specs=[VMEM] * 8,
         scratch_shapes=[pltpu.VMEM((width // LANES, hidden * pitch(rows), LANES), jnp.float32)],
-        compiler_params=params((window + 2) * block, 6 * hidden * rows * width),
+        compiler_params=params((window + 4) * block, 6 * hidden * rows * width),
         cost_estimate=cost(
             4 * window * tokens * channels * hidden, 6 * rows * width * hidden
         ),
@@ -313,16 +335,16 @@
         )(token_count, pair_state, in_gain, in_bias, right_weights, *far)
 
     if by_hops:
+        early = move(right, early)
         arrived.append(move(later_pair, out))
         bands = []
         for (first, count), far in zip(spans, arrived):
             held = right_of(first, count, far)
-            bands.append([held, move(held, near), move(held, cross)])
-        picks = [(0, 1), (1, 2)]
+            bands.append([held, move(held, near), move(held, cross), early])
+        picks, place = [(0, 1, 1), (1, 2, 3)], hop_place
     else:
-        bands, picks = band_by_sums(
-            right_of(0, rows), spans, window, row_count, col_count, columns
-        )
+        bands, picks = band_by_sums(right, spans, window, row_count, col_count, columns)
+        place = lambda: 0
 
     done = []
     for (first, count), band in zip(spans, bands):
@@ -338,7 +360,7 @@
                 pltpu.SemaphoreType.DMA((len(done) + rows // 16,)),
             ]
         filled = pl.pallas_call(
-            functools.partial(product_kernel, picks, len(band), first, last),
+            functools.partial(product_kernel, picks, place, len(band), first, last),
             out_shape=jax.ShapeDtypeStruct(
                 (rows, columns if last else count, channels), jnp.bfloat16
             ),

time: 44.7 us -> 47 us (1.051)
  waiting for transfers between devices: 11.7 us -> 16.1 us
  starting transfers between devices: 15.1 us -> 12.5 us
    ppermute x6 -> x7, waiting for transfers between devices: 9.73 us -> 14.1 us  [move(): lax.ppermute(array, ('row', 'col'), [(r * 4 + c, to_r * 4 + to_c) for (r,...]
    ppermute x6 -> x7, starting transfers between devices: 15.1 us -> 12.4 us  [move(): lax.ppermute(array, ('row', 'col'), [(r * 4 + c, to_r * 4 + to_c) for (r,...]
  transfers between devices with their start and end apart: 7 -> 8, of which waited for: 4 -> 3; matrix products, arithmetic and copies ran while one was open for 5% -> 4% of each run, Pallas kernels for 17% -> 17%
where the time goes in v12:
time: 47 us; the launch traced here: 46.5 us
  waiting for transfers between devices  16.1 us (34%)
  starting transfers between devices  12.5 us (27%)
  Pallas kernels  11.2 us (24%)
  local copies, waits for them, and re-layouts  5.92 us (13%)
  between operations  0.81 us (2%)
    ppermute x7, waiting for transfers between devices, move(): lax.ppermute(array, ('row', 'col'), [(r * 4 + c, to_r * 4 + to_c) for (r,...  14.1 us
    ppermute x7, starting transfers between devices, move(): lax.ppermute(array, ('row', 'col'), [(r * 4 + c, to_r * 4 + to_c) for (r,...  12.4 us
    pallas_call x2, Pallas kernels, on_device(): pl.pallas_call(functools.partial(product_kernel, picks, place, len(band),...  7.02 us
    unnamed x15, local copies, waits for them, and re-layouts  4.01 us
    pallas_call x1, Pallas kernels, on_device(): pl.pallas_call(functools.partial(left_kernel, window, later), out_shape=[...  3 us
    ppermute x1, waiting for transfers between devices, shifted(): lax.ppermute(array, axis, [(i, (i + by) % devices) for i in range(devices)])  1.98 us
    pallas_call x2, Pallas kernels, right_of(): pl.pallas_call(functools.partial(right_kernel, by_hops, first), out_shape...  1.2 us
    slice x1, local copies, waits for them, and re-layouts, on_device(): arrived.append(move(pair_state[:spans[0][1]], out))  1.02 us
  transfers between devices with their start and end apart: 8, of which 3 were waited for; matrix products, arithmetic and copies ran while one was open for 4% of the time, Pallas kernels for 17%

profile of v12, /device:TPU:1, one launch (start us, length us, event | category | flops | bytes accessed | tf_op | source)
XLA Modules:
  0.0 46.5 jit_solution(7482826093951243049)
XLA Ops:
  0.0 0.1 collective-permute-start
  0.1 1.0 %slice.11 = bf16[32,48,128]{2,1,0:T(8,128)(2,1)S(1)} slice(bf16[48,48,128]{2,1,0:T(8,128)(2,1)} %pair_ref.3), slice={[0:32], [0:48], [0:128]} | slice | bytes 786432 | tf_op jit(solution)/shard_map/slice | solution.py:300
  1.1 5.7 %collective-permute-start.5 = (bf16[32,48,128]{2,1,0:T(8,128)(2,1)S(1)}, bf16[32,48,128]{2,1,0:T(8,128)(2,1)S(1)}, u32[]{:S(2)}, u32[]{:S(2)}) collective-permute-start(bf16[32,48,128]{2,1,0:T(8,128)(2,1)S(1)} %slice.11), channel_id=1, source_target_pairs={{0,8},{1,9},{5,13},{6,14},{10,2},{11,3},{12,4},{15,7},{16,24},{17,... | collective-permute-start | bytes 1179656 | tf_op jit(solution)/shard_map/ppermute | solution.py:267
  7.4 0.9 %fusion = (bf16[128,256]{1,0:T(8,128)(2,1)S(1)}, bf16[128,256]{1,0:T(8,128)(2,1)S(1)}) fusion(bf16[128,512]{1,0:T(8,128)(2,1)} %param.13), kind=kLoop, calls=%fused_computation | loop fusion | bytes 262144 | tf_op jit(solution)/shard_map/slice | solution.py:304
  8.3 0.1 copy.11
  8.4 2.0 %collective-permute-done.refs_1_ = bf16[48,48,128]{2,1,0:T(8,128)(2,1)S(1)} collective-permute-done((bf16[48,48,128]{2,1,0:T(8,128)(2,1)}, bf16[48,48,128]{2,1,0:T(8,128)(2,1)S(1)}, u32[]{:S(2)}, u32[]{:S(2)}) %collective-permute-start) | collective-permute-done | bytes 589856 | tf_op jit(solution)/shard_map/ppermute | solution.py:33
  10.4 1.1 %copy-done = bf16[48,48,128]{2,1,0:T(8,128)(2,1)S(1)} copy-done((bf16[48,48,128]{2,1,0:T(8,128)(2,1)S(1)}, bf16[48,48,128]{2,1,0:T(8,128)(2,1)}, u32[]{:S(2)}) %copy-start) | copy-done | bytes 589848
  11.5 0.8 %copy-done.1 = bf16[128,128]{1,0:T(8,128)(2,1)S(1)} copy-done((bf16[128,128]{1,0:T(8,128)(2,1)S(1)}, bf16[128,128]{1,0:T(8,128)(2,1)}, u32[]{:S(2)}) %copy-start.1) | copy-done | bytes 32792
  12.2 0.8 %copy-done.2 = bf16[128,128]{1,0:T(8,128)(2,1)S(1)} copy-done((bf16[128,128]{1,0:T(8,128)(2,1)S(1)}, bf16[128,128]{1,0:T(8,128)(2,1)}, u32[]{:S(2)}) %copy-start.2) | copy-done | bytes 32792
  13.0 0.7 %copy-done.3 = f32[128]{0:T(128)S(1)} copy-done((f32[128]{0:T(128)S(1)}, f32[128]{0:T(128)}, u32[]{:S(2)}) %copy-start.3) | copy-done | bytes 536
  13.6 0.7 %copy-done.4 = f32[128]{0:T(128)S(1)} copy-done((f32[128]{0:T(128)S(1)}, f32[128]{0:T(128)}, u32[]{:S(2)}) %copy-start.4) | copy-done | bytes 536
  14.3 3.0 %left_and_gate.1 = (bf16[128,48,128]{2,1,0:T(8,128)(2,1)S(1)}, f32[48,48,128]{2,1,0:T(8,128)S(1)}, bf16[48,48,128]{2,1,0:T(8,128)(2,1)S(1)}, bf16[16,48,128]{2,1...) custom-call(s32[1]{0:T(128)S(6)} %copy.12.tokens_ref, ...), custom_call_target="tpu_custom_call" | custom-call | flops 301989888 | bytes 4718592 | tf_op jit(solution)/shard_map/left_and_gate/pallas_call | solution.py:306
  17.3 0.0 copy-start.5
  17.3 0.0 copy-start.6
  17.3 2.9 %collective-permute-start.4 = (bf16[48,48,128]{2,1,0:T(8,128)(2,1)S(1)}, bf16[48,48,128]{2,1,0:T(8,128)(2,1)S(1)}, u32[]{:S(2)}, u32[]{:S(2)}) collective-permute-start(bf16[48,48,128]{2,1,0:T(8,128)(2,1)S(1)} %get-tuple-element.17), channel_id=1, source_target_pairs={{1,4},{6,1},{17,20},{22,17}} | collective-permute-start | bytes 1769480 | tf_op jit(solution)/shard_map/ppermute | solution.py:267
  20.2 2.3 %collective-permute-start.1 = (bf16[16,48,128]{2,1,0:T(8,128)(2,1)S(1)}, bf16[16,48,128]{2,1,0:T(8,128)(2,1)S(1)}, u32[]{:S(2)}, u32[]{:S(2)}) collective-permute-start(bf16[16,48,128]{2,1,0:T(8,128)(2,1)S(1)} %get-tuple-element.16), channel_id=1, source_target_pairs={{0,8},{1,9},{5,13},{6,14},{10,2},{11,3},{12,4},{15,7},{16,24},{17,... | collective-permute-start | bytes 589832 | tf_op jit(solution)/shard_map/ppermute | solution.py:267
  22.6 0.0 collective-permute-done.5.refs_0_
  22.6 0.7 %right.3.refs_0_ = bf16[32,48,128]{2,1,0:T(8,128)(2,1)S(1)} custom-call(s32[1]{0:T(128)S(6)} %copy.12.tokens_ref, bf16[48,48,128]{2,1,0:T(8,128)(2,1)S(1)} %copy-done, f32[1,128]{1,0:T(1,128)S(1)} %get-tuple-element.13.gain_ref, f32[1,128]{1,0:T(1,128)S(1)} %get-tuple-element.14.bias_ref, bf16[128,256]{1,0:T(8,128)(2,1)S(1)} %get-tuple-element.15.weights_ref, ...), custom_call_target="tpu_custom_call" | custom-call | flops 100663296 | bytes 1179648 | tf_op jit(solution)/shard_map/right/pallas_call | solution.py:327
  23.3 0.1 collective-permute-start.6
  23.4 0.7 %collective-permute-start.7 = (bf16[32,48,128]{2,1,0:T(8,128)(2,1)S(1)}, bf16[32,48,128]{2,1,0:T(8,128)(2,1)S(1)}, u32[]{:S(2)}, u32[]{:S(2)}) collective-permute-start(bf16[32,48,128]{2,1,0:T(8,128)(2,1)S(1)} %right.3.refs_0_), channel_id=1, source_target_pairs={{3,6},{4,3},{9,12},{11,14},{12,11},{14,9},{19,22},{20,19},{25,28},... | collective-permute-start | bytes 1179656 | tf_op jit(solution)/shard_map/ppermute | solution.py:267
  24.1 11.1 %collective-permute-done.1.refs_0_ = bf16[16,48,128]{2,1,0:T(8,128)(2,1)S(1)} collective-permute-done((bf16[16,48,128]{2,1,0:T(8,128)(2,1)S(1)}, bf16[16,48,128]{2,1,0:T(8,128)(2,1)S(1)}, u32[]{:S(2)}, u32[]{:S(2)}) %collective-permute-start.1) | collective-permute-done | bytes 196640 | tf_op jit(solution)/shard_map/ppermute | solution.py:267
  35.2 0.5 %right.2.refs_0_ = bf16[16,48,128]{2,1,0:T(8,128)(2,1)S(1)} custom-call(s32[1]{0:T(128)S(6)} %copy.12.tokens_ref, bf16[48,48,128]{2,1,0:T(8,128)(2,1)S(1)} %copy-done, f32[1,128]{1,0:T(1,128)S(1)} %get-tuple-element.13.gain_ref, f32[1,128]{1,0:T(1,128)S(1)} %get-tuple-element.14.bias_ref, bf16[128,256]{1,0:T(8,128)(2,1)S(1)} %get-tuple-element.15.weights_ref, ...), custom_call_target="tpu_custom_call" | custom-call | flops 50331648 | bytes 589824 | tf_op jit(solution)/shard_map/right/pallas_call | solution.py:327
  35.7 0.1 collective-permute-start.2
  35.7 0.7 %collective-permute-start.3 = (bf16[16,48,128]{2,1,0:T(8,128)(2,1)S(1)}, bf16[16,48,128]{2,1,0:T(8,128)(2,1)S(1)}, u32[]{:S(2)}, u32[]{:S(2)}) collective-permute-start(bf16[16,48,128]{2,1,0:T(8,128)(2,1)S(1)} %right.2.refs_0_), channel_id=1, source_target_pairs={{3,6},{4,3},{9,12},{11,14},{12,11},{14,9},{19,22},{20,19},{25,28},... | collective-permute-start | bytes 589832 | tf_op jit(solution)/shard_map/ppermute | solution.py:267
  36.4 0.0 collective-permute-done.6.refs_1_
  36.4 0.0 collective-permute-done.7.refs_2_
  36.5 3.0 %collective-permute-done.4.refs_3_ = bf16[48,48,128]{2,1,0:T(8,128)(2,1)S(1)} collective-permute-done((bf16[48,48,128]{2,1,0:T(8,128)(2,1)S(1)}, bf16[48,48,128]{2,1,0:T(8,128)(2,1)S(1)}, u32[]{:S(2)}, u32[]{:S(2)}) %collective-permute-start.4) | collective-permute-done | bytes 589856 | tf_op jit(solution)/shard_map/ppermute | solution.py:267
  39.5 0.0 copy-done.5
  39.5 3.7 %product.2.refs_9_ = bf16[48,32,128]{2,1,0:T(8,128)(2,1)S(1)} custom-call(bf16[32,48,128]{2,1,0:T(8,128)(2,1)S(1)} %right.3.refs_0_, bf16[32,48,128]{2,1,0:T(8,128)(2,1)S(1)} %collective-permute-done.6.refs_1_, bf16[32,48,128]{2,1,0:T(8,128)(2,1)S(1)} %collective-permute-done.7.refs_2_, bf16[48,48,128]{2,1,0:T(8,128)(2,1)S(1)} %collective-permute-done.4.refs_3_, ...), custom_call_target="tpu_custom_call" | custom-call | flops 37748736 | bytes 2359296 | tf_op jit(solution)/shard_map/product/pallas_call | solution.py:362
  43.2 0.0 collective-permute-done.2.refs_1_
  43.2 0.0 collective-permute-done.3.refs_2_
  43.2 3.3 %product.3 = bf16[48,48,128]{2,1,0:T(8,128)(2,1)} custom-call(bf16[16,48,128]{2,1,0:T(8,128)(2,1)S(1)} %right.2.refs_0_, bf16[16,48,128]{2,1,0:T(8,128)(2,1)S(1)} %collective-permute-done.2.refs_1_, bf16[16,48,128]{2,1,0:T(8,128)(2,1)S(1)} %collective-permute-done.3.refs_2_, bf16[48,48,128]{2,1,0:T(8,128)(2,1)S(1)} %collective-permute-done.4.refs_3_, ...), custom_call_target="tpu_custom_call" | custom-call | flops 18874368 | bytes 2359296 | tf_op jit(solution)/shard_map/product/pallas_call | solution.py:362
  (6 shorter events, 0.0 us)
Async XLA Ops:
  0.0 10.4 %collective-permute-start = (bf16[48,48,128]{2,1,0:T(8,128)(2,1)}, bf16[48,48,128]{2,1,0:T(8,128)(2,1)S(1)}, u32[]{:S(2)}, u32[]{:S(2)}) collective-permute-start(bf16[48,48,128]{2,1,0:T(8,128)(2,1)} %pair_ref.3), channel_id=1, source_target_pairs={{0,3},{1,0},{2,1},{3,2},{4,7},{5,4},{6,5},{7,6},{8,11},{9,8},{10,9... | collective-permute-start | bytes 1769480 | tf_op jit(solution)/shard_map/ppermute | solution.py:33
  1.1 21.5 %collective-permute-start.5 = (bf16[32,48,128]{2,1,0:T(8,128)(2,1)S(1)}, bf16[32,48,128]{2,1,0:T(8,128)(2,1)S(1)}, u32[]{:S(2)}, u32[]{:S(2)}) collective-permute-start(bf16[32,48,128]{2,1,0:T(8,128)(2,1)S(1)} %slice.11), channel_id=1, source_target_pairs={{0,8},{1,9},{5,13},{6,14},{10,2},{11,3},{12,4},{15,7},{16,24},{17,... | collective-permute-start | bytes 1179656 | tf_op jit(solution)/shard_map/ppermute | solution.py:267
  10.4 1.1 %copy-start = (bf16[48,48,128]{2,1,0:T(8,128)(2,1)S(1)}, bf16[48,48,128]{2,1,0:T(8,128)(2,1)}, u32[]{:S(2)}) copy-start(bf16[48,48,128]{2,1,0:T(8,128)(2,1)} %pair_ref.3) | copy-start | bytes 1769476
  11.5 0.8 %copy-start.1 = (bf16[128,128]{1,0:T(8,128)(2,1)S(1)}, bf16[128,128]{1,0:T(8,128)(2,1)}, u32[]{:S(2)}) copy-start(bf16[128,128]{1,0:T(8,128)(2,1)} %refs_5_.1) | copy-start | bytes 98308
  12.2 0.8 %copy-start.2 = (bf16[128,128]{1,0:T(8,128)(2,1)S(1)}, bf16[128,128]{1,0:T(8,128)(2,1)}, u32[]{:S(2)}) copy-start(bf16[128,128]{1,0:T(8,128)(2,1)} %refs_9_.1) | copy-start | bytes 98308
  13.0 0.7 %copy-start.3 = (f32[128]{0:T(128)S(1)}, f32[128]{0:T(128)}, u32[]{:S(2)}) copy-start(f32[128]{0:T(128)} %param.11) | copy-start | bytes 1540
  13.6 0.7 %copy-start.4 = (f32[128]{0:T(128)S(1)}, f32[128]{0:T(128)}, u32[]{:S(2)}) copy-start(f32[128]{0:T(128)} %param.12) | copy-start | bytes 1540
  17.3 22.2 %copy-start.5 = (f32[128]{0:T(128)S(1)}, f32[128]{0:T(128)}, u32[]{:S(2)}) copy-start(f32[128]{0:T(128)} %refs_6_.3) | copy-start | bytes 1540
  17.3 22.1 %copy-start.6 = (f32[128]{0:T(128)S(1)}, f32[128]{0:T(128)}, u32[]{:S(2)}) copy-start(f32[128]{0:T(128)} %refs_7_.3) | copy-start | bytes 1540
  17.3 22.1 %collective-permute-start.4 = (bf16[48,48,128]{2,1,0:T(8,128)(2,1)S(1)}, bf16[48,48,128]{2,1,0:T(8,128)(2,1)S(1)}, u32[]{:S(2)}, u32[]{:S(2)}) collective-permute-start(bf16[48,48,128]{2,1,0:T(8,128)(2,1)S(1)} %get-tuple-element.17), channel_id=1, source_target_pairs={{1,4},{6,1},{17,20},{22,17}} | collective-permute-start | bytes 1769480 | tf_op jit(solution)/shard_map/ppermute | solution.py:267
  20.2 15.0 %collective-permute-start.1 = (bf16[16,48,128]{2,1,0:T(8,128)(2,1)S(1)}, bf16[16,48,128]{2,1,0:T(8,128)(2,1)S(1)}, u32[]{:S(2)}, u32[]{:S(2)}) collective-permute-start(bf16[16,48,128]{2,1,0:T(8,128)(2,1)S(1)} %get-tuple-element.16), channel_id=1, source_target_pairs={{0,8},{1,9},{5,13},{6,14},{10,2},{11,3},{12,4},{15,7},{16,24},{17,... | collective-permute-start | bytes 589832 | tf_op jit(solution)/shard_map/ppermute | solution.py:267
  23.3 13.1 %collective-permute-start.6 = (bf16[32,48,128]{2,1,0:T(8,128)(2,1)S(1)}, bf16[32,48,128]{2,1,0:T(8,128)(2,1)S(1)}, u32[]{:S(2)}, u32[]{:S(2)}) collective-permute-start(bf16[32,48,128]{2,1,0:T(8,128)(2,1)S(1)} %right.3.refs_0_), channel_id=1, source_target_pairs={{0,4},{1,0},{2,6},{3,2},{4,7},{5,1},{6,5},{7,3},{8,12},{9,8},{10,1... | collective-permute-start | bytes 1179656 | tf_op jit(solution)/shard_map/ppermute | solution.py:267
  23.4 13.1 %collective-permute-start.7 = (bf16[32,48,128]{2,1,0:T(8,128)(2,1)S(1)}, bf16[32,48,128]{2,1,0:T(8,128)(2,1)S(1)}, u32[]{:S(2)}, u32[]{:S(2)}) collective-permute-start(bf16[32,48,128]{2,1,0:T(8,128)(2,1)S(1)} %right.3.refs_0_), channel_id=1, source_target_pairs={{3,6},{4,3},{9,12},{11,14},{12,11},{14,9},{19,22},{20,19},{25,28},... | collective-permute-start | bytes 1179656 | tf_op jit(solution)/shard_map/ppermute | solution.py:267
  35.7 7.5 %collective-permute-start.2 = (bf16[16,48,128]{2,1,0:T(8,128)(2,1)S(1)}, bf16[16,48,128]{2,1,0:T(8,128)(2,1)S(1)}, u32[]{:S(2)}, u32[]{:S(2)}) collective-permute-start(bf16[16,48,128]{2,1,0:T(8,128)(2,1)S(1)} %right.2.refs_0_), channel_id=1, source_target_pairs={{0,4},{1,0},{2,6},{3,2},{4,7},{5,1},{6,5},{7,3},{8,12},{9,8},{10,1... | collective-permute-start | bytes 589832 | tf_op jit(solution)/shard_map/ppermute | solution.py:267
  35.7 7.5 %collective-permute-start.3 = (bf16[16,48,128]{2,1,0:T(8,128)(2,1)S(1)}, bf16[16,48,128]{2,1,0:T(8,128)(2,1)S(1)}, u32[]{:S(2)}, u32[]{:S(2)}) collective-permute-start(bf16[16,48,128]{2,1,0:T(8,128)(2,1)S(1)} %right.2.refs_0_), channel_id=1, source_target_pairs={{3,6},{4,3},{9,12},{11,14},{12,11},{14,9},{19,22},{20,19},{25,28},... | collective-permute-start | bytes 589832 | tf_op jit(solution)/shard_map/ppermute | solution.py:267

commit v13 on v12

--- a/solution.py
+++ b/solution.py
@@ -51,26 +51,18 @@
     return layer_norm(values, gain_ref[...], bias_ref[...]).astype(jnp.bfloat16)
 
 
-def right_kernel(hops, first, tokens_ref, pair_ref, gain_ref, bias_ref, weights_ref, *refs):
-    out_ref = refs[-1]
-    count, columns, hidden = out_ref.shape
-    row_pos, col_pos = lax.axis_index("row"), lax.axis_index("col")
-    tokens = tokens_ref[0]
-    block_row = row_pos
-    if hops:
-        is_root = (col_pos - row_pos + 4) % 4 < 2
-        block_row = jnp.where((row_pos + col_pos) % 2 == 0, col_pos, (col_pos + 3) % 4)
-    row_start = block_row * pair_ref.shape[0] + first
+def mine_kernel(first, tokens_ref, far_ref, near_ref, gain_ref, bias_ref, weights_ref, out_ref):
+    count, columns, _ = out_ref.shape
+    col_pos, place = lax.axis_index("col"), hop_place()
+    third_block = jnp.where((place == 0) | (place == 3), (col_pos + 1) % 4, col_pos)
+    row_token = col_pos * columns + first
     step = 4
     for at in range(0, count, step):
-        block = pair_ref[pl.ds(first + at, step)]
-        if hops:
-            block = jnp.where(is_root, block, refs[0][pl.ds(at, step)])
+        block = jnp.where(place < 2, near_ref[pl.ds(at, step)], far_ref[pl.ds(at, step)])
         normed = normed_rows(block, gain_ref, bias_ref)
-        both = jnp.dot(
-            normed, weights_ref[...], preferred_element_type=jnp.float32
-        )
-        for row, part in enumerate(masked_right(both, tokens, row_start + at, col_pos, columns)):
+        both = jnp.dot(normed, weights_ref[...], preferred_element_type=jnp.float32)
+        parts = masked_right(both, tokens_ref[0], row_token + at, third_block, columns)
+        for row, part in enumerate(parts):
             out_ref[at + row] = part
 
 
@@ -151,13 +143,12 @@
     )
 
 
-def product_kernel(picks, place, rights, first, last, *refs):
+def product_kernel(picks, place, rights, first, count, last, *refs):
     right_refs, refs = refs[:rights], refs[rights:]
     left_ref, gate_ref, gain_ref, bias_ref, weights_ref, *done, out_ref = refs[: -5 if last else -3]
     right, product, updates = refs[-5:-2] if last else refs[-3:]
     result, sent = refs[-2:] if last else (out_ref, None)
     hidden, rows, width = left_ref.shape
-    count = right_refs[0].shape[0]
     apart = pitch(count)
     mine = place()
 
@@ -243,24 +234,21 @@
 
 
 def hops():
-    out, near, cross, early = [], [], [], []
-    for r in range(4):
-        for c in range(4):
-            before = (c - 1) % 4
-            if (c - r) % 4 < 2:
-                out.append(((r, c), (r ^ 2, c)))
-            if (r + c) % 2 == 0:
-                near.append(((r, c), (r ^ 1, c)))
-            else:
-                near.append(((r, c), (r, before)))
-                (early if (r, c) in ((0, 1), (1, 2)) else cross).append(((r, c), (r ^ 1, before)))
-    return out, near, cross, early
+    near, far, share = [], [], []
+    for c in range(4):
+        first, second = (c, c), (c, (c + 1) % 4)
+        inner, outer = ((2, c), (3, c)) if c < 2 else ((1, c), (0, c))
+        near += [(first, (c ^ 1, c)), (second, first)]
+        far += [(first, inner), (second, outer)]
+        share += [(inner, outer), (outer, inner), (first, (c ^ 1, c))]
+    return near, far, share
 
 
 def hop_place():
-    row_pos, col_pos = lax.axis_index("row"), lax.axis_index("col")
-    odd = (row_pos + col_pos) % 2
-    return jnp.where((row_pos < 2) & (col_pos < 2), 2 * odd, odd)
+    row_pos = lax.axis_index("row")
+    near = row_pos ^ lax.axis_index("col")
+    inner = (row_pos == 1) | (row_pos == 2)
+    return jnp.where(near < 2, near, jnp.where(inner, 2, 3))
 
 
 def move(array, pairs):
@@ -294,10 +282,10 @@
     last = 16
     spans = [(0, columns - last), (columns - last, last)]
 
-    arrived = []
     if by_hops:
-        out, near, cross, early = hops()
-        arrived.append(move(pair_state[: spans[0][1]], out))
+        near, far, share = hops()
+        soon = pair_state[: spans[0][1]]
+        arrived = [(move(soon, far), move(soon, near))]
     pairs = [pair_state]
     for _ in range(window - 1):
         pairs.append(shifted(pairs[-1], "col", -1))
@@ -323,25 +311,25 @@
     )(token_count, *pairs, in_gain, in_bias, in_weights[:, : 2 * hidden].T, gate_weights, *passed)
     in_gain, in_bias, right_weights, out_weights = handed
 
-    def right_of(first, count, *far):
+    def mine_of(first, far_pair, near_pair):
+        count = near_pair.shape[0]
         return pl.pallas_call(
-            functools.partial(right_kernel, by_hops, first),
+            functools.partial(mine_kernel, first),
             out_shape=jax.ShapeDtypeStruct((count, columns, hidden), jnp.bfloat16),
-            in_specs=[SMEM] + [VMEM] * (4 + len(far)),
+            in_specs=[SMEM] + [VMEM] * 5,
             out_specs=VMEM,
             compiler_params=params(2 * block),
             cost_estimate=cost(4 * count * columns * channels * hidden, 6 * count * columns * channels),
-            name="right",
-        )(token_count, pair_state, in_gain, in_bias, right_weights, *far)
+            name="mine",
+        )(token_count, far_pair, near_pair, in_gain, in_bias, right_weights)
 
     if by_hops:
-        early = move(right, early)
-        arrived.append(move(later_pair, out))
+        arrived.append((move(later_pair, far), move(later_pair, near)))
         bands = []
-        for (first, count), far in zip(spans, arrived):
-            held = right_of(first, count, far)
-            bands.append([held, move(held, near), move(held, cross), early])
-        picks, place = [(0, 1, 1), (1, 2, 3)], hop_place
+        for (first, _), pieces in zip(spans, arrived):
+            mine = mine_of(first, *pieces)
+            bands.append([right, mine, move(mine, share)])
+        picks, place = [(0, 1, 1, 2), (1, 2, 2, 1)], hop_place
     else:
         bands, picks = band_by_sums(right, spans, window, row_count, col_count, columns)
         place = lambda: 0
@@ -360,7 +348,7 @@
                 pltpu.SemaphoreType.DMA((len(done) + rows // 16,)),
             ]
         filled = pl.pallas_call(
-            functools.partial(product_kernel, picks, place, len(band), first, last),
+            functools.partial(product_kernel, picks, place, len(band), first, count, last),
             out_shape=jax.ShapeDtypeStruct(
                 (rows, columns if last else count, channels), jnp.bfloat16
             ),

time: 47 us -> 46.6 us (level)
  the two profiles are of different devices: /device:TPU:1 before, /device:TPU:16 now
where the time goes in v13:
time: 46.6 us; the launch traced here: 46.1 us
  starting transfers between devices  18 us (39%)
  Pallas kernels  11.2 us (24%)
  waiting for transfers between devices  10.1 us (22%)
  local copies, waits for them, and re-layouts  5.95 us (13%)
  between operations  0.79 us (2%)
    ppermute x6, starting transfers between devices, move(): lax.ppermute(array, ('row', 'col'), [(r * 4 + c, to_r * 4 + to_c) for (r,...  17 us
    ppermute x6, waiting for transfers between devices, move(): lax.ppermute(array, ('row', 'col'), [(r * 4 + c, to_r * 4 + to_c) for (r,...  7.13 us
    pallas_call x2, Pallas kernels, on_device(): pl.pallas_call(functools.partial(product_kernel, picks, place, len(band),...  7 us
    unnamed x15, local copies, waits for them, and re-layouts  4.01 us
    ppermute x1, waiting for transfers between devices, shifted(): lax.ppermute(array, axis, [(i, (i + by) % devices) for i in range(devices)])  3.01 us
    pallas_call x1, Pallas kernels, on_device(): pl.pallas_call(functools.partial(left_kernel, window, later), out_shape=[...  3 us
    pallas_call x2, Pallas kernels, mine_of(): pl.pallas_call(functools.partial(mine_kernel, first), out_shape=jax.Shape...  1.22 us
    slice x1, local copies, waits for them, and re-layouts, on_device(): soon = pair_state[:spans[0][1]]  1.05 us
  transfers between devices with their start and end apart: 7, of which 2 were waited for; matrix products, arithmetic and copies ran while one was open for 4% of the time, Pallas kernels for 17%

profile of v13, /device:TPU:16, one launch (start us, length us, event | category | flops | bytes accessed | tf_op | source)
XLA Modules:
  0.0 46.1 jit_solution(15451545754609072729)
XLA Ops:
  0.0 1.0 %collective-permute-start = (bf16[48,48,128]{2,1,0:T(8,128)(2,1)}, bf16[48,48,128]{2,1,0:T(8,128)(2,1)S(1)}, u32[]{:S(2)}, u32[]{:S(2)}) collective-permute-start(bf16[48,48,128]{2,1,0:T(8,128)(2,1)} %refs_0_.1), channel_id=1, source_target_pairs={{0,3},{1,0},{2,1},{3,2},{4,7},{5,4},{6,5},{7,6},{8,11},{9,8},{10,9... | collective-permute-start | bytes 1769480 | tf_op jit(solution)/shard_map/ppermute | solution.py:33
  1.0 1.1 %slice.11 = bf16[32,48,128]{2,1,0:T(8,128)(2,1)S(1)} slice(bf16[48,48,128]{2,1,0:T(8,128)(2,1)} %refs_0_.1), slice={[0:32], [0:48], [0:128]} | slice | bytes 786432 | tf_op jit(solution)/shard_map/slice | solution.py:287
  2.0 1.3 %collective-permute-start.4 = (bf16[32,48,128]{2,1,0:T(8,128)(2,1)S(1)}, bf16[32,48,128]{2,1,0:T(8,128)(2,1)S(1)}, u32[]{:S(2)}, u32[]{:S(2)}) collective-permute-start(bf16[32,48,128]{2,1,0:T(8,128)(2,1)S(1)} %slice.11), channel_id=1, source_target_pairs={{0,8},{1,12},{5,9},{6,13},{10,6},{11,2},{15,7},{12,3},{16,24},{17,... | collective-permute-start | bytes 1179656 | tf_op jit(solution)/shard_map/ppermute | solution.py:255
  3.3 0.7 %collective-permute-start.5 = (bf16[32,48,128]{2,1,0:T(8,128)(2,1)S(1)}, bf16[32,48,128]{2,1,0:T(8,128)(2,1)S(1)}, u32[]{:S(2)}, u32[]{:S(2)}) collective-permute-start(bf16[32,48,128]{2,1,0:T(8,128)(2,1)S(1)} %slice.11), channel_id=1, source_target_pairs={{0,4},{1,0},{5,1},{6,5},{10,14},{11,10},{15,11},{12,15},{16,20},{1... | collective-permute-start | bytes 1179656 | tf_op jit(solution)/shard_map/ppermute | solution.py:255
  4.7 0.9 %fusion = (bf16[128,256]{1,0:T(8,128)(2,1)S(1)}, bf16[128,256]{1,0:T(8,128)(2,1)S(1)}) fusion(bf16[128,512]{1,0:T(8,128)(2,1)} %param.13), kind=kLoop, calls=%fused_computation | loop fusion | bytes 262144 | tf_op jit(solution)/shard_map/slice | solution.py:292
  5.5 0.1 copy.11
  5.7 3.0 %collective-permute-done.refs_1_ = bf16[48,48,128]{2,1,0:T(8,128)(2,1)S(1)} collective-permute-done((bf16[48,48,128]{2,1,0:T(8,128)(2,1)}, bf16[48,48,128]{2,1,0:T(8,128)(2,1)S(1)}, u32[]{:S(2)}, u32[]{:S(2)}) %collective-permute-start) | collective-permute-done | bytes 589856 | tf_op jit(solution)/shard_map/ppermute | solution.py:33
  8.7 1.1 %copy-done = bf16[48,48,128]{2,1,0:T(8,128)(2,1)S(1)} copy-done((bf16[48,48,128]{2,1,0:T(8,128)(2,1)S(1)}, bf16[48,48,128]{2,1,0:T(8,128)(2,1)}, u32[]{:S(2)}) %copy-start) | copy-done | bytes 589848
  9.7 0.0 copy-start.1
  9.7 0.8 %copy-done.1 = bf16[128,128]{1,0:T(8,128)(2,1)S(1)} copy-done((bf16[128,128]{1,0:T(8,128)(2,1)S(1)}, bf16[128,128]{1,0:T(8,128)(2,1)}, u32[]{:S(2)}) %copy-start.1) | copy-done | bytes 32792
  10.5 0.0 copy-start.2
  10.5 0.8 %copy-done.2 = bf16[128,128]{1,0:T(8,128)(2,1)S(1)} copy-done((bf16[128,128]{1,0:T(8,128)(2,1)S(1)}, bf16[128,128]{1,0:T(8,128)(2,1)}, u32[]{:S(2)}) %copy-start.2) | copy-done | bytes 32792
  11.3 0.0 copy-start.3
  11.3 0.7 %copy-done.3 = f32[128]{0:T(128)S(1)} copy-done((f32[128]{0:T(128)S(1)}, f32[128]{0:T(128)}, u32[]{:S(2)}) %copy-start.3) | copy-done | bytes 536
  11.9 0.7 %copy-done.4 = f32[128]{0:T(128)S(1)} copy-done((f32[128]{0:T(128)S(1)}, f32[128]{0:T(128)}, u32[]{:S(2)}) %copy-start.4) | copy-done | bytes 536
  12.6 3.0 %left_and_gate.1 = (bf16[128,48,128]{2,1,0:T(8,128)(2,1)S(1)}, f32[48,48,128]{2,1,0:T(8,128)S(1)}, bf16[48,48,128]{2,1,0:T(8,128)(2,1)S(1)}, bf16[16,48,128]{2,1...) custom-call(s32[1]{0:T(128)S(6)} %copy.12.tokens_ref, ...), custom_call_target="tpu_custom_call" | custom-call | flops 301989888 | bytes 4718592 | tf_op jit(solution)/shard_map/left_and_gate/pallas_call | solution.py:294
  15.6 1.3 %collective-permute-start.1 = (bf16[16,48,128]{2,1,0:T(8,128)(2,1)S(1)}, bf16[16,48,128]{2,1,0:T(8,128)(2,1)S(1)}, u32[]{:S(2)}, u32[]{:S(2)}) collective-permute-start(bf16[16,48,128]{2,1,0:T(8,128)(2,1)S(1)} %get-tuple-element.14), channel_id=1, source_target_pairs={{0,8},{1,12},{5,9},{6,13},{10,6},{11,2},{15,7},{12,3},{16,24},{17,... | collective-permute-start | bytes 589832 | tf_op jit(solution)/shard_map/ppermute | solution.py:255
  16.9 0.7 %collective-permute-start.2 = (bf16[16,48,128]{2,1,0:T(8,128)(2,1)S(1)}, bf16[16,48,128]{2,1,0:T(8,128)(2,1)S(1)}, u32[]{:S(2)}, u32[]{:S(2)}) collective-permute-start(bf16[16,48,128]{2,1,0:T(8,128)(2,1)S(1)} %get-tuple-element.14), channel_id=1, source_target_pairs={{0,4},{1,0},{5,1},{6,5},{10,14},{11,10},{15,11},{12,15},{16,20},{1... | collective-permute-start | bytes 589832 | tf_op jit(solution)/shard_map/ppermute | solution.py:255
  17.6 0.0 collective-permute-done.4.far_ref
  17.6 0.0 collective-permute-done.5.near_ref
  17.6 0.7 %mine.3.refs_1_ = bf16[32,48,128]{2,1,0:T(8,128)(2,1)S(1)} custom-call(s32[1]{0:T(128)S(6)} %copy.12.tokens_ref, bf16[32,48,128]{2,1,0:T(8,128)(2,1)S(1)} %collective-permute-done.4.far_ref, bf16[32,48,128]{2,1,0:T(8,128)(2,1)S(1)} %collective-permute-done.5.near_ref, f32[1,128]{1,0:T(1,128)S(1)} %get-tuple-element.15.gain_ref, ...), custom_call_target="tpu_custom_call" | custom-call | flops 100663296 | bytes 1179648 | tf_op jit(solution)/shard_map/mine/pallas_call | solution.py:316
  18.3 10.7 %collective-permute-start.6 = (bf16[32,48,128]{2,1,0:T(8,128)(2,1)S(1)}, bf16[32,48,128]{2,1,0:T(8,128)(2,1)S(1)}, u32[]{:S(2)}, u32[]{:S(2)}) collective-permute-start(bf16[32,48,128]{2,1,0:T(8,128)(2,1)S(1)} %mine.3.refs_1_), channel_id=1, source_target_pairs={{8,12},{12,8},{0,4},{9,13},{13,9},{5,1},{6,2},{2,6},{10,14},{7,3},... | collective-permute-start | bytes 1179656 | tf_op jit(solution)/shard_map/ppermute | solution.py:255
  29.0 0.0 collective-permute-done.1.far_ref
  29.0 0.0 collective-permute-done.2.near_ref
  29.0 0.5 %mine.2.refs_1_ = bf16[16,48,128]{2,1,0:T(8,128)(2,1)S(1)} custom-call(s32[1]{0:T(128)S(6)} %copy.12.tokens_ref, bf16[16,48,128]{2,1,0:T(8,128)(2,1)S(1)} %collective-permute-done.1.far_ref, bf16[16,48,128]{2,1,0:T(8,128)(2,1)S(1)} %collective-permute-done.2.near_ref, f32[1,128]{1,0:T(1,128)S(1)} %get-tuple-element.15.gain_ref, ...), custom_call_target="tpu_custom_call" | custom-call | flops 50331648 | bytes 589824 | tf_op jit(solution)/shard_map/mine/pallas_call | solution.py:316
  29.5 2.4 %collective-permute-start.3 = (bf16[16,48,128]{2,1,0:T(8,128)(2,1)S(1)}, bf16[16,48,128]{2,1,0:T(8,128)(2,1)S(1)}, u32[]{:S(2)}, u32[]{:S(2)}) collective-permute-start(bf16[16,48,128]{2,1,0:T(8,128)(2,1)S(1)} %mine.2.refs_1_), channel_id=1, source_target_pairs={{8,12},{12,8},{0,4},{9,13},{13,9},{5,1},{6,2},{2,6},{10,14},{7,3},... | collective-permute-start | bytes 589832 | tf_op jit(solution)/shard_map/ppermute | solution.py:255
  31.9 7.1 %collective-permute-done.6.refs_2_ = bf16[32,48,128]{2,1,0:T(8,128)(2,1)S(1)} collective-permute-done((bf16[32,48,128]{2,1,0:T(8,128)(2,1)S(1)}, bf16[32,48,128]{2,1,0:T(8,128)(2,1)S(1)}, u32[]{:S(2)}, u32[]{:S(2)}) %collective-permute-start.6) | collective-permute-done | bytes 393248 | tf_op jit(solution)/shard_map/ppermute | solution.py:255
  39.0 0.0 copy-done.5
  39.0 0.0 copy-done.6
  39.0 3.7 %product.2.refs_8_ = bf16[48,32,128]{2,1,0:T(8,128)(2,1)S(1)} custom-call(bf16[48,48,128]{2,1,0:T(8,128)(2,1)S(1)} %get-tuple-element.13.refs_0_, bf16[32,48,128]{2,1,0:T(8,128)(2,1)S(1)} %mine.3.refs_1_, bf16[32,48,128]{2,1,0:T(8,128)(2,1)S(1)} %collective-permute-done.6.refs_2_, bf16[128,48,128]{2,1,0:T(8,128)(2,1)S(1)} %get-tuple-element.18.refs_3_, ...), custom_call_target="tpu_custom_call" | custom-call | flops 37748736 | bytes 2359296 | tf_op jit(solution)/shard_map/product/pallas_call | solution.py:350
  42.8 0.0 collective-permute-done.3.refs_2_
  42.8 3.3 %product.3 = bf16[48,48,128]{2,1,0:T(8,128)(2,1)} custom-call(bf16[48,48,128]{2,1,0:T(8,128)(2,1)S(1)} %get-tuple-element.13.refs_0_, bf16[16,48,128]{2,1,0:T(8,128)(2,1)S(1)} %mine.2.refs_1_, bf16[16,48,128]{2,1,0:T(8,128)(2,1)S(1)} %collective-permute-done.3.refs_2_, bf16[128,48,128]{2,1,0:T(8,128)(2,1)S(1)} %get-tuple-element.18.refs_3_, ...), custom_call_target="tpu_custom_call" | custom-call | flops 18874368 | bytes 2359296 | tf_op jit(solution)/shard_map/product/pallas_call | solution.py:350
  (4 shorter events, 0.0 us)
Async XLA Ops:
  0.0 8.7 %collective-permute-start = (bf16[48,48,128]{2,1,0:T(8,128)(2,1)}, bf16[48,48,128]{2,1,0:T(8,128)(2,1)S(1)}, u32[]{:S(2)}, u32[]{:S(2)}) collective-permute-start(bf16[48,48,128]{2,1,0:T(8,128)(2,1)} %refs_0_.1), channel_id=1, source_target_pairs={{0,3},{1,0},{2,1},{3,2},{4,7},{5,4},{6,5},{7,6},{8,11},{9,8},{10,9... | collective-permute-start | bytes 1769480 | tf_op jit(solution)/shard_map/ppermute | solution.py:33
  2.0 15.5 %collective-permute-start.4 = (bf16[32,48,128]{2,1,0:T(8,128)(2,1)S(1)}, bf16[32,48,128]{2,1,0:T(8,128)(2,1)S(1)}, u32[]{:S(2)}, u32[]{:S(2)}) collective-permute-start(bf16[32,48,128]{2,1,0:T(8,128)(2,1)S(1)} %slice.11), channel_id=1, source_target_pairs={{0,8},{1,12},{5,9},{6,13},{10,6},{11,2},{15,7},{12,3},{16,24},{17,... | collective-permute-start | bytes 1179656 | tf_op jit(solution)/shard_map/ppermute | solution.py:255
  3.3 14.3 %collective-permute-start.5 = (bf16[32,48,128]{2,1,0:T(8,128)(2,1)S(1)}, bf16[32,48,128]{2,1,0:T(8,128)(2,1)S(1)}, u32[]{:S(2)}, u32[]{:S(2)}) collective-permute-start(bf16[32,48,128]{2,1,0:T(8,128)(2,1)S(1)} %slice.11), channel_id=1, source_target_pairs={{0,4},{1,0},{5,1},{6,5},{10,14},{11,10},{15,11},{12,15},{16,20},{1... | collective-permute-start | bytes 1179656 | tf_op jit(solution)/shard_map/ppermute | solution.py:255
  8.7 1.1 %copy-start = (bf16[48,48,128]{2,1,0:T(8,128)(2,1)S(1)}, bf16[48,48,128]{2,1,0:T(8,128)(2,1)}, u32[]{:S(2)}) copy-start(bf16[48,48,128]{2,1,0:T(8,128)(2,1)} %refs_0_.1) | copy-start | bytes 1769476
  9.7 0.8 %copy-start.1 = (bf16[128,128]{1,0:T(8,128)(2,1)S(1)}, bf16[128,128]{1,0:T(8,128)(2,1)}, u32[]{:S(2)}) copy-start(bf16[128,128]{1,0:T(8,128)(2,1)} %refs_5_.3) | copy-start | bytes 98308
  10.5 0.8 %copy-start.2 = (bf16[128,128]{1,0:T(8,128)(2,1)S(1)}, bf16[128,128]{1,0:T(8,128)(2,1)}, u32[]{:S(2)}) copy-start(bf16[128,128]{1,0:T(8,128)(2,1)} %refs_9_.1) | copy-start | bytes 98308
  11.3 0.7 %copy-start.3 = (f32[128]{0:T(128)S(1)}, f32[128]{0:T(128)}, u32[]{:S(2)}) copy-start(f32[128]{0:T(128)} %param.11) | copy-start | bytes 1540
  11.9 0.7 %copy-start.4 = (f32[128]{0:T(128)S(1)}, f32[128]{0:T(128)}, u32[]{:S(2)}) copy-start(f32[128]{0:T(128)} %param.12) | copy-start | bytes 1540
  12.6 26.5 %copy-start.5 = (f32[128]{0:T(128)S(1)}, f32[128]{0:T(128)}, u32[]{:S(2)}) copy-start(f32[128]{0:T(128)} %refs_5_.5) | copy-start | bytes 1540
  12.6 26.5 %copy-start.6 = (f32[128]{0:T(128)S(1)}, f32[128]{0:T(128)}, u32[]{:S(2)}) copy-start(f32[128]{0:T(128)} %refs_6_.3) | copy-start | bytes 1540
  15.6 13.4 %collective-permute-start.1 = (bf16[16,48,128]{2,1,0:T(8,128)(2,1)S(1)}, bf16[16,48,128]{2,1,0:T(8,128)(2,1)S(1)}, u32[]{:S(2)}, u32[]{:S(2)}) collective-permute-start(bf16[16,48,128]{2,1,0:T(8,128)(2,1)S(1)} %get-tuple-element.14), channel_id=1, source_target_pairs={{0,8},{1,12},{5,9},{6,13},{10,6},{11,2},{15,7},{12,3},{16,24},{17,... | collective-permute-start | bytes 589832 | tf_op jit(solution)/shard_map/ppermute | solution.py:255
  16.9 12.1 %collective-permute-start.2 = (bf16[16,48,128]{2,1,0:T(8,128)(2,1)S(1)}, bf16[16,48,128]{2,1,0:T(8,128)(2,1)S(1)}, u32[]{:S(2)}, u32[]{:S(2)}) collective-permute-start(bf16[16,48,128]{2,1,0:T(8,128)(2,1)S(1)} %get-tuple-element.14), channel_id=1, source_target_pairs={{0,4},{1,0},{5,1},{6,5},{10,14},{11,10},{15,11},{12,15},{16,20},{1... | collective-permute-start | bytes 589832 | tf_op jit(solution)/shard_map/ppermute | solution.py:255
  18.3 20.7 %collective-permute-start.6 = (bf16[32,48,128]{2,1,0:T(8,128)(2,1)S(1)}, bf16[32,48,128]{2,1,0:T(8,128)(2,1)S(1)}, u32[]{:S(2)}, u32[]{:S(2)}) collective-permute-start(bf16[32,48,128]{2,1,0:T(8,128)(2,1)S(1)} %mine.3.refs_1_), channel_id=1, source_target_pairs={{8,12},{12,8},{0,4},{9,13},{13,9},{5,1},{6,2},{2,6},{10,14},{7,3},... | collective-permute-start | bytes 1179656 | tf_op jit(solution)/shard_map/ppermute | solution.py:255
  29.5 13.2 %collective-permute-start.3 = (bf16[16,48,128]{2,1,0:T(8,128)(2,1)S(1)}, bf16[16,48,128]{2,1,0:T(8,128)(2,1)S(1)}, u32[]{:S(2)}, u32[]{:S(2)}) collective-permute-start(bf16[16,48,128]{2,1,0:T(8,128)(2,1)S(1)} %mine.2.refs_1_), channel_id=1, source_target_pairs={{8,12},{12,8},{0,4},{9,13},{13,9},{5,1},{6,2},{2,6},{10,14},{7,3},... | collective-permute-start | bytes 589832 | tf_op jit(solution)/shard_map/ppermute | solution.py:255

commit v14 on v13

--- a/solution.py
+++ b/solution.py
@@ -78,13 +78,30 @@
     return parts
 
 
+def own_kernel(passes, tokens_ref, pair_ref, gate_weights_ref, *refs):
+    passed, (gate_ref, right_ref), handed = refs[:passes], refs[passes : passes + 2], refs[passes + 2 :]
+    gain_ref, bias_ref, right_weights_ref = passed[:3]
+    for source, target in zip(passed, handed):
+        target[...] = source[...]
+    rows, columns, channels = pair_ref.shape
+    row_start = lax.axis_index("row") * rows
+    step = 4
+    for first in range(0, rows, step):
+        normed = normed_rows(pair_ref[pl.ds(first, step)], gain_ref, bias_ref)
+        gate = jnp.dot(normed, gate_weights_ref[...], preferred_element_type=jnp.float32)
+        gate_ref[pl.ds(first, step)] = jax.nn.sigmoid(gate).reshape(step, columns, channels)
+        both = jnp.dot(normed, right_weights_ref[...], preferred_element_type=jnp.float32)
+        parts = masked_right(
+            both, tokens_ref[0], row_start + first, lax.axis_index("col"), columns
+        )
+        for row, part in enumerate(parts):
+            right_ref[first + row] = part
+
+
 def left_kernel(blocks, later, tokens_ref, *refs):
     pair_refs, refs = refs[:blocks], refs[blocks:]
-    gain_ref, bias_ref, weights_ref, gate_weights_ref, *passed, scratch = refs
-    passed, (left_ref, gate_ref, right_ref, later_ref), handed = passed[:4], passed[4:8], passed[8:]
+    gain_ref, bias_ref, weights_ref, left_ref, later_ref, scratch = refs
     later_ref[...] = pair_refs[0][pl.ds(later, later_ref.shape[0])]
-    for source, target in zip(passed, handed):
-        target[...] = source[...]
     rows, columns, channels = pair_refs[0].shape
     hidden, _, width = left_ref.shape
     tokens = tokens_ref[0]
@@ -101,11 +118,6 @@
     step = 4
     for first in range(0, rows, step):
         normed = [normed_rows(ref[pl.ds(first, step)], gain_ref, bias_ref) for ref in pair_refs]
-        gate = jnp.dot(normed[0], gate_weights_ref[...], preferred_element_type=jnp.float32)
-        gate_ref[pl.ds(first, step)] = jax.nn.sigmoid(gate).reshape(step, columns, channels)
-        both = jnp.dot(normed[0], passed[2][...], preferred_element_type=jnp.float32)
-        for row, part in enumerate(masked_right(both, tokens, row_start + first, col_pos, columns)):
-            right_ref[first + row] = part
         for row in range(step):
             thirds = [piece[row * columns : (row + 1) * columns] for piece in normed]
             both = lax.dot_general(
@@ -289,27 +301,36 @@
     pairs = [pair_state]
     for _ in range(window - 1):
         pairs.append(shifted(pairs[-1], "col", -1))
-    passed = [in_gain, in_bias, in_weights[:, 2 * hidden :], out_weights]
+    left_weights, right_weights = in_weights[:, : 2 * hidden].T, in_weights[:, 2 * hidden :]
+    passed = [in_gain, in_bias, right_weights, left_weights, out_weights, pair_state]
+    gate, right, *handed = pl.pallas_call(
+        functools.partial(own_kernel, len(passed)),
+        out_shape=[
+            jax.ShapeDtypeStruct((rows, columns, channels), jnp.float32),
+            jax.ShapeDtypeStruct((rows, columns, hidden), jnp.bfloat16),
+        ]
+        + [jax.ShapeDtypeStruct(array.shape, array.dtype) for array in passed],
+        in_specs=[SMEM] + [VMEM] * (2 + len(passed)),
+        out_specs=[VMEM] * (2 + len(passed)),
+        compiler_params=params(6 * block),
+        cost_estimate=cost(6 * tokens * channels * hidden, 8 * tokens * channels),
+        name="own",
+    )(token_count, pair_state, gate_weights, *passed)
+    in_gain, in_bias, right_weights, left_weights, out_weights, pairs[0] = handed
     later = spans[1][0]
-    left, gate, right, later_pair, *handed = pl.pallas_call(
+    left, later_pair = pl.pallas_call(
         functools.partial(left_kernel, window, later),
         out_shape=[
             jax.ShapeDtypeStruct((hidden, rows, width), jnp.bfloat16),
-            jax.ShapeDtypeStruct((rows, columns, channels), jnp.float32),
-            jax.ShapeDtypeStruct((rows, columns, hidden), jnp.bfloat16),
             jax.ShapeDtypeStruct((rows - later, columns, channels), jnp.bfloat16),
-        ]
-        + [jax.ShapeDtypeStruct(array.shape, array.dtype) for array in passed],
-        in_specs=[SMEM] + [VMEM] * (window + 8),
-        out_specs=[VMEM] * 8,
+        ],
+        in_specs=[SMEM] + [VMEM] * (window + 3),
+        out_specs=[VMEM] * 2,
         scratch_shapes=[pltpu.VMEM((width // LANES, hidden * pitch(rows), LANES), jnp.float32)],
-        compiler_params=params((window + 4) * block, 6 * hidden * rows * width),
-        cost_estimate=cost(
-            4 * window * tokens * channels * hidden, 6 * rows * width * hidden
-        ),
-        name="left_and_gate",
-    )(token_count, *pairs, in_gain, in_bias, in_weights[:, : 2 * hidden].T, gate_weights, *passed)
-    in_gain, in_bias, right_weights, out_weights = handed
+        compiler_params=params((window + 2) * block, 6 * hidden * rows * width),
+        cost_estimate=cost(4 * window * tokens * channels * hidden, 6 * rows * width * hidden),
+        name="left",
+    )(token_count, *pairs, in_gain, in_bias, left_weights)
 
     def mine_of(first, far_pair, near_pair):
         count = near_pair.shape[0]

time: 46.6 us -> 43.1 us (0.925)
  the two profiles are of different devices: /device:TPU:16 before, /device:TPU:26 now
where the time goes in v14:
time: 43.1 us; the launch traced here: 42.6 us
  starting transfers between devices  14.9 us (35%)
  Pallas kernels  12.4 us (29%)
  waiting for transfers between devices  9.6 us (22%)
  local copies, waits for them, and re-layouts  4.89 us (11%)
  between operations  0.82 us (2%)
    ppermute x6, starting transfers between devices, move(): lax.ppermute(array, ('row', 'col'), [(r * 4 + c, to_r * 4 + to_c) for (r,...  13.9 us
    ppermute x6, waiting for transfers between devices, move(): lax.ppermute(array, ('row', 'col'), [(r * 4 + c, to_r * 4 + to_c) for (r,...  9.6 us
    pallas_call x2, Pallas kernels, on_device(): pl.pallas_call(functools.partial(product_kernel, picks, place, len(band),...  7 us
    pallas_call x1, Pallas kernels, on_device(): pl.pallas_call(functools.partial(left_kernel, window, later), out_shape=[...  3.01 us
    unnamed x15, local copies, waits for them, and re-layouts  2.95 us
    pallas_call x2, Pallas kernels, mine_of(): pl.pallas_call(functools.partial(mine_kernel, first), out_shape=jax.Shape...  1.21 us
    pallas_call x1, Pallas kernels, on_device(): pl.pallas_call(functools.partial(own_kernel, len(passed)), out_shape=[jax...  1.19 us
    slice x1, local copies, waits for them, and re-layouts, on_device(): soon = pair_state[:spans[0][1]]  1.05 us
  transfers between devices with their start and end apart: 7, of which 2 were waited for; matrix products, arithmetic and copies ran while one was open for 5% of the time, Pallas kernels for 21%

profile of v14, /device:TPU:26, one launch (start us, length us, event | category | flops | bytes accessed | tf_op | source)
XLA Modules:
  0.0 42.6 jit_solution(14099849923917646147)
XLA Ops:
  0.0 1.0 %collective-permute-start = (bf16[48,48,128]{2,1,0:T(8,128)(2,1)}, bf16[48,48,128]{2,1,0:T(8,128)(2,1)S(1)}, u32[]{:S(2)}, u32[]{:S(2)}) collective-permute-start(bf16[48,48,128]{2,1,0:T(8,128)(2,1)} %refs_5_.3), channel_id=1, source_target_pairs={{0,3},{1,0},{2,1},{3,2},{4,7},{5,4},{6,5},{7,6},{8,11},{9,8},{10,9... | collective-permute-start | bytes 1769480 | tf_op jit(solution)/shard_map/ppermute | solution.py:33
  1.0 1.1 %slice.11 = bf16[32,48,128]{2,1,0:T(8,128)(2,1)S(1)} slice(bf16[48,48,128]{2,1,0:T(8,128)(2,1)} %refs_5_.3), slice={[0:32], [0:48], [0:128]} | slice | bytes 786432 | tf_op jit(solution)/shard_map/slice | solution.py:299
  2.0 2.2 %collective-permute-start.4 = (bf16[32,48,128]{2,1,0:T(8,128)(2,1)S(1)}, bf16[32,48,128]{2,1,0:T(8,128)(2,1)S(1)}, u32[]{:S(2)}, u32[]{:S(2)}) collective-permute-start(bf16[32,48,128]{2,1,0:T(8,128)(2,1)S(1)} %slice.11), channel_id=1, source_target_pairs={{0,8},{1,12},{5,9},{6,13},{10,6},{11,2},{15,7},{12,3},{16,24},{17,... | collective-permute-start | bytes 1179656 | tf_op jit(solution)/shard_map/ppermute | solution.py:267
  4.2 2.3 %collective-permute-start.5 = (bf16[32,48,128]{2,1,0:T(8,128)(2,1)S(1)}, bf16[32,48,128]{2,1,0:T(8,128)(2,1)S(1)}, u32[]{:S(2)}, u32[]{:S(2)}) collective-permute-start(bf16[32,48,128]{2,1,0:T(8,128)(2,1)S(1)} %slice.11), channel_id=1, source_target_pairs={{0,4},{1,0},{5,1},{6,5},{10,14},{11,10},{15,11},{12,15},{16,20},{1... | collective-permute-start | bytes 1179656 | tf_op jit(solution)/shard_map/ppermute | solution.py:267
  7.2 0.9 %fusion = (bf16[128,256]{1,0:T(8,128)(2,1)S(1)}, bf16[128,256]{1,0:T(8,128)(2,1)S(1)}) fusion(bf16[128,512]{1,0:T(8,128)(2,1)} %param.13), kind=kLoop, calls=%fused_computation | loop fusion | bytes 262144 | tf_op jit(solution)/shard_map/slice | solution.py:304
  8.1 0.1 copy.11
  8.2 0.0 copy-done
  8.3 0.0 copy-start.1
  8.3 0.7 %copy-done.1 = bf16[128,128]{1,0:T(8,128)(2,1)S(1)} copy-done((bf16[128,128]{1,0:T(8,128)(2,1)S(1)}, bf16[128,128]{1,0:T(8,128)(2,1)}, u32[]{:S(2)}) %copy-start.1) | copy-done | bytes 32792
  9.0 0.8 %copy-done.2 = bf16[128,128]{1,0:T(8,128)(2,1)S(1)} copy-done((bf16[128,128]{1,0:T(8,128)(2,1)S(1)}, bf16[128,128]{1,0:T(8,128)(2,1)}, u32[]{:S(2)}) %copy-start.2) | copy-done | bytes 32792
  9.8 0.7 %copy-done.5 = f32[128]{0:T(128)S(1)} copy-done((f32[128]{0:T(128)S(1)}, f32[128]{0:T(128)}, u32[]{:S(2)}) %copy-start.5) | copy-done | bytes 536
  10.4 0.7 %copy-done.6 = f32[128]{0:T(128)S(1)} copy-done((f32[128]{0:T(128)S(1)}, f32[128]{0:T(128)}, u32[]{:S(2)}) %copy-start.6) | copy-done | bytes 536
  11.1 1.2 %own.1 = (f32[48,48,128]{2,1,0:T(8,128)S(1)}, bf16[48,48,128]{2,1,0:T(8,128)(2,1)S(1)}, f32[1,128]{1,0:T(1,128)S(1)}, f32[1,128]{1,0:T(1,128)S(1)}, bf16[128,256...) custom-call(s32[1]{0:T(128)S(6)} %copy.12.tokens_ref, ...), custom_call_target="tpu_custom_call" | custom-call | flops 226492416 | bytes 2359296 | tf_op jit(solution)/shard_map/own/pallas_call | solution.py:306
  12.3 0.0 collective-permute-done.refs_1_
  12.3 0.0 copy-start.3
  12.3 0.0 copy-start.4
  12.3 3.0 %left.1 = (bf16[128,48,128]{2,1,0:T(8,128)(2,1)S(1)}, bf16[16,48,128]{2,1,0:T(8,128)(2,1)S(1)}) custom-call(s32[1]{0:T(128)S(6)} %copy.12.tokens_ref, bf16[48,48,128]{2,1,0:T(8,128)(2,1)S(1)} %get-tuple-element.16.refs_0_, bf16[48,48,128]{2,1,0:T(8,128)(2,1)S(1)} %collective-permute-done.refs_1_, f32[1,128]{1,0:T(1,128)S(1)} %get-tuple-element.17.refs_2_.gain_ref, ...), custom_call_target="tpu_custom_call" | custom-call | flops 301989888 | bytes 4718592 | tf_op jit(solution)/shard_map/left/pallas_call | solution.py:321
  15.3 4.2 %collective-permute-start.1 = (bf16[16,48,128]{2,1,0:T(8,128)(2,1)S(1)}, bf16[16,48,128]{2,1,0:T(8,128)(2,1)S(1)}, u32[]{:S(2)}, u32[]{:S(2)}) collective-permute-start(bf16[16,48,128]{2,1,0:T(8,128)(2,1)S(1)} %get-tuple-element.20), channel_id=1, source_target_pairs={{0,8},{1,12},{5,9},{6,13},{10,6},{11,2},{15,7},{12,3},{16,24},{17,... | collective-permute-start | bytes 589832 | tf_op jit(solution)/shard_map/ppermute | solution.py:267
  19.6 1.3 %collective-permute-start.2 = (bf16[16,48,128]{2,1,0:T(8,128)(2,1)S(1)}, bf16[16,48,128]{2,1,0:T(8,128)(2,1)S(1)}, u32[]{:S(2)}, u32[]{:S(2)}) collective-permute-start(bf16[16,48,128]{2,1,0:T(8,128)(2,1)S(1)} %get-tuple-element.20), channel_id=1, source_target_pairs={{0,4},{1,0},{5,1},{6,5},{10,14},{11,10},{15,11},{12,15},{16,20},{1... | collective-permute-start | bytes 589832 | tf_op jit(solution)/shard_map/ppermute | solution.py:267
  20.9 0.0 collective-permute-done.4.far_ref
  20.9 0.0 collective-permute-done.5.near_ref
  20.9 0.7 %mine.3.refs_1_ = bf16[32,48,128]{2,1,0:T(8,128)(2,1)S(1)} custom-call(s32[1]{0:T(128)S(6)} %copy.12.tokens_ref, bf16[32,48,128]{2,1,0:T(8,128)(2,1)S(1)} %collective-permute-done.4.far_ref, bf16[32,48,128]{2,1,0:T(8,128)(2,1)S(1)} %collective-permute-done.5.near_ref, f32[1,128]{1,0:T(1,128)S(1)} %get-tuple-element.17.refs_2_.gain_ref, ...), custom_call_target="tpu_custom_call" | custom-call | flops 100663296 | bytes 1179648 | tf_op jit(solution)/shard_map/mine/pallas_call | solution.py:337
  21.7 1.9 %collective-permute-start.6 = (bf16[32,48,128]{2,1,0:T(8,128)(2,1)S(1)}, bf16[32,48,128]{2,1,0:T(8,128)(2,1)S(1)}, u32[]{:S(2)}, u32[]{:S(2)}) collective-permute-start(bf16[32,48,128]{2,1,0:T(8,128)(2,1)S(1)} %mine.3.refs_1_), channel_id=1, source_target_pairs={{8,12},{12,8},{0,4},{9,13},{13,9},{5,1},{6,2},{2,6},{10,14},{7,3},... | collective-permute-start | bytes 1179656 | tf_op jit(solution)/shard_map/ppermute | solution.py:267
  23.6 2.8 %collective-permute-done.1.far_ref = bf16[16,48,128]{2,1,0:T(8,128)(2,1)S(1)} collective-permute-done((bf16[16,48,128]{2,1,0:T(8,128)(2,1)S(1)}, bf16[16,48,128]{2,1,0:T(8,128)(2,1)S(1)}, u32[]{:S(2)}, u32[]{:S(2)}) %collective-permute-start.1) | collective-permute-done | bytes 196640 | tf_op jit(solution)/shard_map/ppermute | solution.py:267
  26.3 0.0 collective-permute-done.2.near_ref
  26.3 0.5 %mine.2.refs_1_ = bf16[16,48,128]{2,1,0:T(8,128)(2,1)S(1)} custom-call(s32[1]{0:T(128)S(6)} %copy.12.tokens_ref, bf16[16,48,128]{2,1,0:T(8,128)(2,1)S(1)} %collective-permute-done.1.far_ref, bf16[16,48,128]{2,1,0:T(8,128)(2,1)S(1)} %collective-permute-done.2.near_ref, f32[1,128]{1,0:T(1,128)S(1)} %get-tuple-element.17.refs_2_.gain_ref, ...), custom_call_target="tpu_custom_call" | custom-call | flops 50331648 | bytes 589824 | tf_op jit(solution)/shard_map/mine/pallas_call | solution.py:337
  26.8 1.9 %collective-permute-start.3 = (bf16[16,48,128]{2,1,0:T(8,128)(2,1)S(1)}, bf16[16,48,128]{2,1,0:T(8,128)(2,1)S(1)}, u32[]{:S(2)}, u32[]{:S(2)}) collective-permute-start(bf16[16,48,128]{2,1,0:T(8,128)(2,1)S(1)} %mine.2.refs_1_), channel_id=1, source_target_pairs={{8,12},{12,8},{0,4},{9,13},{13,9},{5,1},{6,2},{2,6},{10,14},{7,3},... | collective-permute-start | bytes 589832 | tf_op jit(solution)/shard_map/ppermute | solution.py:267
  28.8 6.8 %collective-permute-done.6.refs_2_ = bf16[32,48,128]{2,1,0:T(8,128)(2,1)S(1)} collective-permute-done((bf16[32,48,128]{2,1,0:T(8,128)(2,1)S(1)}, bf16[32,48,128]{2,1,0:T(8,128)(2,1)S(1)}, u32[]{:S(2)}, u32[]{:S(2)}) %collective-permute-start.6) | collective-permute-done | bytes 393248 | tf_op jit(solution)/shard_map/ppermute | solution.py:267
  35.6 0.0 copy-done.3
  35.6 3.7 %product.2.refs_8_ = bf16[48,32,128]{2,1,0:T(8,128)(2,1)S(1)} custom-call(bf16[48,48,128]{2,1,0:T(8,128)(2,1)S(1)} %get-tuple-element.15.refs_0_, bf16[32,48,128]{2,1,0:T(8,128)(2,1)S(1)} %mine.3.refs_1_, bf16[32,48,128]{2,1,0:T(8,128)(2,1)S(1)} %collective-permute-done.6.refs_2_, bf16[128,48,128]{2,1,0:T(8,128)(2,1)S(1)} %get-tuple-element.22.refs_3_, ...), custom_call_target="tpu_custom_call" | custom-call | flops 37748736 | bytes 2359296 | tf_op jit(solution)/shard_map/product/pallas_call | solution.py:371
  39.3 0.0 collective-permute-done.3.refs_2_
  39.3 3.3 %product.3 = bf16[48,48,128]{2,1,0:T(8,128)(2,1)} custom-call(bf16[48,48,128]{2,1,0:T(8,128)(2,1)S(1)} %get-tuple-element.15.refs_0_, bf16[16,48,128]{2,1,0:T(8,128)(2,1)S(1)} %mine.2.refs_1_, bf16[16,48,128]{2,1,0:T(8,128)(2,1)S(1)} %collective-permute-done.3.refs_2_, bf16[128,48,128]{2,1,0:T(8,128)(2,1)S(1)} %get-tuple-element.22.refs_3_, ...), custom_call_target="tpu_custom_call" | custom-call | flops 18874368 | bytes 2359296 | tf_op jit(solution)/shard_map/product/pallas_call | solution.py:371
  (5 shorter events, 0.0 us)
Async XLA Ops:
  0.0 8.2 %copy-start = (bf16[48,48,128]{2,1,0:T(8,128)(2,1)S(1)}, bf16[48,48,128]{2,1,0:T(8,128)(2,1)}, u32[]{:S(2)}) copy-start(bf16[48,48,128]{2,1,0:T(8,128)(2,1)} %refs_5_.3) | copy-start | bytes 1769476
  0.0 12.3 %collective-permute-start = (bf16[48,48,128]{2,1,0:T(8,128)(2,1)}, bf16[48,48,128]{2,1,0:T(8,128)(2,1)S(1)}, u32[]{:S(2)}, u32[]{:S(2)}) collective-permute-start(bf16[48,48,128]{2,1,0:T(8,128)(2,1)} %refs_5_.3), channel_id=1, source_target_pairs={{0,3},{1,0},{2,1},{3,2},{4,7},{5,4},{6,5},{7,6},{8,11},{9,8},{10,9... | collective-permute-start | bytes 1769480 | tf_op jit(solution)/shard_map/ppermute | solution.py:33
  2.0 18.9 %collective-permute-start.4 = (bf16[32,48,128]{2,1,0:T(8,128)(2,1)S(1)}, bf16[32,48,128]{2,1,0:T(8,128)(2,1)S(1)}, u32[]{:S(2)}, u32[]{:S(2)}) collective-permute-start(bf16[32,48,128]{2,1,0:T(8,128)(2,1)S(1)} %slice.11), channel_id=1, source_target_pairs={{0,8},{1,12},{5,9},{6,13},{10,6},{11,2},{15,7},{12,3},{16,24},{17,... | collective-permute-start | bytes 1179656 | tf_op jit(solution)/shard_map/ppermute | solution.py:267
  4.2 16.7 %collective-permute-start.5 = (bf16[32,48,128]{2,1,0:T(8,128)(2,1)S(1)}, bf16[32,48,128]{2,1,0:T(8,128)(2,1)S(1)}, u32[]{:S(2)}, u32[]{:S(2)}) collective-permute-start(bf16[32,48,128]{2,1,0:T(8,128)(2,1)S(1)} %slice.11), channel_id=1, source_target_pairs={{0,4},{1,0},{5,1},{6,5},{10,14},{11,10},{15,11},{12,15},{16,20},{1... | collective-permute-start | bytes 1179656 | tf_op jit(solution)/shard_map/ppermute | solution.py:267
  8.3 0.8 %copy-start.1 = (bf16[128,128]{1,0:T(8,128)(2,1)S(1)}, bf16[128,128]{1,0:T(8,128)(2,1)}, u32[]{:S(2)}) copy-start(bf16[128,128]{1,0:T(8,128)(2,1)} %gate_weights_ref.1) | copy-start | bytes 98308
  9.0 0.8 %copy-start.2 = (bf16[128,128]{1,0:T(8,128)(2,1)S(1)}, bf16[128,128]{1,0:T(8,128)(2,1)}, u32[]{:S(2)}) copy-start(bf16[128,128]{1,0:T(8,128)(2,1)} %refs_4_.1) | copy-start | bytes 98308
  9.8 0.7 %copy-start.5 = (f32[128]{0:T(128)S(1)}, f32[128]{0:T(128)}, u32[]{:S(2)}) copy-start(f32[128]{0:T(128)} %param.11) | copy-start | bytes 1540
  10.4 0.7 %copy-start.6 = (f32[128]{0:T(128)S(1)}, f32[128]{0:T(128)}, u32[]{:S(2)}) copy-start(f32[128]{0:T(128)} %param.12) | copy-start | bytes 1540
  12.3 23.3 %copy-start.3 = (f32[128]{0:T(128)S(1)}, f32[128]{0:T(128)}, u32[]{:S(2)}) copy-start(f32[128]{0:T(128)} %refs_5_.5) | copy-start | bytes 1540
  12.3 23.3 %copy-start.4 = (f32[128]{0:T(128)S(1)}, f32[128]{0:T(128)}, u32[]{:S(2)}) copy-start(f32[128]{0:T(128)} %refs_6_.3) | copy-start | bytes 1540
  15.3 11.0 %collective-permute-start.1 = (bf16[16,48,128]{2,1,0:T(8,128)(2,1)S(1)}, bf16[16,48,128]{2,1,0:T(8,128)(2,1)S(1)}, u32[]{:S(2)}, u32[]{:S(2)}) collective-permute-start(bf16[16,48,128]{2,1,0:T(8,128)(2,1)S(1)} %get-tuple-element.20), channel_id=1, source_target_pairs={{0,8},{1,12},{5,9},{6,13},{10,6},{11,2},{15,7},{12,3},{16,24},{17,... | collective-permute-start | bytes 589832 | tf_op jit(solution)/shard_map/ppermute | solution.py:267
  19.6 6.8 %collective-permute-start.2 = (bf16[16,48,128]{2,1,0:T(8,128)(2,1)S(1)}, bf16[16,48,128]{2,1,0:T(8,128)(2,1)S(1)}, u32[]{:S(2)}, u32[]{:S(2)}) collective-permute-start(bf16[16,48,128]{2,1,0:T(8,128)(2,1)S(1)} %get-tuple-element.20), channel_id=1, source_target_pairs={{0,4},{1,0},{5,1},{6,5},{10,14},{11,10},{15,11},{12,15},{16,20},{1... | collective-permute-start | bytes 589832 | tf_op jit(solution)/shard_map/ppermute | solution.py:267
  21.7 13.9 %collective-permute-start.6 = (bf16[32,48,128]{2,1,0:T(8,128)(2,1)S(1)}, bf16[32,48,128]{2,1,0:T(8,128)(2,1)S(1)}, u32[]{:S(2)}, u32[]{:S(2)}) collective-permute-start(bf16[32,48,128]{2,1,0:T(8,128)(2,1)S(1)} %mine.3.refs_1_), channel_id=1, source_target_pairs={{8,12},{12,8},{0,4},{9,13},{13,9},{5,1},{6,2},{2,6},{10,14},{7,3},... | collective-permute-start | bytes 1179656 | tf_op jit(solution)/shard_map/ppermute | solution.py:267
  26.8 12.5 %collective-permute-start.3 = (bf16[16,48,128]{2,1,0:T(8,128)(2,1)S(1)}, bf16[16,48,128]{2,1,0:T(8,128)(2,1)S(1)}, u32[]{:S(2)}, u32[]{:S(2)}) collective-permute-start(bf16[16,48,128]{2,1,0:T(8,128)(2,1)S(1)} %mine.2.refs_1_), channel_id=1, source_target_pairs={{8,12},{12,8},{0,4},{9,13},{13,9},{5,1},{6,2},{2,6},{10,14},{7,3},... | collective-permute-start | bytes 589832 | tf_op jit(solution)/shard_map/ppermute | solution.py:267

commit v15 on v14

--- a/solution.py
+++ b/solution.py
@@ -98,10 +98,12 @@
             right_ref[first + row] = part
 
 
-def left_kernel(blocks, later, tokens_ref, *refs):
-    pair_refs, refs = refs[:blocks], refs[blocks:]
-    gain_ref, bias_ref, weights_ref, left_ref, later_ref, scratch = refs
-    later_ref[...] = pair_refs[0][pl.ds(later, later_ref.shape[0])]
+def left_kernel(here, blocks, tokens_ref, *refs):
+    pair_refs, refs = refs[: len(here)], refs[len(here) :]
+    gain_ref, bias_ref, weights_ref, *base_refs, left_ref, scratch = refs
+    if here[0] == 0:
+        *base_refs, left_ref, later_ref = (*base_refs, left_ref)
+        later_ref[...] = pair_refs[0][pl.ds(pair_refs[0].shape[0] - later_ref.shape[0], later_ref.shape[0])]
     rows, columns, channels = pair_refs[0].shape
     hidden, _, width = left_ref.shape
     tokens = tokens_ref[0]
@@ -119,7 +121,9 @@
     for first in range(0, rows, step):
         normed = [normed_rows(ref[pl.ds(first, step)], gain_ref, bias_ref) for ref in pair_refs]
         for row in range(step):
-            thirds = [piece[row * columns : (row + 1) * columns] for piece in normed]
+            thirds = [jnp.zeros((columns, channels), jnp.bfloat16)] * blocks
+            for at, piece in zip(here, normed):
+                thirds[at] = piece[row * columns : (row + 1) * columns]
             both = lax.dot_general(
                 weights_ref[...],
                 jnp.concatenate(thirds + padding, axis=0),
@@ -135,8 +139,10 @@
                 ]
     for channel in range(hidden):
         for at in range(0, width, LANES):
-            one = scratch[at // LANES, pl.ds(channel * pitch(rows), rows), :]
-            left_ref[channel, :, at : at + LANES] = one.astype(jnp.bfloat16)
+            one = scratch[at // LANES, pl.ds(channel * pitch(rows), rows), :].astype(jnp.bfloat16)
+            for base_ref in base_refs:
+                one += base_ref[channel, :, at : at + LANES]
+            left_ref[channel, :, at : at + LANES] = one
 
 
 def turned(pieces, width):
@@ -317,20 +323,27 @@
         name="own",
     )(token_count, pair_state, gate_weights, *passed)
     in_gain, in_bias, right_weights, left_weights, out_weights, pairs[0] = handed
-    later = spans[1][0]
-    left, later_pair = pl.pallas_call(
-        functools.partial(left_kernel, window, later),
-        out_shape=[
-            jax.ShapeDtypeStruct((hidden, rows, width), jnp.bfloat16),
-            jax.ShapeDtypeStruct((rows - later, columns, channels), jnp.bfloat16),
-        ],
-        in_specs=[SMEM] + [VMEM] * (window + 3),
-        out_specs=[VMEM] * 2,
-        scratch_shapes=[pltpu.VMEM((width // LANES, hidden * pitch(rows), LANES), jnp.float32)],
-        compiler_params=params((window + 2) * block, 6 * hidden * rows * width),
-        cost_estimate=cost(4 * window * tokens * channels * hidden, 6 * rows * width * hidden),
-        name="left",
-    )(token_count, *pairs, in_gain, in_bias, left_weights)
+
+    def left_of(here, *base):
+        shapes = [jax.ShapeDtypeStruct((hidden, rows, width), jnp.bfloat16)]
+        if here[0] == 0:
+            shapes.append(jax.ShapeDtypeStruct((spans[1][1], columns, channels), jnp.bfloat16))
+        return pl.pallas_call(
+            functools.partial(left_kernel, here, window),
+            out_shape=shapes,
+            in_specs=[SMEM] + [VMEM] * (len(here) + 3 + len(base)),
+            out_specs=[VMEM] * len(shapes),
+            scratch_shapes=[
+                pltpu.VMEM((width // LANES, hidden * pitch(rows), LANES), jnp.float32)
+            ],
+            compiler_params=params((len(here) + 2) * block, 6 * hidden * rows * width),
+            cost_estimate=cost(
+                4 * len(here) * tokens * channels * hidden, 6 * rows * width * hidden
+            ),
+            name="left",
+        )(token_count, *[pairs[at] for at in here], in_gain, in_bias, left_weights, *base)
+
+    left, later_pair = left_of([0])
 
     def mine_of(first, far_pair, near_pair):
         count = near_pair.shape[0]
@@ -350,11 +363,13 @@
         for (first, _), pieces in zip(spans, arrived):
             mine = mine_of(first, *pieces)
             bands.append([right, mine, move(mine, share)])
+        left, _ = lax.optimization_barrier((left, mine))
         picks, place = [(0, 1, 1, 2), (1, 2, 2, 1)], hop_place
     else:
         bands, picks = band_by_sums(right, spans, window, row_count, col_count, columns)
         place = lambda: 0
 
+    (left,) = left_of(list(range(1, window)), left)
     done = []
     for (first, count), band in zip(spans, bands):
         last = first + count == columns

time: 43.1 us -> 43.3 us (level)
  the two profiles are of different devices: /device:TPU:26 before, /device:TPU:0 now
where the time goes in v15:
time: 43.3 us; the launch traced here: 42.9 us
  starting transfers between devices  20.5 us (47%)
  Pallas kernels  14.1 us (33%)
  local copies, waits for them, and re-layouts  4.92 us (11%)
  waiting for transfers between devices  2.52 us (6%)
  between operations  0.85 us (2%)
    ppermute x6, starting transfers between devices, move(): lax.ppermute(array, ('row', 'col'), [(r * 4 + c, to_r * 4 + to_c) for (r,...  20.4 us
    pallas_call x2, Pallas kernels, on_device(): pl.pallas_call(functools.partial(product_kernel, picks, place, len(band),...  7 us
    pallas_call x2, Pallas kernels, left_of(): pl.pallas_call(functools.partial(left_kernel, here, window), out_shape=sh...  4.7 us
    unnamed x15, local copies, waits for them, and re-layouts  2.95 us
    ppermute x6, waiting for transfers between devices, move(): lax.ppermute(array, ('row', 'col'), [(r * 4 + c, to_r * 4 + to_c) for (r,...  2.52 us
    pallas_call x2, Pallas kernels, mine_of(): pl.pallas_call(functools.partial(mine_kernel, first), out_shape=jax.Shape...  1.2 us
    pallas_call x1, Pallas kernels, on_device(): pl.pallas_call(functools.partial(own_kernel, len(passed)), out_shape=[jax...  1.19 us
    slice x1, local copies, waits for them, and re-layouts, on_device(): soon = pair_state[:spans[0][1]]  1.09 us
  transfers between devices with their start and end apart: 7, of which 2 were waited for; matrix products, arithmetic and copies ran while one was open for 2% of the time, Pallas kernels for 25%

profile of v15, /device:TPU:0, one launch (start us, length us, event | category | flops | bytes accessed | tf_op | source)
XLA Modules:
  0.0 42.9 jit_solution(11389943505158733084)
XLA Ops:
  0.0 1.1 %slice.11 = bf16[32,48,128]{2,1,0:T(8,128)(2,1)S(1)} slice(bf16[48,48,128]{2,1,0:T(8,128)(2,1)} %refs_5_.3), slice={[0:32], [0:48], [0:128]} | slice | bytes 786432 | tf_op jit(solution)/shard_map/slice | solution.py:305
  1.1 6.0 %collective-permute-start.4 = (bf16[32,48,128]{2,1,0:T(8,128)(2,1)S(1)}, bf16[32,48,128]{2,1,0:T(8,128)(2,1)S(1)}, u32[]{:S(2)}, u32[]{:S(2)}) collective-permute-start(bf16[32,48,128]{2,1,0:T(8,128)(2,1)S(1)} %slice.11), channel_id=1, source_target_pairs={{0,8},{1,12},{5,9},{6,13},{10,6},{11,2},{15,7},{12,3},{16,24},{17,... | collective-permute-start | bytes 1179656 | tf_op jit(solution)/shard_map/ppermute | solution.py:273
  7.1 1.9 %collective-permute-start.5 = (bf16[32,48,128]{2,1,0:T(8,128)(2,1)S(1)}, bf16[32,48,128]{2,1,0:T(8,128)(2,1)S(1)}, u32[]{:S(2)}, u32[]{:S(2)}) collective-permute-start(bf16[32,48,128]{2,1,0:T(8,128)(2,1)S(1)} %slice.11), channel_id=1, source_target_pairs={{0,4},{1,0},{5,1},{6,5},{10,14},{11,10},{15,11},{12,15},{16,20},{1... | collective-permute-start | bytes 1179656 | tf_op jit(solution)/shard_map/ppermute | solution.py:273
  9.0 0.1 collective-permute-start.3
  9.7 0.9 %fusion = (bf16[128,256]{1,0:T(8,128)(2,1)S(1)}, bf16[128,256]{1,0:T(8,128)(2,1)S(1)}) fusion(bf16[128,512]{1,0:T(8,128)(2,1)} %param.13), kind=kLoop, calls=%fused_computation | loop fusion | bytes 262144 | tf_op jit(solution)/shard_map/slice | solution.py:310
  10.6 0.1 copy.11
  10.7 0.0 copy-done
  10.7 0.0 copy-start.1
  10.7 0.7 %copy-done.1 = bf16[128,128]{1,0:T(8,128)(2,1)S(1)} copy-done((bf16[128,128]{1,0:T(8,128)(2,1)S(1)}, bf16[128,128]{1,0:T(8,128)(2,1)}, u32[]{:S(2)}) %copy-start.1) | copy-done | bytes 32792
  11.5 0.8 %copy-done.2 = bf16[128,128]{1,0:T(8,128)(2,1)S(1)} copy-done((bf16[128,128]{1,0:T(8,128)(2,1)S(1)}, bf16[128,128]{1,0:T(8,128)(2,1)}, u32[]{:S(2)}) %copy-start.2) | copy-done | bytes 32792
  12.3 0.7 %copy-done.5 = f32[128]{0:T(128)S(1)} copy-done((f32[128]{0:T(128)S(1)}, f32[128]{0:T(128)}, u32[]{:S(2)}) %copy-start.5) | copy-done | bytes 536
  12.9 0.7 %copy-done.6 = f32[128]{0:T(128)S(1)} copy-done((f32[128]{0:T(128)S(1)}, f32[128]{0:T(128)}, u32[]{:S(2)}) %copy-start.6) | copy-done | bytes 536
  13.6 1.2 %own.1 = (f32[48,48,128]{2,1,0:T(8,128)S(1)}, bf16[48,48,128]{2,1,0:T(8,128)(2,1)S(1)}, f32[1,128]{1,0:T(1,128)S(1)}, f32[1,128]{1,0:T(1,128)S(1)}, bf16[128,256...) custom-call(s32[1]{0:T(128)S(6)} %copy.12.tokens_ref, ...), custom_call_target="tpu_custom_call" | custom-call | flops 226492416 | bytes 2359296 | tf_op jit(solution)/shard_map/own/pallas_call | solution.py:312
  14.8 2.3 %left.2 = (bf16[128,48,128]{2,1,0:T(8,128)(2,1)S(1)}, bf16[16,48,128]{2,1,0:T(8,128)(2,1)S(1)}) custom-call(s32[1]{0:T(128)S(6)} %copy.12.tokens_ref, bf16[48,48,128]{2,1,0:T(8,128)(2,1)S(1)} %get-tuple-element.17.refs_0_, f32[1,128]{1,0:T(1,128)S(1)} %get-tuple-element.18.refs_1_.gain_ref, f32[1,128]{1,0:T(1,128)S(1)} %get-tuple-element.19.refs_2_.bias_ref, ...), custom_call_target="tpu_custom_call" | custom-call | flops 150994944 | bytes 4718592 | tf_op jit(solution)/shard_map/left/pallas_call | solution.py:331
  17.0 4.0 %collective-permute-start = (bf16[16,48,128]{2,1,0:T(8,128)(2,1)S(1)}, bf16[16,48,128]{2,1,0:T(8,128)(2,1)S(1)}, u32[]{:S(2)}, u32[]{:S(2)}) collective-permute-start(bf16[16,48,128]{2,1,0:T(8,128)(2,1)S(1)} %get-tuple-element.21), channel_id=1, source_target_pairs={{0,8},{1,12},{5,9},{6,13},{10,6},{11,2},{15,7},{12,3},{16,24},{17,... | collective-permute-start | bytes 589832 | tf_op jit(solution)/shard_map/ppermute | solution.py:273
  21.0 1.9 %collective-permute-start.1 = (bf16[16,48,128]{2,1,0:T(8,128)(2,1)S(1)}, bf16[16,48,128]{2,1,0:T(8,128)(2,1)S(1)}, u32[]{:S(2)}, u32[]{:S(2)}) collective-permute-start(bf16[16,48,128]{2,1,0:T(8,128)(2,1)S(1)} %get-tuple-element.21), channel_id=1, source_target_pairs={{0,4},{1,0},{5,1},{6,5},{10,14},{11,10},{15,11},{12,15},{16,20},{1... | collective-permute-start | bytes 589832 | tf_op jit(solution)/shard_map/ppermute | solution.py:273
  22.9 0.0 collective-permute-done.4.far_ref
  23.0 0.0 collective-permute-done.5.near_ref
  23.0 0.7 %mine.3.refs_1_ = bf16[32,48,128]{2,1,0:T(8,128)(2,1)S(1)} custom-call(s32[1]{0:T(128)S(6)} %copy.12.tokens_ref, bf16[32,48,128]{2,1,0:T(8,128)(2,1)S(1)} %collective-permute-done.4.far_ref, bf16[32,48,128]{2,1,0:T(8,128)(2,1)S(1)} %collective-permute-done.5.near_ref, f32[1,128]{1,0:T(1,128)S(1)} %get-tuple-element.18.refs_1_.gain_ref, ...), custom_call_target="tpu_custom_call" | custom-call | flops 100663296 | bytes 1179648 | tf_op jit(solution)/shard_map/mine/pallas_call | solution.py:350
  23.7 2.2 %collective-permute-start.6 = (bf16[32,48,128]{2,1,0:T(8,128)(2,1)S(1)}, bf16[32,48,128]{2,1,0:T(8,128)(2,1)S(1)}, u32[]{:S(2)}, u32[]{:S(2)}) collective-permute-start(bf16[32,48,128]{2,1,0:T(8,128)(2,1)S(1)} %mine.3.refs_1_), channel_id=1, source_target_pairs={{8,12},{12,8},{0,4},{9,13},{13,9},{5,1},{6,2},{2,6},{10,14},{7,3},... | collective-permute-start | bytes 1179656 | tf_op jit(solution)/shard_map/ppermute | solution.py:273
  25.9 0.3 collective-permute-done.far_ref
  26.2 2.2 %collective-permute-done.1.near_ref = bf16[16,48,128]{2,1,0:T(8,128)(2,1)S(1)} collective-permute-done((bf16[16,48,128]{2,1,0:T(8,128)(2,1)S(1)}, bf16[16,48,128]{2,1,0:T(8,128)(2,1)S(1)}, u32[]{:S(2)}, u32[]{:S(2)}) %collective-permute-start.1) | collective-permute-done | bytes 196640 | tf_op jit(solution)/shard_map/ppermute | solution.py:273
  28.4 0.5 %mine.2.refs_1_ = bf16[16,48,128]{2,1,0:T(8,128)(2,1)S(1)} custom-call(s32[1]{0:T(128)S(6)} %copy.12.tokens_ref, bf16[16,48,128]{2,1,0:T(8,128)(2,1)S(1)} %collective-permute-done.far_ref, bf16[16,48,128]{2,1,0:T(8,128)(2,1)S(1)} %collective-permute-done.1.near_ref, f32[1,128]{1,0:T(1,128)S(1)} %get-tuple-element.18.refs_1_.gain_ref, ...), custom_call_target="tpu_custom_call" | custom-call | flops 50331648 | bytes 589824 | tf_op jit(solution)/shard_map/mine/pallas_call | solution.py:350
  28.9 4.4 %collective-permute-start.2 = (bf16[16,48,128]{2,1,0:T(8,128)(2,1)S(1)}, bf16[16,48,128]{2,1,0:T(8,128)(2,1)S(1)}, u32[]{:S(2)}, u32[]{:S(2)}) collective-permute-start(bf16[16,48,128]{2,1,0:T(8,128)(2,1)S(1)} %mine.2.refs_1_), channel_id=1, source_target_pairs={{8,12},{12,8},{0,4},{9,13},{13,9},{5,1},{6,2},{2,6},{10,14},{7,3},... | collective-permute-start | bytes 589832 | tf_op jit(solution)/shard_map/ppermute | solution.py:273
  33.3 0.0 copy-start.3
  33.3 0.0 copy-start.4
  33.4 0.0 collective-permute-done.3.refs_0_
  33.4 2.4 %left.3.refs_3_ = bf16[128,48,128]{2,1,0:T(8,128)(2,1)S(1)} custom-call(s32[1]{0:T(128)S(6)} %copy.12.tokens_ref, bf16[48,48,128]{2,1,0:T(8,128)(2,1)S(1)} %collective-permute-done.3.refs_0_, f32[1,128]{1,0:T(1,128)S(1)} %get-tuple-element.18.refs_1_.gain_ref, f32[1,128]{1,0:T(1,128)S(1)} %get-tuple-element.19.refs_2_.bias_ref, ...), custom_call_target="tpu_custom_call" | custom-call | flops 150994944 | bytes 4718592 | tf_op jit(solution)/shard_map/left/pallas_call | solution.py:331
  35.8 0.0 collective-permute-done.6.refs_2_
  35.8 3.7 %product.2.refs_8_ = bf16[48,32,128]{2,1,0:T(8,128)(2,1)S(1)} custom-call(bf16[48,48,128]{2,1,0:T(8,128)(2,1)S(1)} %get-tuple-element.16.refs_0_, bf16[32,48,128]{2,1,0:T(8,128)(2,1)S(1)} %mine.3.refs_1_, bf16[32,48,128]{2,1,0:T(8,128)(2,1)S(1)} %collective-permute-done.6.refs_2_, bf16[128,48,128]{2,1,0:T(8,128)(2,1)S(1)} %left.3.refs_3_, ...), custom_call_target="tpu_custom_call" | custom-call | flops 37748736 | bytes 2359296 | tf_op jit(solution)/shard_map/product/pallas_call | solution.py:386
  39.6 0.0 collective-permute-done.2.refs_2_
  39.6 3.3 %product.3 = bf16[48,48,128]{2,1,0:T(8,128)(2,1)} custom-call(bf16[48,48,128]{2,1,0:T(8,128)(2,1)S(1)} %get-tuple-element.16.refs_0_, bf16[16,48,128]{2,1,0:T(8,128)(2,1)S(1)} %mine.2.refs_1_, bf16[16,48,128]{2,1,0:T(8,128)(2,1)S(1)} %collective-permute-done.2.refs_2_, bf16[128,48,128]{2,1,0:T(8,128)(2,1)S(1)} %left.3.refs_3_, ...), custom_call_target="tpu_custom_call" | custom-call | flops 18874368 | bytes 2359296 | tf_op jit(solution)/shard_map/product/pallas_call | solution.py:386
  (6 shorter events, 0.0 us)
Async XLA Ops:
  0.0 10.7 %copy-start = (bf16[48,48,128]{2,1,0:T(8,128)(2,1)S(1)}, bf16[48,48,128]{2,1,0:T(8,128)(2,1)}, u32[]{:S(2)}) copy-start(bf16[48,48,128]{2,1,0:T(8,128)(2,1)} %refs_5_.3) | copy-start | bytes 1769476
  1.1 21.9 %collective-permute-start.4 = (bf16[32,48,128]{2,1,0:T(8,128)(2,1)S(1)}, bf16[32,48,128]{2,1,0:T(8,128)(2,1)S(1)}, u32[]{:S(2)}, u32[]{:S(2)}) collective-permute-start(bf16[32,48,128]{2,1,0:T(8,128)(2,1)S(1)} %slice.11), channel_id=1, source_target_pairs={{0,8},{1,12},{5,9},{6,13},{10,6},{11,2},{15,7},{12,3},{16,24},{17,... | collective-permute-start | bytes 1179656 | tf_op jit(solution)/shard_map/ppermute | solution.py:273
  7.1 15.9 %collective-permute-start.5 = (bf16[32,48,128]{2,1,0:T(8,128)(2,1)S(1)}, bf16[32,48,128]{2,1,0:T(8,128)(2,1)S(1)}, u32[]{:S(2)}, u32[]{:S(2)}) collective-permute-start(bf16[32,48,128]{2,1,0:T(8,128)(2,1)S(1)} %slice.11), channel_id=1, source_target_pairs={{0,4},{1,0},{5,1},{6,5},{10,14},{11,10},{15,11},{12,15},{16,20},{1... | collective-permute-start | bytes 1179656 | tf_op jit(solution)/shard_map/ppermute | solution.py:273
  9.0 24.4 %collective-permute-start.3 = (bf16[48,48,128]{2,1,0:T(8,128)(2,1)}, bf16[48,48,128]{2,1,0:T(8,128)(2,1)S(1)}, u32[]{:S(2)}, u32[]{:S(2)}) collective-permute-start(bf16[48,48,128]{2,1,0:T(8,128)(2,1)} %refs_5_.3), channel_id=1, source_target_pairs={{0,3},{1,0},{2,1},{3,2},{4,7},{5,4},{6,5},{7,6},{8,11},{9,8},{10,9... | collective-permute-start | bytes 1769480 | tf_op jit(solution)/shard_map/ppermute | solution.py:33
  10.7 0.8 %copy-start.1 = (bf16[128,128]{1,0:T(8,128)(2,1)S(1)}, bf16[128,128]{1,0:T(8,128)(2,1)}, u32[]{:S(2)}) copy-start(bf16[128,128]{1,0:T(8,128)(2,1)} %gate_weights_ref.1) | copy-start | bytes 98308
  11.5 0.8 %copy-start.2 = (bf16[128,128]{1,0:T(8,128)(2,1)S(1)}, bf16[128,128]{1,0:T(8,128)(2,1)}, u32[]{:S(2)}) copy-start(bf16[128,128]{1,0:T(8,128)(2,1)} %refs_4_.1) | copy-start | bytes 98308
  12.2 0.7 %copy-start.5 = (f32[128]{0:T(128)S(1)}, f32[128]{0:T(128)}, u32[]{:S(2)}) copy-start(f32[128]{0:T(128)} %param.11) | copy-start | bytes 1540
  12.9 0.7 %copy-start.6 = (f32[128]{0:T(128)S(1)}, f32[128]{0:T(128)}, u32[]{:S(2)}) copy-start(f32[128]{0:T(128)} %param.12) | copy-start | bytes 1540
  17.0 9.2 %collective-permute-start = (bf16[16,48,128]{2,1,0:T(8,128)(2,1)S(1)}, bf16[16,48,128]{2,1,0:T(8,128)(2,1)S(1)}, u32[]{:S(2)}, u32[]{:S(2)}) collective-permute-start(bf16[16,48,128]{2,1,0:T(8,128)(2,1)S(1)} %get-tuple-element.21), channel_id=1, source_target_pairs={{0,8},{1,12},{5,9},{6,13},{10,6},{11,2},{15,7},{12,3},{16,24},{17,... | collective-permute-start | bytes 589832 | tf_op jit(solution)/shard_map/ppermute | solution.py:273
  21.0 7.4 %collective-permute-start.1 = (bf16[16,48,128]{2,1,0:T(8,128)(2,1)S(1)}, bf16[16,48,128]{2,1,0:T(8,128)(2,1)S(1)}, u32[]{:S(2)}, u32[]{:S(2)}) collective-permute-start(bf16[16,48,128]{2,1,0:T(8,128)(2,1)S(1)} %get-tuple-element.21), channel_id=1, source_target_pairs={{0,4},{1,0},{5,1},{6,5},{10,14},{11,10},{15,11},{12,15},{16,20},{1... | collective-permute-start | bytes 589832 | tf_op jit(solution)/shard_map/ppermute | solution.py:273
  23.7 12.1 %collective-permute-start.6 = (bf16[32,48,128]{2,1,0:T(8,128)(2,1)S(1)}, bf16[32,48,128]{2,1,0:T(8,128)(2,1)S(1)}, u32[]{:S(2)}, u32[]{:S(2)}) collective-permute-start(bf16[32,48,128]{2,1,0:T(8,128)(2,1)S(1)} %mine.3.refs_1_), channel_id=1, source_target_pairs={{8,12},{12,8},{0,4},{9,13},{13,9},{5,1},{6,2},{2,6},{10,14},{7,3},... | collective-permute-start | bytes 1179656 | tf_op jit(solution)/shard_map/ppermute | solution.py:273
  28.9 10.6 %collective-permute-start.2 = (bf16[16,48,128]{2,1,0:T(8,128)(2,1)S(1)}, bf16[16,48,128]{2,1,0:T(8,128)(2,1)S(1)}, u32[]{:S(2)}, u32[]{:S(2)}) collective-permute-start(bf16[16,48,128]{2,1,0:T(8,128)(2,1)S(1)} %mine.2.refs_1_), channel_id=1, source_target_pairs={{8,12},{12,8},{0,4},{9,13},{13,9},{5,1},{6,2},{2,6},{10,14},{7,3},... | collective-permute-start | bytes 589832 | tf_op jit(solution)/shard_map/ppermute | solution.py:273
  33.3 2.5 %copy-start.3 = (f32[128]{0:T(128)S(1)}, f32[128]{0:T(128)}, u32[]{:S(2)}) copy-start(f32[128]{0:T(128)} %refs_5_.5) | copy-start | bytes 1540
  33.3 2.5 %copy-start.4 = (f32[128]{0:T(128)S(1)}, f32[128]{0:T(128)}, u32[]{:S(2)}) copy-start(f32[128]{0:T(128)} %refs_6_.3) | copy-start | bytes 1540

commit v16 on v15

--- a/solution.py
+++ b/solution.py
@@ -51,7 +51,7 @@
     return layer_norm(values, gain_ref[...], bias_ref[...]).astype(jnp.bfloat16)
 
 
-def mine_kernel(first, tokens_ref, far_ref, near_ref, gain_ref, bias_ref, weights_ref, out_ref):
+def mine_kernel(first, tokens_ref, near_ref, far_ref, gain_ref, bias_ref, weights_ref, out_ref):
     count, columns, _ = out_ref.shape
     col_pos, place = lax.axis_index("col"), hop_place()
     third_block = jnp.where((place == 0) | (place == 3), (col_pos + 1) % 4, col_pos)
@@ -303,7 +303,7 @@
     if by_hops:
         near, far, share = hops()
         soon = pair_state[: spans[0][1]]
-        arrived = [(move(soon, far), move(soon, near))]
+        arrived = [(move(soon, near), move(soon, far))]
     pairs = [pair_state]
     for _ in range(window - 1):
         pairs.append(shifted(pairs[-1], "col", -1))
@@ -344,8 +344,9 @@
         )(token_count, *[pairs[at] for at in here], in_gain, in_bias, left_weights, *base)
 
     left, later_pair = left_of([0])
-
-    def mine_of(first, far_pair, near_pair):
+    rest = list(range(1, window))
+
+    def mine_of(first, near_pair, far_pair):
         count = near_pair.shape[0]
         return pl.pallas_call(
             functools.partial(mine_kernel, first),
@@ -355,21 +356,22 @@
             compiler_params=params(2 * block),
             cost_estimate=cost(4 * count * columns * channels * hidden, 6 * count * columns * channels),
             name="mine",
-        )(token_count, far_pair, near_pair, in_gain, in_bias, right_weights)
+        )(token_count, near_pair, far_pair, in_gain, in_bias, right_weights)
 
     if by_hops:
-        arrived.append((move(later_pair, far), move(later_pair, near)))
-        bands = []
-        for (first, _), pieces in zip(spans, arrived):
-            mine = mine_of(first, *pieces)
-            bands.append([right, mine, move(mine, share)])
-        left, _ = lax.optimization_barrier((left, mine))
+        arrived.append((move(later_pair, near), move(later_pair, far)))
+        mine = [mine_of(0, *arrived[0])]
+        left, mine[0] = lax.optimization_barrier((left, mine[0]))
+        (left,) = left_of(rest, left)
+        left, *last = lax.optimization_barrier((left, *arrived[1]))
+        mine.append(mine_of(spans[1][0], *last))
+        bands = [[right, piece, move(piece, share)] for piece in mine]
         picks, place = [(0, 1, 1, 2), (1, 2, 2, 1)], hop_place
     else:
+        (left,) = left_of(rest, left)
         bands, picks = band_by_sums(right, spans, window, row_count, col_count, columns)
         place = lambda: 0
 
-    (left,) = left_of(list(range(1, window)), left)
     done = []
     for (first, count), band in zip(spans, bands):
         last = first + count == columns

time: 43.3 us -> 41 us (0.947)
  the two profiles are of different devices: /device:TPU:0 before, /device:TPU:12 now
where the time goes in v16:
time: 41 us; the launch traced here: 40.5 us
  starting transfers between devices  17.7 us (43%)
  Pallas kernels  14.1 us (34%)
  local copies, waits for them, and re-layouts  4.99 us (12%)
  waiting for transfers between devices  2.86 us (7%)
  between operations  0.82 us (2%)
    ppermute x6, starting transfers between devices, move(): lax.ppermute(array, ('row', 'col'), [(r * 4 + c, to_r * 4 + to_c) for (r,...  17.7 us
    pallas_call x2, Pallas kernels, on_device(): pl.pallas_call(functools.partial(product_kernel, picks, place, len(band),...  7 us
    pallas_call x2, Pallas kernels, left_of(): pl.pallas_call(functools.partial(left_kernel, here, window), out_shape=sh...  4.71 us
    unnamed x15, local copies, waits for them, and re-layouts  2.95 us
    ppermute x6, waiting for transfers between devices, move(): lax.ppermute(array, ('row', 'col'), [(r * 4 + c, to_r * 4 + to_c) for (r,...  2.86 us
    pallas_call x2, Pallas kernels, mine_of(): pl.pallas_call(functools.partial(mine_kernel, first), out_shape=jax.Shape...  1.21 us
    pallas_call x1, Pallas kernels, on_device(): pl.pallas_call(functools.partial(own_kernel, len(passed)), out_shape=[jax...  1.2 us
    slice x1, local copies, waits for them, and re-layouts, on_device(): soon = pair_state[:spans[0][1]]  1.16 us
  transfers between devices with their start and end apart: 7, of which 2 were waited for; matrix products, arithmetic and copies ran while one was open for 5% of the time, Pallas kernels for 27%

profile of v16, /device:TPU:12, one launch (start us, length us, event | category | flops | bytes accessed | tf_op | source)
XLA Modules:
  0.0 40.5 jit_solution(5719880770823894964)
XLA Ops:
  0.0 0.0 collective-permute-start
  0.0 1.2 %slice.11 = bf16[32,48,128]{2,1,0:T(8,128)(2,1)S(1)} slice(bf16[48,48,128]{2,1,0:T(8,128)(2,1)} %refs_5_.3), slice={[0:32], [0:48], [0:128]} | slice | bytes 786432 | tf_op jit(solution)/shard_map/slice | solution.py:305
  1.2 4.4 %collective-permute-start.2 = (bf16[32,48,128]{2,1,0:T(8,128)(2,1)S(1)}, bf16[32,48,128]{2,1,0:T(8,128)(2,1)S(1)}, u32[]{:S(2)}, u32[]{:S(2)}) collective-permute-start(bf16[32,48,128]{2,1,0:T(8,128)(2,1)S(1)} %slice.11), channel_id=1, source_target_pairs={{0,8},{1,12},{5,9},{6,13},{10,6},{11,2},{15,7},{12,3},{16,24},{17,... | collective-permute-start | bytes 1179656 | tf_op jit(solution)/shard_map/ppermute | solution.py:273
  5.6 1.3 %collective-permute-start.1 = (bf16[32,48,128]{2,1,0:T(8,128)(2,1)S(1)}, bf16[32,48,128]{2,1,0:T(8,128)(2,1)S(1)}, u32[]{:S(2)}, u32[]{:S(2)}) collective-permute-start(bf16[32,48,128]{2,1,0:T(8,128)(2,1)S(1)} %slice.11), channel_id=1, source_target_pairs={{0,4},{1,0},{5,1},{6,5},{10,14},{11,10},{15,11},{12,15},{16,20},{1... | collective-permute-start | bytes 1179656 | tf_op jit(solution)/shard_map/ppermute | solution.py:273
  7.6 0.9 %fusion = (bf16[128,256]{1,0:T(8,128)(2,1)S(1)}, bf16[128,256]{1,0:T(8,128)(2,1)S(1)}) fusion(bf16[128,512]{1,0:T(8,128)(2,1)} %param.13), kind=kLoop, calls=%fused_computation | loop fusion | bytes 262144 | tf_op jit(solution)/shard_map/slice | solution.py:310
  8.4 0.1 copy.11
  8.6 0.0 copy-start.1
  8.6 0.7 %copy-done.1 = bf16[128,128]{1,0:T(8,128)(2,1)S(1)} copy-done((bf16[128,128]{1,0:T(8,128)(2,1)S(1)}, bf16[128,128]{1,0:T(8,128)(2,1)}, u32[]{:S(2)}) %copy-start.1) | copy-done | bytes 32792
  9.3 0.8 %copy-done.2 = bf16[128,128]{1,0:T(8,128)(2,1)S(1)} copy-done((bf16[128,128]{1,0:T(8,128)(2,1)S(1)}, bf16[128,128]{1,0:T(8,128)(2,1)}, u32[]{:S(2)}) %copy-start.2) | copy-done | bytes 32792
  10.1 0.7 %copy-done.5 = f32[128]{0:T(128)S(1)} copy-done((f32[128]{0:T(128)S(1)}, f32[128]{0:T(128)}, u32[]{:S(2)}) %copy-start.5) | copy-done | bytes 536
  10.8 0.7 %copy-done.6 = f32[128]{0:T(128)S(1)} copy-done((f32[128]{0:T(128)S(1)}, f32[128]{0:T(128)}, u32[]{:S(2)}) %copy-start.6) | copy-done | bytes 536
  11.4 1.2 %own.1 = (f32[48,48,128]{2,1,0:T(8,128)S(1)}, bf16[48,48,128]{2,1,0:T(8,128)(2,1)S(1)}, f32[1,128]{1,0:T(1,128)S(1)}, f32[1,128]{1,0:T(1,128)S(1)}, bf16[128,256...) custom-call(s32[1]{0:T(128)S(6)} %copy.12.tokens_ref, ...), custom_call_target="tpu_custom_call" | custom-call | flops 226492416 | bytes 2359296 | tf_op jit(solution)/shard_map/own/pallas_call | solution.py:312
  12.6 2.3 %left.2 = (bf16[128,48,128]{2,1,0:T(8,128)(2,1)S(1)}, bf16[16,48,128]{2,1,0:T(8,128)(2,1)S(1)}) custom-call(s32[1]{0:T(128)S(6)} %copy.12.tokens_ref, bf16[48,48,128]{2,1,0:T(8,128)(2,1)S(1)} %get-tuple-element.24.refs_0_, f32[1,128]{1,0:T(1,128)S(1)} %get-tuple-element.21.refs_1_.gain_ref, f32[1,128]{1,0:T(1,128)S(1)} %get-tuple-element.22.refs_2_.bias_ref, ...), custom_call_target="tpu_custom_call" | custom-call | flops 150994944 | bytes 4718592 | tf_op jit(solution)/shard_map/left/pallas_call | solution.py:331
  14.9 1.9 %collective-permute-start.4 = (bf16[16,48,128]{2,1,0:T(8,128)(2,1)S(1)}, bf16[16,48,128]{2,1,0:T(8,128)(2,1)S(1)}, u32[]{:S(2)}, u32[]{:S(2)}) collective-permute-start(bf16[16,48,128]{2,1,0:T(8,128)(2,1)S(1)} %get-tuple-element.28), channel_id=1, source_target_pairs={{0,8},{1,12},{5,9},{6,13},{10,6},{11,2},{15,7},{12,3},{16,24},{17,... | collective-permute-start | bytes 589832 | tf_op jit(solution)/shard_map/ppermute | solution.py:273
  16.8 4.3 %collective-permute-start.3 = (bf16[16,48,128]{2,1,0:T(8,128)(2,1)S(1)}, bf16[16,48,128]{2,1,0:T(8,128)(2,1)S(1)}, u32[]{:S(2)}, u32[]{:S(2)}) collective-permute-start(bf16[16,48,128]{2,1,0:T(8,128)(2,1)S(1)} %get-tuple-element.28), channel_id=1, source_target_pairs={{0,4},{1,0},{5,1},{6,5},{10,14},{11,10},{15,11},{12,15},{16,20},{1... | collective-permute-start | bytes 589832 | tf_op jit(solution)/shard_map/ppermute | solution.py:273
  21.1 0.2 collective-permute-done.2.far_ref
  21.3 0.0 collective-permute-done.1.near_ref
  21.3 0.7 %mine.2.refs_1_ = bf16[32,48,128]{2,1,0:T(8,128)(2,1)S(1)} custom-call(s32[1]{0:T(128)S(6)} %copy.12.tokens_ref, bf16[32,48,128]{2,1,0:T(8,128)(2,1)S(1)} %collective-permute-done.1.near_ref, bf16[32,48,128]{2,1,0:T(8,128)(2,1)S(1)} %collective-permute-done.2.far_ref, f32[1,128]{1,0:T(1,128)S(1)} %get-tuple-element.21.refs_1_.gain_ref, ...), custom_call_target="tpu_custom_call" | custom-call | flops 100663296 | bytes 1179648 | tf_op jit(solution)/shard_map/mine/pallas_call | solution.py:351
  22.1 0.0 copy-start.3
  22.1 0.0 copy-start.4
  22.1 1.9 %collective-permute-start.6 = (bf16[32,48,128]{2,1,0:T(8,128)(2,1)S(1)}, bf16[32,48,128]{2,1,0:T(8,128)(2,1)S(1)}, u32[]{:S(2)}, u32[]{:S(2)}) collective-permute-start(bf16[32,48,128]{2,1,0:T(8,128)(2,1)S(1)} %mine.2.refs_1_), channel_id=1, source_target_pairs={{8,12},{12,8},{0,4},{9,13},{13,9},{5,1},{6,2},{2,6},{10,14},{7,3},... | collective-permute-start | bytes 1179656 | tf_op jit(solution)/shard_map/ppermute | solution.py:273
  24.0 0.0 collective-permute-done.refs_0_
  24.0 2.4 %left.3.refs_3_ = bf16[128,48,128]{2,1,0:T(8,128)(2,1)S(1)} custom-call(s32[1]{0:T(128)S(6)} %copy.12.tokens_ref, bf16[48,48,128]{2,1,0:T(8,128)(2,1)S(1)} %collective-permute-done.refs_0_, f32[1,128]{1,0:T(1,128)S(1)} %get-tuple-element.21.refs_1_.gain_ref, f32[1,128]{1,0:T(1,128)S(1)} %get-tuple-element.22.refs_2_.bias_ref, ...), custom_call_target="tpu_custom_call" | custom-call | flops 150994944 | bytes 4718592 | tf_op jit(solution)/shard_map/left/pallas_call | solution.py:331
  26.5 0.0 collective-permute-done.4.far_ref
  26.5 0.0 collective-permute-done.3.near_ref
  26.5 0.5 %mine.3.refs_1_ = bf16[16,48,128]{2,1,0:T(8,128)(2,1)S(1)} custom-call(s32[1]{0:T(128)S(6)} %copy.12.tokens_ref, bf16[16,48,128]{2,1,0:T(8,128)(2,1)S(1)} %collective-permute-done.3.near_ref, bf16[16,48,128]{2,1,0:T(8,128)(2,1)S(1)} %collective-permute-done.4.far_ref, f32[1,128]{1,0:T(1,128)S(1)} %get-tuple-element.21.refs_1_.gain_ref, ...), custom_call_target="tpu_custom_call" | custom-call | flops 50331648 | bytes 589824 | tf_op jit(solution)/shard_map/mine/pallas_call | solution.py:351
  27.0 3.9 %collective-permute-start.5 = (bf16[16,48,128]{2,1,0:T(8,128)(2,1)S(1)}, bf16[16,48,128]{2,1,0:T(8,128)(2,1)S(1)}, u32[]{:S(2)}, u32[]{:S(2)}) collective-permute-start(bf16[16,48,128]{2,1,0:T(8,128)(2,1)S(1)} %mine.3.refs_1_), channel_id=1, source_target_pairs={{8,12},{12,8},{0,4},{9,13},{13,9},{5,1},{6,2},{2,6},{10,14},{7,3},... | collective-permute-start | bytes 589832 | tf_op jit(solution)/shard_map/ppermute | solution.py:273
  30.9 2.6 %collective-permute-done.6.refs_2_ = bf16[32,48,128]{2,1,0:T(8,128)(2,1)S(1)} collective-permute-done((bf16[32,48,128]{2,1,0:T(8,128)(2,1)S(1)}, bf16[32,48,128]{2,1,0:T(8,128)(2,1)S(1)}, u32[]{:S(2)}, u32[]{:S(2)}) %collective-permute-start.6) | collective-permute-done | bytes 393248 | tf_op jit(solution)/shard_map/ppermute | solution.py:273
  33.5 0.0 copy-done.3
  33.5 3.7 %product.2.refs_8_ = bf16[48,32,128]{2,1,0:T(8,128)(2,1)S(1)} custom-call(bf16[48,48,128]{2,1,0:T(8,128)(2,1)S(1)} %get-tuple-element.20.refs_0_, bf16[32,48,128]{2,1,0:T(8,128)(2,1)S(1)} %mine.2.refs_1_, bf16[32,48,128]{2,1,0:T(8,128)(2,1)S(1)} %collective-permute-done.6.refs_2_, bf16[128,48,128]{2,1,0:T(8,128)(2,1)S(1)} %left.3.refs_3_, ...), custom_call_target="tpu_custom_call" | custom-call | flops 37748736 | bytes 2359296 | tf_op jit(solution)/shard_map/product/pallas_call | solution.py:388
  37.2 0.0 collective-permute-done.5.refs_2_
  37.2 3.3 %product.3 = bf16[48,48,128]{2,1,0:T(8,128)(2,1)} custom-call(bf16[48,48,128]{2,1,0:T(8,128)(2,1)S(1)} %get-tuple-element.20.refs_0_, bf16[16,48,128]{2,1,0:T(8,128)(2,1)S(1)} %mine.3.refs_1_, bf16[16,48,128]{2,1,0:T(8,128)(2,1)S(1)} %collective-permute-done.5.refs_2_, bf16[128,48,128]{2,1,0:T(8,128)(2,1)S(1)} %left.3.refs_3_, ...), custom_call_target="tpu_custom_call" | custom-call | flops 18874368 | bytes 2359296 | tf_op jit(solution)/shard_map/product/pallas_call | solution.py:388
  (6 shorter events, 0.0 us)
Async XLA Ops:
  0.0 8.6 %copy-start = (bf16[48,48,128]{2,1,0:T(8,128)(2,1)S(1)}, bf16[48,48,128]{2,1,0:T(8,128)(2,1)}, u32[]{:S(2)}) copy-start(bf16[48,48,128]{2,1,0:T(8,128)(2,1)} %refs_5_.3) | copy-start | bytes 1769476
  0.0 24.0 %collective-permute-start = (bf16[48,48,128]{2,1,0:T(8,128)(2,1)}, bf16[48,48,128]{2,1,0:T(8,128)(2,1)S(1)}, u32[]{:S(2)}, u32[]{:S(2)}) collective-permute-start(bf16[48,48,128]{2,1,0:T(8,128)(2,1)} %refs_5_.3), channel_id=1, source_target_pairs={{0,3},{1,0},{2,1},{3,2},{4,7},{5,4},{6,5},{7,6},{8,11},{9,8},{10,9... | collective-permute-start | bytes 1769480 | tf_op jit(solution)/shard_map/ppermute | solution.py:33
  1.2 20.2 %collective-permute-start.2 = (bf16[32,48,128]{2,1,0:T(8,128)(2,1)S(1)}, bf16[32,48,128]{2,1,0:T(8,128)(2,1)S(1)}, u32[]{:S(2)}, u32[]{:S(2)}) collective-permute-start(bf16[32,48,128]{2,1,0:T(8,128)(2,1)S(1)} %slice.11), channel_id=1, source_target_pairs={{0,8},{1,12},{5,9},{6,13},{10,6},{11,2},{15,7},{12,3},{16,24},{17,... | collective-permute-start | bytes 1179656 | tf_op jit(solution)/shard_map/ppermute | solution.py:273
  5.6 15.7 %collective-permute-start.1 = (bf16[32,48,128]{2,1,0:T(8,128)(2,1)S(1)}, bf16[32,48,128]{2,1,0:T(8,128)(2,1)S(1)}, u32[]{:S(2)}, u32[]{:S(2)}) collective-permute-start(bf16[32,48,128]{2,1,0:T(8,128)(2,1)S(1)} %slice.11), channel_id=1, source_target_pairs={{0,4},{1,0},{5,1},{6,5},{10,14},{11,10},{15,11},{12,15},{16,20},{1... | collective-permute-start | bytes 1179656 | tf_op jit(solution)/shard_map/ppermute | solution.py:273
  8.6 0.8 %copy-start.1 = (bf16[128,128]{1,0:T(8,128)(2,1)S(1)}, bf16[128,128]{1,0:T(8,128)(2,1)}, u32[]{:S(2)}) copy-start(bf16[128,128]{1,0:T(8,128)(2,1)} %gate_weights_ref.1) | copy-start | bytes 98308
  9.3 0.8 %copy-start.2 = (bf16[128,128]{1,0:T(8,128)(2,1)S(1)}, bf16[128,128]{1,0:T(8,128)(2,1)}, u32[]{:S(2)}) copy-start(bf16[128,128]{1,0:T(8,128)(2,1)} %refs_4_.1) | copy-start | bytes 98308
  10.1 0.7 %copy-start.5 = (f32[128]{0:T(128)S(1)}, f32[128]{0:T(128)}, u32[]{:S(2)}) copy-start(f32[128]{0:T(128)} %param.11) | copy-start | bytes 1540
  10.7 0.7 %copy-start.6 = (f32[128]{0:T(128)S(1)}, f32[128]{0:T(128)}, u32[]{:S(2)}) copy-start(f32[128]{0:T(128)} %param.12) | copy-start | bytes 1540
  14.9 11.6 %collective-permute-start.4 = (bf16[16,48,128]{2,1,0:T(8,128)(2,1)S(1)}, bf16[16,48,128]{2,1,0:T(8,128)(2,1)S(1)}, u32[]{:S(2)}, u32[]{:S(2)}) collective-permute-start(bf16[16,48,128]{2,1,0:T(8,128)(2,1)S(1)} %get-tuple-element.28), channel_id=1, source_target_pairs={{0,8},{1,12},{5,9},{6,13},{10,6},{11,2},{15,7},{12,3},{16,24},{17,... | collective-permute-start | bytes 589832 | tf_op jit(solution)/shard_map/ppermute | solution.py:273
  16.8 9.6 %collective-permute-start.3 = (bf16[16,48,128]{2,1,0:T(8,128)(2,1)S(1)}, bf16[16,48,128]{2,1,0:T(8,128)(2,1)S(1)}, u32[]{:S(2)}, u32[]{:S(2)}) collective-permute-start(bf16[16,48,128]{2,1,0:T(8,128)(2,1)S(1)} %get-tuple-element.28), channel_id=1, source_target_pairs={{0,4},{1,0},{5,1},{6,5},{10,14},{11,10},{15,11},{12,15},{16,20},{1... | collective-permute-start | bytes 589832 | tf_op jit(solution)/shard_map/ppermute | solution.py:273
  22.1 11.5 %copy-start.3 = (f32[128]{0:T(128)S(1)}, f32[128]{0:T(128)}, u32[]{:S(2)}) copy-start(f32[128]{0:T(128)} %refs_5_.5) | copy-start | bytes 1540
  22.1 11.4 %copy-start.4 = (f32[128]{0:T(128)S(1)}, f32[128]{0:T(128)}, u32[]{:S(2)}) copy-start(f32[128]{0:T(128)} %refs_6_.3) | copy-start | bytes 1540
  22.1 11.4 %collective-permute-start.6 = (bf16[32,48,128]{2,1,0:T(8,128)(2,1)S(1)}, bf16[32,48,128]{2,1,0:T(8,128)(2,1)S(1)}, u32[]{:S(2)}, u32[]{:S(2)}) collective-permute-start(bf16[32,48,128]{2,1,0:T(8,128)(2,1)S(1)} %mine.2.refs_1_), channel_id=1, source_target_pairs={{8,12},{12,8},{0,4},{9,13},{13,9},{5,1},{6,2},{2,6},{10,14},{7,3},... | collective-permute-start | bytes 1179656 | tf_op jit(solution)/shard_map/ppermute | solution.py:273
  27.0 10.3 %collective-permute-start.5 = (bf16[16,48,128]{2,1,0:T(8,128)(2,1)S(1)}, bf16[16,48,128]{2,1,0:T(8,128)(2,1)S(1)}, u32[]{:S(2)}, u32[]{:S(2)}) collective-permute-start(bf16[16,48,128]{2,1,0:T(8,128)(2,1)S(1)} %mine.3.refs_1_), channel_id=1, source_target_pairs={{8,12},{12,8},{0,4},{9,13},{13,9},{5,1},{6,2},{2,6},{10,14},{7,3},... | collective-permute-start | bytes 589832 | tf_op jit(solution)/shard_map/ppermute | solution.py:273

commit v17 on v16

--- a/solution.py
+++ b/solution.py
@@ -78,18 +78,22 @@
     return parts
 
 
-def own_kernel(passes, tokens_ref, pair_ref, gate_weights_ref, *refs):
-    passed, (gate_ref, right_ref), handed = refs[:passes], refs[passes : passes + 2], refs[passes + 2 :]
-    gain_ref, bias_ref, right_weights_ref = passed[:3]
-    for source, target in zip(passed, handed):
+def own_kernel(
+    tokens_ref, weights_ref, pair_ref, gain_ref, bias_ref, right_ref, left_weights_ref, right_weights_ref, *handed
+):
+    for source, target in zip((pair_ref, gain_ref, bias_ref), handed):
         target[...] = source[...]
     rows, columns, channels = pair_ref.shape
+    hidden = right_ref.shape[2]
+    for at in range(0, 2 * hidden, hidden):
+        left_weights_ref[pl.ds(at, hidden)] = turned(
+            [weights_ref[:, at : at + hidden]], channels
+        ).astype(jnp.bfloat16)
+    right_weights_ref[...] = weights_ref[:, 2 * hidden :]
     row_start = lax.axis_index("row") * rows
     step = 4
     for first in range(0, rows, step):
         normed = normed_rows(pair_ref[pl.ds(first, step)], gain_ref, bias_ref)
-        gate = jnp.dot(normed, gate_weights_ref[...], preferred_element_type=jnp.float32)
-        gate_ref[pl.ds(first, step)] = jax.nn.sigmoid(gate).reshape(step, columns, channels)
         both = jnp.dot(normed, right_weights_ref[...], preferred_element_type=jnp.float32)
         parts = masked_right(
             both, tokens_ref[0], row_start + first, lax.axis_index("col"), columns
@@ -99,11 +103,13 @@
 
 
 def left_kernel(here, blocks, tokens_ref, *refs):
-    pair_refs, refs = refs[: len(here)], refs[len(here) :]
-    gain_ref, bias_ref, weights_ref, *base_refs, left_ref, scratch = refs
+    pair_refs, (gain_ref, bias_ref, weights_ref, *refs) = refs[: len(here)], refs[len(here) :]
+    base_ref = None
     if here[0] == 0:
-        *base_refs, left_ref, later_ref = (*base_refs, left_ref)
+        left_ref, later_ref, scratch = refs
         later_ref[...] = pair_refs[0][pl.ds(pair_refs[0].shape[0] - later_ref.shape[0], later_ref.shape[0])]
+    else:
+        base_ref, own_ref, gate_weights_ref, left_ref, gate_ref, scratch = refs
     rows, columns, channels = pair_refs[0].shape
     hidden, _, width = left_ref.shape
     tokens = tokens_ref[0]
@@ -120,6 +126,10 @@
     step = 4
     for first in range(0, rows, step):
         normed = [normed_rows(ref[pl.ds(first, step)], gain_ref, bias_ref) for ref in pair_refs]
+        if base_ref is not None:
+            own = normed_rows(own_ref[pl.ds(first, step)], gain_ref, bias_ref)
+            gate = jnp.dot(own, gate_weights_ref[...], preferred_element_type=jnp.float32)
+            gate_ref[pl.ds(first, step)] = jax.nn.sigmoid(gate).reshape(step, columns, channels)
         for row in range(step):
             thirds = [jnp.zeros((columns, channels), jnp.bfloat16)] * blocks
             for at, piece in zip(here, normed):
@@ -140,7 +150,7 @@
     for channel in range(hidden):
         for at in range(0, width, LANES):
             one = scratch[at // LANES, pl.ds(channel * pitch(rows), rows), :].astype(jnp.bfloat16)
-            for base_ref in base_refs:
+            if base_ref is not None:
                 one += base_ref[channel, :, at : at + LANES]
             left_ref[channel, :, at : at + LANES] = one
 
@@ -307,36 +317,37 @@
     pairs = [pair_state]
     for _ in range(window - 1):
         pairs.append(shifted(pairs[-1], "col", -1))
-    left_weights, right_weights = in_weights[:, : 2 * hidden].T, in_weights[:, 2 * hidden :]
-    passed = [in_gain, in_bias, right_weights, left_weights, out_weights, pair_state]
-    gate, right, *handed = pl.pallas_call(
-        functools.partial(own_kernel, len(passed)),
+    copied = [pair_state, in_gain, in_bias]
+    right, left_weights, right_weights, pairs[0], in_gain, in_bias = pl.pallas_call(
+        own_kernel,
         out_shape=[
-            jax.ShapeDtypeStruct((rows, columns, channels), jnp.float32),
             jax.ShapeDtypeStruct((rows, columns, hidden), jnp.bfloat16),
+            jax.ShapeDtypeStruct((2 * hidden, channels), jnp.bfloat16),
+            jax.ShapeDtypeStruct((channels, 2 * hidden), jnp.bfloat16),
         ]
-        + [jax.ShapeDtypeStruct(array.shape, array.dtype) for array in passed],
-        in_specs=[SMEM] + [VMEM] * (2 + len(passed)),
-        out_specs=[VMEM] * (2 + len(passed)),
-        compiler_params=params(6 * block),
+        + [jax.ShapeDtypeStruct(array.shape, array.dtype) for array in copied],
+        in_specs=[SMEM] + [VMEM] * 4,
+        out_specs=[VMEM] * 6,
+        compiler_params=params(5 * block),
         cost_estimate=cost(6 * tokens * channels * hidden, 8 * tokens * channels),
         name="own",
-    )(token_count, pair_state, gate_weights, *passed)
-    in_gain, in_bias, right_weights, left_weights, out_weights, pairs[0] = handed
+    )(token_count, in_weights, *copied)
 
     def left_of(here, *base):
         shapes = [jax.ShapeDtypeStruct((hidden, rows, width), jnp.bfloat16)]
         if here[0] == 0:
             shapes.append(jax.ShapeDtypeStruct((spans[1][1], columns, channels), jnp.bfloat16))
+        else:
+            shapes.append(jax.ShapeDtypeStruct((rows, columns, channels), jnp.float32))
         return pl.pallas_call(
             functools.partial(left_kernel, here, window),
             out_shape=shapes,
             in_specs=[SMEM] + [VMEM] * (len(here) + 3 + len(base)),
-            out_specs=[VMEM] * len(shapes),
+            out_specs=[VMEM] * 2,
             scratch_shapes=[
                 pltpu.VMEM((width // LANES, hidden * pitch(rows), LANES), jnp.float32)
             ],
-            compiler_params=params((len(here) + 2) * block, 6 * hidden * rows * width),
+            compiler_params=params((len(here) + 4) * block, 6 * hidden * rows * width),
             cost_estimate=cost(
                 4 * len(here) * tokens * channels * hidden, 6 * rows * width * hidden
             ),
@@ -362,13 +373,13 @@
         arrived.append((move(later_pair, near), move(later_pair, far)))
         mine = [mine_of(0, *arrived[0])]
         left, mine[0] = lax.optimization_barrier((left, mine[0]))
-        (left,) = left_of(rest, left)
+        left, gate = left_of(rest, left, pairs[0], gate_weights)
         left, *last = lax.optimization_barrier((left, *arrived[1]))
         mine.append(mine_of(spans[1][0], *last))
         bands = [[right, piece, move(piece, share)] for piece in mine]
         picks, place = [(0, 1, 1, 2), (1, 2, 2, 1)], hop_place
     else:
-        (left,) = left_of(rest, left)
+        left, gate = left_of(rest, left, pairs[0], gate_weights)
         bands, picks = band_by_sums(right, spans, window, row_count, col_count, columns)
         place = lambda: 0
 

time: 41 us -> 41 us (level)
  the two profiles are of different devices: /device:TPU:12 before, /device:TPU:6 now
where the time goes in v17:
time: 41 us; the launch traced here: 40.6 us
  Pallas kernels  14.3 us (35%)
  waiting for transfers between devices  11.3 us (28%)
  starting transfers between devices  9.92 us (24%)
  local copies, waits for them, and re-layouts  4.35 us (11%)
  between operations  0.83 us (2%)
    ppermute x6, waiting for transfers between devices, move(): lax.ppermute(array, ('row', 'col'), [(r * 4 + c, to_r * 4 + to_c) for (r,...  11.3 us
    ppermute x6, starting transfers between devices, move(): lax.ppermute(array, ('row', 'col'), [(r * 4 + c, to_r * 4 + to_c) for (r,...  9.92 us
    pallas_call x2, Pallas kernels, on_device(): pl.pallas_call(functools.partial(product_kernel, picks, place, len(band),...  7 us
    pallas_call x2, Pallas kernels, left_of(): pl.pallas_call(functools.partial(left_kernel, here, window), out_shape=sh...  4.99 us
    unnamed x16, local copies, waits for them, and re-layouts  3.3 us
    pallas_call x2, Pallas kernels, mine_of(): pl.pallas_call(functools.partial(mine_kernel, first), out_shape=jax.Shape...  1.21 us
    pallas_call x1, Pallas kernels, on_device(): pl.pallas_call(own_kernel, out_shape=[jax.ShapeDtypeStruct((rows, columns...  1.08 us
    slice x1, local copies, waits for them, and re-layouts, on_device(): soon = pair_state[:spans[0][1]]  1.05 us
  transfers between devices with their start and end apart: 7, of which 2 were waited for; matrix products, arithmetic and copies ran while one was open for 3% of the time, Pallas kernels for 27%

profile of v17, /device:TPU:6, one launch (start us, length us, event | category | flops | bytes accessed | tf_op | source)
XLA Modules:
  0.0 40.6 jit_solution(6665545962436687599)
XLA Ops:
  0.0 0.0 collective-permute-start
  0.0 1.1 %slice.3 = bf16[32,48,128]{2,1,0:T(8,128)(2,1)S(1)} slice(bf16[48,48,128]{2,1,0:T(8,128)(2,1)} %pair_ref.1), slice={[0:32], [0:48], [0:128]} | slice | bytes 786432 | tf_op jit(solution)/shard_map/slice | solution.py:315
  1.1 1.3 %collective-permute-start.2 = (bf16[32,48,128]{2,1,0:T(8,128)(2,1)S(1)}, bf16[32,48,128]{2,1,0:T(8,128)(2,1)S(1)}, u32[]{:S(2)}, u32[]{:S(2)}) collective-permute-start(bf16[32,48,128]{2,1,0:T(8,128)(2,1)S(1)} %slice.3), channel_id=1, source_target_pairs={{0,8},{1,12},{5,9},{6,13},{10,6},{11,2},{15,7},{12,3},{16,24},{17,... | collective-permute-start | bytes 1179656 | tf_op jit(solution)/shard_map/ppermute | solution.py:283
  2.4 0.7 %collective-permute-start.1 = (bf16[32,48,128]{2,1,0:T(8,128)(2,1)S(1)}, bf16[32,48,128]{2,1,0:T(8,128)(2,1)S(1)}, u32[]{:S(2)}, u32[]{:S(2)}) collective-permute-start(bf16[32,48,128]{2,1,0:T(8,128)(2,1)S(1)} %slice.3), channel_id=1, source_target_pairs={{0,4},{1,0},{5,1},{6,5},{10,14},{11,10},{15,11},{12,15},{16,20},{1... | collective-permute-start | bytes 1179656 | tf_op jit(solution)/shard_map/ppermute | solution.py:283
  3.7 0.0 copy-start
  3.7 1.1 %copy-done = bf16[48,48,128]{2,1,0:T(8,128)(2,1)S(1)} copy-done((bf16[48,48,128]{2,1,0:T(8,128)(2,1)S(1)}, bf16[48,48,128]{2,1,0:T(8,128)(2,1)}, u32[]{:S(2)}) %copy-start) | copy-done | bytes 589848
  4.8 0.9 %copy-done.5 = bf16[128,512]{1,0:T(8,128)(2,1)S(1)} copy-done((bf16[128,512]{1,0:T(8,128)(2,1)S(1)}, bf16[128,512]{1,0:T(8,128)(2,1)}, u32[]{:S(2)}) %copy-start.5) | copy-done | bytes 131096
  5.7 0.7 %copy-done.6 = f32[128]{0:T(128)S(1)} copy-done((f32[128]{0:T(128)S(1)}, f32[128]{0:T(128)}, u32[]{:S(2)}) %copy-start.6) | copy-done | bytes 536
  6.3 0.7 %copy-done.7 = f32[128]{0:T(128)S(1)} copy-done((f32[128]{0:T(128)S(1)}, f32[128]{0:T(128)}, u32[]{:S(2)}) %copy-start.7) | copy-done | bytes 536
  7.0 1.1 %own.1 = (bf16[48,48,128]{2,1,0:T(8,128)(2,1)S(1)}, bf16[256,128]{1,0:T(8,128)(2,1)S(1)}, bf16[128,256]{1,0:T(8,128)(2,1)S(1)}, bf16[48,48,128]{2,1,0:T(8,128)(2...) custom-call(s32[1]{0:T(128)S(6)} %copy.10.tokens_ref, bf16[128,512]{1,0:T(8,128)(2,1)S(1)} %copy-done.5, ...), custom_call_target="tpu_custom_call" | custom-call | flops 226492416 | bytes 2359296 | tf_op jit(solution)/shard_map/own/pallas_call | solution.py:321
  8.1 2.3 %left.2 = (bf16[128,48,128]{2,1,0:T(8,128)(2,1)S(1)}, bf16[16,48,128]{2,1,0:T(8,128)(2,1)S(1)}) custom-call(s32[1]{0:T(128)S(6)} %copy.10.tokens_ref, bf16[48,48,128]{2,1,0:T(8,128)(2,1)S(1)} %get-tuple-element.24.refs_0_.refs_5_, f32[1,128]{1,0:T(1,128)S(1)} %get-tuple-element.21.refs_1_.gain_ref, f32[1,128]{1,0:T(1,128)S(1)} %get-tuple-element.22.refs_2_.bias_ref, ...), custom_call_target="tpu_custom_call" | custom-call | flops 150994944 | bytes 4718592 | tf_op jit(solution)/shard_map/left/pallas_call | solution.py:342
  10.3 1.3 %collective-permute-start.4 = (bf16[16,48,128]{2,1,0:T(8,128)(2,1)S(1)}, bf16[16,48,128]{2,1,0:T(8,128)(2,1)S(1)}, u32[]{:S(2)}, u32[]{:S(2)}) collective-permute-start(bf16[16,48,128]{2,1,0:T(8,128)(2,1)S(1)} %get-tuple-element.29), channel_id=1, source_target_pairs={{0,8},{1,12},{5,9},{6,13},{10,6},{11,2},{15,7},{12,3},{16,24},{17,... | collective-permute-start | bytes 589832 | tf_op jit(solution)/shard_map/ppermute | solution.py:283
  11.6 0.7 %collective-permute-start.3 = (bf16[16,48,128]{2,1,0:T(8,128)(2,1)S(1)}, bf16[16,48,128]{2,1,0:T(8,128)(2,1)S(1)}, u32[]{:S(2)}, u32[]{:S(2)}) collective-permute-start(bf16[16,48,128]{2,1,0:T(8,128)(2,1)S(1)} %get-tuple-element.29), channel_id=1, source_target_pairs={{0,4},{1,0},{5,1},{6,5},{10,14},{11,10},{15,11},{12,15},{16,20},{1... | collective-permute-start | bytes 589832 | tf_op jit(solution)/shard_map/ppermute | solution.py:283
  12.3 8.6 %collective-permute-done.2.far_ref = bf16[32,48,128]{2,1,0:T(8,128)(2,1)S(1)} collective-permute-done((bf16[32,48,128]{2,1,0:T(8,128)(2,1)S(1)}, bf16[32,48,128]{2,1,0:T(8,128)(2,1)S(1)}, u32[]{:S(2)}, u32[]{:S(2)}) %collective-permute-start.2) | collective-permute-done | bytes 393248 | tf_op jit(solution)/shard_map/ppermute | solution.py:283
  20.9 0.0 collective-permute-done.1.near_ref
  20.9 0.7 %mine.2.refs_1_ = bf16[32,48,128]{2,1,0:T(8,128)(2,1)S(1)} custom-call(s32[1]{0:T(128)S(6)} %copy.10.tokens_ref, bf16[32,48,128]{2,1,0:T(8,128)(2,1)S(1)} %collective-permute-done.1.near_ref, bf16[32,48,128]{2,1,0:T(8,128)(2,1)S(1)} %collective-permute-done.2.far_ref, f32[1,128]{1,0:T(1,128)S(1)} %get-tuple-element.21.refs_1_.gain_ref, ...), custom_call_target="tpu_custom_call" | custom-call | flops 100663296 | bytes 1179648 | tf_op jit(solution)/shard_map/mine/pallas_call | solution.py:362
  21.7 0.0 copy-start.1
  21.7 0.0 copy-start.3
  21.7 0.0 copy-start.4
  21.7 3.9 %collective-permute-start.6 = (bf16[32,48,128]{2,1,0:T(8,128)(2,1)S(1)}, bf16[32,48,128]{2,1,0:T(8,128)(2,1)S(1)}, u32[]{:S(2)}, u32[]{:S(2)}) collective-permute-start(bf16[32,48,128]{2,1,0:T(8,128)(2,1)S(1)} %mine.2.refs_1_), channel_id=1, source_target_pairs={{8,12},{12,8},{0,4},{9,13},{13,9},{5,1},{6,2},{2,6},{10,14},{7,3},... | collective-permute-start | bytes 1179656 | tf_op jit(solution)/shard_map/ppermute | solution.py:283
  25.6 0.0 collective-permute-done.refs_0_
  25.6 0.0 copy-done.2
  25.6 2.7 %left.3 = (bf16[128,48,128]{2,1,0:T(8,128)(2,1)S(1)}, f32[48,48,128]{2,1,0:T(8,128)S(1)}) custom-call(s32[1]{0:T(128)S(6)} %copy.10.tokens_ref, bf16[48,48,128]{2,1,0:T(8,128)(2,1)S(1)} %collective-permute-done.refs_0_, f32[1,128]{1,0:T(1,128)S(1)} %get-tuple-element.21.refs_1_.gain_ref, f32[1,128]{1,0:T(1,128)S(1)} %get-tuple-element.22.refs_2_.bias_ref, ...), custom_call_target="tpu_custom_call" | custom-call | flops 150994944 | bytes 4718592 | tf_op jit(solution)/shard_map/left/pallas_call | solution.py:342
  28.4 0.0 collective-permute-done.4.far_ref
  28.4 0.0 collective-permute-done.3.near_ref
  28.4 0.5 %mine.3.refs_1_ = bf16[16,48,128]{2,1,0:T(8,128)(2,1)S(1)} custom-call(s32[1]{0:T(128)S(6)} %copy.10.tokens_ref, bf16[16,48,128]{2,1,0:T(8,128)(2,1)S(1)} %collective-permute-done.3.near_ref, bf16[16,48,128]{2,1,0:T(8,128)(2,1)S(1)} %collective-permute-done.4.far_ref, f32[1,128]{1,0:T(1,128)S(1)} %get-tuple-element.21.refs_1_.gain_ref, ...), custom_call_target="tpu_custom_call" | custom-call | flops 50331648 | bytes 589824 | tf_op jit(solution)/shard_map/mine/pallas_call | solution.py:362
  28.9 2.1 %collective-permute-start.5 = (bf16[16,48,128]{2,1,0:T(8,128)(2,1)S(1)}, bf16[16,48,128]{2,1,0:T(8,128)(2,1)S(1)}, u32[]{:S(2)}, u32[]{:S(2)}) collective-permute-start(bf16[16,48,128]{2,1,0:T(8,128)(2,1)S(1)} %mine.3.refs_1_), channel_id=1, source_target_pairs={{8,12},{12,8},{0,4},{9,13},{13,9},{5,1},{6,2},{2,6},{10,14},{7,3},... | collective-permute-start | bytes 589832 | tf_op jit(solution)/shard_map/ppermute | solution.py:283
  31.0 2.6 %collective-permute-done.6.refs_2_ = bf16[32,48,128]{2,1,0:T(8,128)(2,1)S(1)} collective-permute-done((bf16[32,48,128]{2,1,0:T(8,128)(2,1)S(1)}, bf16[32,48,128]{2,1,0:T(8,128)(2,1)S(1)}, u32[]{:S(2)}, u32[]{:S(2)}) %collective-permute-start.6) | collective-permute-done | bytes 393248 | tf_op jit(solution)/shard_map/ppermute | solution.py:283
  33.6 0.0 copy-done.1
  33.6 3.7 %product.2.refs_8_ = bf16[48,32,128]{2,1,0:T(8,128)(2,1)S(1)} custom-call(bf16[48,48,128]{2,1,0:T(8,128)(2,1)S(1)} %get-tuple-element.20.refs_0_, bf16[32,48,128]{2,1,0:T(8,128)(2,1)S(1)} %mine.2.refs_1_, bf16[32,48,128]{2,1,0:T(8,128)(2,1)S(1)} %collective-permute-done.6.refs_2_, bf16[128,48,128]{2,1,0:T(8,128)(2,1)S(1)} %get-tuple-element.32.refs_3_, ...), custom_call_target="tpu_custom_call" | custom-call | flops 37748736 | bytes 2359296 | tf_op jit(solution)/shard_map/product/pallas_call | solution.py:399
  37.4 0.0 collective-permute-done.5.refs_2_
  37.4 3.3 %product.3 = bf16[48,48,128]{2,1,0:T(8,128)(2,1)} custom-call(bf16[48,48,128]{2,1,0:T(8,128)(2,1)S(1)} %get-tuple-element.20.refs_0_, bf16[16,48,128]{2,1,0:T(8,128)(2,1)S(1)} %mine.3.refs_1_, bf16[16,48,128]{2,1,0:T(8,128)(2,1)S(1)} %collective-permute-done.5.refs_2_, bf16[128,48,128]{2,1,0:T(8,128)(2,1)S(1)} %get-tuple-element.32.refs_3_, ...), custom_call_target="tpu_custom_call" | custom-call | flops 18874368 | bytes 2359296 | tf_op jit(solution)/shard_map/product/pallas_call | solution.py:399
  (6 shorter events, 0.0 us)
Async XLA Ops:
  0.0 25.6 %collective-permute-start = (bf16[48,48,128]{2,1,0:T(8,128)(2,1)}, bf16[48,48,128]{2,1,0:T(8,128)(2,1)S(1)}, u32[]{:S(2)}, u32[]{:S(2)}) collective-permute-start(bf16[48,48,128]{2,1,0:T(8,128)(2,1)} %pair_ref.1), channel_id=1, source_target_pairs={{0,3},{1,0},{2,1},{3,2},{4,7},{5,4},{6,5},{7,6},{8,11},{9,8},{10,9... | collective-permute-start | bytes 1769480 | tf_op jit(solution)/shard_map/ppermute | solution.py:33
  0.0 25.6 %copy-start.2 = (bf16[128,128]{1,0:T(8,128)(2,1)S(1)}, bf16[128,128]{1,0:T(8,128)(2,1)}, u32[]{:S(2)}) copy-start(bf16[128,128]{1,0:T(8,128)(2,1)} %refs_6_.3) | copy-start | bytes 98308
  1.1 19.9 %collective-permute-start.2 = (bf16[32,48,128]{2,1,0:T(8,128)(2,1)S(1)}, bf16[32,48,128]{2,1,0:T(8,128)(2,1)S(1)}, u32[]{:S(2)}, u32[]{:S(2)}) collective-permute-start(bf16[32,48,128]{2,1,0:T(8,128)(2,1)S(1)} %slice.3), channel_id=1, source_target_pairs={{0,8},{1,12},{5,9},{6,13},{10,6},{11,2},{15,7},{12,3},{16,24},{17,... | collective-permute-start | bytes 1179656 | tf_op jit(solution)/shard_map/ppermute | solution.py:283
  2.4 18.6 %collective-permute-start.1 = (bf16[32,48,128]{2,1,0:T(8,128)(2,1)S(1)}, bf16[32,48,128]{2,1,0:T(8,128)(2,1)S(1)}, u32[]{:S(2)}, u32[]{:S(2)}) collective-permute-start(bf16[32,48,128]{2,1,0:T(8,128)(2,1)S(1)} %slice.3), channel_id=1, source_target_pairs={{0,4},{1,0},{5,1},{6,5},{10,14},{11,10},{15,11},{12,15},{16,20},{1... | collective-permute-start | bytes 1179656 | tf_op jit(solution)/shard_map/ppermute | solution.py:283
  3.7 1.1 %copy-start = (bf16[48,48,128]{2,1,0:T(8,128)(2,1)S(1)}, bf16[48,48,128]{2,1,0:T(8,128)(2,1)}, u32[]{:S(2)}) copy-start(bf16[48,48,128]{2,1,0:T(8,128)(2,1)} %pair_ref.1) | copy-start | bytes 1769476
  4.8 0.9 %copy-start.5 = (bf16[128,512]{1,0:T(8,128)(2,1)S(1)}, bf16[128,512]{1,0:T(8,128)(2,1)}, u32[]{:S(2)}) copy-start(bf16[128,512]{1,0:T(8,128)(2,1)} %weights_ref.1) | copy-start | bytes 393220
  5.7 0.7 %copy-start.6 = (f32[128]{0:T(128)S(1)}, f32[128]{0:T(128)}, u32[]{:S(2)}) copy-start(f32[128]{0:T(128)} %param.11) | copy-start | bytes 1540
  6.3 0.7 %copy-start.7 = (f32[128]{0:T(128)S(1)}, f32[128]{0:T(128)}, u32[]{:S(2)}) copy-start(f32[128]{0:T(128)} %param.12) | copy-start | bytes 1540
  10.3 18.0 %collective-permute-start.4 = (bf16[16,48,128]{2,1,0:T(8,128)(2,1)S(1)}, bf16[16,48,128]{2,1,0:T(8,128)(2,1)S(1)}, u32[]{:S(2)}, u32[]{:S(2)}) collective-permute-start(bf16[16,48,128]{2,1,0:T(8,128)(2,1)S(1)} %get-tuple-element.29), channel_id=1, source_target_pairs={{0,8},{1,12},{5,9},{6,13},{10,6},{11,2},{15,7},{12,3},{16,24},{17,... | collective-permute-start | bytes 589832 | tf_op jit(solution)/shard_map/ppermute | solution.py:283
  11.6 16.7 %collective-permute-start.3 = (bf16[16,48,128]{2,1,0:T(8,128)(2,1)S(1)}, bf16[16,48,128]{2,1,0:T(8,128)(2,1)S(1)}, u32[]{:S(2)}, u32[]{:S(2)}) collective-permute-start(bf16[16,48,128]{2,1,0:T(8,128)(2,1)S(1)} %get-tuple-element.29), channel_id=1, source_target_pairs={{0,4},{1,0},{5,1},{6,5},{10,14},{11,10},{15,11},{12,15},{16,20},{1... | collective-permute-start | bytes 589832 | tf_op jit(solution)/shard_map/ppermute | solution.py:283
  21.7 11.9 %copy-start.1 = (bf16[128,128]{1,0:T(8,128)(2,1)S(1)}, bf16[128,128]{1,0:T(8,128)(2,1)}, u32[]{:S(2)}) copy-start(bf16[128,128]{1,0:T(8,128)(2,1)} %refs_7_.3) | copy-start | bytes 98308
  21.7 11.9 %copy-start.3 = (f32[128]{0:T(128)S(1)}, f32[128]{0:T(128)}, u32[]{:S(2)}) copy-start(f32[128]{0:T(128)} %refs_5_.3) | copy-start | bytes 1540
  21.7 11.9 %copy-start.4 = (f32[128]{0:T(128)S(1)}, f32[128]{0:T(128)}, u32[]{:S(2)}) copy-start(f32[128]{0:T(128)} %refs_6_.5) | copy-start | bytes 1540
  21.7 11.9 %collective-permute-start.6 = (bf16[32,48,128]{2,1,0:T(8,128)(2,1)S(1)}, bf16[32,48,128]{2,1,0:T(8,128)(2,1)S(1)}, u32[]{:S(2)}, u32[]{:S(2)}) collective-permute-start(bf16[32,48,128]{2,1,0:T(8,128)(2,1)S(1)} %mine.2.refs_1_), channel_id=1, source_target_pairs={{8,12},{12,8},{0,4},{9,13},{13,9},{5,1},{6,2},{2,6},{10,14},{7,3},... | collective-permute-start | bytes 1179656 | tf_op jit(solution)/shard_map/ppermute | solution.py:283
  28.9 8.5 %collective-permute-start.5 = (bf16[16,48,128]{2,1,0:T(8,128)(2,1)S(1)}, bf16[16,48,128]{2,1,0:T(8,128)(2,1)S(1)}, u32[]{:S(2)}, u32[]{:S(2)}) collective-permute-start(bf16[16,48,128]{2,1,0:T(8,128)(2,1)S(1)} %mine.3.refs_1_), channel_id=1, source_target_pairs={{8,12},{12,8},{0,4},{9,13},{13,9},{5,1},{6,2},{2,6},{10,14},{7,3},... | collective-permute-start | bytes 589832 | tf_op jit(solution)/shard_map/ppermute | solution.py:283

commit v18 on v17

--- a/solution.py
+++ b/solution.py
@@ -51,7 +51,11 @@
     return layer_norm(values, gain_ref[...], bias_ref[...]).astype(jnp.bfloat16)
 
 
-def mine_kernel(first, tokens_ref, near_ref, far_ref, gain_ref, bias_ref, weights_ref, out_ref):
+def mine_kernel(first, tokens_ref, near_ref, far_ref, gain_ref, bias_ref, weights_ref, *refs):
+    out_ref = refs[-1]
+    if len(refs) > 1:
+        own_ref, out_ref, later_ref = refs
+        later_ref[...] = own_ref[pl.ds(out_ref.shape[0], later_ref.shape[0])]
     count, columns, _ = out_ref.shape
     col_pos, place = lax.axis_index("col"), hop_place()
     third_block = jnp.where((place == 0) | (place == 3), (col_pos + 1) % 4, col_pos)
@@ -106,8 +110,7 @@
     pair_refs, (gain_ref, bias_ref, weights_ref, *refs) = refs[: len(here)], refs[len(here) :]
     base_ref = None
     if here[0] == 0:
-        left_ref, later_ref, scratch = refs
-        later_ref[...] = pair_refs[0][pl.ds(pair_refs[0].shape[0] - later_ref.shape[0], later_ref.shape[0])]
+        left_ref, scratch = refs
     else:
         base_ref, own_ref, gate_weights_ref, left_ref, gate_ref, scratch = refs
     rows, columns, channels = pair_refs[0].shape
@@ -313,7 +316,7 @@
     if by_hops:
         near, far, share = hops()
         soon = pair_state[: spans[0][1]]
-        arrived = [(move(soon, near), move(soon, far))]
+        arrived = move(soon, near), move(soon, far)
     pairs = [pair_state]
     for _ in range(window - 1):
         pairs.append(shifted(pairs[-1], "col", -1))
@@ -335,15 +338,13 @@
 
     def left_of(here, *base):
         shapes = [jax.ShapeDtypeStruct((hidden, rows, width), jnp.bfloat16)]
-        if here[0] == 0:
-            shapes.append(jax.ShapeDtypeStruct((spans[1][1], columns, channels), jnp.bfloat16))
-        else:
+        if here[0] > 0:
             shapes.append(jax.ShapeDtypeStruct((rows, columns, channels), jnp.float32))
         return pl.pallas_call(
             functools.partial(left_kernel, here, window),
             out_shape=shapes,
             in_specs=[SMEM] + [VMEM] * (len(here) + 3 + len(base)),
-            out_specs=[VMEM] * 2,
+            out_specs=[VMEM] * len(shapes),
             scratch_shapes=[
                 pltpu.VMEM((width // LANES, hidden * pitch(rows), LANES), jnp.float32)
             ],
@@ -354,28 +355,32 @@
             name="left",
         )(token_count, *[pairs[at] for at in here], in_gain, in_bias, left_weights, *base)
 
-    left, later_pair = left_of([0])
+    (left,) = left_of([0])
     rest = list(range(1, window))
 
-    def mine_of(first, near_pair, far_pair):
+    def mine_of(first, near_pair, far_pair, *own):
+        shapes = [jax.ShapeDtypeStruct(near_pair.shape, jnp.bfloat16)]
+        if own:
+            shapes.append(jax.ShapeDtypeStruct((spans[1][1], columns, channels), jnp.bfloat16))
         count = near_pair.shape[0]
         return pl.pallas_call(
             functools.partial(mine_kernel, first),
-            out_shape=jax.ShapeDtypeStruct((count, columns, hidden), jnp.bfloat16),
-            in_specs=[SMEM] + [VMEM] * 5,
-            out_specs=VMEM,
+            out_shape=shapes,
+            in_specs=[SMEM] + [VMEM] * (5 + len(own)),
+            out_specs=[VMEM] * len(shapes),
             compiler_params=params(2 * block),
             cost_estimate=cost(4 * count * columns * channels * hidden, 6 * count * columns * channels),
             name="mine",
-        )(token_count, near_pair, far_pair, in_gain, in_bias, right_weights)
+        )(token_count, near_pair, far_pair, in_gain, in_bias, right_weights, *own)
 
     if by_hops:
-        arrived.append((move(later_pair, near), move(later_pair, far)))
-        mine = [mine_of(0, *arrived[0])]
-        left, mine[0] = lax.optimization_barrier((left, mine[0]))
+        left, *arrived = lax.optimization_barrier((left, *arrived))
+        mine, later = mine_of(0, *arrived, pairs[0])
+        arrived = move(later, near), move(later, far)
+        left, mine = lax.optimization_barrier((left, mine))
         left, gate = left_of(rest, left, pairs[0], gate_weights)
-        left, *last = lax.optimization_barrier((left, *arrived[1]))
-        mine.append(mine_of(spans[1][0], *last))
+        left, *arrived = lax.optimization_barrier((left, *arrived))
+        mine = [mine, *mine_of(spans[1][0], *arrived)]
         bands = [[right, piece, move(piece, share)] for piece in mine]
         picks, place = [(0, 1, 1, 2), (1, 2, 2, 1)], hop_place
     else:

time: 41 us -> 43.9 us (1.071)
  the two profiles are of different devices: /device:TPU:6 before, /device:TPU:12 now
where the time goes in v18:
time: 43.9 us; the launch traced here: 43.4 us
  starting transfers between devices  17.1 us (39%)
  Pallas kernels  14.3 us (33%)
  waiting for transfers between devices  6.88 us (16%)
  local copies, waits for them, and re-layouts  4.35 us (10%)
  between operations  0.83 us (2%)
    ppermute x6, starting transfers between devices, move(): lax.ppermute(array, ('row', 'col'), [(r * 4 + c, to_r * 4 + to_c) for (r,...  17.1 us
    pallas_call x2, Pallas kernels, on_device(): pl.pallas_call(functools.partial(product_kernel, picks, place, len(band),...  7.01 us
    ppermute x6, waiting for transfers between devices, move(): lax.ppermute(array, ('row', 'col'), [(r * 4 + c, to_r * 4 + to_c) for (r,...  6.87 us
    pallas_call x2, Pallas kernels, left_of(): pl.pallas_call(functools.partial(left_kernel, here, window), out_shape=sh...  5.02 us
    unnamed x16, local copies, waits for them, and re-layouts  3.3 us
    pallas_call x2, Pallas kernels, mine_of(): pl.pallas_call(functools.partial(mine_kernel, first), out_shape=shapes, i...  1.21 us
    pallas_call x1, Pallas kernels, on_device(): pl.pallas_call(own_kernel, out_shape=[jax.ShapeDtypeStruct((rows, columns...  1.09 us
    slice x1, local copies, waits for them, and re-layouts, on_device(): soon = pair_state[:spans[0][1]]  1.05 us
  transfers between devices with their start and end apart: 7, of which 2 were waited for; matrix products, arithmetic and copies ran while one was open for 2% of the time, Pallas kernels for 25%

profile of v18, /device:TPU:12, one launch (start us, length us, event | category | flops | bytes accessed | tf_op | source)
XLA Modules:
  0.0 43.4 jit_solution(9493466189083584756)
XLA Ops:
  0.0 0.0 collective-permute-start
  0.0 1.1 %slice.3 = bf16[32,48,128]{2,1,0:T(8,128)(2,1)S(1)} slice(bf16[48,48,128]{2,1,0:T(8,128)(2,1)} %pair_ref.1), slice={[0:32], [0:48], [0:128]} | slice | bytes 786432 | tf_op jit(solution)/shard_map/slice | solution.py:318
  1.1 4.5 %collective-permute-start.2 = (bf16[32,48,128]{2,1,0:T(8,128)(2,1)S(1)}, bf16[32,48,128]{2,1,0:T(8,128)(2,1)S(1)}, u32[]{:S(2)}, u32[]{:S(2)}) collective-permute-start(bf16[32,48,128]{2,1,0:T(8,128)(2,1)S(1)} %slice.3), channel_id=1, source_target_pairs={{0,8},{1,12},{5,9},{6,13},{10,6},{11,2},{15,7},{12,3},{16,24},{17,... | collective-permute-start | bytes 1179656 | tf_op jit(solution)/shard_map/ppermute | solution.py:286
  5.6 1.3 %collective-permute-start.1 = (bf16[32,48,128]{2,1,0:T(8,128)(2,1)S(1)}, bf16[32,48,128]{2,1,0:T(8,128)(2,1)S(1)}, u32[]{:S(2)}, u32[]{:S(2)}) collective-permute-start(bf16[32,48,128]{2,1,0:T(8,128)(2,1)S(1)} %slice.3), channel_id=1, source_target_pairs={{0,4},{1,0},{5,1},{6,5},{10,14},{11,10},{15,11},{12,15},{16,20},{1... | collective-permute-start | bytes 1179656 | tf_op jit(solution)/shard_map/ppermute | solution.py:286
  7.6 0.0 copy-start
  7.6 1.1 %copy-done = bf16[48,48,128]{2,1,0:T(8,128)(2,1)S(1)} copy-done((bf16[48,48,128]{2,1,0:T(8,128)(2,1)S(1)}, bf16[48,48,128]{2,1,0:T(8,128)(2,1)}, u32[]{:S(2)}) %copy-start) | copy-done | bytes 589848
  8.6 0.9 %copy-done.5 = bf16[128,512]{1,0:T(8,128)(2,1)S(1)} copy-done((bf16[128,512]{1,0:T(8,128)(2,1)S(1)}, bf16[128,512]{1,0:T(8,128)(2,1)}, u32[]{:S(2)}) %copy-start.5) | copy-done | bytes 131096
  9.5 0.7 %copy-done.6 = f32[128]{0:T(128)S(1)} copy-done((f32[128]{0:T(128)S(1)}, f32[128]{0:T(128)}, u32[]{:S(2)}) %copy-start.6) | copy-done | bytes 536
  10.2 0.7 %copy-done.7 = f32[128]{0:T(128)S(1)} copy-done((f32[128]{0:T(128)S(1)}, f32[128]{0:T(128)}, u32[]{:S(2)}) %copy-start.7) | copy-done | bytes 536
  10.8 1.1 %own.1 = (bf16[48,48,128]{2,1,0:T(8,128)(2,1)S(1)}, bf16[256,128]{1,0:T(8,128)(2,1)S(1)}, bf16[128,256]{1,0:T(8,128)(2,1)S(1)}, bf16[48,48,128]{2,1,0:T(8,128)(2...) custom-call(s32[1]{0:T(128)S(6)} %copy.10.tokens_ref, bf16[128,512]{1,0:T(8,128)(2,1)S(1)} %copy-done.5, ...), custom_call_target="tpu_custom_call" | custom-call | flops 226492416 | bytes 2359296 | tf_op jit(solution)/shard_map/own/pallas_call | solution.py:324
  11.9 0.0 copy-start.2
  11.9 2.3 %left.2.refs_4_ = bf16[128,48,128]{2,1,0:T(8,128)(2,1)S(1)} custom-call(s32[1]{0:T(128)S(6)} %copy.10.tokens_ref, bf16[48,48,128]{2,1,0:T(8,128)(2,1)S(1)} %get-tuple-element.27.refs_0_.refs_5_, f32[1,128]{1,0:T(1,128)S(1)} %get-tuple-element.24.refs_1_.gain_ref, f32[1,128]{1,0:T(1,128)S(1)} %get-tuple-element.25.refs_2_.bias_ref, ...), custom_call_target="tpu_custom_call" | custom-call | flops 150994944 | bytes 4718592 | tf_op jit(solution)/shard_map/left/pallas_call | solution.py:343
  14.2 4.2 %collective-permute-done.2.far_ref = bf16[32,48,128]{2,1,0:T(8,128)(2,1)S(1)} collective-permute-done((bf16[32,48,128]{2,1,0:T(8,128)(2,1)S(1)}, bf16[32,48,128]{2,1,0:T(8,128)(2,1)S(1)}, u32[]{:S(2)}, u32[]{:S(2)}) %collective-permute-start.2) | collective-permute-done | bytes 393248 | tf_op jit(solution)/shard_map/ppermute | solution.py:286
  18.5 0.0 collective-permute-done.1.near_ref
  18.5 0.7 %mine.2 = (bf16[32,48,128]{2,1,0:T(8,128)(2,1)S(1)}, bf16[16,48,128]{2,1,0:T(8,128)(2,1)S(1)}) custom-call(s32[1]{0:T(128)S(6)} %copy.10.tokens_ref, bf16[32,48,128]{2,1,0:T(8,128)(2,1)S(1)} %collective-permute-done.1.near_ref, bf16[32,48,128]{2,1,0:T(8,128)(2,1)S(1)} %collective-permute-done.2.far_ref, f32[1,128]{1,0:T(1,128)S(1)} %get-tuple-element.24.refs_1_.gain_ref, ...), custom_call_target="tpu_custom_call" | custom-call | flops 100663296 | bytes 1179648 | tf_op jit(solution)/shard_map/mine/pallas_call | solution.py:366
  19.2 1.9 %collective-permute-start.4 = (bf16[16,48,128]{2,1,0:T(8,128)(2,1)S(1)}, bf16[16,48,128]{2,1,0:T(8,128)(2,1)S(1)}, u32[]{:S(2)}, u32[]{:S(2)}) collective-permute-start(bf16[16,48,128]{2,1,0:T(8,128)(2,1)S(1)} %get-tuple-element.35), channel_id=1, source_target_pairs={{0,8},{1,12},{5,9},{6,13},{10,6},{11,2},{15,7},{12,3},{16,24},{17,... | collective-permute-start | bytes 589832 | tf_op jit(solution)/shard_map/ppermute | solution.py:286
  21.1 3.3 %collective-permute-start.3 = (bf16[16,48,128]{2,1,0:T(8,128)(2,1)S(1)}, bf16[16,48,128]{2,1,0:T(8,128)(2,1)S(1)}, u32[]{:S(2)}, u32[]{:S(2)}) collective-permute-start(bf16[16,48,128]{2,1,0:T(8,128)(2,1)S(1)} %get-tuple-element.35), channel_id=1, source_target_pairs={{0,4},{1,0},{5,1},{6,5},{10,14},{11,10},{15,11},{12,15},{16,20},{1... | collective-permute-start | bytes 589832 | tf_op jit(solution)/shard_map/ppermute | solution.py:286
  24.5 0.0 copy-start.1
  24.5 0.0 copy-start.3
  24.5 0.0 copy-start.4
  24.5 2.1 %collective-permute-start.6 = (bf16[32,48,128]{2,1,0:T(8,128)(2,1)S(1)}, bf16[32,48,128]{2,1,0:T(8,128)(2,1)S(1)}, u32[]{:S(2)}, u32[]{:S(2)}) collective-permute-start(bf16[32,48,128]{2,1,0:T(8,128)(2,1)S(1)} %get-tuple-element.40.refs_1_), channel_id=1, source_target_pairs={{8,12},{12,8},{0,4},{9,13},{13,9},{5,1},{6,2},{2,6},{10,14},{7,3},... | collective-permute-start | bytes 1179656 | tf_op jit(solution)/shard_map/ppermute | solution.py:286
  26.6 0.0 collective-permute-done.refs_0_
  26.6 0.0 copy-done.2
  26.6 2.7 %left.3 = (bf16[128,48,128]{2,1,0:T(8,128)(2,1)S(1)}, f32[48,48,128]{2,1,0:T(8,128)S(1)}) custom-call(s32[1]{0:T(128)S(6)} %copy.10.tokens_ref, bf16[48,48,128]{2,1,0:T(8,128)(2,1)S(1)} %collective-permute-done.refs_0_, f32[1,128]{1,0:T(1,128)S(1)} %get-tuple-element.24.refs_1_.gain_ref, f32[1,128]{1,0:T(1,128)S(1)} %get-tuple-element.25.refs_2_.bias_ref, ...), custom_call_target="tpu_custom_call" | custom-call | flops 150994944 | bytes 4718592 | tf_op jit(solution)/shard_map/left/pallas_call | solution.py:343
  29.3 0.0 collective-permute-done.4.far_ref
  29.3 0.0 collective-permute-done.3.near_ref
  29.4 0.5 %mine.3.refs_1_ = bf16[16,48,128]{2,1,0:T(8,128)(2,1)S(1)} custom-call(s32[1]{0:T(128)S(6)} %copy.10.tokens_ref, bf16[16,48,128]{2,1,0:T(8,128)(2,1)S(1)} %collective-permute-done.3.near_ref, bf16[16,48,128]{2,1,0:T(8,128)(2,1)S(1)} %collective-permute-done.4.far_ref, f32[1,128]{1,0:T(1,128)S(1)} %get-tuple-element.24.refs_1_.gain_ref, ...), custom_call_target="tpu_custom_call" | custom-call | flops 50331648 | bytes 589824 | tf_op jit(solution)/shard_map/mine/pallas_call | solution.py:366
  29.9 3.9 %collective-permute-start.5 = (bf16[16,48,128]{2,1,0:T(8,128)(2,1)S(1)}, bf16[16,48,128]{2,1,0:T(8,128)(2,1)S(1)}, u32[]{:S(2)}, u32[]{:S(2)}) collective-permute-start(bf16[16,48,128]{2,1,0:T(8,128)(2,1)S(1)} %mine.3.refs_1_), channel_id=1, source_target_pairs={{8,12},{12,8},{0,4},{9,13},{13,9},{5,1},{6,2},{2,6},{10,14},{7,3},... | collective-permute-start | bytes 589832 | tf_op jit(solution)/shard_map/ppermute | solution.py:286
  33.8 2.6 %collective-permute-done.6.refs_2_ = bf16[32,48,128]{2,1,0:T(8,128)(2,1)S(1)} collective-permute-done((bf16[32,48,128]{2,1,0:T(8,128)(2,1)S(1)}, bf16[32,48,128]{2,1,0:T(8,128)(2,1)S(1)}, u32[]{:S(2)}, u32[]{:S(2)}) %collective-permute-start.6) | collective-permute-done | bytes 393248 | tf_op jit(solution)/shard_map/ppermute | solution.py:286
  36.4 3.7 %product.2.refs_8_ = bf16[48,32,128]{2,1,0:T(8,128)(2,1)S(1)} custom-call(bf16[48,48,128]{2,1,0:T(8,128)(2,1)S(1)} %get-tuple-element.23.refs_0_, bf16[32,48,128]{2,1,0:T(8,128)(2,1)S(1)} %get-tuple-element.40.refs_1_, bf16[32,48,128]{2,1,0:T(8,128)(2,1)S(1)} %collective-permute-done.6.refs_2_, bf16[128,48,128]{2,1,0:T(8,128)(2,1)S(1)} %get-tuple-element.38.refs_3_, ...), custom_call_target="tpu_custom_call" | custom-call | flops 37748736 | bytes 2359296 | tf_op jit(solution)/shard_map/product/pallas_call | solution.py:404
  40.1 0.0 collective-permute-done.5.refs_2_
  40.2 3.3 %product.3 = bf16[48,48,128]{2,1,0:T(8,128)(2,1)} custom-call(bf16[48,48,128]{2,1,0:T(8,128)(2,1)S(1)} %get-tuple-element.23.refs_0_, bf16[16,48,128]{2,1,0:T(8,128)(2,1)S(1)} %mine.3.refs_1_, bf16[16,48,128]{2,1,0:T(8,128)(2,1)S(1)} %collective-permute-done.5.refs_2_, bf16[128,48,128]{2,1,0:T(8,128)(2,1)S(1)} %get-tuple-element.38.refs_3_, ...), custom_call_target="tpu_custom_call" | custom-call | flops 18874368 | bytes 2359296 | tf_op jit(solution)/shard_map/product/pallas_call | solution.py:404
  (6 shorter events, 0.0 us)
Async XLA Ops:
  0.0 26.6 %collective-permute-start = (bf16[48,48,128]{2,1,0:T(8,128)(2,1)}, bf16[48,48,128]{2,1,0:T(8,128)(2,1)S(1)}, u32[]{:S(2)}, u32[]{:S(2)}) collective-permute-start(bf16[48,48,128]{2,1,0:T(8,128)(2,1)} %pair_ref.1), channel_id=1, source_target_pairs={{0,3},{1,0},{2,1},{3,2},{4,7},{5,4},{6,5},{7,6},{8,11},{9,8},{10,9... | collective-permute-start | bytes 1769480 | tf_op jit(solution)/shard_map/ppermute | solution.py:33
  1.1 17.4 %collective-permute-start.2 = (bf16[32,48,128]{2,1,0:T(8,128)(2,1)S(1)}, bf16[32,48,128]{2,1,0:T(8,128)(2,1)S(1)}, u32[]{:S(2)}, u32[]{:S(2)}) collective-permute-start(bf16[32,48,128]{2,1,0:T(8,128)(2,1)S(1)} %slice.3), channel_id=1, source_target_pairs={{0,8},{1,12},{5,9},{6,13},{10,6},{11,2},{15,7},{12,3},{16,24},{17,... | collective-permute-start | bytes 1179656 | tf_op jit(solution)/shard_map/ppermute | solution.py:286
  5.6 12.9 %collective-permute-start.1 = (bf16[32,48,128]{2,1,0:T(8,128)(2,1)S(1)}, bf16[32,48,128]{2,1,0:T(8,128)(2,1)S(1)}, u32[]{:S(2)}, u32[]{:S(2)}) collective-permute-start(bf16[32,48,128]{2,1,0:T(8,128)(2,1)S(1)} %slice.3), channel_id=1, source_target_pairs={{0,4},{1,0},{5,1},{6,5},{10,14},{11,10},{15,11},{12,15},{16,20},{1... | collective-permute-start | bytes 1179656 | tf_op jit(solution)/shard_map/ppermute | solution.py:286
  7.6 1.1 %copy-start = (bf16[48,48,128]{2,1,0:T(8,128)(2,1)S(1)}, bf16[48,48,128]{2,1,0:T(8,128)(2,1)}, u32[]{:S(2)}) copy-start(bf16[48,48,128]{2,1,0:T(8,128)(2,1)} %pair_ref.1) | copy-start | bytes 1769476
  8.6 0.9 %copy-start.5 = (bf16[128,512]{1,0:T(8,128)(2,1)S(1)}, bf16[128,512]{1,0:T(8,128)(2,1)}, u32[]{:S(2)}) copy-start(bf16[128,512]{1,0:T(8,128)(2,1)} %weights_ref.1) | copy-start | bytes 393220
  9.5 0.7 %copy-start.6 = (f32[128]{0:T(128)S(1)}, f32[128]{0:T(128)}, u32[]{:S(2)}) copy-start(f32[128]{0:T(128)} %param.11) | copy-start | bytes 1540
  10.2 0.7 %copy-start.7 = (f32[128]{0:T(128)S(1)}, f32[128]{0:T(128)}, u32[]{:S(2)}) copy-start(f32[128]{0:T(128)} %param.12) | copy-start | bytes 1540
  11.9 14.6 %copy-start.2 = (bf16[128,128]{1,0:T(8,128)(2,1)S(1)}, bf16[128,128]{1,0:T(8,128)(2,1)}, u32[]{:S(2)}) copy-start(bf16[128,128]{1,0:T(8,128)(2,1)} %refs_6_.3) | copy-start | bytes 98308
  19.2 10.1 %collective-permute-start.4 = (bf16[16,48,128]{2,1,0:T(8,128)(2,1)S(1)}, bf16[16,48,128]{2,1,0:T(8,128)(2,1)S(1)}, u32[]{:S(2)}, u32[]{:S(2)}) collective-permute-start(bf16[16,48,128]{2,1,0:T(8,128)(2,1)S(1)} %get-tuple-element.35), channel_id=1, source_target_pairs={{0,8},{1,12},{5,9},{6,13},{10,6},{11,2},{15,7},{12,3},{16,24},{17,... | collective-permute-start | bytes 589832 | tf_op jit(solution)/shard_map/ppermute | solution.py:286
  21.1 8.2 %collective-permute-start.3 = (bf16[16,48,128]{2,1,0:T(8,128)(2,1)S(1)}, bf16[16,48,128]{2,1,0:T(8,128)(2,1)S(1)}, u32[]{:S(2)}, u32[]{:S(2)}) collective-permute-start(bf16[16,48,128]{2,1,0:T(8,128)(2,1)S(1)} %get-tuple-element.35), channel_id=1, source_target_pairs={{0,4},{1,0},{5,1},{6,5},{10,14},{11,10},{15,11},{12,15},{16,20},{1... | collective-permute-start | bytes 589832 | tf_op jit(solution)/shard_map/ppermute | solution.py:286
  24.5 11.9 %copy-start.1 = (bf16[128,128]{1,0:T(8,128)(2,1)S(1)}, bf16[128,128]{1,0:T(8,128)(2,1)}, u32[]{:S(2)}) copy-start(bf16[128,128]{1,0:T(8,128)(2,1)} %refs_7_.3) | copy-start | bytes 98308
  24.5 11.9 %copy-start.3 = (f32[128]{0:T(128)S(1)}, f32[128]{0:T(128)}, u32[]{:S(2)}) copy-start(f32[128]{0:T(128)} %refs_5_.3) | copy-start | bytes 1540
  24.5 11.9 %copy-start.4 = (f32[128]{0:T(128)S(1)}, f32[128]{0:T(128)}, u32[]{:S(2)}) copy-start(f32[128]{0:T(128)} %refs_6_.5) | copy-start | bytes 1540
  24.5 11.9 %collective-permute-start.6 = (bf16[32,48,128]{2,1,0:T(8,128)(2,1)S(1)}, bf16[32,48,128]{2,1,0:T(8,128)(2,1)S(1)}, u32[]{:S(2)}, u32[]{:S(2)}) collective-permute-start(bf16[32,48,128]{2,1,0:T(8,128)(2,1)S(1)} %get-tuple-element.40.refs_1_), channel_id=1, source_target_pairs={{8,12},{12,8},{0,4},{9,13},{13,9},{5,1},{6,2},{2,6},{10,14},{7,3},... | collective-permute-start | bytes 1179656 | tf_op jit(solution)/shard_map/ppermute | solution.py:286
  29.9 10.3 %collective-permute-start.5 = (bf16[16,48,128]{2,1,0:T(8,128)(2,1)S(1)}, bf16[16,48,128]{2,1,0:T(8,128)(2,1)S(1)}, u32[]{:S(2)}, u32[]{:S(2)}) collective-permute-start(bf16[16,48,128]{2,1,0:T(8,128)(2,1)S(1)} %mine.3.refs_1_), channel_id=1, source_target_pairs={{8,12},{12,8},{0,4},{9,13},{13,9},{5,1},{6,2},{2,6},{10,14},{7,3},... | collective-permute-start | bytes 589832 | tf_op jit(solution)/shard_map/ppermute | solution.py:286

commit v19 on v18

--- a/solution.py
+++ b/solution.py
@@ -369,7 +369,7 @@
             in_specs=[SMEM] + [VMEM] * (5 + len(own)),
             out_specs=[VMEM] * len(shapes),
             compiler_params=params(2 * block),
-            cost_estimate=cost(4 * count * columns * channels * hidden, 6 * count * columns * channels),
+            cost_estimate=cost(1024, 1024),
             name="mine",
         )(token_count, near_pair, far_pair, in_gain, in_bias, right_weights, *own)
 

time: 43.9 us -> 50.3 us (1.15)
  the two profiles are of different devices: /device:TPU:12 before, /device:TPU:0 now
where the time goes in v19:
time: 50.3 us; the launch traced here: 49.9 us
  starting transfers between devices  21 us (42%)
  Pallas kernels  14.3 us (28%)
  waiting for transfers between devices  9.35 us (19%)
  local copies, waits for them, and re-layouts  4.35 us (9%)
  between operations  0.85 us (2%)
    ppermute x6, starting transfers between devices, move(): lax.ppermute(array, ('row', 'col'), [(r * 4 + c, to_r * 4 + to_c) for (r,...  18.6 us
    ppermute x6, waiting for transfers between devices, move(): lax.ppermute(array, ('row', 'col'), [(r * 4 + c, to_r * 4 + to_c) for (r,...  9.35 us
    pallas_call x2, Pallas kernels, on_device(): pl.pallas_call(functools.partial(product_kernel, picks, place, len(band),...  7.01 us
    pallas_call x2, Pallas kernels, left_of(): pl.pallas_call(functools.partial(left_kernel, here, window), out_shape=sh...  5.01 us
    unnamed x16, local copies, waits for them, and re-layouts  3.3 us
    ppermute x1, starting transfers between devices, shifted(): lax.ppermute(array, axis, [(i, (i + by) % devices) for i in range(devices)])  2.41 us
    pallas_call x2, Pallas kernels, mine_of(): pl.pallas_call(functools.partial(mine_kernel, first), out_shape=shapes, i...  1.19 us
    pallas_call x1, Pallas kernels, on_device(): pl.pallas_call(own_kernel, out_shape=[jax.ShapeDtypeStruct((rows, columns...  1.09 us
  transfers between devices with their start and end apart: 7, of which 3 were waited for; matrix products, arithmetic and copies ran while one was open for 2% of the time, Pallas kernels for 22%

profile of v19, /device:TPU:0, one launch (start us, length us, event | category | flops | bytes accessed | tf_op | source)
XLA Modules:
  0.0 49.9 jit_solution(15357332250762201528)
XLA Ops:
  0.0 2.4 %collective-permute-start = (bf16[48,48,128]{2,1,0:T(8,128)(2,1)}, bf16[48,48,128]{2,1,0:T(8,128)(2,1)S(1)}, u32[]{:S(2)}, u32[]{:S(2)}) collective-permute-start(bf16[48,48,128]{2,1,0:T(8,128)(2,1)} %pair_ref.1), channel_id=1, source_target_pairs={{0,3},{1,0},{2,1},{3,2},{4,7},{5,4},{6,5},{7,6},{8,11},{9,8},{10,9... | collective-permute-start | bytes 1769480 | tf_op jit(solution)/shard_map/ppermute | solution.py:33
  2.4 1.1 %slice.3 = bf16[32,48,128]{2,1,0:T(8,128)(2,1)S(1)} slice(bf16[48,48,128]{2,1,0:T(8,128)(2,1)} %pair_ref.1), slice={[0:32], [0:48], [0:128]} | slice | bytes 786432 | tf_op jit(solution)/shard_map/slice | solution.py:318
  3.5 4.5 %collective-permute-start.2 = (bf16[32,48,128]{2,1,0:T(8,128)(2,1)S(1)}, bf16[32,48,128]{2,1,0:T(8,128)(2,1)S(1)}, u32[]{:S(2)}, u32[]{:S(2)}) collective-permute-start(bf16[32,48,128]{2,1,0:T(8,128)(2,1)S(1)} %slice.3), channel_id=1, source_target_pairs={{0,8},{1,12},{5,9},{6,13},{10,6},{11,2},{15,7},{12,3},{16,24},{17,... | collective-permute-start | bytes 1179656 | tf_op jit(solution)/shard_map/ppermute | solution.py:286
  8.0 1.9 %collective-permute-start.1 = (bf16[32,48,128]{2,1,0:T(8,128)(2,1)S(1)}, bf16[32,48,128]{2,1,0:T(8,128)(2,1)S(1)}, u32[]{:S(2)}, u32[]{:S(2)}) collective-permute-start(bf16[32,48,128]{2,1,0:T(8,128)(2,1)S(1)} %slice.3), channel_id=1, source_target_pairs={{0,4},{1,0},{5,1},{6,5},{10,14},{11,10},{15,11},{12,15},{16,20},{1... | collective-permute-start | bytes 1179656 | tf_op jit(solution)/shard_map/ppermute | solution.py:286
  10.6 0.0 copy-start
  10.6 1.1 %copy-done = bf16[48,48,128]{2,1,0:T(8,128)(2,1)S(1)} copy-done((bf16[48,48,128]{2,1,0:T(8,128)(2,1)S(1)}, bf16[48,48,128]{2,1,0:T(8,128)(2,1)}, u32[]{:S(2)}) %copy-start) | copy-done | bytes 589848
  11.6 0.9 %copy-done.5 = bf16[128,512]{1,0:T(8,128)(2,1)S(1)} copy-done((bf16[128,512]{1,0:T(8,128)(2,1)S(1)}, bf16[128,512]{1,0:T(8,128)(2,1)}, u32[]{:S(2)}) %copy-start.5) | copy-done | bytes 131096
  12.5 0.7 %copy-done.6 = f32[128]{0:T(128)S(1)} copy-done((f32[128]{0:T(128)S(1)}, f32[128]{0:T(128)}, u32[]{:S(2)}) %copy-start.6) | copy-done | bytes 536
  13.2 0.7 %copy-done.7 = f32[128]{0:T(128)S(1)} copy-done((f32[128]{0:T(128)S(1)}, f32[128]{0:T(128)}, u32[]{:S(2)}) %copy-start.7) | copy-done | bytes 536
  13.9 1.1 %own.1 = (bf16[48,48,128]{2,1,0:T(8,128)(2,1)S(1)}, bf16[256,128]{1,0:T(8,128)(2,1)S(1)}, bf16[128,256]{1,0:T(8,128)(2,1)S(1)}, bf16[48,48,128]{2,1,0:T(8,128)(2...) custom-call(s32[1]{0:T(128)S(6)} %copy.10.tokens_ref, bf16[128,512]{1,0:T(8,128)(2,1)S(1)} %copy-done.5, ...), custom_call_target="tpu_custom_call" | custom-call | flops 226492416 | bytes 2359296 | tf_op jit(solution)/shard_map/own/pallas_call | solution.py:324
  14.9 0.0 copy-start.2
  15.0 2.3 %left.2.refs_4_ = bf16[128,48,128]{2,1,0:T(8,128)(2,1)S(1)} custom-call(s32[1]{0:T(128)S(6)} %copy.10.tokens_ref, bf16[48,48,128]{2,1,0:T(8,128)(2,1)S(1)} %get-tuple-element.27.refs_0_.refs_5_, f32[1,128]{1,0:T(1,128)S(1)} %get-tuple-element.24.refs_1_.gain_ref, f32[1,128]{1,0:T(1,128)S(1)} %get-tuple-element.25.refs_2_.bias_ref, ...), custom_call_target="tpu_custom_call" | custom-call | flops 150994944 | bytes 4718592 | tf_op jit(solution)/shard_map/left/pallas_call | solution.py:343
  17.2 0.0 collective-permute-done.2.far_ref
  17.2 4.5 %collective-permute-done.1.near_ref = bf16[32,48,128]{2,1,0:T(8,128)(2,1)S(1)} collective-permute-done((bf16[32,48,128]{2,1,0:T(8,128)(2,1)S(1)}, bf16[32,48,128]{2,1,0:T(8,128)(2,1)S(1)}, u32[]{:S(2)}, u32[]{:S(2)}) %collective-permute-start.1) | collective-permute-done | bytes 393248 | tf_op jit(solution)/shard_map/ppermute | solution.py:286
  21.7 0.7 %mine.2 = (bf16[32,48,128]{2,1,0:T(8,128)(2,1)S(1)}, bf16[16,48,128]{2,1,0:T(8,128)(2,1)S(1)}) custom-call(s32[1]{0:T(128)S(6)} %copy.10.tokens_ref, bf16[32,48,128]{2,1,0:T(8,128)(2,1)S(1)} %collective-permute-done.1.near_ref, bf16[32,48,128]{2,1,0:T(8,128)(2,1)S(1)} %collective-permute-done.2.far_ref, f32[1,128]{1,0:T(1,128)S(1)} %get-tuple-element.24.refs_1_.gain_ref, ...), custom_call_target="tpu_custom_call" | custom-call | flops 1024 | bytes 1024 | tf_op jit(solution)/shard_map/mine/pallas_call | solution.py:366
  22.4 4.4 %collective-permute-start.6 = (bf16[32,48,128]{2,1,0:T(8,128)(2,1)S(1)}, bf16[32,48,128]{2,1,0:T(8,128)(2,1)S(1)}, u32[]{:S(2)}, u32[]{:S(2)}) collective-permute-start(bf16[32,48,128]{2,1,0:T(8,128)(2,1)S(1)} %get-tuple-element.40.refs_1_), channel_id=1, source_target_pairs={{8,12},{12,8},{0,4},{9,13},{13,9},{5,1},{6,2},{2,6},{10,14},{7,3},... | collective-permute-start | bytes 1179656 | tf_op jit(solution)/shard_map/ppermute | solution.py:286
  26.8 0.0 copy-start.1
  26.9 0.0 copy-start.3
  26.9 0.0 copy-start.4
  26.9 1.4 %collective-permute-start.4 = (bf16[16,48,128]{2,1,0:T(8,128)(2,1)S(1)}, bf16[16,48,128]{2,1,0:T(8,128)(2,1)S(1)}, u32[]{:S(2)}, u32[]{:S(2)}) collective-permute-start(bf16[16,48,128]{2,1,0:T(8,128)(2,1)S(1)} %get-tuple-element.35), channel_id=1, source_target_pairs={{0,8},{1,12},{5,9},{6,13},{10,6},{11,2},{15,7},{12,3},{16,24},{17,... | collective-permute-start | bytes 589832 | tf_op jit(solution)/shard_map/ppermute | solution.py:286
  28.3 1.9 %collective-permute-start.3 = (bf16[16,48,128]{2,1,0:T(8,128)(2,1)S(1)}, bf16[16,48,128]{2,1,0:T(8,128)(2,1)S(1)}, u32[]{:S(2)}, u32[]{:S(2)}) collective-permute-start(bf16[16,48,128]{2,1,0:T(8,128)(2,1)S(1)} %get-tuple-element.35), channel_id=1, source_target_pairs={{0,4},{1,0},{5,1},{6,5},{10,14},{11,10},{15,11},{12,15},{16,20},{1... | collective-permute-start | bytes 589832 | tf_op jit(solution)/shard_map/ppermute | solution.py:286
  30.3 0.0 collective-permute-done.refs_0_
  30.3 0.0 copy-done.2
  30.3 2.7 %left.3 = (bf16[128,48,128]{2,1,0:T(8,128)(2,1)S(1)}, f32[48,48,128]{2,1,0:T(8,128)S(1)}) custom-call(s32[1]{0:T(128)S(6)} %copy.10.tokens_ref, bf16[48,48,128]{2,1,0:T(8,128)(2,1)S(1)} %collective-permute-done.refs_0_, f32[1,128]{1,0:T(1,128)S(1)} %get-tuple-element.24.refs_1_.gain_ref, f32[1,128]{1,0:T(1,128)S(1)} %get-tuple-element.25.refs_2_.bias_ref, ...), custom_call_target="tpu_custom_call" | custom-call | flops 150994944 | bytes 4718592 | tf_op jit(solution)/shard_map/left/pallas_call | solution.py:343
  33.0 2.8 %collective-permute-done.4.far_ref = bf16[16,48,128]{2,1,0:T(8,128)(2,1)S(1)} collective-permute-done((bf16[16,48,128]{2,1,0:T(8,128)(2,1)S(1)}, bf16[16,48,128]{2,1,0:T(8,128)(2,1)S(1)}, u32[]{:S(2)}, u32[]{:S(2)}) %collective-permute-start.4) | collective-permute-done | bytes 196640 | tf_op jit(solution)/shard_map/ppermute | solution.py:286
  35.8 2.1 %collective-permute-done.3.near_ref = bf16[16,48,128]{2,1,0:T(8,128)(2,1)S(1)} collective-permute-done((bf16[16,48,128]{2,1,0:T(8,128)(2,1)S(1)}, bf16[16,48,128]{2,1,0:T(8,128)(2,1)S(1)}, u32[]{:S(2)}, u32[]{:S(2)}) %collective-permute-start.3) | collective-permute-done | bytes 196640 | tf_op jit(solution)/shard_map/ppermute | solution.py:286
  37.9 0.5 mine.3.refs_1_
  38.4 4.4 %collective-permute-start.5 = (bf16[16,48,128]{2,1,0:T(8,128)(2,1)S(1)}, bf16[16,48,128]{2,1,0:T(8,128)(2,1)S(1)}, u32[]{:S(2)}, u32[]{:S(2)}) collective-permute-start(bf16[16,48,128]{2,1,0:T(8,128)(2,1)S(1)} %mine.3.refs_1_), channel_id=1, source_target_pairs={{8,12},{12,8},{0,4},{9,13},{13,9},{5,1},{6,2},{2,6},{10,14},{7,3},... | collective-permute-start | bytes 589832 | tf_op jit(solution)/shard_map/ppermute | solution.py:286
  42.8 0.0 collective-permute-done.6.refs_2_
  42.8 3.7 %product.2.refs_8_ = bf16[48,32,128]{2,1,0:T(8,128)(2,1)S(1)} custom-call(bf16[48,48,128]{2,1,0:T(8,128)(2,1)S(1)} %get-tuple-element.23.refs_0_, bf16[32,48,128]{2,1,0:T(8,128)(2,1)S(1)} %get-tuple-element.40.refs_1_, bf16[32,48,128]{2,1,0:T(8,128)(2,1)S(1)} %collective-permute-done.6.refs_2_, bf16[128,48,128]{2,1,0:T(8,128)(2,1)S(1)} %get-tuple-element.38.refs_3_, ...), custom_call_target="tpu_custom_call" | custom-call | flops 37748736 | bytes 2359296 | tf_op jit(solution)/shard_map/product/pallas_call | solution.py:404
  46.6 0.0 collective-permute-done.5.refs_2_
  46.6 3.3 %product.3 = bf16[48,48,128]{2,1,0:T(8,128)(2,1)} custom-call(bf16[48,48,128]{2,1,0:T(8,128)(2,1)S(1)} %get-tuple-element.23.refs_0_, bf16[16,48,128]{2,1,0:T(8,128)(2,1)S(1)} %mine.3.refs_1_, bf16[16,48,128]{2,1,0:T(8,128)(2,1)S(1)} %collective-permute-done.5.refs_2_, bf16[128,48,128]{2,1,0:T(8,128)(2,1)S(1)} %get-tuple-element.38.refs_3_, ...), custom_call_target="tpu_custom_call" | custom-call | flops 18874368 | bytes 2359296 | tf_op jit(solution)/shard_map/product/pallas_call | solution.py:404
  (6 shorter events, 0.0 us)
Async XLA Ops:
  0.0 30.3 %collective-permute-start = (bf16[48,48,128]{2,1,0:T(8,128)(2,1)}, bf16[48,48,128]{2,1,0:T(8,128)(2,1)S(1)}, u32[]{:S(2)}, u32[]{:S(2)}) collective-permute-start(bf16[48,48,128]{2,1,0:T(8,128)(2,1)} %pair_ref.1), channel_id=1, source_target_pairs={{0,3},{1,0},{2,1},{3,2},{4,7},{5,4},{6,5},{7,6},{8,11},{9,8},{10,9... | collective-permute-start | bytes 1769480 | tf_op jit(solution)/shard_map/ppermute | solution.py:33
  3.5 13.8 %collective-permute-start.2 = (bf16[32,48,128]{2,1,0:T(8,128)(2,1)S(1)}, bf16[32,48,128]{2,1,0:T(8,128)(2,1)S(1)}, u32[]{:S(2)}, u32[]{:S(2)}) collective-permute-start(bf16[32,48,128]{2,1,0:T(8,128)(2,1)S(1)} %slice.3), channel_id=1, source_target_pairs={{0,8},{1,12},{5,9},{6,13},{10,6},{11,2},{15,7},{12,3},{16,24},{17,... | collective-permute-start | bytes 1179656 | tf_op jit(solution)/shard_map/ppermute | solution.py:286
  8.0 13.7 %collective-permute-start.1 = (bf16[32,48,128]{2,1,0:T(8,128)(2,1)S(1)}, bf16[32,48,128]{2,1,0:T(8,128)(2,1)S(1)}, u32[]{:S(2)}, u32[]{:S(2)}) collective-permute-start(bf16[32,48,128]{2,1,0:T(8,128)(2,1)S(1)} %slice.3), channel_id=1, source_target_pairs={{0,4},{1,0},{5,1},{6,5},{10,14},{11,10},{15,11},{12,15},{16,20},{1... | collective-permute-start | bytes 1179656 | tf_op jit(solution)/shard_map/ppermute | solution.py:286
  10.6 1.1 %copy-start = (bf16[48,48,128]{2,1,0:T(8,128)(2,1)S(1)}, bf16[48,48,128]{2,1,0:T(8,128)(2,1)}, u32[]{:S(2)}) copy-start(bf16[48,48,128]{2,1,0:T(8,128)(2,1)} %pair_ref.1) | copy-start | bytes 1769476
  11.6 0.9 %copy-start.5 = (bf16[128,512]{1,0:T(8,128)(2,1)S(1)}, bf16[128,512]{1,0:T(8,128)(2,1)}, u32[]{:S(2)}) copy-start(bf16[128,512]{1,0:T(8,128)(2,1)} %weights_ref.1) | copy-start | bytes 393220
  12.5 0.7 %copy-start.6 = (f32[128]{0:T(128)S(1)}, f32[128]{0:T(128)}, u32[]{:S(2)}) copy-start(f32[128]{0:T(128)} %param.11) | copy-start | bytes 1540
  13.2 0.7 %copy-start.7 = (f32[128]{0:T(128)S(1)}, f32[128]{0:T(128)}, u32[]{:S(2)}) copy-start(f32[128]{0:T(128)} %param.12) | copy-start | bytes 1540
  14.9 15.3 %copy-start.2 = (bf16[128,128]{1,0:T(8,128)(2,1)S(1)}, bf16[128,128]{1,0:T(8,128)(2,1)}, u32[]{:S(2)}) copy-start(bf16[128,128]{1,0:T(8,128)(2,1)} %refs_6_.3) | copy-start | bytes 98308
  22.4 20.4 %collective-permute-start.6 = (bf16[32,48,128]{2,1,0:T(8,128)(2,1)S(1)}, bf16[32,48,128]{2,1,0:T(8,128)(2,1)S(1)}, u32[]{:S(2)}, u32[]{:S(2)}) collective-permute-start(bf16[32,48,128]{2,1,0:T(8,128)(2,1)S(1)} %get-tuple-element.40.refs_1_), channel_id=1, source_target_pairs={{8,12},{12,8},{0,4},{9,13},{13,9},{5,1},{6,2},{2,6},{10,14},{7,3},... | collective-permute-start | bytes 1179656 | tf_op jit(solution)/shard_map/ppermute | solution.py:286
  26.8 15.9 %copy-start.1 = (bf16[128,128]{1,0:T(8,128)(2,1)S(1)}, bf16[128,128]{1,0:T(8,128)(2,1)}, u32[]{:S(2)}) copy-start(bf16[128,128]{1,0:T(8,128)(2,1)} %refs_7_.3) | copy-start | bytes 98308
  26.9 15.9 %copy-start.3 = (f32[128]{0:T(128)S(1)}, f32[128]{0:T(128)}, u32[]{:S(2)}) copy-start(f32[128]{0:T(128)} %refs_5_.3) | copy-start | bytes 1540
  26.9 15.9 %copy-start.4 = (f32[128]{0:T(128)S(1)}, f32[128]{0:T(128)}, u32[]{:S(2)}) copy-start(f32[128]{0:T(128)} %refs_6_.5) | copy-start | bytes 1540
  26.9 8.9 %collective-permute-start.4 = (bf16[16,48,128]{2,1,0:T(8,128)(2,1)S(1)}, bf16[16,48,128]{2,1,0:T(8,128)(2,1)S(1)}, u32[]{:S(2)}, u32[]{:S(2)}) collective-permute-start(bf16[16,48,128]{2,1,0:T(8,128)(2,1)S(1)} %get-tuple-element.35), channel_id=1, source_target_pairs={{0,8},{1,12},{5,9},{6,13},{10,6},{11,2},{15,7},{12,3},{16,24},{17,... | collective-permute-start | bytes 589832 | tf_op jit(solution)/shard_map/ppermute | solution.py:286
  28.3 9.6 %collective-permute-start.3 = (bf16[16,48,128]{2,1,0:T(8,128)(2,1)S(1)}, bf16[16,48,128]{2,1,0:T(8,128)(2,1)S(1)}, u32[]{:S(2)}, u32[]{:S(2)}) collective-permute-start(bf16[16,48,128]{2,1,0:T(8,128)(2,1)S(1)} %get-tuple-element.35), channel_id=1, source_target_pairs={{0,4},{1,0},{5,1},{6,5},{10,14},{11,10},{15,11},{12,15},{16,20},{1... | collective-permute-start | bytes 589832 | tf_op jit(solution)/shard_map/ppermute | solution.py:286
  38.4 8.2 %collective-permute-start.5 = (bf16[16,48,128]{2,1,0:T(8,128)(2,1)S(1)}, bf16[16,48,128]{2,1,0:T(8,128)(2,1)S(1)}, u32[]{:S(2)}, u32[]{:S(2)}) collective-permute-start(bf16[16,48,128]{2,1,0:T(8,128)(2,1)S(1)} %mine.3.refs_1_), channel_id=1, source_target_pairs={{8,12},{12,8},{0,4},{9,13},{13,9},{5,1},{6,2},{2,6},{10,14},{7,3},... | collective-permute-start | bytes 589832 | tf_op jit(solution)/shard_map/ppermute | solution.py:286

commit v20 on v16

--- a/solution.py
+++ b/solution.py
@@ -212,12 +212,13 @@
         centered = product[pl.ds(channel * apart, count), :rows] - average
         totals[channel % ways] += centered * centered
     scale = lax.rsqrt(sum(totals) / hidden + 1e-05)
-    for channel in range(hidden):
-        place = pl.ds(channel * apart, count)
-        centered = product[place, :rows] - average
-        product[place, :rows] = centered * scale * gain_ref[channel] + bias_ref[channel]
+    gain, bias = (
+        jnp.broadcast_to(ref[...], (LANES, hidden)).T[:, :rows] for ref in (gain_ref, bias_ref)
+    )
     for token in range(count):
-        mixed = product[pl.ds(token, hidden, stride=apart), :][:, :rows].astype(jnp.bfloat16)
+        values = product[pl.ds(token, hidden, stride=apart), :][:, :rows]
+        centered = values - average[token : token + 1]
+        mixed = (centered * scale[token : token + 1] * gain + bias).astype(jnp.bfloat16)
         updates[pl.ds(token, rows, stride=apart), :] = lax.dot_general(
             mixed, weights_ref[...], (((0,), (0,)), ((), ())), preferred_element_type=jnp.float32
         )
@@ -295,6 +296,7 @@
     depth = window * columns
     width = -(-depth // LANES) * LANES
     in_gain, in_bias = in_gain.reshape(1, channels), in_bias.reshape(1, channels)
+    out_gain, out_bias = out_gain.reshape(1, hidden), out_bias.reshape(1, hidden)
     block = 2 * tokens * max(channels, hidden)
     by_hops = row_count == 4 and col_count == 4
     last = 16
@@ -390,7 +392,7 @@
             out_shape=jax.ShapeDtypeStruct(
                 (rows, columns if last else count, channels), jnp.bfloat16
             ),
-            in_specs=[VMEM] * (len(band) + 2) + [SMEM, SMEM, VMEM] + [VMEM] * len(done) * last,
+            in_specs=[VMEM] * (len(band) + 2) + [VMEM] * (3 + len(done) * last),
             out_specs=ANY if last else VMEM,
             scratch_shapes=scratch,
             compiler_params=params(2 * block, 2 * hidden * (rows + 2 * count) * width),

time: 41 us -> 39.8 us (0.971)
  the two profiles are of different devices: /device:TPU:12 before, /device:TPU:24 now
where the time goes in v20:
time: 39.8 us; the launch traced here: 39.3 us
  starting transfers between devices  12.7 us (32%)
  Pallas kernels  12.3 us (31%)
  waiting for transfers between devices  8.48 us (21%)
  local copies, waits for them, and re-layouts  4.89 us (12%)
  between operations  0.82 us (2%)
    ppermute x6, starting transfers between devices, move(): lax.ppermute(array, ('row', 'col'), [(r * 4 + c, to_r * 4 + to_c) for (r,...  11.8 us
    ppermute x6, waiting for transfers between devices, move(): lax.ppermute(array, ('row', 'col'), [(r * 4 + c, to_r * 4 + to_c) for (r,...  8.48 us
    pallas_call x2, Pallas kernels, on_device(): pl.pallas_call(functools.partial(product_kernel, picks, place, len(band),...  5.24 us
    pallas_call x2, Pallas kernels, left_of(): pl.pallas_call(functools.partial(left_kernel, here, window), out_shape=sh...  4.71 us
    unnamed x15, local copies, waits for them, and re-layouts  2.95 us
    pallas_call x2, Pallas kernels, mine_of(): pl.pallas_call(functools.partial(mine_kernel, first), out_shape=jax.Shape...  1.21 us
    pallas_call x1, Pallas kernels, on_device(): pl.pallas_call(functools.partial(own_kernel, len(passed)), out_shape=[jax...  1.2 us
    slice x1, local copies, waits for them, and re-layouts, on_device(): soon = pair_state[:spans[0][1]]  1.05 us
  transfers between devices with their start and end apart: 7, of which 3 were waited for; matrix products, arithmetic and copies ran while one was open for 5% of the time, Pallas kernels for 25%

profile of v20, /device:TPU:24, one launch (start us, length us, event | category | flops | bytes accessed | tf_op | source)
XLA Modules:
  0.0 39.3 jit_solution(11404789273877885955)
XLA Ops:
  0.0 1.0 %collective-permute-start = (bf16[48,48,128]{2,1,0:T(8,128)(2,1)}, bf16[48,48,128]{2,1,0:T(8,128)(2,1)S(1)}, u32[]{:S(2)}, u32[]{:S(2)}) collective-permute-start(bf16[48,48,128]{2,1,0:T(8,128)(2,1)} %refs_5_.1), channel_id=1, source_target_pairs={{0,3},{1,0},{2,1},{3,2},{4,7},{5,4},{6,5},{7,6},{8,11},{9,8},{10,9... | collective-permute-start | bytes 1769480 | tf_op jit(solution)/shard_map/ppermute | solution.py:33
  1.0 1.1 %slice.11 = bf16[32,48,128]{2,1,0:T(8,128)(2,1)S(1)} slice(bf16[48,48,128]{2,1,0:T(8,128)(2,1)} %refs_5_.1), slice={[0:32], [0:48], [0:128]} | slice | bytes 786432 | tf_op jit(solution)/shard_map/slice | solution.py:307
  2.0 2.2 %collective-permute-start.2 = (bf16[32,48,128]{2,1,0:T(8,128)(2,1)S(1)}, bf16[32,48,128]{2,1,0:T(8,128)(2,1)S(1)}, u32[]{:S(2)}, u32[]{:S(2)}) collective-permute-start(bf16[32,48,128]{2,1,0:T(8,128)(2,1)S(1)} %slice.11), channel_id=1, source_target_pairs={{0,8},{1,12},{5,9},{6,13},{10,6},{11,2},{15,7},{12,3},{16,24},{17,... | collective-permute-start | bytes 1179656 | tf_op jit(solution)/shard_map/ppermute | solution.py:274
  4.2 2.3 %collective-permute-start.1 = (bf16[32,48,128]{2,1,0:T(8,128)(2,1)S(1)}, bf16[32,48,128]{2,1,0:T(8,128)(2,1)S(1)}, u32[]{:S(2)}, u32[]{:S(2)}) collective-permute-start(bf16[32,48,128]{2,1,0:T(8,128)(2,1)S(1)} %slice.11), channel_id=1, source_target_pairs={{0,4},{1,0},{5,1},{6,5},{10,14},{11,10},{15,11},{12,15},{16,20},{1... | collective-permute-start | bytes 1179656 | tf_op jit(solution)/shard_map/ppermute | solution.py:274
  7.2 0.9 %fusion = (bf16[128,256]{1,0:T(8,128)(2,1)S(1)}, bf16[128,256]{1,0:T(8,128)(2,1)S(1)}) fusion(bf16[128,512]{1,0:T(8,128)(2,1)} %param.13), kind=kLoop, calls=%fused_computation | loop fusion | bytes 262144 | tf_op jit(solution)/shard_map/slice | solution.py:312
  8.1 0.1 copy.11
  8.3 0.0 copy-start.1
  8.3 0.7 %copy-done.1 = bf16[128,128]{1,0:T(8,128)(2,1)S(1)} copy-done((bf16[128,128]{1,0:T(8,128)(2,1)S(1)}, bf16[128,128]{1,0:T(8,128)(2,1)}, u32[]{:S(2)}) %copy-start.1) | copy-done | bytes 32792
  9.0 0.8 %copy-done.2 = bf16[128,128]{1,0:T(8,128)(2,1)S(1)} copy-done((bf16[128,128]{1,0:T(8,128)(2,1)S(1)}, bf16[128,128]{1,0:T(8,128)(2,1)}, u32[]{:S(2)}) %copy-start.2) | copy-done | bytes 32792
  9.8 0.7 %copy-done.5 = f32[128]{0:T(128)S(1)} copy-done((f32[128]{0:T(128)S(1)}, f32[128]{0:T(128)}, u32[]{:S(2)}) %copy-start.5) | copy-done | bytes 536
  10.4 0.7 %copy-done.6 = f32[128]{0:T(128)S(1)} copy-done((f32[128]{0:T(128)S(1)}, f32[128]{0:T(128)}, u32[]{:S(2)}) %copy-start.6) | copy-done | bytes 536
  11.1 1.2 %own.1 = (f32[48,48,128]{2,1,0:T(8,128)S(1)}, bf16[48,48,128]{2,1,0:T(8,128)(2,1)S(1)}, f32[1,128]{1,0:T(1,128)S(1)}, f32[1,128]{1,0:T(1,128)S(1)}, bf16[128,256...) custom-call(s32[1]{0:T(128)S(6)} %copy.12.tokens_ref, ...), custom_call_target="tpu_custom_call" | custom-call | flops 226492416 | bytes 2359296 | tf_op jit(solution)/shard_map/own/pallas_call | solution.py:314
  12.3 2.3 %left.2 = (bf16[128,48,128]{2,1,0:T(8,128)(2,1)S(1)}, bf16[16,48,128]{2,1,0:T(8,128)(2,1)S(1)}) custom-call(s32[1]{0:T(128)S(6)} %copy.12.tokens_ref, bf16[48,48,128]{2,1,0:T(8,128)(2,1)S(1)} %get-tuple-element.24.refs_0_, f32[1,128]{1,0:T(1,128)S(1)} %get-tuple-element.21.refs_1_.gain_ref, f32[1,128]{1,0:T(1,128)S(1)} %get-tuple-element.22.refs_2_.bias_ref, ...), custom_call_target="tpu_custom_call" | custom-call | flops 150994944 | bytes 4718592 | tf_op jit(solution)/shard_map/left/pallas_call | solution.py:333
  14.6 1.9 %collective-permute-start.4 = (bf16[16,48,128]{2,1,0:T(8,128)(2,1)S(1)}, bf16[16,48,128]{2,1,0:T(8,128)(2,1)S(1)}, u32[]{:S(2)}, u32[]{:S(2)}) collective-permute-start(bf16[16,48,128]{2,1,0:T(8,128)(2,1)S(1)} %get-tuple-element.28), channel_id=1, source_target_pairs={{0,8},{1,12},{5,9},{6,13},{10,6},{11,2},{15,7},{12,3},{16,24},{17,... | collective-permute-start | bytes 589832 | tf_op jit(solution)/shard_map/ppermute | solution.py:274
  16.5 1.5 %collective-permute-start.3 = (bf16[16,48,128]{2,1,0:T(8,128)(2,1)S(1)}, bf16[16,48,128]{2,1,0:T(8,128)(2,1)S(1)}, u32[]{:S(2)}, u32[]{:S(2)}) collective-permute-start(bf16[16,48,128]{2,1,0:T(8,128)(2,1)S(1)} %get-tuple-element.28), channel_id=1, source_target_pairs={{0,4},{1,0},{5,1},{6,5},{10,14},{11,10},{15,11},{12,15},{16,20},{1... | collective-permute-start | bytes 589832 | tf_op jit(solution)/shard_map/ppermute | solution.py:274
  18.0 0.0 collective-permute-done.2.far_ref
  18.0 0.0 collective-permute-done.1.near_ref
  18.0 0.7 %mine.2.refs_1_ = bf16[32,48,128]{2,1,0:T(8,128)(2,1)S(1)} custom-call(s32[1]{0:T(128)S(6)} %copy.12.tokens_ref, bf16[32,48,128]{2,1,0:T(8,128)(2,1)S(1)} %collective-permute-done.1.near_ref, bf16[32,48,128]{2,1,0:T(8,128)(2,1)S(1)} %collective-permute-done.2.far_ref, f32[1,128]{1,0:T(1,128)S(1)} %get-tuple-element.21.refs_1_.gain_ref, ...), custom_call_target="tpu_custom_call" | custom-call | flops 100663296 | bytes 1179648 | tf_op jit(solution)/shard_map/mine/pallas_call | solution.py:353
  18.7 0.0 copy-start.3
  18.7 0.0 copy-start.4
  18.7 1.9 %collective-permute-start.6 = (bf16[32,48,128]{2,1,0:T(8,128)(2,1)S(1)}, bf16[32,48,128]{2,1,0:T(8,128)(2,1)S(1)}, u32[]{:S(2)}, u32[]{:S(2)}) collective-permute-start(bf16[32,48,128]{2,1,0:T(8,128)(2,1)S(1)} %mine.2.refs_1_), channel_id=1, source_target_pairs={{8,12},{12,8},{0,4},{9,13},{13,9},{5,1},{6,2},{2,6},{10,14},{7,3},... | collective-permute-start | bytes 1179656 | tf_op jit(solution)/shard_map/ppermute | solution.py:274
  20.7 0.0 collective-permute-done.refs_0_
  20.7 2.4 %left.3.refs_3_ = bf16[128,48,128]{2,1,0:T(8,128)(2,1)S(1)} custom-call(s32[1]{0:T(128)S(6)} %copy.12.tokens_ref, bf16[48,48,128]{2,1,0:T(8,128)(2,1)S(1)} %collective-permute-done.refs_0_, f32[1,128]{1,0:T(1,128)S(1)} %get-tuple-element.21.refs_1_.gain_ref, f32[1,128]{1,0:T(1,128)S(1)} %get-tuple-element.22.refs_2_.bias_ref, ...), custom_call_target="tpu_custom_call" | custom-call | flops 150994944 | bytes 4718592 | tf_op jit(solution)/shard_map/left/pallas_call | solution.py:333
  23.1 2.5 %collective-permute-done.4.far_ref = bf16[16,48,128]{2,1,0:T(8,128)(2,1)S(1)} collective-permute-done((bf16[16,48,128]{2,1,0:T(8,128)(2,1)S(1)}, bf16[16,48,128]{2,1,0:T(8,128)(2,1)S(1)}, u32[]{:S(2)}, u32[]{:S(2)}) %collective-permute-start.4) | collective-permute-done | bytes 196640 | tf_op jit(solution)/shard_map/ppermute | solution.py:274
  25.6 0.0 collective-permute-done.3.near_ref
  25.6 0.5 %mine.3.refs_1_ = bf16[16,48,128]{2,1,0:T(8,128)(2,1)S(1)} custom-call(s32[1]{0:T(128)S(6)} %copy.12.tokens_ref, bf16[16,48,128]{2,1,0:T(8,128)(2,1)S(1)} %collective-permute-done.3.near_ref, bf16[16,48,128]{2,1,0:T(8,128)(2,1)S(1)} %collective-permute-done.4.far_ref, f32[1,128]{1,0:T(1,128)S(1)} %get-tuple-element.21.refs_1_.gain_ref, ...), custom_call_target="tpu_custom_call" | custom-call | flops 50331648 | bytes 589824 | tf_op jit(solution)/shard_map/mine/pallas_call | solution.py:353
  26.1 1.9 %collective-permute-start.5 = (bf16[16,48,128]{2,1,0:T(8,128)(2,1)S(1)}, bf16[16,48,128]{2,1,0:T(8,128)(2,1)S(1)}, u32[]{:S(2)}, u32[]{:S(2)}) collective-permute-start(bf16[16,48,128]{2,1,0:T(8,128)(2,1)S(1)} %mine.3.refs_1_), channel_id=1, source_target_pairs={{8,12},{12,8},{0,4},{9,13},{13,9},{5,1},{6,2},{2,6},{10,14},{7,3},... | collective-permute-start | bytes 589832 | tf_op jit(solution)/shard_map/ppermute | solution.py:274
  28.0 5.4 %collective-permute-done.6.refs_2_ = bf16[32,48,128]{2,1,0:T(8,128)(2,1)S(1)} collective-permute-done((bf16[32,48,128]{2,1,0:T(8,128)(2,1)S(1)}, bf16[32,48,128]{2,1,0:T(8,128)(2,1)S(1)}, u32[]{:S(2)}, u32[]{:S(2)}) %collective-permute-start.6) | collective-permute-done | bytes 393248 | tf_op jit(solution)/shard_map/ppermute | solution.py:274
  33.4 0.0 copy-done.4
  33.4 2.6 %product.2.refs_8_ = bf16[48,32,128]{2,1,0:T(8,128)(2,1)S(1)} custom-call(bf16[48,48,128]{2,1,0:T(8,128)(2,1)S(1)} %get-tuple-element.20.refs_0_, bf16[32,48,128]{2,1,0:T(8,128)(2,1)S(1)} %mine.2.refs_1_, bf16[32,48,128]{2,1,0:T(8,128)(2,1)S(1)} %collective-permute-done.6.refs_2_, bf16[128,48,128]{2,1,0:T(8,128)(2,1)S(1)} %left.3.refs_3_, ...), custom_call_target="tpu_custom_call" | custom-call | flops 37748736 | bytes 2359296 | tf_op jit(solution)/shard_map/product/pallas_call | solution.py:390
  36.1 0.6 %collective-permute-done.5.refs_2_ = bf16[16,48,128]{2,1,0:T(8,128)(2,1)S(1)} collective-permute-done((bf16[16,48,128]{2,1,0:T(8,128)(2,1)S(1)}, bf16[16,48,128]{2,1,0:T(8,128)(2,1)S(1)}, u32[]{:S(2)}, u32[]{:S(2)}) %collective-permute-start.5) | collective-permute-done | bytes 196640 | tf_op jit(solution)/shard_map/ppermute | solution.py:274
  36.7 2.6 %product.3 = bf16[48,48,128]{2,1,0:T(8,128)(2,1)} custom-call(bf16[48,48,128]{2,1,0:T(8,128)(2,1)S(1)} %get-tuple-element.20.refs_0_, bf16[16,48,128]{2,1,0:T(8,128)(2,1)S(1)} %mine.3.refs_1_, bf16[16,48,128]{2,1,0:T(8,128)(2,1)S(1)} %collective-permute-done.5.refs_2_, bf16[128,48,128]{2,1,0:T(8,128)(2,1)S(1)} %left.3.refs_3_, ...), custom_call_target="tpu_custom_call" | custom-call | flops 18874368 | bytes 2359296 | tf_op jit(solution)/shard_map/product/pallas_call | solution.py:390
  (6 shorter events, 0.0 us)
Async XLA Ops:
  0.0 8.2 %copy-start = (bf16[48,48,128]{2,1,0:T(8,128)(2,1)S(1)}, bf16[48,48,128]{2,1,0:T(8,128)(2,1)}, u32[]{:S(2)}) copy-start(bf16[48,48,128]{2,1,0:T(8,128)(2,1)} %refs_5_.1) | copy-start | bytes 1769476
  0.0 20.7 %collective-permute-start = (bf16[48,48,128]{2,1,0:T(8,128)(2,1)}, bf16[48,48,128]{2,1,0:T(8,128)(2,1)S(1)}, u32[]{:S(2)}, u32[]{:S(2)}) collective-permute-start(bf16[48,48,128]{2,1,0:T(8,128)(2,1)} %refs_5_.1), channel_id=1, source_target_pairs={{0,3},{1,0},{2,1},{3,2},{4,7},{5,4},{6,5},{7,6},{8,11},{9,8},{10,9... | collective-permute-start | bytes 1769480 | tf_op jit(solution)/shard_map/ppermute | solution.py:33
  2.0 16.0 %collective-permute-start.2 = (bf16[32,48,128]{2,1,0:T(8,128)(2,1)S(1)}, bf16[32,48,128]{2,1,0:T(8,128)(2,1)S(1)}, u32[]{:S(2)}, u32[]{:S(2)}) collective-permute-start(bf16[32,48,128]{2,1,0:T(8,128)(2,1)S(1)} %slice.11), channel_id=1, source_target_pairs={{0,8},{1,12},{5,9},{6,13},{10,6},{11,2},{15,7},{12,3},{16,24},{17,... | collective-permute-start | bytes 1179656 | tf_op jit(solution)/shard_map/ppermute | solution.py:274
  4.2 13.8 %collective-permute-start.1 = (bf16[32,48,128]{2,1,0:T(8,128)(2,1)S(1)}, bf16[32,48,128]{2,1,0:T(8,128)(2,1)S(1)}, u32[]{:S(2)}, u32[]{:S(2)}) collective-permute-start(bf16[32,48,128]{2,1,0:T(8,128)(2,1)S(1)} %slice.11), channel_id=1, source_target_pairs={{0,4},{1,0},{5,1},{6,5},{10,14},{11,10},{15,11},{12,15},{16,20},{1... | collective-permute-start | bytes 1179656 | tf_op jit(solution)/shard_map/ppermute | solution.py:274
  8.3 0.8 %copy-start.1 = (bf16[128,128]{1,0:T(8,128)(2,1)S(1)}, bf16[128,128]{1,0:T(8,128)(2,1)}, u32[]{:S(2)}) copy-start(bf16[128,128]{1,0:T(8,128)(2,1)} %gate_weights_ref.1) | copy-start | bytes 98308
  9.0 0.8 %copy-start.2 = (bf16[128,128]{1,0:T(8,128)(2,1)S(1)}, bf16[128,128]{1,0:T(8,128)(2,1)}, u32[]{:S(2)}) copy-start(bf16[128,128]{1,0:T(8,128)(2,1)} %refs_4_.1) | copy-start | bytes 98308
  9.8 0.7 %copy-start.5 = (f32[128]{0:T(128)S(1)}, f32[128]{0:T(128)}, u32[]{:S(2)}) copy-start(f32[128]{0:T(128)} %param.11) | copy-start | bytes 1540
  10.4 0.7 %copy-start.6 = (f32[128]{0:T(128)S(1)}, f32[128]{0:T(128)}, u32[]{:S(2)}) copy-start(f32[128]{0:T(128)} %param.12) | copy-start | bytes 1540
  14.6 11.0 %collective-permute-start.4 = (bf16[16,48,128]{2,1,0:T(8,128)(2,1)S(1)}, bf16[16,48,128]{2,1,0:T(8,128)(2,1)S(1)}, u32[]{:S(2)}, u32[]{:S(2)}) collective-permute-start(bf16[16,48,128]{2,1,0:T(8,128)(2,1)S(1)} %get-tuple-element.28), channel_id=1, source_target_pairs={{0,8},{1,12},{5,9},{6,13},{10,6},{11,2},{15,7},{12,3},{16,24},{17,... | collective-permute-start | bytes 589832 | tf_op jit(solution)/shard_map/ppermute | solution.py:274
  16.5 9.1 %collective-permute-start.3 = (bf16[16,48,128]{2,1,0:T(8,128)(2,1)S(1)}, bf16[16,48,128]{2,1,0:T(8,128)(2,1)S(1)}, u32[]{:S(2)}, u32[]{:S(2)}) collective-permute-start(bf16[16,48,128]{2,1,0:T(8,128)(2,1)S(1)} %get-tuple-element.28), channel_id=1, source_target_pairs={{0,4},{1,0},{5,1},{6,5},{10,14},{11,10},{15,11},{12,15},{16,20},{1... | collective-permute-start | bytes 589832 | tf_op jit(solution)/shard_map/ppermute | solution.py:274
  18.7 14.7 %copy-start.3 = (f32[128]{0:T(128)S(1)}, f32[128]{0:T(128)}, u32[]{:S(2)}) copy-start(f32[128]{0:T(128)} %param.15) | copy-start | bytes 1540
  18.7 14.7 %copy-start.4 = (f32[128]{0:T(128)S(1)}, f32[128]{0:T(128)}, u32[]{:S(2)}) copy-start(f32[128]{0:T(128)} %param.16) | copy-start | bytes 1540
  18.7 14.7 %collective-permute-start.6 = (bf16[32,48,128]{2,1,0:T(8,128)(2,1)S(1)}, bf16[32,48,128]{2,1,0:T(8,128)(2,1)S(1)}, u32[]{:S(2)}, u32[]{:S(2)}) collective-permute-start(bf16[32,48,128]{2,1,0:T(8,128)(2,1)S(1)} %mine.2.refs_1_), channel_id=1, source_target_pairs={{8,12},{12,8},{0,4},{9,13},{13,9},{5,1},{6,2},{2,6},{10,14},{7,3},... | collective-permute-start | bytes 1179656 | tf_op jit(solution)/shard_map/ppermute | solution.py:274
  26.1 10.6 %collective-permute-start.5 = (bf16[16,48,128]{2,1,0:T(8,128)(2,1)S(1)}, bf16[16,48,128]{2,1,0:T(8,128)(2,1)S(1)}, u32[]{:S(2)}, u32[]{:S(2)}) collective-permute-start(bf16[16,48,128]{2,1,0:T(8,128)(2,1)S(1)} %mine.3.refs_1_), channel_id=1, source_target_pairs={{8,12},{12,8},{0,4},{9,13},{13,9},{5,1},{6,2},{2,6},{10,14},{7,3},... | collective-permute-start | bytes 589832 | tf_op jit(solution)/shard_map/ppermute | solution.py:274

commit v21 on v20

--- a/solution.py
+++ b/solution.py
@@ -51,7 +51,7 @@
     return layer_norm(values, gain_ref[...], bias_ref[...]).astype(jnp.bfloat16)
 
 
-def mine_kernel(first, tokens_ref, near_ref, far_ref, gain_ref, bias_ref, weights_ref, out_ref):
+def mine_kernel(first, tokens_ref, far_ref, near_ref, gain_ref, bias_ref, weights_ref, out_ref):
     count, columns, _ = out_ref.shape
     col_pos, place = lax.axis_index("col"), hop_place()
     third_block = jnp.where((place == 0) | (place == 3), (col_pos + 1) % 4, col_pos)
@@ -79,7 +79,12 @@
 
 
 def own_kernel(passes, tokens_ref, pair_ref, gate_weights_ref, *refs):
-    passed, (gate_ref, right_ref), handed = refs[:passes], refs[passes : passes + 2], refs[passes + 2 :]
+    passed, (gate_ref, right_ref, later_ref), handed = (
+        refs[:passes],
+        refs[passes : passes + 3],
+        refs[passes + 3 :],
+    )
+    later_ref[...] = pair_ref[pl.ds(pair_ref.shape[0] - later_ref.shape[0], later_ref.shape[0])]
     gain_ref, bias_ref, right_weights_ref = passed[:3]
     for source, target in zip(passed, handed):
         target[...] = source[...]
@@ -98,12 +103,8 @@
             right_ref[first + row] = part
 
 
-def left_kernel(here, blocks, tokens_ref, *refs):
-    pair_refs, refs = refs[: len(here)], refs[len(here) :]
-    gain_ref, bias_ref, weights_ref, *base_refs, left_ref, scratch = refs
-    if here[0] == 0:
-        *base_refs, left_ref, later_ref = (*base_refs, left_ref)
-        later_ref[...] = pair_refs[0][pl.ds(pair_refs[0].shape[0] - later_ref.shape[0], later_ref.shape[0])]
+def left_kernel(blocks, tokens_ref, *refs):
+    pair_refs, (gain_ref, bias_ref, weights_ref, left_ref, scratch) = refs[:blocks], refs[blocks:]
     rows, columns, channels = pair_refs[0].shape
     hidden, _, width = left_ref.shape
     tokens = tokens_ref[0]
@@ -121,9 +122,7 @@
     for first in range(0, rows, step):
         normed = [normed_rows(ref[pl.ds(first, step)], gain_ref, bias_ref) for ref in pair_refs]
         for row in range(step):
-            thirds = [jnp.zeros((columns, channels), jnp.bfloat16)] * blocks
-            for at, piece in zip(here, normed):
-                thirds[at] = piece[row * columns : (row + 1) * columns]
+            thirds = [piece[row * columns : (row + 1) * columns] for piece in normed]
             both = lax.dot_general(
                 weights_ref[...],
                 jnp.concatenate(thirds + padding, axis=0),
@@ -140,8 +139,6 @@
     for channel in range(hidden):
         for at in range(0, width, LANES):
             one = scratch[at // LANES, pl.ds(channel * pitch(rows), rows), :].astype(jnp.bfloat16)
-            for base_ref in base_refs:
-                one += base_ref[channel, :, at : at + LANES]
             left_ref[channel, :, at : at + LANES] = one
 
 
@@ -305,50 +302,43 @@
     if by_hops:
         near, far, share = hops()
         soon = pair_state[: spans[0][1]]
-        arrived = [(move(soon, near), move(soon, far))]
+        arrived = [(move(soon, far), move(soon, near))]
     pairs = [pair_state]
     for _ in range(window - 1):
         pairs.append(shifted(pairs[-1], "col", -1))
     left_weights, right_weights = in_weights[:, : 2 * hidden].T, in_weights[:, 2 * hidden :]
     passed = [in_gain, in_bias, right_weights, left_weights, out_weights, pair_state]
-    gate, right, *handed = pl.pallas_call(
+    gate, right, later, *handed = pl.pallas_call(
         functools.partial(own_kernel, len(passed)),
         out_shape=[
             jax.ShapeDtypeStruct((rows, columns, channels), jnp.float32),
             jax.ShapeDtypeStruct((rows, columns, hidden), jnp.bfloat16),
+            jax.ShapeDtypeStruct((spans[1][1], columns, channels), jnp.bfloat16),
         ]
         + [jax.ShapeDtypeStruct(array.shape, array.dtype) for array in passed],
         in_specs=[SMEM] + [VMEM] * (2 + len(passed)),
-        out_specs=[VMEM] * (2 + len(passed)),
+        out_specs=[VMEM] * (3 + len(passed)),
         compiler_params=params(6 * block),
         cost_estimate=cost(6 * tokens * channels * hidden, 8 * tokens * channels),
         name="own",
     )(token_count, pair_state, gate_weights, *passed)
     in_gain, in_bias, right_weights, left_weights, out_weights, pairs[0] = handed
 
-    def left_of(here, *base):
-        shapes = [jax.ShapeDtypeStruct((hidden, rows, width), jnp.bfloat16)]
-        if here[0] == 0:
-            shapes.append(jax.ShapeDtypeStruct((spans[1][1], columns, channels), jnp.bfloat16))
+    def left_of(pairs):
         return pl.pallas_call(
-            functools.partial(left_kernel, here, window),
-            out_shape=shapes,
-            in_specs=[SMEM] + [VMEM] * (len(here) + 3 + len(base)),
-            out_specs=[VMEM] * len(shapes),
+            functools.partial(left_kernel, window),
+            out_shape=jax.ShapeDtypeStruct((hidden, rows, width), jnp.bfloat16),
+            in_specs=[SMEM] + [VMEM] * (window + 3),
+            out_specs=VMEM,
             scratch_shapes=[
                 pltpu.VMEM((width // LANES, hidden * pitch(rows), LANES), jnp.float32)
             ],
-            compiler_params=params((len(here) + 2) * block, 6 * hidden * rows * width),
-            cost_estimate=cost(
-                4 * len(here) * tokens * channels * hidden, 6 * rows * width * hidden
-            ),
+            compiler_params=params((window + 2) * block, 6 * hidden * rows * width),
+            cost_estimate=cost(4 * window * tokens * channels * hidden, 6 * rows * width * hidden),
             name="left",
-        )(token_count, *[pairs[at] for at in here], in_gain, in_bias, left_weights, *base)
-
-    left, later_pair = left_of([0])
-    rest = list(range(1, window))
-
-    def mine_of(first, near_pair, far_pair):
+        )(token_count, *pairs, in_gain, in_bias, left_weights)
+
+    def mine_of(first, far_pair, near_pair):
         count = near_pair.shape[0]
         return pl.pallas_call(
             functools.partial(mine_kernel, first),
@@ -358,19 +348,19 @@
             compiler_params=params(2 * block),
             cost_estimate=cost(4 * count * columns * channels * hidden, 6 * count * columns * channels),
             name="mine",
-        )(token_count, near_pair, far_pair, in_gain, in_bias, right_weights)
+        )(token_count, far_pair, near_pair, in_gain, in_bias, right_weights)
 
     if by_hops:
-        arrived.append((move(later_pair, near), move(later_pair, far)))
+        arrived.append((move(later, far), move(later, near)))
         mine = [mine_of(0, *arrived[0])]
-        left, mine[0] = lax.optimization_barrier((left, mine[0]))
-        (left,) = left_of(rest, left)
+        pairs[0], mine[0] = lax.optimization_barrier((pairs[0], mine[0]))
+        left = left_of(pairs)
         left, *last = lax.optimization_barrier((left, *arrived[1]))
         mine.append(mine_of(spans[1][0], *last))
         bands = [[right, piece, move(piece, share)] for piece in mine]
         picks, place = [(0, 1, 1, 2), (1, 2, 2, 1)], hop_place
     else:
-        (left,) = left_of(rest, left)
+        left = left_of(pairs)
         bands, picks = band_by_sums(right, spans, window, row_count, col_count, columns)
         place = lambda: 0
 

time: 39.8 us -> 39.9 us (level)
  the two profiles are of different devices: /device:TPU:24 before, /device:TPU:0 now
where the time goes in v21:
time: 39.9 us; the launch traced here: 39.4 us
  starting transfers between devices  17.8 us (45%)
  Pallas kernels  10.7 us (27%)
  waiting for transfers between devices  5.26 us (13%)
  local copies, waits for them, and re-layouts  4.89 us (12%)
  between operations  0.82 us (2%)
    ppermute x6, starting transfers between devices, move(): lax.ppermute(array, ('row', 'col'), [(r * 4 + c, to_r * 4 + to_c) for (r,...  15.4 us
    ppermute x6, waiting for transfers between devices, move(): lax.ppermute(array, ('row', 'col'), [(r * 4 + c, to_r * 4 + to_c) for (r,...  5.26 us
    pallas_call x2, Pallas kernels, on_device(): pl.pallas_call(functools.partial(product_kernel, picks, place, len(band),...  5.24 us
    pallas_call x1, Pallas kernels, left_of(): pl.pallas_call(functools.partial(left_kernel, window), out_shape=jax.Shap...  3.01 us
    unnamed x15, local copies, waits for them, and re-layouts  2.95 us
    ppermute x1, starting transfers between devices, shifted(): lax.ppermute(array, axis, [(i, (i + by) % devices) for i in range(devices)])  2.41 us
    pallas_call x1, Pallas kernels, on_device(): pl.pallas_call(functools.partial(own_kernel, len(passed)), out_shape=[jax...  1.2 us
    pallas_call x2, Pallas kernels, mine_of(): pl.pallas_call(functools.partial(mine_kernel, first), out_shape=jax.Shape...  1.2 us
  transfers between devices with their start and end apart: 7, of which 3 were waited for; matrix products, arithmetic and copies ran while one was open for 5% of the time, Pallas kernels for 20%

profile of v21, /device:TPU:0, one launch (start us, length us, event | category | flops | bytes accessed | tf_op | source)
XLA Modules:
  0.0 39.4 jit_solution(4735202013677488684)
XLA Ops:
  0.0 2.4 %collective-permute-start.2 = (bf16[48,48,128]{2,1,0:T(8,128)(2,1)}, bf16[48,48,128]{2,1,0:T(8,128)(2,1)S(1)}, u32[]{:S(2)}, u32[]{:S(2)}) collective-permute-start(bf16[48,48,128]{2,1,0:T(8,128)(2,1)} %refs_5_.1), channel_id=1, source_target_pairs={{0,3},{1,0},{2,1},{3,2},{4,7},{5,4},{6,5},{7,6},{8,11},{9,8},{10,9... | collective-permute-start | bytes 1769480 | tf_op jit(solution)/shard_map/ppermute | solution.py:33
  2.4 1.1 %slice.11 = bf16[32,48,128]{2,1,0:T(8,128)(2,1)S(1)} slice(bf16[48,48,128]{2,1,0:T(8,128)(2,1)} %refs_5_.1), slice={[0:32], [0:48], [0:128]} | slice | bytes 786432 | tf_op jit(solution)/shard_map/slice | solution.py:304
  3.5 4.5 %collective-permute-start = (bf16[32,48,128]{2,1,0:T(8,128)(2,1)S(1)}, bf16[32,48,128]{2,1,0:T(8,128)(2,1)S(1)}, u32[]{:S(2)}, u32[]{:S(2)}) collective-permute-start(bf16[32,48,128]{2,1,0:T(8,128)(2,1)S(1)} %slice.11), channel_id=1, source_target_pairs={{0,8},{1,12},{5,9},{6,13},{10,6},{11,2},{15,7},{12,3},{16,24},{17,... | collective-permute-start | bytes 1179656 | tf_op jit(solution)/shard_map/ppermute | solution.py:271
  8.0 1.9 %collective-permute-start.1 = (bf16[32,48,128]{2,1,0:T(8,128)(2,1)S(1)}, bf16[32,48,128]{2,1,0:T(8,128)(2,1)S(1)}, u32[]{:S(2)}, u32[]{:S(2)}) collective-permute-start(bf16[32,48,128]{2,1,0:T(8,128)(2,1)S(1)} %slice.11), channel_id=1, source_target_pairs={{0,4},{1,0},{5,1},{6,5},{10,14},{11,10},{15,11},{12,15},{16,20},{1... | collective-permute-start | bytes 1179656 | tf_op jit(solution)/shard_map/ppermute | solution.py:271
  10.6 0.9 %fusion = (bf16[128,256]{1,0:T(8,128)(2,1)S(1)}, bf16[128,256]{1,0:T(8,128)(2,1)S(1)}) fusion(bf16[128,512]{1,0:T(8,128)(2,1)} %param.13), kind=kLoop, calls=%fused_computation | loop fusion | bytes 262144 | tf_op jit(solution)/shard_map/slice | solution.py:309
  11.5 0.1 copy.11
  11.6 0.0 copy-done
  11.6 0.0 copy-start.1
  11.6 0.7 %copy-done.1 = bf16[128,128]{1,0:T(8,128)(2,1)S(1)} copy-done((bf16[128,128]{1,0:T(8,128)(2,1)S(1)}, bf16[128,128]{1,0:T(8,128)(2,1)}, u32[]{:S(2)}) %copy-start.1) | copy-done | bytes 32792
  12.3 0.8 %copy-done.2 = bf16[128,128]{1,0:T(8,128)(2,1)S(1)} copy-done((bf16[128,128]{1,0:T(8,128)(2,1)S(1)}, bf16[128,128]{1,0:T(8,128)(2,1)}, u32[]{:S(2)}) %copy-start.2) | copy-done | bytes 32792
  13.1 0.7 %copy-done.5 = f32[128]{0:T(128)S(1)} copy-done((f32[128]{0:T(128)S(1)}, f32[128]{0:T(128)}, u32[]{:S(2)}) %copy-start.5) | copy-done | bytes 536
  13.8 0.7 %copy-done.6 = f32[128]{0:T(128)S(1)} copy-done((f32[128]{0:T(128)S(1)}, f32[128]{0:T(128)}, u32[]{:S(2)}) %copy-start.6) | copy-done | bytes 536
  14.4 1.2 %own.1 = (f32[48,48,128]{2,1,0:T(8,128)S(1)}, bf16[48,48,128]{2,1,0:T(8,128)(2,1)S(1)}, bf16[16,48,128]{2,1,0:T(8,128)(2,1)S(1)}, f32[1,128]{1,0:T(1,128)S(1)}, ...) custom-call(s32[1]{0:T(128)S(6)} %copy.12.tokens_ref, ...), custom_call_target="tpu_custom_call" | custom-call | flops 226492416 | bytes 2359296 | tf_op jit(solution)/shard_map/own/pallas_call | solution.py:311
  15.6 1.3 %collective-permute-start.3 = (bf16[16,48,128]{2,1,0:T(8,128)(2,1)S(1)}, bf16[16,48,128]{2,1,0:T(8,128)(2,1)S(1)}, u32[]{:S(2)}, u32[]{:S(2)}) collective-permute-start(bf16[16,48,128]{2,1,0:T(8,128)(2,1)S(1)} %get-tuple-element.26), channel_id=1, source_target_pairs={{0,8},{1,12},{5,9},{6,13},{10,6},{11,2},{15,7},{12,3},{16,24},{17,... | collective-permute-start | bytes 589832 | tf_op jit(solution)/shard_map/ppermute | solution.py:271
  16.9 1.9 %collective-permute-start.4 = (bf16[16,48,128]{2,1,0:T(8,128)(2,1)S(1)}, bf16[16,48,128]{2,1,0:T(8,128)(2,1)S(1)}, u32[]{:S(2)}, u32[]{:S(2)}) collective-permute-start(bf16[16,48,128]{2,1,0:T(8,128)(2,1)S(1)} %get-tuple-element.26), channel_id=1, source_target_pairs={{0,4},{1,0},{5,1},{6,5},{10,14},{11,10},{15,11},{12,15},{16,20},{1... | collective-permute-start | bytes 589832 | tf_op jit(solution)/shard_map/ppermute | solution.py:271
  18.9 0.0 collective-permute-done.far_ref
  18.9 4.7 %collective-permute-done.1.near_ref = bf16[32,48,128]{2,1,0:T(8,128)(2,1)S(1)} collective-permute-done((bf16[32,48,128]{2,1,0:T(8,128)(2,1)S(1)}, bf16[32,48,128]{2,1,0:T(8,128)(2,1)S(1)}, u32[]{:S(2)}, u32[]{:S(2)}) %collective-permute-start.1) | collective-permute-done | bytes 393248 | tf_op jit(solution)/shard_map/ppermute | solution.py:271
  23.6 0.7 %mine.2.refs_1_ = bf16[32,48,128]{2,1,0:T(8,128)(2,1)S(1)} custom-call(s32[1]{0:T(128)S(6)} %copy.12.tokens_ref, bf16[32,48,128]{2,1,0:T(8,128)(2,1)S(1)} %collective-permute-done.far_ref, bf16[32,48,128]{2,1,0:T(8,128)(2,1)S(1)} %collective-permute-done.1.near_ref, f32[1,128]{1,0:T(1,128)S(1)} %get-tuple-element.21.gain_ref.refs_2_, ...), custom_call_target="tpu_custom_call" | custom-call | flops 100663296 | bytes 1179648 | tf_op jit(solution)/shard_map/mine/pallas_call | solution.py:343
  24.3 4.4 %collective-permute-start.6 = (bf16[32,48,128]{2,1,0:T(8,128)(2,1)S(1)}, bf16[32,48,128]{2,1,0:T(8,128)(2,1)S(1)}, u32[]{:S(2)}, u32[]{:S(2)}) collective-permute-start(bf16[32,48,128]{2,1,0:T(8,128)(2,1)S(1)} %mine.2.refs_1_), channel_id=1, source_target_pairs={{8,12},{12,8},{0,4},{9,13},{13,9},{5,1},{6,2},{2,6},{10,14},{7,3},... | collective-permute-start | bytes 1179656 | tf_op jit(solution)/shard_map/ppermute | solution.py:271
  28.8 0.0 collective-permute-done.2.refs_1_
  28.8 0.0 copy-start.3
  28.8 0.0 copy-start.4
  28.8 3.0 %left.1.refs_3_ = bf16[128,48,128]{2,1,0:T(8,128)(2,1)S(1)} custom-call(s32[1]{0:T(128)S(6)} %copy.12.tokens_ref, bf16[48,48,128]{2,1,0:T(8,128)(2,1)S(1)} %get-tuple-element.24.refs_0_, bf16[48,48,128]{2,1,0:T(8,128)(2,1)S(1)} %collective-permute-done.2.refs_1_, f32[1,128]{1,0:T(1,128)S(1)} %get-tuple-element.21.gain_ref.refs_2_, ...), custom_call_target="tpu_custom_call" | custom-call | flops 301989888 | bytes 4718592 | tf_op jit(solution)/shard_map/left/pallas_call | solution.py:328
  31.8 0.0 collective-permute-done.3.far_ref
  31.8 0.0 collective-permute-done.4.near_ref
  31.8 0.5 %mine.3.refs_1_ = bf16[16,48,128]{2,1,0:T(8,128)(2,1)S(1)} custom-call(s32[1]{0:T(128)S(6)} %copy.12.tokens_ref, bf16[16,48,128]{2,1,0:T(8,128)(2,1)S(1)} %collective-permute-done.3.far_ref, bf16[16,48,128]{2,1,0:T(8,128)(2,1)S(1)} %collective-permute-done.4.near_ref, f32[1,128]{1,0:T(1,128)S(1)} %get-tuple-element.21.gain_ref.refs_2_, ...), custom_call_target="tpu_custom_call" | custom-call | flops 50331648 | bytes 589824 | tf_op jit(solution)/shard_map/mine/pallas_call | solution.py:343
  32.3 1.3 %collective-permute-start.5 = (bf16[16,48,128]{2,1,0:T(8,128)(2,1)S(1)}, bf16[16,48,128]{2,1,0:T(8,128)(2,1)S(1)}, u32[]{:S(2)}, u32[]{:S(2)}) collective-permute-start(bf16[16,48,128]{2,1,0:T(8,128)(2,1)S(1)} %mine.3.refs_1_), channel_id=1, source_target_pairs={{8,12},{12,8},{0,4},{9,13},{13,9},{5,1},{6,2},{2,6},{10,14},{7,3},... | collective-permute-start | bytes 589832 | tf_op jit(solution)/shard_map/ppermute | solution.py:271
  33.6 0.4 collective-permute-done.6.refs_2_
  34.0 0.0 copy-done.4
  34.0 2.6 %product.2.refs_8_ = bf16[48,32,128]{2,1,0:T(8,128)(2,1)S(1)} custom-call(bf16[48,48,128]{2,1,0:T(8,128)(2,1)S(1)} %get-tuple-element.19.refs_0_, bf16[32,48,128]{2,1,0:T(8,128)(2,1)S(1)} %mine.2.refs_1_, bf16[32,48,128]{2,1,0:T(8,128)(2,1)S(1)} %collective-permute-done.6.refs_2_, bf16[128,48,128]{2,1,0:T(8,128)(2,1)S(1)} %left.1.refs_3_, ...), custom_call_target="tpu_custom_call" | custom-call | flops 37748736 | bytes 2359296 | tf_op jit(solution)/shard_map/product/pallas_call | solution.py:380
  36.7 0.1 collective-permute-done.5.refs_2_
  36.8 2.6 %product.3 = bf16[48,48,128]{2,1,0:T(8,128)(2,1)} custom-call(bf16[48,48,128]{2,1,0:T(8,128)(2,1)S(1)} %get-tuple-element.19.refs_0_, bf16[16,48,128]{2,1,0:T(8,128)(2,1)S(1)} %mine.3.refs_1_, bf16[16,48,128]{2,1,0:T(8,128)(2,1)S(1)} %collective-permute-done.5.refs_2_, bf16[128,48,128]{2,1,0:T(8,128)(2,1)S(1)} %left.1.refs_3_, ...), custom_call_target="tpu_custom_call" | custom-call | flops 18874368 | bytes 2359296 | tf_op jit(solution)/shard_map/product/pallas_call | solution.py:380
  (5 shorter events, 0.0 us)
Async XLA Ops:
  0.0 11.6 %copy-start = (bf16[48,48,128]{2,1,0:T(8,128)(2,1)S(1)}, bf16[48,48,128]{2,1,0:T(8,128)(2,1)}, u32[]{:S(2)}) copy-start(bf16[48,48,128]{2,1,0:T(8,128)(2,1)} %refs_5_.1) | copy-start | bytes 1769476
  0.0 28.8 %collective-permute-start.2 = (bf16[48,48,128]{2,1,0:T(8,128)(2,1)}, bf16[48,48,128]{2,1,0:T(8,128)(2,1)S(1)}, u32[]{:S(2)}, u32[]{:S(2)}) collective-permute-start(bf16[48,48,128]{2,1,0:T(8,128)(2,1)} %refs_5_.1), channel_id=1, source_target_pairs={{0,3},{1,0},{2,1},{3,2},{4,7},{5,4},{6,5},{7,6},{8,11},{9,8},{10,9... | collective-permute-start | bytes 1769480 | tf_op jit(solution)/shard_map/ppermute | solution.py:33
  3.5 15.4 %collective-permute-start = (bf16[32,48,128]{2,1,0:T(8,128)(2,1)S(1)}, bf16[32,48,128]{2,1,0:T(8,128)(2,1)S(1)}, u32[]{:S(2)}, u32[]{:S(2)}) collective-permute-start(bf16[32,48,128]{2,1,0:T(8,128)(2,1)S(1)} %slice.11), channel_id=1, source_target_pairs={{0,8},{1,12},{5,9},{6,13},{10,6},{11,2},{15,7},{12,3},{16,24},{17,... | collective-permute-start | bytes 1179656 | tf_op jit(solution)/shard_map/ppermute | solution.py:271
  8.0 15.6 %collective-permute-start.1 = (bf16[32,48,128]{2,1,0:T(8,128)(2,1)S(1)}, bf16[32,48,128]{2,1,0:T(8,128)(2,1)S(1)}, u32[]{:S(2)}, u32[]{:S(2)}) collective-permute-start(bf16[32,48,128]{2,1,0:T(8,128)(2,1)S(1)} %slice.11), channel_id=1, source_target_pairs={{0,4},{1,0},{5,1},{6,5},{10,14},{11,10},{15,11},{12,15},{16,20},{1... | collective-permute-start | bytes 1179656 | tf_op jit(solution)/shard_map/ppermute | solution.py:271
  11.6 0.8 %copy-start.1 = (bf16[128,128]{1,0:T(8,128)(2,1)S(1)}, bf16[128,128]{1,0:T(8,128)(2,1)}, u32[]{:S(2)}) copy-start(bf16[128,128]{1,0:T(8,128)(2,1)} %gate_weights_ref.1) | copy-start | bytes 98308
  12.3 0.8 %copy-start.2 = (bf16[128,128]{1,0:T(8,128)(2,1)S(1)}, bf16[128,128]{1,0:T(8,128)(2,1)}, u32[]{:S(2)}) copy-start(bf16[128,128]{1,0:T(8,128)(2,1)} %refs_4_.1) | copy-start | bytes 98308
  13.1 0.7 %copy-start.5 = (f32[128]{0:T(128)S(1)}, f32[128]{0:T(128)}, u32[]{:S(2)}) copy-start(f32[128]{0:T(128)} %param.11) | copy-start | bytes 1540
  13.8 0.7 %copy-start.6 = (f32[128]{0:T(128)S(1)}, f32[128]{0:T(128)}, u32[]{:S(2)}) copy-start(f32[128]{0:T(128)} %param.12) | copy-start | bytes 1540
  15.6 16.2 %collective-permute-start.3 = (bf16[16,48,128]{2,1,0:T(8,128)(2,1)S(1)}, bf16[16,48,128]{2,1,0:T(8,128)(2,1)S(1)}, u32[]{:S(2)}, u32[]{:S(2)}) collective-permute-start(bf16[16,48,128]{2,1,0:T(8,128)(2,1)S(1)} %get-tuple-element.26), channel_id=1, source_target_pairs={{0,8},{1,12},{5,9},{6,13},{10,6},{11,2},{15,7},{12,3},{16,24},{17,... | collective-permute-start | bytes 589832 | tf_op jit(solution)/shard_map/ppermute | solution.py:271
  16.9 14.9 %collective-permute-start.4 = (bf16[16,48,128]{2,1,0:T(8,128)(2,1)S(1)}, bf16[16,48,128]{2,1,0:T(8,128)(2,1)S(1)}, u32[]{:S(2)}, u32[]{:S(2)}) collective-permute-start(bf16[16,48,128]{2,1,0:T(8,128)(2,1)S(1)} %get-tuple-element.26), channel_id=1, source_target_pairs={{0,4},{1,0},{5,1},{6,5},{10,14},{11,10},{15,11},{12,15},{16,20},{1... | collective-permute-start | bytes 589832 | tf_op jit(solution)/shard_map/ppermute | solution.py:271
  24.3 9.7 %collective-permute-start.6 = (bf16[32,48,128]{2,1,0:T(8,128)(2,1)S(1)}, bf16[32,48,128]{2,1,0:T(8,128)(2,1)S(1)}, u32[]{:S(2)}, u32[]{:S(2)}) collective-permute-start(bf16[32,48,128]{2,1,0:T(8,128)(2,1)S(1)} %mine.2.refs_1_), channel_id=1, source_target_pairs={{8,12},{12,8},{0,4},{9,13},{13,9},{5,1},{6,2},{2,6},{10,14},{7,3},... | collective-permute-start | bytes 1179656 | tf_op jit(solution)/shard_map/ppermute | solution.py:271
  28.8 5.2 %copy-start.3 = (f32[128]{0:T(128)S(1)}, f32[128]{0:T(128)}, u32[]{:S(2)}) copy-start(f32[128]{0:T(128)} %param.15) | copy-start | bytes 1540
  28.8 5.2 %copy-start.4 = (f32[128]{0:T(128)S(1)}, f32[128]{0:T(128)}, u32[]{:S(2)}) copy-start(f32[128]{0:T(128)} %param.16) | copy-start | bytes 1540
  32.3 4.5 %collective-permute-start.5 = (bf16[16,48,128]{2,1,0:T(8,128)(2,1)S(1)}, bf16[16,48,128]{2,1,0:T(8,128)(2,1)S(1)}, u32[]{:S(2)}, u32[]{:S(2)}) collective-permute-start(bf16[16,48,128]{2,1,0:T(8,128)(2,1)S(1)} %mine.3.refs_1_), channel_id=1, source_target_pairs={{8,12},{12,8},{0,4},{9,13},{13,9},{5,1},{6,2},{2,6},{10,14},{7,3},... | collective-permute-start | bytes 589832 | tf_op jit(solution)/shard_map/ppermute | solution.py:271

commit v22 on v21

--- a/solution.py
+++ b/solution.py
@@ -51,7 +51,7 @@
     return layer_norm(values, gain_ref[...], bias_ref[...]).astype(jnp.bfloat16)
 
 
-def mine_kernel(first, tokens_ref, far_ref, near_ref, gain_ref, bias_ref, weights_ref, out_ref):
+def mine_kernel(first, tokens_ref, near_ref, far_ref, gain_ref, bias_ref, weights_ref, out_ref):
     count, columns, _ = out_ref.shape
     col_pos, place = lax.axis_index("col"), hop_place()
     third_block = jnp.where((place == 0) | (place == 3), (col_pos + 1) % 4, col_pos)
@@ -302,7 +302,7 @@
     if by_hops:
         near, far, share = hops()
         soon = pair_state[: spans[0][1]]
-        arrived = [(move(soon, far), move(soon, near))]
+        arrived = [(move(soon, near), move(soon, far))]
     pairs = [pair_state]
     for _ in range(window - 1):
         pairs.append(shifted(pairs[-1], "col", -1))
@@ -338,7 +338,7 @@
             name="left",
         )(token_count, *pairs, in_gain, in_bias, left_weights)
 
-    def mine_of(first, far_pair, near_pair):
+    def mine_of(first, near_pair, far_pair):
         count = near_pair.shape[0]
         return pl.pallas_call(
             functools.partial(mine_kernel, first),
@@ -348,10 +348,10 @@
             compiler_params=params(2 * block),
             cost_estimate=cost(4 * count * columns * channels * hidden, 6 * count * columns * channels),
             name="mine",
-        )(token_count, far_pair, near_pair, in_gain, in_bias, right_weights)
+        )(token_count, near_pair, far_pair, in_gain, in_bias, right_weights)
 
     if by_hops:
-        arrived.append((move(later, far), move(later, near)))
+        arrived.append((move(later, near), move(later, far)))
         mine = [mine_of(0, *arrived[0])]
         pairs[0], mine[0] = lax.optimization_barrier((pairs[0], mine[0]))
         left = left_of(pairs)

time: 39.9 us -> 42.3 us (1.060)
  the two profiles are of different devices: /device:TPU:0 before, /device:TPU:6 now
where the time goes in v22:
time: 42.3 us; the launch traced here: 41.8 us
  starting transfers between devices  14.1 us (33%)
  waiting for transfers between devices  11.3 us (27%)
  Pallas kernels  10.7 us (25%)
  local copies, waits for them, and re-layouts  4.99 us (12%)
  between operations  0.81 us (2%)
    ppermute x6, starting transfers between devices, move(): lax.ppermute(array, ('row', 'col'), [(r * 4 + c, to_r * 4 + to_c) for (r,...  14.1 us
    ppermute x6, waiting for transfers between devices, move(): lax.ppermute(array, ('row', 'col'), [(r * 4 + c, to_r * 4 + to_c) for (r,...  11.3 us
    pallas_call x2, Pallas kernels, on_device(): pl.pallas_call(functools.partial(product_kernel, picks, place, len(band),...  5.24 us
    pallas_call x1, Pallas kernels, left_of(): pl.pallas_call(functools.partial(left_kernel, window), out_shape=jax.Shap...  3.02 us
    unnamed x15, local copies, waits for them, and re-layouts  2.95 us
    pallas_call x2, Pallas kernels, mine_of(): pl.pallas_call(functools.partial(mine_kernel, first), out_shape=jax.Shape...  1.2 us
    pallas_call x1, Pallas kernels, on_device(): pl.pallas_call(functools.partial(own_kernel, len(passed)), out_shape=[jax...  1.2 us
    slice x1, local copies, waits for them, and re-layouts, on_device(): soon = pair_state[:spans[0][1]]  1.16 us
  transfers between devices with their start and end apart: 7, of which 3 were waited for; matrix products, arithmetic and copies ran while one was open for 5% of the time, Pallas kernels for 19%

profile of v22, /device:TPU:6, one launch (start us, length us, event | category | flops | bytes accessed | tf_op | source)
XLA Modules:
  0.0 41.8 jit_solution(11342375729377465729)
XLA Ops:
  0.0 0.0 collective-permute-start.2
  0.0 1.2 %slice.11 = bf16[32,48,128]{2,1,0:T(8,128)(2,1)S(1)} slice(bf16[48,48,128]{2,1,0:T(8,128)(2,1)} %refs_5_.1), slice={[0:32], [0:48], [0:128]} | slice | bytes 786432 | tf_op jit(solution)/shard_map/slice | solution.py:304
  1.2 0.7 %collective-permute-start = (bf16[32,48,128]{2,1,0:T(8,128)(2,1)S(1)}, bf16[32,48,128]{2,1,0:T(8,128)(2,1)S(1)}, u32[]{:S(2)}, u32[]{:S(2)}) collective-permute-start(bf16[32,48,128]{2,1,0:T(8,128)(2,1)S(1)} %slice.11), channel_id=1, source_target_pairs={{0,4},{1,0},{5,1},{6,5},{10,14},{11,10},{15,11},{12,15},{16,20},{1... | collective-permute-start | bytes 1179656 | tf_op jit(solution)/shard_map/ppermute | solution.py:271
  1.9 1.3 %collective-permute-start.1 = (bf16[32,48,128]{2,1,0:T(8,128)(2,1)S(1)}, bf16[32,48,128]{2,1,0:T(8,128)(2,1)S(1)}, u32[]{:S(2)}, u32[]{:S(2)}) collective-permute-start(bf16[32,48,128]{2,1,0:T(8,128)(2,1)S(1)} %slice.11), channel_id=1, source_target_pairs={{0,8},{1,12},{5,9},{6,13},{10,6},{11,2},{15,7},{12,3},{16,24},{17,... | collective-permute-start | bytes 1179656 | tf_op jit(solution)/shard_map/ppermute | solution.py:271
  3.8 0.9 %fusion = (bf16[128,256]{1,0:T(8,128)(2,1)S(1)}, bf16[128,256]{1,0:T(8,128)(2,1)S(1)}) fusion(bf16[128,512]{1,0:T(8,128)(2,1)} %param.13), kind=kLoop, calls=%fused_computation | loop fusion | bytes 262144 | tf_op jit(solution)/shard_map/slice | solution.py:309
  4.7 0.1 copy.11
  4.8 0.0 copy-done
  4.8 0.0 copy-start.1
  4.8 0.7 %copy-done.1 = bf16[128,128]{1,0:T(8,128)(2,1)S(1)} copy-done((bf16[128,128]{1,0:T(8,128)(2,1)S(1)}, bf16[128,128]{1,0:T(8,128)(2,1)}, u32[]{:S(2)}) %copy-start.1) | copy-done | bytes 32792
  5.6 0.8 %copy-done.2 = bf16[128,128]{1,0:T(8,128)(2,1)S(1)} copy-done((bf16[128,128]{1,0:T(8,128)(2,1)S(1)}, bf16[128,128]{1,0:T(8,128)(2,1)}, u32[]{:S(2)}) %copy-start.2) | copy-done | bytes 32792
  6.3 0.7 %copy-done.5 = f32[128]{0:T(128)S(1)} copy-done((f32[128]{0:T(128)S(1)}, f32[128]{0:T(128)}, u32[]{:S(2)}) %copy-start.5) | copy-done | bytes 536
  7.0 0.7 %copy-done.6 = f32[128]{0:T(128)S(1)} copy-done((f32[128]{0:T(128)S(1)}, f32[128]{0:T(128)}, u32[]{:S(2)}) %copy-start.6) | copy-done | bytes 536
  7.7 1.2 %own.1 = (f32[48,48,128]{2,1,0:T(8,128)S(1)}, bf16[48,48,128]{2,1,0:T(8,128)(2,1)S(1)}, bf16[16,48,128]{2,1,0:T(8,128)(2,1)S(1)}, f32[1,128]{1,0:T(1,128)S(1)}, ...) custom-call(s32[1]{0:T(128)S(6)} %copy.12.tokens_ref, ...), custom_call_target="tpu_custom_call" | custom-call | flops 226492416 | bytes 2359296 | tf_op jit(solution)/shard_map/own/pallas_call | solution.py:311
  8.9 0.7 %collective-permute-start.3 = (bf16[16,48,128]{2,1,0:T(8,128)(2,1)S(1)}, bf16[16,48,128]{2,1,0:T(8,128)(2,1)S(1)}, u32[]{:S(2)}, u32[]{:S(2)}) collective-permute-start(bf16[16,48,128]{2,1,0:T(8,128)(2,1)S(1)} %get-tuple-element.26), channel_id=1, source_target_pairs={{0,4},{1,0},{5,1},{6,5},{10,14},{11,10},{15,11},{12,15},{16,20},{1... | collective-permute-start | bytes 589832 | tf_op jit(solution)/shard_map/ppermute | solution.py:271
  9.5 1.3 %collective-permute-start.4 = (bf16[16,48,128]{2,1,0:T(8,128)(2,1)S(1)}, bf16[16,48,128]{2,1,0:T(8,128)(2,1)S(1)}, u32[]{:S(2)}, u32[]{:S(2)}) collective-permute-start(bf16[16,48,128]{2,1,0:T(8,128)(2,1)S(1)} %get-tuple-element.26), channel_id=1, source_target_pairs={{0,8},{1,12},{5,9},{6,13},{10,6},{11,2},{15,7},{12,3},{16,24},{17,... | collective-permute-start | bytes 589832 | tf_op jit(solution)/shard_map/ppermute | solution.py:271
  10.8 0.0 collective-permute-done.near_ref
  10.9 8.3 %collective-permute-done.1.far_ref = bf16[32,48,128]{2,1,0:T(8,128)(2,1)S(1)} collective-permute-done((bf16[32,48,128]{2,1,0:T(8,128)(2,1)S(1)}, bf16[32,48,128]{2,1,0:T(8,128)(2,1)S(1)}, u32[]{:S(2)}, u32[]{:S(2)}) %collective-permute-start.1) | collective-permute-done | bytes 393248 | tf_op jit(solution)/shard_map/ppermute | solution.py:271
  19.1 0.7 %mine.2.refs_1_ = bf16[32,48,128]{2,1,0:T(8,128)(2,1)S(1)} custom-call(s32[1]{0:T(128)S(6)} %copy.12.tokens_ref, bf16[32,48,128]{2,1,0:T(8,128)(2,1)S(1)} %collective-permute-done.near_ref, bf16[32,48,128]{2,1,0:T(8,128)(2,1)S(1)} %collective-permute-done.1.far_ref, f32[1,128]{1,0:T(1,128)S(1)} %get-tuple-element.21.gain_ref.refs_2_, ...), custom_call_target="tpu_custom_call" | custom-call | flops 100663296 | bytes 1179648 | tf_op jit(solution)/shard_map/mine/pallas_call | solution.py:343
  19.8 8.2 %collective-permute-start.6 = (bf16[32,48,128]{2,1,0:T(8,128)(2,1)S(1)}, bf16[32,48,128]{2,1,0:T(8,128)(2,1)S(1)}, u32[]{:S(2)}, u32[]{:S(2)}) collective-permute-start(bf16[32,48,128]{2,1,0:T(8,128)(2,1)S(1)} %mine.2.refs_1_), channel_id=1, source_target_pairs={{8,12},{12,8},{0,4},{9,13},{13,9},{5,1},{6,2},{2,6},{10,14},{7,3},... | collective-permute-start | bytes 1179656 | tf_op jit(solution)/shard_map/ppermute | solution.py:271
  28.1 0.0 collective-permute-done.2.refs_1_
  28.1 0.0 copy-start.3
  28.1 0.0 copy-start.4
  28.1 3.0 %left.1.refs_3_ = bf16[128,48,128]{2,1,0:T(8,128)(2,1)S(1)} custom-call(s32[1]{0:T(128)S(6)} %copy.12.tokens_ref, bf16[48,48,128]{2,1,0:T(8,128)(2,1)S(1)} %get-tuple-element.24.refs_0_, bf16[48,48,128]{2,1,0:T(8,128)(2,1)S(1)} %collective-permute-done.2.refs_1_, f32[1,128]{1,0:T(1,128)S(1)} %get-tuple-element.21.gain_ref.refs_2_, ...), custom_call_target="tpu_custom_call" | custom-call | flops 301989888 | bytes 4718592 | tf_op jit(solution)/shard_map/left/pallas_call | solution.py:328
  31.1 0.0 collective-permute-done.3.near_ref
  31.2 0.0 collective-permute-done.4.far_ref
  31.2 0.5 %mine.3.refs_1_ = bf16[16,48,128]{2,1,0:T(8,128)(2,1)S(1)} custom-call(s32[1]{0:T(128)S(6)} %copy.12.tokens_ref, bf16[16,48,128]{2,1,0:T(8,128)(2,1)S(1)} %collective-permute-done.3.near_ref, bf16[16,48,128]{2,1,0:T(8,128)(2,1)S(1)} %collective-permute-done.4.far_ref, f32[1,128]{1,0:T(1,128)S(1)} %get-tuple-element.21.gain_ref.refs_2_, ...), custom_call_target="tpu_custom_call" | custom-call | flops 50331648 | bytes 589824 | tf_op jit(solution)/shard_map/mine/pallas_call | solution.py:343
  31.7 1.9 %collective-permute-start.5 = (bf16[16,48,128]{2,1,0:T(8,128)(2,1)S(1)}, bf16[16,48,128]{2,1,0:T(8,128)(2,1)S(1)}, u32[]{:S(2)}, u32[]{:S(2)}) collective-permute-start(bf16[16,48,128]{2,1,0:T(8,128)(2,1)S(1)} %mine.3.refs_1_), channel_id=1, source_target_pairs={{8,12},{12,8},{0,4},{9,13},{13,9},{5,1},{6,2},{2,6},{10,14},{7,3},... | collective-permute-start | bytes 589832 | tf_op jit(solution)/shard_map/ppermute | solution.py:271
  33.6 2.3 %collective-permute-done.6.refs_2_ = bf16[32,48,128]{2,1,0:T(8,128)(2,1)S(1)} collective-permute-done((bf16[32,48,128]{2,1,0:T(8,128)(2,1)S(1)}, bf16[32,48,128]{2,1,0:T(8,128)(2,1)S(1)}, u32[]{:S(2)}, u32[]{:S(2)}) %collective-permute-start.6) | collective-permute-done | bytes 393248 | tf_op jit(solution)/shard_map/ppermute | solution.py:271
  35.9 0.0 copy-done.3
  35.9 2.6 %product.2.refs_8_ = bf16[48,32,128]{2,1,0:T(8,128)(2,1)S(1)} custom-call(bf16[48,48,128]{2,1,0:T(8,128)(2,1)S(1)} %get-tuple-element.19.refs_0_, bf16[32,48,128]{2,1,0:T(8,128)(2,1)S(1)} %mine.2.refs_1_, bf16[32,48,128]{2,1,0:T(8,128)(2,1)S(1)} %collective-permute-done.6.refs_2_, bf16[128,48,128]{2,1,0:T(8,128)(2,1)S(1)} %left.1.refs_3_, ...), custom_call_target="tpu_custom_call" | custom-call | flops 37748736 | bytes 2359296 | tf_op jit(solution)/shard_map/product/pallas_call | solution.py:380
  38.6 0.7 %collective-permute-done.5.refs_2_ = bf16[16,48,128]{2,1,0:T(8,128)(2,1)S(1)} collective-permute-done((bf16[16,48,128]{2,1,0:T(8,128)(2,1)S(1)}, bf16[16,48,128]{2,1,0:T(8,128)(2,1)S(1)}, u32[]{:S(2)}, u32[]{:S(2)}) %collective-permute-start.5) | collective-permute-done | bytes 196640 | tf_op jit(solution)/shard_map/ppermute | solution.py:271
  39.2 2.6 %product.3 = bf16[48,48,128]{2,1,0:T(8,128)(2,1)} custom-call(bf16[48,48,128]{2,1,0:T(8,128)(2,1)S(1)} %get-tuple-element.19.refs_0_, bf16[16,48,128]{2,1,0:T(8,128)(2,1)S(1)} %mine.3.refs_1_, bf16[16,48,128]{2,1,0:T(8,128)(2,1)S(1)} %collective-permute-done.5.refs_2_, bf16[128,48,128]{2,1,0:T(8,128)(2,1)S(1)} %left.1.refs_3_, ...), custom_call_target="tpu_custom_call" | custom-call | flops 18874368 | bytes 2359296 | tf_op jit(solution)/shard_map/product/pallas_call | solution.py:380
  (5 shorter events, 0.0 us)
Async XLA Ops:
  0.0 4.8 %copy-start = (bf16[48,48,128]{2,1,0:T(8,128)(2,1)S(1)}, bf16[48,48,128]{2,1,0:T(8,128)(2,1)}, u32[]{:S(2)}) copy-start(bf16[48,48,128]{2,1,0:T(8,128)(2,1)} %refs_5_.1) | copy-start | bytes 1769476
  0.0 28.1 %collective-permute-start.2 = (bf16[48,48,128]{2,1,0:T(8,128)(2,1)}, bf16[48,48,128]{2,1,0:T(8,128)(2,1)S(1)}, u32[]{:S(2)}, u32[]{:S(2)}) collective-permute-start(bf16[48,48,128]{2,1,0:T(8,128)(2,1)} %refs_5_.1), channel_id=1, source_target_pairs={{0,3},{1,0},{2,1},{3,2},{4,7},{5,4},{6,5},{7,6},{8,11},{9,8},{10,9... | collective-permute-start | bytes 1769480 | tf_op jit(solution)/shard_map/ppermute | solution.py:33
  1.2 9.7 %collective-permute-start = (bf16[32,48,128]{2,1,0:T(8,128)(2,1)S(1)}, bf16[32,48,128]{2,1,0:T(8,128)(2,1)S(1)}, u32[]{:S(2)}, u32[]{:S(2)}) collective-permute-start(bf16[32,48,128]{2,1,0:T(8,128)(2,1)S(1)} %slice.11), channel_id=1, source_target_pairs={{0,4},{1,0},{5,1},{6,5},{10,14},{11,10},{15,11},{12,15},{16,20},{1... | collective-permute-start | bytes 1179656 | tf_op jit(solution)/shard_map/ppermute | solution.py:271
  1.9 17.3 %collective-permute-start.1 = (bf16[32,48,128]{2,1,0:T(8,128)(2,1)S(1)}, bf16[32,48,128]{2,1,0:T(8,128)(2,1)S(1)}, u32[]{:S(2)}, u32[]{:S(2)}) collective-permute-start(bf16[32,48,128]{2,1,0:T(8,128)(2,1)S(1)} %slice.11), channel_id=1, source_target_pairs={{0,8},{1,12},{5,9},{6,13},{10,6},{11,2},{15,7},{12,3},{16,24},{17,... | collective-permute-start | bytes 1179656 | tf_op jit(solution)/shard_map/ppermute | solution.py:271
  4.8 0.8 %copy-start.1 = (bf16[128,128]{1,0:T(8,128)(2,1)S(1)}, bf16[128,128]{1,0:T(8,128)(2,1)}, u32[]{:S(2)}) copy-start(bf16[128,128]{1,0:T(8,128)(2,1)} %gate_weights_ref.1) | copy-start | bytes 98308
  5.6 0.8 %copy-start.2 = (bf16[128,128]{1,0:T(8,128)(2,1)S(1)}, bf16[128,128]{1,0:T(8,128)(2,1)}, u32[]{:S(2)}) copy-start(bf16[128,128]{1,0:T(8,128)(2,1)} %refs_4_.1) | copy-start | bytes 98308
  6.3 0.7 %copy-start.5 = (f32[128]{0:T(128)S(1)}, f32[128]{0:T(128)}, u32[]{:S(2)}) copy-start(f32[128]{0:T(128)} %param.11) | copy-start | bytes 1540
  7.0 0.7 %copy-start.6 = (f32[128]{0:T(128)S(1)}, f32[128]{0:T(128)}, u32[]{:S(2)}) copy-start(f32[128]{0:T(128)} %param.12) | copy-start | bytes 1540
  8.9 22.3 %collective-permute-start.3 = (bf16[16,48,128]{2,1,0:T(8,128)(2,1)S(1)}, bf16[16,48,128]{2,1,0:T(8,128)(2,1)S(1)}, u32[]{:S(2)}, u32[]{:S(2)}) collective-permute-start(bf16[16,48,128]{2,1,0:T(8,128)(2,1)S(1)} %get-tuple-element.26), channel_id=1, source_target_pairs={{0,4},{1,0},{5,1},{6,5},{10,14},{11,10},{15,11},{12,15},{16,20},{1... | collective-permute-start | bytes 589832 | tf_op jit(solution)/shard_map/ppermute | solution.py:271
  9.5 21.6 %collective-permute-start.4 = (bf16[16,48,128]{2,1,0:T(8,128)(2,1)S(1)}, bf16[16,48,128]{2,1,0:T(8,128)(2,1)S(1)}, u32[]{:S(2)}, u32[]{:S(2)}) collective-permute-start(bf16[16,48,128]{2,1,0:T(8,128)(2,1)S(1)} %get-tuple-element.26), channel_id=1, source_target_pairs={{0,8},{1,12},{5,9},{6,13},{10,6},{11,2},{15,7},{12,3},{16,24},{17,... | collective-permute-start | bytes 589832 | tf_op jit(solution)/shard_map/ppermute | solution.py:271
  19.8 16.1 %collective-permute-start.6 = (bf16[32,48,128]{2,1,0:T(8,128)(2,1)S(1)}, bf16[32,48,128]{2,1,0:T(8,128)(2,1)S(1)}, u32[]{:S(2)}, u32[]{:S(2)}) collective-permute-start(bf16[32,48,128]{2,1,0:T(8,128)(2,1)S(1)} %mine.2.refs_1_), channel_id=1, source_target_pairs={{8,12},{12,8},{0,4},{9,13},{13,9},{5,1},{6,2},{2,6},{10,14},{7,3},... | collective-permute-start | bytes 1179656 | tf_op jit(solution)/shard_map/ppermute | solution.py:271
  28.1 7.8 %copy-start.3 = (f32[128]{0:T(128)S(1)}, f32[128]{0:T(128)}, u32[]{:S(2)}) copy-start(f32[128]{0:T(128)} %param.15) | copy-start | bytes 1540
  28.1 7.8 %copy-start.4 = (f32[128]{0:T(128)S(1)}, f32[128]{0:T(128)}, u32[]{:S(2)}) copy-start(f32[128]{0:T(128)} %param.16) | copy-start | bytes 1540
  31.7 7.6 %collective-permute-start.5 = (bf16[16,48,128]{2,1,0:T(8,128)(2,1)S(1)}, bf16[16,48,128]{2,1,0:T(8,128)(2,1)S(1)}, u32[]{:S(2)}, u32[]{:S(2)}) collective-permute-start(bf16[16,48,128]{2,1,0:T(8,128)(2,1)S(1)} %mine.3.refs_1_), channel_id=1, source_target_pairs={{8,12},{12,8},{0,4},{9,13},{13,9},{5,1},{6,2},{2,6},{10,14},{7,3},... | collective-permute-start | bytes 589832 | tf_op jit(solution)/shard_map/ppermute | solution.py:271

commit v23 on v21

--- a/solution.py
+++ b/solution.py
@@ -307,7 +307,7 @@
     for _ in range(window - 1):
         pairs.append(shifted(pairs[-1], "col", -1))
     left_weights, right_weights = in_weights[:, : 2 * hidden].T, in_weights[:, 2 * hidden :]
-    passed = [in_gain, in_bias, right_weights, left_weights, out_weights, pair_state]
+    passed = [in_gain, in_bias, right_weights, left_weights, pair_state]
     gate, right, later, *handed = pl.pallas_call(
         functools.partial(own_kernel, len(passed)),
         out_shape=[
@@ -322,7 +322,7 @@
         cost_estimate=cost(6 * tokens * channels * hidden, 8 * tokens * channels),
         name="own",
     )(token_count, pair_state, gate_weights, *passed)
-    in_gain, in_bias, right_weights, left_weights, out_weights, pairs[0] = handed
+    in_gain, in_bias, right_weights, left_weights, pairs[0] = handed
 
     def left_of(pairs):
         return pl.pallas_call(

time: 39.9 us -> 40 us (level)
  waiting for transfers between devices: 5.26 us -> 6.22 us
  local copies, waits for them, and re-layouts: 4.89 us -> 4.13 us
    ppermute x6, waiting for transfers between devices: 5.26 us -> 6.22 us  [move(): lax.ppermute(array, ('row', 'col'), [(r * 4 + c, to_r * 4 + to_c) for (r,...]
    unnamed x15, local copies, waits for them, and re-layouts: 2.95 us -> 2.2 us
where the time goes in v23:
time: 40 us; the launch traced here: 39.6 us
  starting transfers between devices  17.8 us (44%)
  Pallas kernels  10.7 us (27%)
  waiting for transfers between devices  6.22 us (16%)
  local copies, waits for them, and re-layouts  4.13 us (10%)
  between operations  0.82 us (2%)
    ppermute x6, starting transfers between devices, move(): lax.ppermute(array, ('row', 'col'), [(r * 4 + c, to_r * 4 + to_c) for (r,...  15.4 us
    ppermute x6, waiting for transfers between devices, move(): lax.ppermute(array, ('row', 'col'), [(r * 4 + c, to_r * 4 + to_c) for (r,...  6.22 us
    pallas_call x2, Pallas kernels, on_device(): pl.pallas_call(functools.partial(product_kernel, picks, place, len(band),...  5.24 us
    pallas_call x1, Pallas kernels, left_of(): pl.pallas_call(functools.partial(left_kernel, window), out_shape=jax.Shap...  3.01 us
    ppermute x1, starting transfers between devices, shifted(): lax.ppermute(array, axis, [(i, (i + by) % devices) for i in range(devices)])  2.41 us
    unnamed x15, local copies, waits for them, and re-layouts  2.2 us
    pallas_call x1, Pallas kernels, on_device(): pl.pallas_call(functools.partial(own_kernel, len(passed)), out_shape=[jax...  1.21 us
    pallas_call x2, Pallas kernels, mine_of(): pl.pallas_call(functools.partial(mine_kernel, first), out_shape=jax.Shape...  1.2 us
  transfers between devices with their start and end apart: 7, of which 3 were waited for; matrix products, arithmetic and copies ran while one was open for 5% of the time, Pallas kernels for 20%

profile of v23, /device:TPU:0, one launch (start us, length us, event | category | flops | bytes accessed | tf_op | source)
XLA Modules:
  0.0 39.6 jit_solution(4720678280035746925)
XLA Ops:
  0.0 2.4 %collective-permute-start.2 = (bf16[48,48,128]{2,1,0:T(8,128)(2,1)}, bf16[48,48,128]{2,1,0:T(8,128)(2,1)S(1)}, u32[]{:S(2)}, u32[]{:S(2)}) collective-permute-start(bf16[48,48,128]{2,1,0:T(8,128)(2,1)} %refs_4_.1), channel_id=1, source_target_pairs={{0,3},{1,0},{2,1},{3,2},{4,7},{5,4},{6,5},{7,6},{8,11},{9,8},{10,9... | collective-permute-start | bytes 1769480 | tf_op jit(solution)/shard_map/ppermute | solution.py:33
  2.4 1.1 %slice.11 = bf16[32,48,128]{2,1,0:T(8,128)(2,1)S(1)} slice(bf16[48,48,128]{2,1,0:T(8,128)(2,1)} %refs_4_.1), slice={[0:32], [0:48], [0:128]} | slice | bytes 786432 | tf_op jit(solution)/shard_map/slice | solution.py:304
  3.5 4.5 %collective-permute-start = (bf16[32,48,128]{2,1,0:T(8,128)(2,1)S(1)}, bf16[32,48,128]{2,1,0:T(8,128)(2,1)S(1)}, u32[]{:S(2)}, u32[]{:S(2)}) collective-permute-start(bf16[32,48,128]{2,1,0:T(8,128)(2,1)S(1)} %slice.11), channel_id=1, source_target_pairs={{0,8},{1,12},{5,9},{6,13},{10,6},{11,2},{15,7},{12,3},{16,24},{17,... | collective-permute-start | bytes 1179656 | tf_op jit(solution)/shard_map/ppermute | solution.py:271
  8.0 1.9 %collective-permute-start.1 = (bf16[32,48,128]{2,1,0:T(8,128)(2,1)S(1)}, bf16[32,48,128]{2,1,0:T(8,128)(2,1)S(1)}, u32[]{:S(2)}, u32[]{:S(2)}) collective-permute-start(bf16[32,48,128]{2,1,0:T(8,128)(2,1)S(1)} %slice.11), channel_id=1, source_target_pairs={{0,4},{1,0},{5,1},{6,5},{10,14},{11,10},{15,11},{12,15},{16,20},{1... | collective-permute-start | bytes 1179656 | tf_op jit(solution)/shard_map/ppermute | solution.py:271
  10.6 0.9 %fusion = (bf16[128,256]{1,0:T(8,128)(2,1)S(1)}, bf16[128,256]{1,0:T(8,128)(2,1)S(1)}) fusion(bf16[128,512]{1,0:T(8,128)(2,1)} %param.13), kind=kLoop, calls=%fused_computation | loop fusion | bytes 262144 | tf_op jit(solution)/shard_map/slice | solution.py:309
  11.5 0.1 copy.11
  11.6 0.0 copy-done
  11.6 0.0 copy-start.2
  11.6 0.7 %copy-done.2 = bf16[128,128]{1,0:T(8,128)(2,1)S(1)} copy-done((bf16[128,128]{1,0:T(8,128)(2,1)S(1)}, bf16[128,128]{1,0:T(8,128)(2,1)}, u32[]{:S(2)}) %copy-start.2) | copy-done | bytes 32792
  12.3 0.7 %copy-done.5 = f32[128]{0:T(128)S(1)} copy-done((f32[128]{0:T(128)S(1)}, f32[128]{0:T(128)}, u32[]{:S(2)}) %copy-start.5) | copy-done | bytes 536
  13.0 0.7 %copy-done.6 = f32[128]{0:T(128)S(1)} copy-done((f32[128]{0:T(128)S(1)}, f32[128]{0:T(128)}, u32[]{:S(2)}) %copy-start.6) | copy-done | bytes 536
  13.7 1.2 %own.1 = (f32[48,48,128]{2,1,0:T(8,128)S(1)}, bf16[48,48,128]{2,1,0:T(8,128)(2,1)S(1)}, bf16[16,48,128]{2,1,0:T(8,128)(2,1)S(1)}, f32[1,128]{1,0:T(1,128)S(1)}, ...) custom-call(s32[1]{0:T(128)S(6)} %copy.12.tokens_ref, ...), custom_call_target="tpu_custom_call" | custom-call | flops 226492416 | bytes 2359296 | tf_op jit(solution)/shard_map/own/pallas_call | solution.py:311
  14.9 1.3 %collective-permute-start.3 = (bf16[16,48,128]{2,1,0:T(8,128)(2,1)S(1)}, bf16[16,48,128]{2,1,0:T(8,128)(2,1)S(1)}, u32[]{:S(2)}, u32[]{:S(2)}) collective-permute-start(bf16[16,48,128]{2,1,0:T(8,128)(2,1)S(1)} %get-tuple-element.25), channel_id=1, source_target_pairs={{0,8},{1,12},{5,9},{6,13},{10,6},{11,2},{15,7},{12,3},{16,24},{17,... | collective-permute-start | bytes 589832 | tf_op jit(solution)/shard_map/ppermute | solution.py:271
  16.2 1.9 %collective-permute-start.4 = (bf16[16,48,128]{2,1,0:T(8,128)(2,1)S(1)}, bf16[16,48,128]{2,1,0:T(8,128)(2,1)S(1)}, u32[]{:S(2)}, u32[]{:S(2)}) collective-permute-start(bf16[16,48,128]{2,1,0:T(8,128)(2,1)S(1)} %get-tuple-element.25), channel_id=1, source_target_pairs={{0,4},{1,0},{5,1},{6,5},{10,14},{11,10},{15,11},{12,15},{16,20},{1... | collective-permute-start | bytes 589832 | tf_op jit(solution)/shard_map/ppermute | solution.py:271
  18.1 0.0 collective-permute-done.far_ref
  18.1 5.7 %collective-permute-done.1.near_ref = bf16[32,48,128]{2,1,0:T(8,128)(2,1)S(1)} collective-permute-done((bf16[32,48,128]{2,1,0:T(8,128)(2,1)S(1)}, bf16[32,48,128]{2,1,0:T(8,128)(2,1)S(1)}, u32[]{:S(2)}, u32[]{:S(2)}) %collective-permute-start.1) | collective-permute-done | bytes 393248 | tf_op jit(solution)/shard_map/ppermute | solution.py:271
  23.8 0.7 %mine.2.refs_1_ = bf16[32,48,128]{2,1,0:T(8,128)(2,1)S(1)} custom-call(s32[1]{0:T(128)S(6)} %copy.12.tokens_ref, bf16[32,48,128]{2,1,0:T(8,128)(2,1)S(1)} %collective-permute-done.far_ref, bf16[32,48,128]{2,1,0:T(8,128)(2,1)S(1)} %collective-permute-done.1.near_ref, f32[1,128]{1,0:T(1,128)S(1)} %get-tuple-element.20.gain_ref.refs_2_, ...), custom_call_target="tpu_custom_call" | custom-call | flops 100663296 | bytes 1179648 | tf_op jit(solution)/shard_map/mine/pallas_call | solution.py:343
  24.5 4.4 %collective-permute-start.6 = (bf16[32,48,128]{2,1,0:T(8,128)(2,1)S(1)}, bf16[32,48,128]{2,1,0:T(8,128)(2,1)S(1)}, u32[]{:S(2)}, u32[]{:S(2)}) collective-permute-start(bf16[32,48,128]{2,1,0:T(8,128)(2,1)S(1)} %mine.2.refs_1_), channel_id=1, source_target_pairs={{8,12},{12,8},{0,4},{9,13},{13,9},{5,1},{6,2},{2,6},{10,14},{7,3},... | collective-permute-start | bytes 1179656 | tf_op jit(solution)/shard_map/ppermute | solution.py:271
  29.0 0.0 collective-permute-done.2.refs_1_
  29.0 0.0 copy-start.1
  29.0 0.0 copy-start.3
  29.0 0.0 copy-start.4
  29.0 3.0 %left.1.refs_3_ = bf16[128,48,128]{2,1,0:T(8,128)(2,1)S(1)} custom-call(s32[1]{0:T(128)S(6)} %copy.12.tokens_ref, bf16[48,48,128]{2,1,0:T(8,128)(2,1)S(1)} %get-tuple-element.23.refs_0_, bf16[48,48,128]{2,1,0:T(8,128)(2,1)S(1)} %collective-permute-done.2.refs_1_, f32[1,128]{1,0:T(1,128)S(1)} %get-tuple-element.20.gain_ref.refs_2_, ...), custom_call_target="tpu_custom_call" | custom-call | flops 301989888 | bytes 4718592 | tf_op jit(solution)/shard_map/left/pallas_call | solution.py:328
  32.0 0.0 collective-permute-done.3.far_ref
  32.0 0.0 collective-permute-done.4.near_ref
  32.0 0.5 %mine.3.refs_1_ = bf16[16,48,128]{2,1,0:T(8,128)(2,1)S(1)} custom-call(s32[1]{0:T(128)S(6)} %copy.12.tokens_ref, bf16[16,48,128]{2,1,0:T(8,128)(2,1)S(1)} %collective-permute-done.3.far_ref, bf16[16,48,128]{2,1,0:T(8,128)(2,1)S(1)} %collective-permute-done.4.near_ref, f32[1,128]{1,0:T(1,128)S(1)} %get-tuple-element.20.gain_ref.refs_2_, ...), custom_call_target="tpu_custom_call" | custom-call | flops 50331648 | bytes 589824 | tf_op jit(solution)/shard_map/mine/pallas_call | solution.py:343
  32.5 1.3 %collective-permute-start.5 = (bf16[16,48,128]{2,1,0:T(8,128)(2,1)S(1)}, bf16[16,48,128]{2,1,0:T(8,128)(2,1)S(1)}, u32[]{:S(2)}, u32[]{:S(2)}) collective-permute-start(bf16[16,48,128]{2,1,0:T(8,128)(2,1)S(1)} %mine.3.refs_1_), channel_id=1, source_target_pairs={{8,12},{12,8},{0,4},{9,13},{13,9},{5,1},{6,2},{2,6},{10,14},{7,3},... | collective-permute-start | bytes 589832 | tf_op jit(solution)/shard_map/ppermute | solution.py:271
  33.9 0.4 collective-permute-done.6.refs_2_
  34.2 0.0 copy-done.1
  34.2 2.6 %product.2.refs_8_ = bf16[48,32,128]{2,1,0:T(8,128)(2,1)S(1)} custom-call(bf16[48,48,128]{2,1,0:T(8,128)(2,1)S(1)} %get-tuple-element.18.refs_0_, bf16[32,48,128]{2,1,0:T(8,128)(2,1)S(1)} %mine.2.refs_1_, bf16[32,48,128]{2,1,0:T(8,128)(2,1)S(1)} %collective-permute-done.6.refs_2_, bf16[128,48,128]{2,1,0:T(8,128)(2,1)S(1)} %left.1.refs_3_, ...), custom_call_target="tpu_custom_call" | custom-call | flops 37748736 | bytes 2359296 | tf_op jit(solution)/shard_map/product/pallas_call | solution.py:380
  36.9 0.2 collective-permute-done.5.refs_2_
  37.0 2.6 %product.3 = bf16[48,48,128]{2,1,0:T(8,128)(2,1)} custom-call(bf16[48,48,128]{2,1,0:T(8,128)(2,1)S(1)} %get-tuple-element.18.refs_0_, bf16[16,48,128]{2,1,0:T(8,128)(2,1)S(1)} %mine.3.refs_1_, bf16[16,48,128]{2,1,0:T(8,128)(2,1)S(1)} %collective-permute-done.5.refs_2_, bf16[128,48,128]{2,1,0:T(8,128)(2,1)S(1)} %left.1.refs_3_, ...), custom_call_target="tpu_custom_call" | custom-call | flops 18874368 | bytes 2359296 | tf_op jit(solution)/shard_map/product/pallas_call | solution.py:380
  (5 shorter events, 0.0 us)
Async XLA Ops:
  0.0 11.6 %copy-start = (bf16[48,48,128]{2,1,0:T(8,128)(2,1)S(1)}, bf16[48,48,128]{2,1,0:T(8,128)(2,1)}, u32[]{:S(2)}) copy-start(bf16[48,48,128]{2,1,0:T(8,128)(2,1)} %refs_4_.1) | copy-start | bytes 1769476
  0.0 29.0 %collective-permute-start.2 = (bf16[48,48,128]{2,1,0:T(8,128)(2,1)}, bf16[48,48,128]{2,1,0:T(8,128)(2,1)S(1)}, u32[]{:S(2)}, u32[]{:S(2)}) collective-permute-start(bf16[48,48,128]{2,1,0:T(8,128)(2,1)} %refs_4_.1), channel_id=1, source_target_pairs={{0,3},{1,0},{2,1},{3,2},{4,7},{5,4},{6,5},{7,6},{8,11},{9,8},{10,9... | collective-permute-start | bytes 1769480 | tf_op jit(solution)/shard_map/ppermute | solution.py:33
  3.5 14.6 %collective-permute-start = (bf16[32,48,128]{2,1,0:T(8,128)(2,1)S(1)}, bf16[32,48,128]{2,1,0:T(8,128)(2,1)S(1)}, u32[]{:S(2)}, u32[]{:S(2)}) collective-permute-start(bf16[32,48,128]{2,1,0:T(8,128)(2,1)S(1)} %slice.11), channel_id=1, source_target_pairs={{0,8},{1,12},{5,9},{6,13},{10,6},{11,2},{15,7},{12,3},{16,24},{17,... | collective-permute-start | bytes 1179656 | tf_op jit(solution)/shard_map/ppermute | solution.py:271
  8.0 15.8 %collective-permute-start.1 = (bf16[32,48,128]{2,1,0:T(8,128)(2,1)S(1)}, bf16[32,48,128]{2,1,0:T(8,128)(2,1)S(1)}, u32[]{:S(2)}, u32[]{:S(2)}) collective-permute-start(bf16[32,48,128]{2,1,0:T(8,128)(2,1)S(1)} %slice.11), channel_id=1, source_target_pairs={{0,4},{1,0},{5,1},{6,5},{10,14},{11,10},{15,11},{12,15},{16,20},{1... | collective-permute-start | bytes 1179656 | tf_op jit(solution)/shard_map/ppermute | solution.py:271
  11.6 0.8 %copy-start.2 = (bf16[128,128]{1,0:T(8,128)(2,1)S(1)}, bf16[128,128]{1,0:T(8,128)(2,1)}, u32[]{:S(2)}) copy-start(bf16[128,128]{1,0:T(8,128)(2,1)} %gate_weights_ref.1) | copy-start | bytes 98308
  12.3 0.7 %copy-start.5 = (f32[128]{0:T(128)S(1)}, f32[128]{0:T(128)}, u32[]{:S(2)}) copy-start(f32[128]{0:T(128)} %param.11) | copy-start | bytes 1540
  13.0 0.7 %copy-start.6 = (f32[128]{0:T(128)S(1)}, f32[128]{0:T(128)}, u32[]{:S(2)}) copy-start(f32[128]{0:T(128)} %param.12) | copy-start | bytes 1540
  14.9 17.2 %collective-permute-start.3 = (bf16[16,48,128]{2,1,0:T(8,128)(2,1)S(1)}, bf16[16,48,128]{2,1,0:T(8,128)(2,1)S(1)}, u32[]{:S(2)}, u32[]{:S(2)}) collective-permute-start(bf16[16,48,128]{2,1,0:T(8,128)(2,1)S(1)} %get-tuple-element.25), channel_id=1, source_target_pairs={{0,8},{1,12},{5,9},{6,13},{10,6},{11,2},{15,7},{12,3},{16,24},{17,... | collective-permute-start | bytes 589832 | tf_op jit(solution)/shard_map/ppermute | solution.py:271
  16.2 15.9 %collective-permute-start.4 = (bf16[16,48,128]{2,1,0:T(8,128)(2,1)S(1)}, bf16[16,48,128]{2,1,0:T(8,128)(2,1)S(1)}, u32[]{:S(2)}, u32[]{:S(2)}) collective-permute-start(bf16[16,48,128]{2,1,0:T(8,128)(2,1)S(1)} %get-tuple-element.25), channel_id=1, source_target_pairs={{0,4},{1,0},{5,1},{6,5},{10,14},{11,10},{15,11},{12,15},{16,20},{1... | collective-permute-start | bytes 589832 | tf_op jit(solution)/shard_map/ppermute | solution.py:271
  24.5 9.7 %collective-permute-start.6 = (bf16[32,48,128]{2,1,0:T(8,128)(2,1)S(1)}, bf16[32,48,128]{2,1,0:T(8,128)(2,1)S(1)}, u32[]{:S(2)}, u32[]{:S(2)}) collective-permute-start(bf16[32,48,128]{2,1,0:T(8,128)(2,1)S(1)} %mine.2.refs_1_), channel_id=1, source_target_pairs={{8,12},{12,8},{0,4},{9,13},{13,9},{5,1},{6,2},{2,6},{10,14},{7,3},... | collective-permute-start | bytes 1179656 | tf_op jit(solution)/shard_map/ppermute | solution.py:271
  29.0 5.2 %copy-start.1 = (bf16[128,128]{1,0:T(8,128)(2,1)S(1)}, bf16[128,128]{1,0:T(8,128)(2,1)}, u32[]{:S(2)}) copy-start(bf16[128,128]{1,0:T(8,128)(2,1)} %refs_7_.3) | copy-start | bytes 98308
  29.0 5.2 %copy-start.3 = (f32[128]{0:T(128)S(1)}, f32[128]{0:T(128)}, u32[]{:S(2)}) copy-start(f32[128]{0:T(128)} %param.15) | copy-start | bytes 1540
  29.0 5.2 %copy-start.4 = (f32[128]{0:T(128)S(1)}, f32[128]{0:T(128)}, u32[]{:S(2)}) copy-start(f32[128]{0:T(128)} %param.16) | copy-start | bytes 1540
  32.5 4.5 %collective-permute-start.5 = (bf16[16,48,128]{2,1,0:T(8,128)(2,1)S(1)}, bf16[16,48,128]{2,1,0:T(8,128)(2,1)S(1)}, u32[]{:S(2)}, u32[]{:S(2)}) collective-permute-start(bf16[16,48,128]{2,1,0:T(8,128)(2,1)S(1)} %mine.3.refs_1_), channel_id=1, source_target_pairs={{8,12},{12,8},{0,4},{9,13},{13,9},{5,1},{6,2},{2,6},{10,14},{7,3},... | collective-permute-start | bytes 589832 | tf_op jit(solution)/shard_map/ppermute | solution.py:271
